TPU v7x, 32 devices: a whole 2x2x4 slice. The times are simulated.
32 devices in a mesh: tm: 8 (over z, x), chan: 4 (over y, core).
Axes of the slice: x: 2, y: 2, z: 4, core: 2. Of those that a mesh axis runs over, the one named last changes fastest.
Arguments:
- features: bfloat16 [512, 4, 512], P('tm', None, 'chan'), may hold values from -6 to 6
- conv1_weight: bfloat16 [3, 3, 512, 1024], P(None, None, None, 'chan'), may hold values from -0.09375 to 0.09375
- norm1_gain: float32 [1024], P('chan'), may hold values from 0.1 to 1.9
- norm1_bias: float32 [1024], P('chan'), may hold values from -0.5 to 0.5
- conv2_weight: bfloat16 [3, 3, 1024, 1024], P(None, None, None, 'chan'), may hold values from -0.0625 to 0.0625
- norm2_gain: float32 [1024], P('chan'), may hold values from 0.1 to 1.9
- norm2_bias: float32 [1024], P('chan'), may hold values from -0.5 to 0.5
- clip_starts: int32 [3], replicated, may hold values from 0 to 506, as said below
- valid: int32 [512], P('tm'), may hold values from 0 to 1, as said below
- readout_grad: float32 [256, 1024], P('tm', 'chan'), may hold values from -6 to 6
Outputs:
- readout: float32 [256, 1024], P('tm', 'chan')
- features_grad: float32 [512, 4, 512], P('tm', None, 'chan')
- conv1_weight_grad: float32 [3, 3, 512, 1024], P(None, None, None, 'chan')
- norm1_gain_grad: float32 [1024], P('chan')
- norm1_bias_grad: float32 [1024], P('chan')
- conv2_weight_grad: float32 [3, 3, 1024, 1024], P(None, None, None, 'chan')
- norm2_gain_grad: float32 [1024], P('chan')
- norm2_bias_grad: float32 [1024], P('chan')
Inputs may be any that keep to these rules, and one draw needn't show every extreme that they name: `clip_starts`: increasing even frame numbers, the first 0. Every clip has 6 to 32 frames, except one that begins within the first 64 frames and ends within the last 64. `valid`: within each clip, 1 on the leading frames and 0 on a tail of even length; the first two frames of every clip are 1; the clip that crosses the stream ends in a tail of 0s.
All inputs are finite; a program needn't handle non-finite values.
Results may differ from a plain program's by a relative error of at most 0.0054.
Values may be sent and summed in bfloat16 or wider, within the bound.
No kernel may reach another device: no remote copies, remote signals or barrier semaphores. Data moves between devices by JAX's collectives and lax.ppermute only.
A program may use at most 128 MiB of HBM per device.

v0:
```python
import jax
import jax.numpy as jnp
from jax import lax
from jax.sharding import PartitionSpec as P

EPS = 1e-05
highest = lax.Precision.HIGHEST


def padded_2(shard, sides, width):
    for axis, dim in sides:
        count, length = (lax.axis_size(axis), shard.shape[dim])
        up = [(i, (i + 1) % count) for i in range(count - 1)]
        down = [(j, i) for i, j in up]
        last = lax.slice_in_dim(shard, length - width, length, axis=dim)
        leading = lax.slice_in_dim(shard, 0, width, axis=dim)
        before = lax.ppermute(last, axis, up)
        after = lax.ppermute(leading, axis, down)
        shard = jnp.concatenate([before, shard, after], axis=dim)
    return shard


def entering(part, axis, combine, identity, reverse):
    count = lax.axis_size(axis)
    place = lax.axis_index(axis)
    ahead = count - 1 - place if reverse else place
    gathered = jax.tree.map(lambda a: lax.all_gather(a, axis), part)
    state = jax.tree.map(lambda a, e: jnp.zeros_like(a) + jnp.asarray(e, a.dtype), part, identity)

    def one(step, state):
        source = count - 1 - step if reverse else step
        return combine(
            state, jax.tree.map(lambda a: lax.dynamic_index_in_dim(a, source, 0, False), gathered)
        )

    return lax.fori_loop(0, ahead, one, state)


def frame_flags(clip_starts, first_frame, frame_count, frame_total):
    position = first_frame - 2 + jnp.arange(frame_count + 4, dtype=jnp.int32)
    segment = jnp.sum((clip_starts[None, :] <= position[:, None]).astype(jnp.int32), axis=1) - 1
    inside = (position >= 0) & (position < frame_total)
    middle = segment[1:-1]
    before_same = inside[1:-1] & inside[:-2] & (middle == segment[:-2])
    after_same = inside[1:-1] & inside[2:] & (middle == segment[2:])
    return (segment[2:-2], before_same, after_same)


def conv_forward(padded, weight, factors):
    frame_count = padded.shape[0] - 2
    mel_count = padded.shape[1]
    wide_field = jnp.pad(padded, ((0, 0), (1, 1), (0, 0)))
    result = jnp.zeros((frame_count, mel_count, weight.shape[3]), jnp.float32)
    for tap_row in range(3):
        partial_value = jnp.zeros((frame_count * mel_count, weight.shape[3]), jnp.float32)
        for tap_col in range(3):
            window = wide_field[
                tap_row : tap_row + frame_count, tap_col : tap_col + mel_count, :
            ].reshape(frame_count * mel_count, -1)
            partial_value = partial_value + jnp.dot(
                window, weight[tap_row, tap_col], preferred_element_type=jnp.float32
            )
        result = (
            result
            + partial_value.reshape(frame_count, mel_count, -1) * factors[tap_row][:, None, None]
        )
    return result


def conv_weight_grad(padded, grad_out, factors):
    frame_count = grad_out.shape[0]
    mel_count = grad_out.shape[1]
    wide_field = jnp.pad(padded, ((0, 0), (1, 1), (0, 0)))
    rows_out = []
    for tap_row in range(3):
        scaled = (grad_out * factors[tap_row][:, None, None].astype(jnp.bfloat16)).reshape(
            frame_count * mel_count, -1
        )
        taps_out = []
        for tap_col in range(3):
            window = wide_field[
                tap_row : tap_row + frame_count, tap_col : tap_col + mel_count, :
            ].reshape(frame_count * mel_count, -1)
            taps_out.append(
                lax.dot_general(
                    window, scaled, (((0,), (0,)), ((), ())), preferred_element_type=jnp.float32
                )
            )
        rows_out.append(jnp.stack(taps_out))
    return jnp.stack(rows_out)


def conv_input_grad(grad_padded, weight, edge_factors):
    frame_count = grad_padded.shape[0] - 2
    mel_count = grad_padded.shape[1]
    wide_field = jnp.pad(grad_padded, ((0, 0), (1, 1), (0, 0)))
    result = jnp.zeros((frame_count * mel_count, weight.shape[2]), jnp.float32)
    for tap_row in range(3):
        scaled = wide_field * edge_factors[tap_row][:, None, None]
        for tap_col in range(3):
            window = scaled[
                2 - tap_row : 2 - tap_row + frame_count, 2 - tap_col : 2 - tap_col + mel_count, :
            ].reshape(frame_count * mel_count, -1)
            result = result + lax.dot_general(
                window,
                weight[tap_row, tap_col],
                (((1,), (1,)), ((), ())),
                preferred_element_type=jnp.float32,
            )
    return result.reshape(frame_count, mel_count, -1)


def join_keyed(earlier_item, later_item):
    keep_first = later_item[0] < 0.0
    same_key = later_item[0] == earlier_item[0]
    merged = [jnp.where(keep_first, earlier_item[0], later_item[0])]
    for first_part, second_part in zip(earlier_item[1:], later_item[1:]):
        extra = (1,) * (first_part.ndim - keep_first.ndim)
        keep_wide = jnp.reshape(keep_first, keep_first.shape + extra)
        same_wide = jnp.reshape(same_key, same_key.shape + extra)
        merged.append(
            jnp.where(
                keep_wide, first_part, jnp.where(same_wide, first_part + second_part, second_part)
            )
        )
    return tuple(merged)


def smooth(argument):
    return jax.nn.gelu(argument, approximate=False)


def shards(
    features,
    conv1_weight,
    norm1_gain,
    norm1_bias,
    conv2_weight,
    norm2_gain,
    norm2_bias,
    clip_starts,
    valid,
    readout_grad,
):
    frame_count = features.shape[0]
    mel_count = features.shape[1]
    cycle_size = lax.axis_size("tm")
    cycle_index = lax.axis_index("tm")
    segment, before_same, after_same = frame_flags(
        clip_starts, cycle_index * frame_count, frame_count, frame_count * cycle_size
    )
    keep_mask = valid.astype(jnp.float32)
    keep_cube = keep_mask[:, None, None]
    own_factors = (
        before_same[1:-1].astype(jnp.float32),
        jnp.ones((frame_count,), jnp.float32),
        after_same[1:-1].astype(jnp.float32),
    )
    edge_factors = (
        before_same.astype(jnp.bfloat16),
        jnp.ones((frame_count + 2,), jnp.bfloat16),
        after_same.astype(jnp.bfloat16),
    )
    local_count = jnp.sum(keep_mask) * mel_count

    def spread(shard):
        padded = padded_2(shard, (("tm", 0),), 1)
        return lax.all_gather(padded, "chan", axis=2, tiled=True)

    def normalize(field_in, gain_vec, shift_vec):
        value_sums, squares, pixel_count = lax.psum(
            (
                jnp.sum(field_in * keep_cube, axis=(0, 1)),
                jnp.sum(field_in * field_in * keep_cube, axis=(0, 1)),
                local_count,
            ),
            "tm",
        )
        center = value_sums / pixel_count
        variance = squares / pixel_count - center * center
        inverse_std = lax.rsqrt(variance + EPS)
        normed = (field_in - center) * inverse_std
        return (gain_vec * normed + shift_vec, normed, inverse_std, pixel_count)

    def norm_back(grad_norm, normed, inverse_std, gain_vec, pixel_count):
        bias_grad, gain_grad = lax.psum(
            (jnp.sum(grad_norm, axis=(0, 1)), jnp.sum(grad_norm * normed, axis=(0, 1))), "tm"
        )
        grad_pre = (
            keep_cube
            * (gain_vec * inverse_std)
            * (grad_norm - bias_grad / pixel_count - normed * (gain_grad / pixel_count))
        )
        return (grad_pre.astype(jnp.bfloat16), gain_grad, bias_grad)

    def send_back(grad_pre, weight):
        padded = padded_2(grad_pre, (("tm", 0),), 1)
        partial_sum = conv_input_grad(padded, weight, edge_factors)
        return lax.psum_scatter(partial_sum, "chan", scatter_dimension=2, tiled=True)

    wide_in = spread(features * keep_cube.astype(jnp.bfloat16))
    first_pre = conv_forward(wide_in, conv1_weight, own_factors)
    first_norm, first_hat, first_scale, pixel_count = normalize(first_pre, norm1_gain, norm1_bias)
    first_act, first_pull = jax.vjp(smooth, first_norm)
    hidden = (first_act * keep_cube).astype(jnp.bfloat16)
    wide_mid = spread(hidden)
    second_pre = conv_forward(wide_mid, conv2_weight, own_factors)
    second_norm, second_hat, second_scale, pixel_count = normalize(
        second_pre, norm2_gain, norm2_bias
    )
    second_act, second_pull = jax.vjp(smooth, second_norm)
    pooled = (second_act * keep_cube).reshape(frame_count // 2, 2, mel_count, -1).mean(axis=(1, 2))
    pooled_keep = keep_mask[0::2]
    pooled_segment = segment[0::2]
    segment_key = pooled_segment.astype(jnp.float32)
    row_order = jnp.arange(frame_count // 2)
    lower_runs = (
        (pooled_segment[:, None] == pooled_segment[None, :])
        & (row_order[:, None] >= row_order[None, :])
    ).astype(jnp.float32)
    exponent = jnp.exp(pooled)
    counts = jnp.dot(lower_runs, pooled_keep, precision=highest)
    totals = jnp.dot(lower_runs, pooled_keep[:, None] * pooled, precision=highest)
    expsums = jnp.dot(lower_runs, pooled_keep[:, None] * exponent, precision=highest)
    zero_row = jnp.zeros_like(totals[0])
    prior_runs = entering(
        (segment_key[-1], counts[-1], totals[-1], expsums[-1]),
        "tm",
        join_keyed,
        (jnp.float32(-1.0), jnp.float32(0.0), zero_row, zero_row),
        False,
    )
    joined = (segment_key == prior_runs[0]).astype(jnp.float32)
    counts = counts + joined * prior_runs[1]
    totals = totals + joined[:, None] * prior_runs[2]
    expsums = expsums + joined[:, None] * prior_runs[3]
    readout = totals / counts[:, None] + jnp.log(expsums)
    by_count = readout_grad / counts[:, None]
    by_expsum = readout_grad / expsums
    later_mean = lax.dot_general(lower_runs, by_count, (((0,), (0,)), ((), ())), precision=highest)
    later_soft = lax.dot_general(lower_runs, by_expsum, (((0,), (0,)), ((), ())), precision=highest)
    beyond = entering(
        (segment_key[0], later_mean[0], later_soft[0]),
        "tm",
        join_keyed,
        (jnp.float32(-1.0), zero_row, zero_row),
        True,
    )
    joined_back = (segment_key == beyond[0]).astype(jnp.float32)[:, None]
    later_mean = later_mean + joined_back * beyond[1]
    later_soft = later_soft + joined_back * beyond[2]
    pooled_grad = pooled_keep[:, None] * (later_mean + exponent * later_soft)
    spread_grad = jnp.broadcast_to(
        (pooled_grad / (2 * mel_count))[:, None, None, :],
        (frame_count // 2, 2, mel_count, pooled_grad.shape[1]),
    )
    act_grad = spread_grad.reshape(frame_count, mel_count, -1) * keep_cube
    second_grad_norm = second_pull(act_grad)[0]
    second_grad_pre, gain2_grad, bias2_grad = norm_back(
        second_grad_norm, second_hat, second_scale, norm2_gain, pixel_count
    )
    weight2_grad = conv_weight_grad(wide_mid, second_grad_pre, own_factors)
    weight2_grad = lax.psum(weight2_grad, "tm")
    hidden_grad = send_back(second_grad_pre, conv2_weight)
    first_grad_norm = first_pull(hidden_grad * keep_cube)[0]
    first_grad_pre, gain1_grad, bias1_grad = norm_back(
        first_grad_norm, first_hat, first_scale, norm1_gain, pixel_count
    )
    weight1_grad = conv_weight_grad(wide_in, first_grad_pre, own_factors)
    weight1_grad = lax.psum(weight1_grad, "tm")
    input_grad = send_back(first_grad_pre, conv1_weight) * keep_cube
    return (
        readout,
        input_grad,
        weight1_grad,
        gain1_grad,
        bias1_grad,
        weight2_grad,
        gain2_grad,
        bias2_grad,
    )


def solution(mesh):
    return jax.shard_map(
        shards,
        mesh=mesh,
        in_specs=(
            P("tm", None, "chan"),
            P(None, None, None, "chan"),
            P("chan"),
            P("chan"),
            P(None, None, None, "chan"),
            P("chan"),
            P("chan"),
            P(),
            P("tm"),
            P("tm", "chan"),
        ),
        out_specs=(
            P("tm", "chan"),
            P("tm", None, "chan"),
            P(None, None, None, "chan"),
            P("chan"),
            P("chan"),
            P(None, None, None, "chan"),
            P("chan"),
            P("chan"),
        ),
        check_vma=False,
    )
```

profile of v0, /device:TPU:0, one launch (start us, length us, event | category | flops | bytes accessed | tf_op | source)
XLA Modules:
  0.0 1023.7 jit_solution(9963228884751804387)
XLA Ops:
  10.1 5.5 collective-permute-start
  26.3 6.5 all_gather.27
  60.2 20.3 %all-reduce.10 = (f32[256]{0:T(256)S(1)}, f32[]{:T(128)}, f32[256]{0:T(256)S(1)}) all-reduce(f32[256]{0:T(256)S(1)} %get-tuple-element.180, f32[]{:T(128)S(6)} %mul.598, f32[256]{0:T(256)S(1)} %get-tuple-element.179), channel_id=1, replica_groups=mesh['tm'=8,'chan'=4] {'tm'}, use_global_device_ids=true, to_apply=%region_2.3 | all-reduce | flops 513 | bytes 4104 | tf_op jit(solution)/shard_map/psum | solution.py:171
  81.7 2.5 multiply_convert_fusion.2
  85.5 4.5 collective-permute-start.2
  91.4 7.6 all_gather.28
  154.9 3.0 multiply_reduce_fusion.2
  163.9 20.1 %all-reduce.9 = (f32[256]{0:T(256)}, f32[256]{0:T(256)}, f32[8]{0:T(128)}, f32[8]{0:T(128)}, f32[8]{0:T(128)}) all-reduce(f32[256]{0:T(256)} %get-tuple-element.178, f32[256]{0:T(256)} %get-tuple-element.177, f32[8]{0:T(128)} %copy-done.67, f32[8]{0:T(128)} %copy-done.66, ...), channel_id=1, replica_groups=mesh['tm'=8,'chan'=4] {'tm'}, use_global_device_ids=true, to_apply=%region_8.9 | all-reduce | flops 536 | bytes 4288 | tf_op jit(solution)/shard_map/psum | solution.py:171
  185.9 2.6 fusion.112
  190.5 16.3 %all-gather = f32[8,1,256]{2,1,0:T(1,128)S(1)} all-gather(f32[1,1,256]{2,1,0:T(1,128)S(1)} %slice_bitcast_fusion.3), channel_id=1, replica_groups=mesh['tm'=8,'chan'=4] {'tm'}, dimensions={0}, use_global_device_ids=true | all-gather | bytes 9216 | tf_op jit(solution)/shard_map/all_gather | solution.py:27
  206.7 18.3 %all-gather.1 = f32[8,1,256]{2,1,0:T(1,128)S(1)} all-gather(f32[1,1,256]{2,1,0:T(1,128)S(1)} %slice_bitcast_fusion.2), channel_id=1, replica_groups=mesh['tm'=8,'chan'=4] {'tm'}, dimensions={0}, use_global_device_ids=true | all-gather | bytes 9216 | tf_op jit(solution)/shard_map/all_gather | solution.py:27
  228.1 61.2 %all-gather.2 = f32[8,1,256]{2,1,0:T(1,128)S(1)} all-gather(f32[1,1,256]{2,1,0:T(1,128)S(1)} %slice_bitcast_fusion.1), channel_id=1, replica_groups=mesh['tm'=8,'chan'=4] {'tm'}, dimensions={0}, use_global_device_ids=true | all-gather | bytes 9216 | tf_op jit(solution)/shard_map/all_gather | solution.py:27
  291.0 16.3 %all-gather.3 = f32[8,1,256]{2,1,0:T(1,128)S(1)} all-gather(f32[1,1,256]{2,1,0:T(1,128)S(1)} %slice_bitcast_fusion), channel_id=1, replica_groups=mesh['tm'=8,'chan'=4] {'tm'}, dimensions={0}, use_global_device_ids=true | all-gather | bytes 9216 | tf_op jit(solution)/shard_map/all_gather | solution.py:27
  307.9 32.5 %while.33 = (s32[]{:T(128)}, f32[]{:T(128)}, f32[256]{0:T(256)S(1)}, f32[256]{0:T(256)S(1)}, s32[]{:T(128)}, /*index=5*/f32[8]{0:T(128)}, f32[8,256]{1,0:T(8,128...) while((s32[]{:T(128)}, f32[]{:T(128)}, f32[256]{0:T(256)S(1)}, ...), condition=%wide.region_15.16_spmd, body=%wide.region_14.15_spmd.sunk | while | flops 1545 | bytes 10480 | solution.py:36
  346.1 17.1 %all-reduce.8 = (f32[256]{0:T(256)S(1)}, f32[256]{0:T(256)S(1)}) all-reduce(f32[256]{0:T(256)S(1)} %get-tuple-element.184, f32[256]{0:T(256)S(1)} %get-tuple-element.183), channel_id=1, replica_groups=mesh['tm'=8,'chan'=4] {'tm'}, use_global_device_ids=true, to_apply=%region_19.20 | all-reduce | flops 512 | bytes 4096 | tf_op jit(solution)/shard_map/psum | solution.py:186
  375.3 4.5 collective-permute-start.4
  389.4 2.4 fusion.22
  418.1 2.5 reshape.354
  420.6 2.8 copy.153
  429.2 4.7 pad_maximum_fusion
  433.9 13.4 %reduce-scatter.5.cloned.1.call-done = f32[64,4,256]{2,0,1:T(8,128)} async-done(((f32[64,4,1024]{2,0,1:T(8,128)}), f32[64,4,256]{2,0,1:T(8,128)}) %reduce-scatter.5.cloned.1.call-update) | async-done | bytes 262160 | tf_op jit(solution)/shard_map/reduce_scatter | solution.py:199
  449.2 21.3 %all-reduce.7 = (f32[256]{0:T(256)S(1)}, f32[256]{0:T(256)S(1)}) all-reduce(f32[256]{0:T(256)S(1)} %get-tuple-element.182, f32[256]{0:T(256)S(1)} %get-tuple-element.181), channel_id=1, replica_groups=mesh['tm'=8,'chan'=4] {'tm'}, use_global_device_ids=true, to_apply=%region_24.25 | all-reduce | flops 512 | bytes 4096 | tf_op jit(solution)/shard_map/psum | solution.py:186
  480.7 4.5 collective-permute-start.6
  514.5 13.7 %copy.163 = f32[64,4,512]{1,0,2:T(8,128)} copy(f32[64,4,512]{2,1,0:T(4,128)S(1)} %reshape.364) | data formatting | bytes 1048576
  528.2 15.6 %reshape.410 = f32[512,256]{1,0:T(8,128)} reshape(f32[512,64,4]{2,1,0:T(8,128)} %bitcast.252) | data formatting | bytes 1048576
  547.7 2.5 pad_maximum_fusion.1
  551.7 11.5 %reduce-scatter.7.cloned.1.call-done = f32[128,256]{1,0:T(8,128)} async-done(((f32[512,256]{1,0:T(8,128)}), f32[128,256]{1,0:T(8,128)}) %reduce-scatter.7.cloned.1.call-update) | async-done | bytes 131088
  563.2 6.5 reshape.411
  569.7 3.8 copy.164
  574.3 431.9 %all-reduce.14.cloned.1.call-done = (f32[3,3,512,256]{3,2,1,0:T(8,128)}, f32[3,3,1024,256]{3,2,1,0:T(8,128)}) async-done(((f32[3,3,512,256]{3,2,1,0:T(8,128)}, f32[3,3,1024,256]{3,2,1,0:T(8,128)}), (f32[3,3,512,256]{3,2,1,0:T(8,128)}, f32[3,3,1024,256]{3,2,1,0:T(8,128)})) %all-reduce.14.cloned.1.call-update) | async-done | bytes 14155792 | tf_op jit(solution)/shard_map/psum | solution.py:270
  1006.2 5.2 copy.251
  1013.0 3.7 copy.252
  (416 shorter events, 240.8 us)
Async XLA Ops:
  7.2 440.1 %reduce-scatter.5.cloned.1.call-start = ((), (), s32[]{:S(2)}) async-start(), calls=%async_computation.2 | async-start | bytes 1310720 | tf_op jit(solution)/shard_map/reduce_scatter | solution.py:199
  7.9 83.0 %copy-start.31 = (f32[64]{0:T(128)}, f32[64]{0:T(128)S(1)}, u32[]{:S(2)}) copy-start(f32[64]{0:T(128)S(1)} %get-tuple-element.310) | copy-start | bytes 772
  8.8 17.5 %collective-permute-start.1 = (bf16[1,4,128]{2,0,1:T(2,128)(2,1)S(1)}, bf16[1,4,128]{2,0,1:T(2,128)(2,1)S(1)}, u32[]{:S(2)}, u32[]{:S(2)}) collective-permute-start(bf16[1,4,128]{2,0,1:T(2,128)(2,1)S(1)} %get-tuple-element.300), channel_id=1, source_target_pairs={{4,0},{8,4},{12,8},{16,12},{20,16},{24,20},{28,24},{5,1},{9,5},{13... | collective-permute-start | bytes 3080 | tf_op jit(solution)/shard_map/ppermute | solution.py:18
  10.1 16.2 %collective-permute-start = (bf16[1,4,128]{2,0,1:T(2,128)(2,1)S(1)}, bf16[1,4,128]{2,0,1:T(2,128)(2,1)S(1)}, u32[]{:S(2)}, u32[]{:S(2)}) collective-permute-start(bf16[1,4,128]{2,0,1:T(2,128)(2,1)S(1)} %get-tuple-element.299), channel_id=1, source_target_pairs={{0,4},{4,8},{8,12},{12,16},{16,20},{20,24},{24,28},{1,5},{5,9},{9,... | collective-permute-start | bytes 3080 | tf_op jit(solution)/shard_map/ppermute | solution.py:17
  18.5 71.6 %copy-start.65 = (f32[32]{0:T(128)}, f32[32]{0:T(128)S(1)}, u32[]{:S(2)}) copy-start(f32[32]{0:T(128)S(1)} %convolution_bitcast_fusion.18) | copy-start | bytes 388
  20.4 70.6 %copy-start.41 = (f32[64]{0:T(128)}, f32[64]{0:T(128)S(1)}, u32[]{:S(2)}) copy-start(f32[64]{0:T(128)S(1)} %get-tuple-element.315) | copy-start | bytes 772
  20.4 70.7 %copy-start.40 = (f32[64]{0:T(128)}, f32[64]{0:T(128)S(1)}, u32[]{:S(2)}) copy-start(f32[64]{0:T(128)S(1)} %get-tuple-element.304) | copy-start | bytes 772
  25.2 33.6 %copy-start.38 = (f32[256]{0:T(256)}, f32[256]{0:T(256)S(1)}, u32[]{:S(2)}) copy-start(f32[256]{0:T(256)S(1)} %mul.595) | copy-start | bytes 3076
  25.4 33.4 %copy-start.43 = (f32[256]{0:T(256)}, f32[256]{0:T(256)S(1)}, u32[]{:S(2)}) copy-start(f32[256]{0:T(256)S(1)} %mul.591) | copy-start | bytes 3076
  25.6 33.2 %copy-start.44 = (f32[256]{0:T(256)}, f32[256]{0:T(256)S(1)}, u32[]{:S(2)}) copy-start(f32[256]{0:T(256)S(1)} %mul.587) | copy-start | bytes 3076
  53.6 26.8 %copy-start.45 = (f32[256]{0:T(256)S(1)}, f32[256]{0:T(256)}, u32[]{:S(2)}) copy-start(f32[256]{0:T(256)} %param.16) | copy-start | bytes 3076
  53.6 28.0 %copy-start.53 = (f32[256]{0:T(256)S(1)}, f32[256]{0:T(256)}, u32[]{:S(2)}) copy-start(f32[256]{0:T(256)} %param.17) | copy-start | bytes 3076
  84.2 7.0 collective-permute-start.3
  85.5 5.9 collective-permute-start.2
  162.1 182.3 %copy-start.6 = (f32[256,256]{1,0:T(8,128)S(1)}, f32[256,256]{1,0:T(8,128)}, u32[]{:S(2)}) copy-start(f32[256,256]{1,0:T(8,128)} %get-tuple-element.248) | copy-start | bytes 786436
  185.9 39.7 %copy-start.34 = (f32[256]{0:T(256)}, f32[256]{0:T(256)S(1)}, u32[]{:S(2)}) copy-start(f32[256]{0:T(256)S(1)} %get-tuple-element.244) | copy-start | bytes 3076
  185.9 39.7 %copy-start.36 = (f32[256]{0:T(256)}, f32[256]{0:T(256)S(1)}, u32[]{:S(2)}) copy-start(f32[256]{0:T(256)S(1)} %get-tuple-element.245) | copy-start | bytes 3076
  189.5 118.4 %copy-start.25 = (f32[32,256]{1,0:T(8,128)}, f32[32,256]{1,0:T(8,128)S(1)}, u32[]{:S(2)}) copy-start(f32[32,256]{1,0:T(8,128)S(1)} %fusion.175) | copy-start | bytes 98308
  190.4 35.2 %copy-start.27 = (f32[32,256]{1,0:T(8,128)}, f32[32,256]{1,0:T(8,128)S(1)}, u32[]{:S(2)}) copy-start(f32[32,256]{1,0:T(8,128)S(1)} %fusion.177) | copy-start | bytes 98308
  226.3 64.6 %copy-start.62 = (f32[32]{0:T(128)}, f32[32]{0:T(128)S(1)}, u32[]{:S(2)}) copy-start(f32[32]{0:T(128)S(1)} %compare_convert_fusion.1) | copy-start | bytes 388
  228.1 79.8 %copy-start.29 = (f32[32,256]{1,0:T(8,128)}, f32[32,256]{1,0:T(8,128)S(1)}, u32[]{:S(2)}) copy-start(f32[32,256]{1,0:T(8,128)S(1)} %fusion.173) | copy-start | bytes 98308
  374.1 12.1 %collective-permute-start.5 = (bf16[1,4,256]{2,0,1:T(2,128)(2,1)S(1)}, bf16[1,4,256]{2,0,1:T(2,128)(2,1)S(1)}, u32[]{:S(2)}, u32[]{:S(2)}) collective-permute-start(bf16[1,4,256]{2,0,1:T(2,128)(2,1)S(1)} %get-tuple-element.296), channel_id=1, source_target_pairs={{4,0},{8,4},{12,8},{16,12},{20,16},{24,20},{28,24},{5,1},{9,5},{13... | collective-permute-start | bytes 6152 | tf_op jit(solution)/shard_map/ppermute | solution.py:18
  375.3 10.9 %collective-permute-start.4 = (bf16[1,4,256]{2,0,1:T(2,128)(2,1)S(1)}, bf16[1,4,256]{2,0,1:T(2,128)(2,1)S(1)}, u32[]{:S(2)}, u32[]{:S(2)}) collective-permute-start(bf16[1,4,256]{2,0,1:T(2,128)(2,1)S(1)} %get-tuple-element.295), channel_id=1, source_target_pairs={{0,4},{4,8},{8,12},{12,16},{16,20},{20,24},{24,28},{1,5},{5,9},{9,... | collective-permute-start | bytes 6152 | tf_op jit(solution)/shard_map/ppermute | solution.py:17
  423.5 139.7 %reduce-scatter.7.cloned.1.call-start = ((), (), s32[]{:S(2)}) async-start(), calls=%async_computation.3 | async-start | bytes 655360
  429.1 18.2 %copy-start.3 = (f32[64,4,256]{2,0,1:T(8,128)S(1)}, f32[64,4,256]{2,0,1:T(8,128)}, u32[]{:S(2)}) copy-start(f32[64,4,256]{2,0,1:T(8,128)} %get-tuple-element.251) | copy-start | bytes 786436
  429.1 18.2 %copy-start.9 = (f32[64,4,256]{2,0,1:T(8,128)S(1)}, f32[64,4,256]{2,0,1:T(8,128)}, u32[]{:S(2)}) copy-start(f32[64,4,256]{2,0,1:T(8,128)} %get-tuple-element.250) | copy-start | bytes 786436
  429.1 18.2 %copy-start.32 = (f32[64]{0:T(128)S(1)}, f32[64]{0:T(128)}, u32[]{:S(2)}) copy-start(f32[64]{0:T(128)} %copy-done.31) | copy-start | bytes 772
  429.1 42.6 %copy-start.23 = (f32[64,256]{1,0:T(8,128)S(1)}, f32[64,256]{1,0:T(8,128)}, u32[]{:S(2)}) copy-start(f32[64,256]{1,0:T(8,128)} %get-tuple-element.307) | copy-start | bytes 196612
  429.1 43.7 %copy-start.70 = (bf16[64]{0:T(256)(128)(2,1)S(1)}, bf16[64]{0:T(256)(128)(2,1)}, u32[]{:S(2)}) copy-start(bf16[64]{0:T(256)(128)(2,1)} %get-tuple-element.316) | copy-start | bytes 388
  479.4 7.7 collective-permute-start.7
  480.7 6.4 collective-permute-start.6
  543.9 462.3 %all-reduce.14.cloned.1.call-start = ((), (), s32[]{:S(2)}) async-start(), calls=%async_computation.4 | async-start | bytes 28311552 | tf_op jit(solution)/shard_map/psum | solution.py:270
  (50 other events, 217.7 us)
Sparse Core Ops, SparseCore 0:
  423.6 23.6 reduce-scatter.4
  544.0 19.1 reduce-scatter.6
  568.0 438.1 all-reduce.13
where the time goes:
time: 1030 us; the launch traced here: 1020 us
  waiting for transfers between devices  457 us (44%)
  blocking collectives  205 us (20%)
  local copies, waits for them, and re-layouts  194 us (19%)
  matrix products  69.8 us (7%)
  other arithmetic  42.8 us (4%)
  starting transfers between devices  24.9 us (2%)
  between operations  16.3 us (2%)
  loops' own time  14.1 us (1%)
    psum x1, waiting for transfers between devices, shards(): weight1_grad = lax.psum(weight1_grad, 'tm')  432 us
    all_gather x4, blocking collectives, entering(): gathered = jax.tree.map(lambda a: lax.all_gather(a, axis), part)  112 us
    unnamed x163, local copies, waits for them, and re-layouts  59.8 us
    psum x2, blocking collectives, normalize(): lax.psum((jnp.sum(field_in * keep_cube, axis=(0, 1)), jnp.sum(field_in *...  40.4 us
    psum x2, blocking collectives, norm_back(): lax.psum((jnp.sum(grad_norm, axis=(0, 1)), jnp.sum(grad_norm * normed, ax...  38.5 us
    slice x20, local copies, waits for them, and re-layouts, conv_forward(): wide_field[tap_row:tap_row + frame_count, tap_col:tap_col + mel_count, :]  32 us
    dot_general x18, matrix products, conv_forward(): jnp.dot(window, weight[tap_row, tap_col], preferred_element_type=jnp.floa...  26.5 us
    reshape x18, local copies, waits for them, and re-layouts, conv_forward(): window = wide_field[tap_row:tap_row + frame_count, tap_col:tap_col + mel_...  23.4 us
  transfers between devices with their start and end apart: 11, of which 4 were waited for; matrix products, arithmetic and copies ran while one was open for 4% of the time, Pallas kernels for 0%

commit v1 on v0

--- a/solution.py
+++ b/solution.py
@@ -1,10 +1,16 @@
+import functools
+
 import jax
 import jax.numpy as jnp
 from jax import lax
+from jax.experimental import pallas as pl
+from jax.experimental.pallas import tpu as pltpu
 from jax.sharding import PartitionSpec as P
 
 EPS = 1e-05
 highest = lax.Precision.HIGHEST
+f32 = jnp.float32
+bf16 = jnp.bfloat16
 
 
 def padded_2(shard, sides, width):
@@ -130,7 +136,7 @@
     return jax.nn.gelu(argument, approximate=False)
 
 
-def shards(
+def split_frames(
     features,
     conv1_weight,
     norm1_gain,
@@ -279,6 +285,852 @@
         gain2_grad,
         bias2_grad,
     )
+
+
+ABSENT = 1024.0
+ROWS = 32
+TILE = 8
+LANES = 128
+
+
+def whole_spec():
+    return pl.BlockSpec(memory_space=pltpu.VMEM)
+
+
+def place_spec():
+    return pl.BlockSpec(memory_space=pl.ANY)
+
+
+def scalar_spec():
+    return pl.BlockSpec(memory_space=pltpu.SMEM)
+
+
+def call(body, operands, in_specs, outs, out_specs, scratch, flops, megabytes):
+    return pl.pallas_call(
+        body,
+        out_shape=tuple(jax.ShapeDtypeStruct(s, d) for s, d in outs),
+        in_specs=in_specs,
+        out_specs=tuple(out_specs),
+        scratch_shapes=scratch,
+        compiler_params=pltpu.CompilerParams(vmem_limit_bytes=megabytes * 2**20),
+        cost_estimate=pl.CostEstimate(flops=flops, bytes_accessed=2**22, transcendentals=0),
+    )(*operands)
+
+
+def swap(shard, axis, bit):
+    count = lax.axis_size(axis)
+    return lax.ppermute(shard, axis, [(i, i ^ bit) for i in range(count)])
+
+
+def swap_both(shard, first, first_bit, second, second_bit):
+    rows, columns = lax.axis_size(first), lax.axis_size(second)
+    pairs = [
+        (i * columns + j, (i ^ first_bit) * columns + (j ^ second_bit))
+        for i in range(rows)
+        for j in range(columns)
+    ]
+    return lax.ppermute(shard, (first, second), pairs)
+
+
+def same_clip(starts, at, shape, total):
+    frame = lax.broadcasted_iota(jnp.int32, shape, 0) + at
+    before = frame != starts[0]
+    after = frame != total - 1
+    for k in range(1, starts.shape[0]):
+        before = before & (frame != starts[k])
+        after = after & (frame != starts[k] - 1)
+    return before, after
+
+
+def widen(mask, width):
+    return jnp.concatenate([mask] * (width // mask.shape[1]), axis=1)
+
+
+def fold(value):
+    total = value[:TILE]
+    for k in range(TILE, value.shape[0], TILE):
+        total = total + value[k : k + TILE]
+    return total
+
+
+def column_sum(value):
+    return jnp.sum(value, axis=0, keepdims=True)
+
+
+def taps(mel, mel_count):
+    return [b for b in range(3) if 0 <= mel + b - 1 < mel_count]
+
+
+def convolve(fields, weights, lower, middle, upper, total, add):
+    mel_count = middle.shape[0]
+    for m in range(mel_count):
+        for a in range(3):
+            acc = None
+            for field, weight in zip(fields, weights):
+                for b in taps(m, mel_count):
+                    part = jnp.dot(field(m + b - 1), weight(a, b), preferred_element_type=f32)
+                    acc = part if acc is None else acc + part
+            if a == 0:
+                lower[m, TILE : TILE + total] = acc
+            elif a == 1:
+                middle[m] = middle[m] + acc if add else acc
+            else:
+                upper[m, TILE : TILE + total] = acc
+
+
+def convolve_back(fields, weights, lower, middle, upper, total):
+    mel_count = middle.shape[0]
+    for n in range(mel_count):
+        for a in range(3):
+            acc = None
+            for field, weight in zip(fields, weights):
+                for b in range(3):
+                    if 0 <= n - b + 1 < mel_count:
+                        part = lax.dot_general(
+                            field(n - b + 1),
+                            weight(a, b),
+                            (((1,), (1,)), ((), ())),
+                            preferred_element_type=f32,
+                        )
+                        acc = part if acc is None else acc + part
+            if a == 2:
+                lower[n, TILE : TILE + total] = acc
+            elif a == 1:
+                middle[n] = acc
+            else:
+                upper[n, TILE : TILE + total] = acc
+
+
+def joined(lower, middle, upper, m, at, before, after):
+    low = lower[m, pl.ds(at, ROWS + 2 * TILE)]
+    high = upper[m, pl.ds(at, ROWS + 2 * TILE)]
+    return (
+        middle[m, pl.ds(at, ROWS)]
+        + jnp.where(before, low[TILE - 1 : TILE - 1 + ROWS], 0.0)
+        + jnp.where(after, high[TILE + 1 : TILE + 1 + ROWS], 0.0)
+    )
+
+
+def by_rows(total, body, init):
+    return lax.fori_loop(
+        0, total // ROWS, lambda i, c: body(pl.multiple_of(i * ROWS, ROWS), c), init
+    )
+
+
+def clear_edges(lower, upper, total):
+    for m in range(lower.shape[0]):
+        for ref in (lower, upper):
+            ref[m, :TILE] = jnp.zeros((TILE, ref.shape[2]), f32)
+            ref[m, TILE + total :] = jnp.zeros((TILE, ref.shape[2]), f32)
+
+
+def moments(field, keep, count):
+    first, second = column_sum(field[0]), column_sum(field[1])
+    center = first / count
+    return center, lax.rsqrt(second / count - center * center + EPS)
+
+
+def phi_parts(value):
+    return 0.5 * (1.0 + lax.erf(value * 0.7071067811865476))
+
+
+def bell(value):
+    return 0.3989422804014327 * jnp.exp(-0.5 * value * value)
+
+
+def first_kernel(starts, *refs):
+    blocks, (weight_in, gain, shift) = refs[:8], refs[8:11]
+    hidden, field_out, pre_out, keep, stats = refs[11:16]
+    field, weight, lower, middle, upper, sems = refs[16:]
+    mel_count, total, width = field.shape
+    out_width = middle.shape[2]
+    place, column = lax.axis_index("tm"), lax.axis_index("chan")
+    copies = [pltpu.make_async_copy(weight_in, weight, sems.at[0])]
+    frames, lanes = blocks[0].shape[2], blocks[0].shape[3]
+    count = blocks[0].shape[0]
+    for i, block in enumerate(blocks):
+        core, row, side = i // 4, (i // 2) % 2, i % 2
+        from_column = column ^ (2 * row + core)
+        for k in range(count):
+            from_place = place ^ (2 * k + side)
+            copies.append(
+                pltpu.make_async_copy(
+                    block.at[k],
+                    field.at[
+                        :,
+                        pl.ds(pl.multiple_of(from_place * frames, frames), frames),
+                        pl.ds(pl.multiple_of(from_column * lanes, lanes), lanes),
+                    ],
+                    sems.at[1 + i * count + k],
+                )
+            )
+    for copy in copies:
+        copy.start()
+    clear_edges(lower, upper, total)
+    for copy in copies:
+        copy.wait()
+
+    def decode(at, carry):
+        for m in range(mel_count):
+            rows = field[m, pl.ds(at, ROWS)]
+            if m == 0:
+                keep[pl.ds(at, ROWS)] = (rows[:, :LANES].astype(f32) < ABSENT / 2).astype(f32)
+            field[m, pl.ds(at, ROWS)] = jnp.where(rows < ABSENT / 2, rows, jnp.zeros_like(rows))
+        return carry
+
+    by_rows(total, decode, 0)
+    save = pltpu.make_async_copy(field, field_out, sems.at[1])
+    save.start()
+    convolve(
+        [lambda m: field[m]], [lambda a, b: weight[a, b]], lower, middle, upper, total, False
+    )
+
+    def combine(at, sums):
+        before, after = same_clip(starts, at, (ROWS, out_width), total)
+        mask = widen(keep[pl.ds(at, ROWS)], out_width)
+        one, two, num = sums
+        num = num + fold(mask)
+        for m in range(mel_count):
+            rows = joined(lower, middle, upper, m, at, before, after)
+            middle[m, pl.ds(at, ROWS)] = rows
+            kept = rows * mask
+            one = one + fold(kept)
+            two = two + fold(kept * rows)
+        return one, two, num
+
+    blank = jnp.zeros((TILE, out_width), f32)
+    one, two, num = by_rows(total, combine, (blank, blank, blank))
+    save_pre = pltpu.make_async_copy(middle, pre_out, sems.at[0])
+    save_pre.start()
+    pixels = column_sum(num) * mel_count
+    center, inverse = moments((one, two), keep, pixels)
+    stats[0:1] = center
+    stats[1:2] = inverse
+    stats[2:3] = pixels
+    scale = gain[...] * inverse
+    offset = shift[...] - center * scale
+
+    def activate(at, carry):
+        mask = widen(keep[pl.ds(at, ROWS)], out_width)
+        for m in range(mel_count):
+            value = middle[m, pl.ds(at, ROWS)] * scale + offset
+            hidden[m, pl.ds(at, ROWS)] = (value * phi_parts(value) * mask).astype(bf16)
+        return carry
+
+    by_rows(total, activate, 0)
+    save.wait()
+    save_pre.wait()
+
+
+def first_block(blocks, weight, gain, shift, starts, total):
+    count, mel_count, frames, lanes = blocks[0].shape
+    width, out_width = weight.shape[2], weight.shape[3]
+    padded = (mel_count, total + 2 * TILE, out_width)
+    return call(
+        first_kernel,
+        (starts, *blocks, weight, gain, shift),
+        [scalar_spec()] + [place_spec()] * 9 + [whole_spec()] * 2,
+        [
+            ((mel_count, total, out_width), bf16),
+            ((mel_count, total, width), bf16),
+            ((mel_count, total, out_width), f32),
+            ((total, LANES), f32),
+            ((TILE, out_width), f32),
+        ],
+        [whole_spec(), place_spec(), place_spec(), whole_spec(), whole_spec()],
+        [
+            pltpu.VMEM((mel_count, total, width), bf16),
+            pltpu.VMEM(weight.shape, bf16),
+            pltpu.VMEM(padded, f32),
+            pltpu.VMEM((mel_count, total, out_width), f32),
+            pltpu.VMEM(padded, f32),
+            pltpu.SemaphoreType.DMA((1 + 8 * count,)),
+        ],
+        2 * 9 * mel_count * total * width * out_width,
+        32,
+    )
+
+
+def slope_kernel(pre, stats, gain, shift, keep, slope):
+    mel_count, total, width = pre.shape
+    center, inverse = stats[0:1], stats[1:2]
+    scale = gain[...] * inverse
+    offset = shift[...] - center * scale
+
+    def rows(at, carry):
+        mask = widen(keep[pl.ds(at, ROWS)], width)
+        for m in range(mel_count):
+            value = pre[m, pl.ds(at, ROWS)] * scale + offset
+            slope[m, pl.ds(at, ROWS)] = mask * (phi_parts(value) + value * bell(value))
+        return carry
+
+    by_rows(total, rows, 0)
+
+
+def first_slope(pre, stats, gain, shift, keep):
+    return call(
+        slope_kernel,
+        (pre, stats, gain, shift, keep),
+        [whole_spec()] * 5,
+        [(pre.shape, f32)],
+        [whole_spec()],
+        [],
+        2**28,
+        10,
+    )[0]
+
+
+def partial_kernel(places, starts, one, two, weight, out, lower, upper):
+    mel_count, total, width = out.shape
+    column = lax.axis_index("chan")
+
+    def group(place):
+        start = pl.multiple_of((column ^ place) * width, width)
+        return lambda a, b: weight[a, b, pl.ds(start, width)]
+
+    clear_edges(lower, upper, total)
+    convolve(
+        [lambda m: one[m], lambda m: two[m]],
+        [group(p) for p in places],
+        lower,
+        out,
+        upper,
+        total,
+        False,
+    )
+
+    def combine(at, carry):
+        before, after = same_clip(starts, at, (ROWS, width), total)
+        for m in range(mel_count):
+            out[m, pl.ds(at, ROWS)] = joined(lower, out, upper, m, at, before, after)
+        return carry
+
+    by_rows(total, combine, 0)
+
+
+def second_partial(one, two, weight, starts):
+    mel_count, total, width = one.shape
+    padded = (mel_count, total + 2 * TILE, width)
+    return call(
+        functools.partial(partial_kernel, (0, 1)),
+        (starts, one, two, weight),
+        [scalar_spec()] + [whole_spec()] * 3,
+        [((mel_count, total, width), f32)],
+        [whole_spec()],
+        [pltpu.VMEM(padded, f32)] * 2,
+        2 * 18 * mel_count * total * width * width,
+        20,
+    )[0]
+
+
+def second_kernel(starts, one, two, weight, middle_in, keep, gain, shift, cotangents, *refs):
+    readout, grad, gain_grad, shift_grad = refs[:4]
+    middle, slope, lower, upper, hold, wide, full, sems = refs[4:]
+    mel_count, total, width = one.shape
+    place, column = lax.axis_index("tm"), lax.axis_index("chan")
+    pooled_total = total // 2
+    own = readout.shape[0]
+    copies = []
+    for k in range(cotangents.shape[0]):
+        copies.append(
+            pltpu.make_async_copy(
+                cotangents.at[k],
+                full.at[pl.ds(pl.multiple_of((place ^ k) * own, own), own)],
+                sems.at[k],
+            )
+        )
+    for copy in copies:
+        copy.start()
+
+    def group(bit):
+        start = pl.multiple_of((column ^ bit) * width, width)
+        return lambda a, b: weight[a, b, pl.ds(start, width)]
+
+    clear_edges(lower, upper, total)
+    convolve(
+        [lambda m: one[m], lambda m: two[m]], [group(2), group(3)], lower, middle, upper, total, False
+    )
+    blank = jnp.zeros((TILE, width), f32)
+
+    def combine(at, sums):
+        before, after = same_clip(starts, at, (ROWS, width), total)
+        mask = widen(keep[pl.ds(at, ROWS)], width)
+        first, second, num = sums
+        num = num + fold(mask)
+        for m in range(mel_count):
+            rows = joined(lower, middle, upper, m, at, before, after)
+            rows = rows + middle_in[m, pl.ds(at, ROWS)]
+            middle[m, pl.ds(at, ROWS)] = rows
+            kept = rows * mask
+            first = first + fold(kept)
+            second = second + fold(kept * rows)
+        return first, second, num
+
+    first, second, num = by_rows(total, combine, (blank, blank, blank))
+    pixels = column_sum(num) * mel_count
+    center, inverse = moments((first, second), keep, pixels)
+    scale = gain[...] * inverse
+    offset = shift[...] - center * scale
+
+    def activate(at, carry):
+        mask = widen(keep[pl.ds(at, ROWS)], width)
+        pooled = jnp.zeros((ROWS, width), f32)
+        for m in range(mel_count):
+            value = middle[m, pl.ds(at, ROWS)] * scale + offset
+            share = phi_parts(value)
+            pooled = pooled + value * share
+            slope[m, pl.ds(at, ROWS)] = mask * (share + value * bell(value))
+        pooled = pooled * mask
+        for c in range(width // LANES):
+            hold[c, pl.ds(at, ROWS)] = pooled[:, c * LANES : (c + 1) * LANES]
+        return carry
+
+    by_rows(total, activate, 0)
+
+    even = pl.ds(0, pooled_total, stride=2)
+    odd = pl.ds(1, pooled_total, stride=2)
+    pooled = jnp.concatenate(
+        [hold[c, even] + hold[c, odd] for c in range(width // LANES)], axis=1
+    ) * (0.5 / mel_count)
+    present = widen(keep[even], width)
+    square = (pooled_total, pooled_total)
+    row = lax.broadcasted_iota(jnp.int32, square, 0)
+    col = lax.broadcasted_iota(jnp.int32, square, 1)
+    same = row >= col
+    back = row <= col
+    for k in range(1, starts.shape[0]):
+        crossed = (2 * row < starts[k]) != (2 * col < starts[k])
+        same = same & ~crossed
+        back = back & ~crossed
+    ahead, behind = same.astype(f32), back.astype(f32)
+    exact = functools.partial(jnp.dot, precision=highest, preferred_element_type=f32)
+    exponent = jnp.exp(pooled)
+    counts = jnp.dot(ahead, present, preferred_element_type=f32)
+    totals = exact(ahead, present * pooled)
+    sums = exact(ahead, present * exponent)
+    wide[...] = totals / counts + jnp.log(sums)
+    readout[...] = wide[pl.ds(pl.multiple_of(place * own, own), own)]
+    for copy in copies:
+        copy.wait()
+    cotangent = full[...]
+    by_count = exact(behind, cotangent / counts)
+    by_sum = exact(behind, cotangent / sums)
+    down = present * (by_count + exponent * by_sum) * (0.5 / mel_count)
+    for c in range(width // LANES):
+        hold[c, even] = down[:, c * LANES : (c + 1) * LANES]
+        hold[c, odd] = down[:, c * LANES : (c + 1) * LANES]
+
+    def slopes(at, sums):
+        down_rows = jnp.concatenate(
+            [hold[c, pl.ds(at, ROWS)] for c in range(width // LANES)], axis=1
+        )
+        plain, along = sums
+        for m in range(mel_count):
+            step = down_rows * slope[m, pl.ds(at, ROWS)]
+            slope[m, pl.ds(at, ROWS)] = step
+            plain = plain + fold(step)
+            along = along + fold(step * ((middle[m, pl.ds(at, ROWS)] - center) * inverse))
+        return plain, along
+
+    plain, along = by_rows(total, slopes, (blank, blank))
+    plain, along = column_sum(plain), column_sum(along)
+    shift_grad[...] = plain
+    gain_grad[...] = along
+    plain, along = plain / pixels, along / pixels
+
+    def finish(at, carry):
+        mask = widen(keep[pl.ds(at, ROWS)], width)
+        for m in range(mel_count):
+            normed = (middle[m, pl.ds(at, ROWS)] - center) * inverse
+            rows = slope[m, pl.ds(at, ROWS)] - plain - normed * along
+            grad[m, pl.ds(at, ROWS)] = (mask * (scale * rows)).astype(bf16)
+        return carry
+
+    by_rows(total, finish, 0)
+
+
+def second_block(one, two, weight, partial, keep, gain, shift, starts, cotangents, own):
+    mel_count, total, width = one.shape
+    padded = (mel_count, total + 2 * TILE, width)
+    full = (mel_count, total, width)
+    return call(
+        second_kernel,
+        (starts, one, two, weight, partial, keep, gain, shift, cotangents),
+        [scalar_spec()] + [whole_spec()] * 7 + [place_spec()],
+        [((own, width), f32), (full, bf16), ((1, width), f32), ((1, width), f32)],
+        [whole_spec()] * 4,
+        [
+            pltpu.VMEM(full, f32),
+            pltpu.VMEM(full, f32),
+            pltpu.VMEM(padded, f32),
+            pltpu.VMEM(padded, f32),
+            pltpu.VMEM((width // LANES, total, LANES), f32),
+            pltpu.VMEM((total // 2, width), f32),
+            pltpu.VMEM((total // 2, width), f32),
+            pltpu.SemaphoreType.DMA((cotangents.shape[0],)),
+        ],
+        2 * 18 * mel_count * total * width * width,
+        40,
+    )
+
+
+def back_kernel(bit, starts, one, two, weight, weight_two, out, lower, middle, upper):
+    mel_count, total, width = one.shape
+    column = lax.axis_index("chan")
+    start = pl.multiple_of((column ^ bit) * width, width)
+    clear_edges(lower, upper, total)
+    convolve_back(
+        [lambda m: one[m], lambda m: two[m]],
+        [
+            lambda a, b: weight[a, b, pl.ds(start, width)],
+            lambda a, b: weight_two[a, b, pl.ds(start, width)],
+        ],
+        lower,
+        middle,
+        upper,
+        total,
+    )
+
+    def combine(at, carry):
+        before, after = same_clip(starts, at, (ROWS, width), total)
+        for m in range(mel_count):
+            rows = joined(lower, middle, upper, m, at, before, after)
+            out[m, pl.ds(at, ROWS)] = rows.astype(out.dtype)
+        return carry
+
+    by_rows(total, combine, 0)
+
+
+def hidden_back(bit, one, two, weight, weight_two, starts, kind):
+    mel_count, total, width = one.shape
+    padded = (mel_count, total + 2 * TILE, width)
+    return call(
+        functools.partial(back_kernel, bit),
+        (starts, one, two, weight, weight_two),
+        [scalar_spec()] + [whole_spec()] * 4,
+        [((mel_count, total, width), kind)],
+        [whole_spec()],
+        [
+            pltpu.VMEM(padded, f32),
+            pltpu.VMEM((mel_count, total, width), f32),
+            pltpu.VMEM(padded, f32),
+        ],
+        2 * 18 * mel_count * total * width * width,
+        28,
+    )[0]
+
+
+def norm_kernel(mine, other, slope, pre, stats, gain, keep, *refs):
+    grad, window, gain_grad, shift_grad, padded = refs
+    mel_count, total, width = mine.shape
+    center, inverse, pixels = stats[0:1], stats[1:2], stats[2:3]
+    blank = jnp.zeros((TILE, width), f32)
+    edge = (padded.shape[1] - total) // 2
+    reach = window.shape[1]
+    frames = reach - 2 * edge
+    place = lax.axis_index("tm")
+
+    def slopes(at, sums):
+        plain, along = sums
+        for m in range(mel_count):
+            rows = mine[m, pl.ds(at, ROWS)] + other[m, pl.ds(at, ROWS)].astype(f32)
+            step = rows * slope[m, pl.ds(at, ROWS)]
+            mine[m, pl.ds(at, ROWS)] = step
+            plain = plain + fold(step)
+            along = along + fold(step * ((pre[m, pl.ds(at, ROWS)] - center) * inverse))
+        return plain, along
+
+    plain, along = by_rows(total, slopes, (blank, blank))
+    plain, along = column_sum(plain), column_sum(along)
+    shift_grad[...] = plain
+    gain_grad[...] = along
+    plain, along = plain / pixels, along / pixels
+    scale = gain[...] * inverse
+    for m in range(mel_count):
+        padded[m, :edge] = jnp.zeros((edge, width), bf16)
+        padded[m, edge + total :] = jnp.zeros((edge, width), bf16)
+
+    def finish(at, carry):
+        mask = widen(keep[pl.ds(at, ROWS)], width)
+        for m in range(mel_count):
+            normed = (pre[m, pl.ds(at, ROWS)] - center) * inverse
+            rows = mine[m, pl.ds(at, ROWS)] - plain - normed * along
+            rows = (mask * (scale * rows)).astype(bf16)
+            grad[m, pl.ds(at, ROWS)] = rows
+            padded[m, pl.ds(pl.multiple_of(at + edge, 16), ROWS)] = rows
+        return carry
+
+    by_rows(total, finish, 0)
+    for m in range(mel_count):
+        window[m] = padded[m, pl.ds(pl.multiple_of(place * frames, frames), reach)]
+
+
+def norm_back_first(mine, other, slope, pre, stats, gain, keep, frames):
+    mel_count, total, width = mine.shape
+    edge = 16
+    return call(
+        norm_kernel,
+        (mine, other, slope, pre, stats, gain, keep),
+        [whole_spec()] * 7,
+        [
+            ((mel_count, total, width), bf16),
+            ((mel_count, frames + 2 * edge, width), bf16),
+            ((1, width), f32),
+            ((1, width), f32),
+        ],
+        [whole_spec()] * 4,
+        [pltpu.VMEM((mel_count, total + 2 * edge, width), bf16)],
+        2**28,
+        20,
+    )
+
+
+def weight_kernel(group_count, starts, *refs):
+    fields = refs[:group_count]
+    grad, out = refs[group_count : group_count + 2]
+    spaced, steps, results, sems = refs[group_count + 2 :]
+    mel_count, total, out_width = grad.shape
+    column = lax.axis_index("chan")
+    for m in range(mel_count):
+        spaced[m, :TILE] = jnp.zeros((TILE, out_width), f32)
+        spaced[m, TILE + total :] = jnp.zeros((TILE, out_width), f32)
+
+    def expand(at, carry):
+        for m in range(mel_count):
+            spaced[m, pl.ds(pl.multiple_of(at + TILE, TILE), ROWS)] = grad[
+                m, pl.ds(at, ROWS)
+            ].astype(f32)
+        return carry
+
+    by_rows(total, expand, 0)
+
+    def shift(at, carry):
+        before, after = same_clip(starts, at, (ROWS, out_width), total)
+        for m in range(mel_count):
+            rows = spaced[m, pl.ds(at, ROWS + 2 * TILE)]
+            ahead = jnp.where(after, rows[TILE + 1 : TILE + 1 + ROWS], 0.0)
+            behind = jnp.where(before, rows[TILE - 1 : TILE - 1 + ROWS], 0.0)
+            steps[0, m, pl.ds(at, ROWS)] = ahead.astype(bf16)
+            steps[1, m, pl.ds(at, ROWS)] = behind.astype(bf16)
+        return carry
+
+    by_rows(total, shift, 0)
+    width = results.shape[3]
+    copies = [None, None]
+    count = 0
+    for i, field in enumerate(fields):
+        for part in range(field.shape[2] // width):
+            slot = count % 2
+            if copies[slot] is not None:
+                copies[slot].wait()
+            for a in range(3):
+                for b in range(3):
+                    acc = None
+                    for m in range(mel_count):
+                        if 0 <= m + b - 1 < mel_count:
+                            right = grad[m] if a == 1 else steps[a // 2, m]
+                            left = field[m + b - 1, :, part * width : (part + 1) * width]
+                            piece = lax.dot_general(
+                                left,
+                                right,
+                                (((0,), (0,)), ((), ())),
+                                preferred_element_type=f32,
+                            )
+                            acc = piece if acc is None else acc + piece
+                    results[slot, 3 * a + b] = acc
+            if group_count > 1:
+                start = pl.multiple_of((column ^ i) * width, width)
+            else:
+                start = part * width
+            copies[slot] = pltpu.make_async_copy(
+                results.at[slot], out.at[:, pl.ds(start, width)], sems.at[slot]
+            )
+            copies[slot].start()
+            count += 1
+    for copy in copies:
+        if copy is not None:
+            copy.wait()
+
+
+def weight_back(fields, grad, starts):
+    mel_count, total, out_width = grad.shape
+    in_width = sum(f.shape[2] for f in fields)
+    width = 256
+    out = call(
+        functools.partial(weight_kernel, len(fields)),
+        (starts, *fields, grad),
+        [scalar_spec()] + [whole_spec()] * (len(fields) + 1),
+        [((9, in_width, out_width), f32)],
+        [place_spec()],
+        [
+            pltpu.VMEM((mel_count, total + 2 * TILE, out_width), f32),
+            pltpu.VMEM((2, mel_count, total, out_width), bf16),
+            pltpu.VMEM((2, 9, width, out_width), f32),
+            pltpu.SemaphoreType.DMA((2,)),
+        ],
+        2 * 9 * mel_count * total * in_width * out_width,
+        24,
+    )[0]
+    return out.reshape(3, 3, in_width, out_width)
+
+
+def input_kernel(starts, one, two, weight, weight_two, mine, other, lower, middle, upper):
+    mel_count, reach, width = one.shape
+    frames, lanes = mine.shape[1], mine.shape[2]
+    edge = (reach - frames) // 2
+    total = frames * lax.axis_size("tm")
+    place, column = lax.axis_index("tm"), lax.axis_index("chan")
+    for bit, out in ((2, other), (0, mine)):
+        start = pl.multiple_of((column ^ bit) * lanes, lanes)
+        convolve_back(
+            [lambda m: one[m], lambda m: two[m]],
+            [
+                lambda a, b: weight[a, b, pl.ds(start, lanes)],
+                lambda a, b: weight_two[a, b, pl.ds(start, lanes)],
+            ],
+            lower,
+            middle,
+            upper,
+            reach,
+        )
+        before, after = same_clip(starts, place * frames, (frames, lanes), total)
+        for m in range(mel_count):
+            low = lower[m, TILE + edge - 1 : TILE + edge - 1 + frames]
+            high = upper[m, TILE + edge + 1 : TILE + edge + 1 + frames]
+            out[m] = (
+                middle[m, edge : edge + frames]
+                + jnp.where(before, low, 0.0)
+                + jnp.where(after, high, 0.0)
+            )
+
+
+def input_back(one, two, weight, weight_two, starts, frames, lanes):
+    mel_count, reach, width = one.shape
+    shape = (mel_count, frames, lanes)
+    return call(
+        input_kernel,
+        (starts, one, two, weight, weight_two),
+        [scalar_spec()] + [whole_spec()] * 4,
+        [(shape, f32), (shape, f32)],
+        [whole_spec()] * 2,
+        [
+            pltpu.VMEM((mel_count, reach + 2 * TILE, lanes), f32),
+            pltpu.VMEM((mel_count, reach, lanes), f32),
+            pltpu.VMEM((mel_count, reach + 2 * TILE, lanes), f32),
+        ],
+        2**28,
+        20,
+    )
+
+
+def whole_frames(
+    features,
+    conv1_weight,
+    norm1_gain,
+    norm1_bias,
+    conv2_weight,
+    norm2_gain,
+    norm2_bias,
+    clip_starts,
+    valid,
+    readout_grad,
+):
+    frames, mel_count, lanes = features.shape
+    places = lax.axis_size("tm")
+    total = frames * places
+    gain1, shift1 = norm1_gain[None], norm1_bias[None]
+    gain2, shift2 = norm2_gain[None], norm2_bias[None]
+
+    marked = jnp.where(valid[:, None, None] > 0, features, jnp.asarray(ABSENT, bf16))
+    own = jnp.transpose(marked, (1, 0, 2))
+    along = jnp.stack([own] + [swap(own, "tm", 2 * k) for k in range(1, places // 2)])
+    near = [
+        along,
+        swap(along, "tm", 1),
+        swap(along, "chan", 2),
+        swap_both(along, "tm", 1, "chan", 2),
+    ]
+    blocks = near + [swap(block, "chan", 1) for block in near]
+    other_conv2 = swap(conv2_weight, "chan", 1)
+    other_conv1 = swap(conv1_weight, "chan", 1)
+    cotangent = readout_grad[None]
+    bit = 1
+    while bit < places:
+        cotangent = jnp.concatenate([cotangent, swap(cotangent, "tm", bit)])
+        bit *= 2
+
+    hidden, field, pre, keep, stats = first_block(
+        blocks, conv1_weight, gain1, shift1, clip_starts, total
+    )
+    hidden_far = swap(hidden, "chan", 2)
+    hidden_near = swap(hidden, "chan", 1)
+    slope = first_slope(pre, stats, gain1, shift1, keep)
+    partial = second_partial(hidden, hidden_near, conv2_weight, clip_starts)
+    hidden_last = swap(hidden_far, "chan", 1)
+    readout, grad2, gain2_grad, shift2_grad = second_block(
+        hidden_far,
+        hidden_last,
+        conv2_weight,
+        partial,
+        keep,
+        gain2,
+        shift2,
+        clip_starts,
+        cotangent,
+        readout_grad.shape[0],
+    )
+    grad2_near = swap(grad2, "chan", 1)
+    away = hidden_back(2, grad2, grad2_near, conv2_weight, other_conv2, clip_starts, bf16)
+    came = swap(away, "chan", 2)
+    mine = hidden_back(0, grad2, grad2_near, conv2_weight, other_conv2, clip_starts, f32)
+    weight2_grad = weight_back(
+        [hidden, hidden_near, hidden_far, hidden_last], grad2, clip_starts
+    )
+    grad1, window, gain1_grad, shift1_grad = norm_back_first(
+        mine, came, slope, pre, stats, gain1, keep, frames
+    )
+    window_near = swap(window, "chan", 1)
+    input_mine, input_away = input_back(
+        window, window_near, conv1_weight, other_conv1, clip_starts, frames, lanes
+    )
+    input_came = swap(input_away, "chan", 2)
+    weight1_grad = weight_back([field], grad1, clip_starts)
+    live = (valid > 0).astype(f32)[None, :, None]
+    input_grad = jnp.transpose((input_mine + input_came) * live, (1, 0, 2))
+    return (
+        readout,
+        input_grad,
+        weight1_grad,
+        gain1_grad[0],
+        shift1_grad[0],
+        weight2_grad,
+        gain2_grad[0],
+        shift2_grad[0],
+    )
+
+
+def fits_whole(frames, places, columns, widths):
+    return (
+        places > 1
+        and places & (places - 1) == 0
+        and columns == 4
+        and frames % 32 == 0
+        and frames * places <= 512
+        and all(w % (columns * LANES) == 0 for w in widths)
+        and widths[1] == columns * 256
+    )
+
+
+def shards(*arrays):
+    features, conv1_weight, conv2_weight = arrays[0], arrays[1], arrays[4]
+    if fits_whole(
+        features.shape[0],
+        lax.axis_size("tm"),
+        lax.axis_size("chan"),
+        (conv1_weight.shape[2], conv2_weight.shape[2]),
+    ):
+        return whole_frames(*arrays)
+    return split_frames(*arrays)
 
 
 def solution(mesh):

time: 1030 us -> 160 us (0.16)
  waiting for transfers between devices: 457 us -> 74.7 us
  blocking collectives: 205 us -> 0 us
  local copies, waits for them, and re-layouts: 194 us -> 4.51 us
  matrix products: 69.8 us -> 0 us
  Pallas kernels: 0 us -> 61.3 us
  other arithmetic: 42.8 us -> 1.73 us
  between operations: 16.3 us -> 0.99 us
  loops' own time: 14.1 us -> 0 us
    psum x1 -> x0, waiting for transfers between devices: 432 us -> none  [shards(): weight1_grad = lax.psum(weight1_grad, 'tm')]
    all_gather x6 -> x0, blocking collectives: 126 us -> none  [the longest x4 112 us: entering(): gathered = jax.tree.map(lambda a: lax.all_gather(a, axis), part)]
    psum x4 -> x0, blocking collectives: 78.8 us -> none  [the longest x2 40.4 us: normalize(): lax.psum((jnp.sum(field_in * keep_cube, axis=(0, 1)), jnp.sum(field_in *...]
    ppermute x8 -> x22, waiting for transfers between devices: 0.16 us -> 74.7 us  [the longest x21 74.7 us: swap(): return lax.ppermute(shard, axis, [(i, i ^ bit) for i in range(count)])]
    dot_general x59 -> x0, matrix products: 69.8 us -> none  [the longest x18 26.5 us: conv_forward(): jnp.dot(window, weight[tap_row, tap_col], preferred_element_type=jnp.floa...]
    pallas_call x0 -> x10, Pallas kernels: none -> 61.3 us  [call(): pl.pallas_call(body, out_shape=tuple((jax.ShapeDtypeStruct(s, d) for s, d...]
    reshape x48 -> x0, local copies, waits for them, and re-layouts: 55.9 us -> none  [the longest x18 23.4 us: conv_forward(): window = wide_field[tap_row:tap_row + frame_count, tap_col:tap_col + mel_...]
    unnamed x163 -> x41, local copies, waits for them, and re-layouts: 59.8 us -> 4.51 us
  transfers between devices with their start and end apart: 11 -> 22, of which waited for: 4 -> 12; matrix products, arithmetic and copies ran while one was open for 4% -> 0% of each run, Pallas kernels for 0% -> 36%
where the time goes in v1:
time: 160 us; the launch traced here: 159 us
  waiting for transfers between devices  74.7 us (47%)
  Pallas kernels  61.3 us (38%)
  starting transfers between devices  16.3 us (10%)
  local copies, waits for them, and re-layouts  4.51 us (3%)
  other arithmetic  1.73 us (1%)
    ppermute x21, waiting for transfers between devices, swap(): return lax.ppermute(shard, axis, [(i, i ^ bit) for i in range(count)])  74.7 us
    pallas_call x10, Pallas kernels, call(): pl.pallas_call(body, out_shape=tuple((jax.ShapeDtypeStruct(s, d) for s, d...  61.3 us
    ppermute x21, starting transfers between devices, swap(): return lax.ppermute(shard, axis, [(i, i ^ bit) for i in range(count)])  15.8 us
    unnamed x41, local copies, waits for them, and re-layouts  4.51 us
  transfers between devices with their start and end apart: 22, of which 12 were waited for; matrix products, arithmetic and copies ran while one was open for 0% of the time, Pallas kernels for 36%

profile of v1, /device:TPU:0, one launch (start us, length us, event | category | flops | bytes accessed | tf_op | source)
XLA Modules:
  0.0 159.5 jit_solution(2058758235369398713)
XLA Ops:
  1.3 0.9 fusion
  2.2 5.1 %collective-permute-start.2 = (bf16[4,64,128]{2,1,0:T(8,128)(2,1)S(1)}, bf16[4,64,128]{2,1,0:T(8,128)(2,1)S(1)}, u32[]{:S(2)}, u32[]{:S(2)}) collective-permute-start(bf16[4,64,128]{2,1,0:T(8,128)(2,1)S(1)} %get-tuple-element.47), channel_id=1, source_target_pairs={{0,24},{4,28},{8,16},{12,20},{16,8},{20,12},{24,0},{28,4},{1,25},{... | collective-permute-start | bytes 196616 | tf_op jit(solution)/shard_map/ppermute | solution.py:322
  8.0 1.9 %collective-permute-done.2 = bf16[4,64,128]{2,1,0:T(8,128)(2,1)S(1)} collective-permute-done((bf16[4,64,128]{2,1,0:T(8,128)(2,1)S(1)}, bf16[4,64,128]{2,1,0:T(8,128)(2,1)S(1)}, u32[]{:S(2)}, u32[]{:S(2)}) %collective-permute-start.2) | collective-permute-done | bytes 65568 | tf_op jit(solution)/shard_map/ppermute | solution.py:322
  9.9 3.0 %collective-permute-done.1 = bf16[4,64,128]{2,1,0:T(8,128)(2,1)S(1)} collective-permute-done((bf16[4,64,128]{2,1,0:T(8,128)(2,1)S(1)}, bf16[4,64,128]{2,1,0:T(8,128)(2,1)S(1)}, u32[]{:S(2)}, u32[]{:S(2)}) %collective-permute-start.1) | collective-permute-done | bytes 65568 | tf_op jit(solution)/shard_map/ppermute | solution.py:322
  13.0 1.6 collective-permute-start.3
  14.5 1.5 collective-permute-start.4
  16.5 5.7 %collective-permute-done.3.refs_1_ = bf16[4,4,64,128]{3,2,1,0:T(8,128)(2,1)S(1)} collective-permute-done((bf16[4,4,64,128]{3,2,1,0:T(8,128)(2,1)S(1)}, bf16[4,4,64,128]{3,2,1,0:T(8,128)(2,1)S(1)}, u32[]{:S(2)}, u32[]{:S(2)}) %collective-permute-start.3) | collective-permute-done | bytes 262176 | tf_op jit(solution)/shard_map/ppermute | solution.py:322
  22.3 5.7 %collective-permute-done.4.refs_2_ = bf16[4,4,64,128]{3,2,1,0:T(8,128)(2,1)S(1)} collective-permute-done((bf16[4,4,64,128]{3,2,1,0:T(8,128)(2,1)S(1)}, bf16[4,4,64,128]{3,2,1,0:T(8,128)(2,1)S(1)}, u32[]{:S(2)}, u32[]{:S(2)}) %collective-permute-start.4) | collective-permute-done | bytes 262176 | tf_op jit(solution)/shard_map/ppermute | solution.py:322
  28.5 1.0 collective-permute-done.8.refs_6_
  29.8 1.7 %copy-done = bf16[3,3,512,256]{3,2,1,0:T(8,128)(2,1)S(1)} copy-done((bf16[3,3,512,256]{3,2,1,0:T(8,128)(2,1)S(1)}, bf16[3,3,512,256]{3,2,1,0:T(8,128)(2,1)}, u32[]{:S(2)}) %copy-start) | copy-done | bytes 2359320
  31.5 0.7 copy-done.2
  33.5 8.1 %shard_map.161 = (bf16[4,512,256]{2,1,0:T(8,128)(2,1)S(1)}, bf16[4,512,512]{2,1,0:T(8,128)(2,1)S(1)}, f32[4,512,256]{2,1,0:T(8,128)S(1)}, f32[512,128]{1,0:T(8,128)S(1)}, f32[8,256]{1,0:T(8,128)S(1)}) custom-call(s32[3]{0:T(128)S(1)} %copy-done.6, bf16[4,4,64,128]{3,2,1,0:T(8,128)(2,1)S(1)} %pad_maximum_fusion.refs_0_, ...), custom_call_target="tpu_custom_call" | custom-call | flops 4831838208 | bytes 4194304 | tf_op jit(solution)/shard_map/pallas_call | solution.py:309
  41.7 1.6 collective-permute-start.10
  43.3 23.7 %collective-permute-done.10.one.refs_2_ = bf16[4,512,256]{2,1,0:T(8,128)(2,1)S(1)} collective-permute-done((bf16[4,512,256]{2,1,0:T(8,128)(2,1)S(1)}, bf16[4,512,256]{2,1,0:T(8,128)(2,1)S(1)}, u32[]{:S(2)}, u32[]{:S(2)}) %collective-permute-start.10) | collective-permute-done | bytes 1048608 | tf_op jit(solution)/shard_map/ppermute | solution.py:322
  66.9 0.9 collective-permute-start.13
  67.9 3.1 %collective-permute-done.13 = f32[1,32,256]{2,1,0:T(8,128)S(1)} collective-permute-done((f32[1,32,256]{2,1,0:T(8,128)S(1)}, f32[1,32,256]{2,1,0:T(8,128)S(1)}, u32[]{:S(2)}, u32[]{:S(2)}) %collective-permute-start.13) | collective-permute-done | bytes 32800 | tf_op jit(solution)/shard_map/ppermute | solution.py:322
  70.9 4.3 %collective-permute-done.14 = f32[2,32,256]{2,1,0:T(8,128)S(1)} collective-permute-done((f32[2,32,256]{2,1,0:T(8,128)S(1)}, f32[2,32,256]{2,1,0:T(8,128)S(1)}, u32[]{:S(2)}, u32[]{:S(2)}) %collective-permute-start.14) | collective-permute-done | bytes 65568 | tf_op jit(solution)/shard_map/ppermute | solution.py:322
  75.4 6.8 %collective-permute-done.15 = f32[4,32,256]{2,1,0:T(8,128)S(1)} collective-permute-done((f32[4,32,256]{2,1,0:T(8,128)S(1)}, f32[4,32,256]{2,1,0:T(8,128)S(1)}, u32[]{:S(2)}, u32[]{:S(2)}) %collective-permute-start.15) | collective-permute-done | bytes 131104 | tf_op jit(solution)/shard_map/ppermute | solution.py:322
  82.3 5.6 %shard_map.162.middle_in = f32[4,512,256]{2,1,0:T(8,128)S(1)} custom-call(s32[3]{0:T(128)S(1)} %copy-done.6, bf16[4,512,256]{2,1,0:T(8,128)(2,1)S(1)} %get-tuple-element.23.one.refs_0_, bf16[4,512,256]{2,1,0:T(8,128)(2,1)S(1)} %collective-permute-done.12.two.refs_1_, bf16[3,3,1024,256]{3,2,1,0:T(8,128)(2,1)S(1)} %copy-done.8), custom_call_target="tpu_custom_call" | custom-call | flops 4831838208 | bytes 4194304 | tf_op jit(solution)/shard_map/pallas_call | solution.py:309
  88.0 10.9 %shard_map.163 = (f32[32,256]{1,0:T(8,128)}, bf16[4,512,256]{2,1,0:T(8,128)(2,1)S(1)}, f32[1,256]{1,0:T(1,128)}, f32[1,256]{1,0:T(1,128)}) custom-call(s32[3]{0:T(128)S(1)} %copy-done.7, bf16[4,512,256]{2,1,0:T(8,128)(2,1)S(1)} %collective-permute-done.10.one.refs_2_, bf16[4,512,256]{2,1,0:T(8,128)(2,1)S(1)} %collective-permute-done.11.two.refs_3_, ...), custom_call_target="tpu_custom_call" | custom-call | flops 4831838208 | bytes 4194304 | tf_op jit(solution)/shard_map/pallas_call | solution.py:309
  99.5 2.1 %collective-permute-done.16.two = bf16[4,512,256]{2,1,0:T(8,128)(2,1)S(1)} collective-permute-done((bf16[4,512,256]{2,1,0:T(8,128)(2,1)S(1)}, bf16[4,512,256]{2,1,0:T(8,128)(2,1)S(1)}, u32[]{:S(2)}, u32[]{:S(2)}) %collective-permute-start.16) | collective-permute-done | bytes 1048608 | tf_op jit(solution)/shard_map/ppermute | solution.py:322
  101.7 5.6 %shard_map.165 = bf16[4,512,256]{2,1,0:T(8,128)(2,1)S(1)} custom-call(s32[3]{0:T(128)S(1)} %copy-done.7, bf16[4,512,256]{2,1,0:T(8,128)(2,1)S(1)} %get-tuple-element.26.one.refs_4_, bf16[4,512,256]{2,1,0:T(8,128)(2,1)S(1)} %collective-permute-done.16.two, bf16[3,3,1024,256]{3,2,1,0:T(8,128)(2,1)S(1)} %copy-done.8, ...), custom_call_target="tpu_custom_call" | custom-call | flops 4831838208 | bytes 4194304 | tf_op jit(solution)/shard_map/pallas_call | solution.py:309
  107.3 1.6 collective-permute-start.18
  108.9 1.1 shard_map.166.slope
  110.0 5.6 %shard_map.164.mine = f32[4,512,256]{2,1,0:T(8,128)S(1)} custom-call(s32[3]{0:T(128)S(1)} %copy-done.7, bf16[4,512,256]{2,1,0:T(8,128)(2,1)S(1)} %get-tuple-element.26.one.refs_4_, bf16[4,512,256]{2,1,0:T(8,128)(2,1)S(1)} %collective-permute-done.16.two, bf16[3,3,1024,256]{3,2,1,0:T(8,128)(2,1)S(1)} %copy-done.8, ...), custom_call_target="tpu_custom_call" | custom-call | flops 4831838208 | bytes 4194304 | tf_op jit(solution)/shard_map/pallas_call | solution.py:309
  115.6 16.9 %collective-permute-done.18.other = bf16[4,512,256]{2,1,0:T(8,128)(2,1)S(1)} collective-permute-done((bf16[4,512,256]{2,1,0:T(8,128)(2,1)S(1)}, bf16[4,512,256]{2,1,0:T(8,128)(2,1)S(1)}, u32[]{:S(2)}, u32[]{:S(2)}) %collective-permute-start.18) | collective-permute-done | bytes 1048608 | tf_op jit(solution)/shard_map/ppermute | solution.py:322
  132.5 1.9 %shard_map.167 = (bf16[4,512,256]{2,1,0:T(8,128)(2,1)S(1)}, bf16[4,96,256]{2,1,0:T(8,128)(2,1)S(1)}, f32[1,256]{1,0:T(1,128)}, f32[1,256]{1,0:T(1,128)}) custom-call(f32[4,512,256]{2,1,0:T(8,128)S(1)} %shard_map.164.mine, bf16[4,512,256]{2,1,0:T(8,128)(2,1)S(1)} %collective-permute-done.18.other, f32[4,512,256]{2,1,0:T(8,128)S(1)} %shard_map.166.slope, ...), custom_call_target="tpu_custom_call" | custom-call | flops 268435456 | bytes 4194304 | tf_op jit(solution)/shard_map/pallas_call | solution.py:309
  134.5 12.0 %shard_map.170 = f32[9,1024,256]{2,1,0:T(8,128)} custom-call(s32[3]{0:T(128)S(1)} %copy-done.7, bf16[4,512,256]{2,1,0:T(8,128)(2,1)S(1)} %copy-done.10, bf16[4,512,256]{2,1,0:T(8,128)(2,1)S(1)} %collective-permute-done.12.two.refs_1_, bf16[4,512,256]{2,1,0:T(8,128)(2,1)S(1)} %copy-done.12, bf16[4,512,256]{2,1,0:T(8,128)(2,1)S(1)} %copy-done.14, ...), custom_call_target="tpu_custom_call" | custom-call | flops 9663676416 | bytes 4194304 | tf_op jit(solution)/shard_map/pallas_call | solution.py:309
  146.5 3.2 %shard_map.168 = (f32[4,64,128]{2,1,0:T(8,128)S(1)}, f32[4,64,128]{2,1,0:T(8,128)S(1)}) custom-call(s32[3]{0:T(128)S(1)} %copy-done.7, bf16[4,96,256]{2,1,0:T(8,128)(2,1)S(1)} %get-tuple-element.29.one, bf16[4,96,256]{2,1,0:T(8,128)(2,1)S(1)} %collective-permute-done.19.two, bf16[3,3,512,256]{3,2,1,0:T(8,128)(2,1)S(1)} %copy-done.1, ...), custom_call_target="tpu_custom_call" | custom-call | flops 268435456 | bytes 4194304 | tf_op jit(solution)/shard_map/pallas_call | solution.py:309
  149.7 1.6 collective-permute-start.21
  151.3 7.3 %shard_map.169 = f32[9,512,256]{2,1,0:T(8,128)} custom-call(s32[3]{0:T(128)S(1)} %copy-done.7, bf16[4,512,512]{2,1,0:T(8,128)(2,1)S(1)} %copy-done.18, bf16[4,512,256]{2,1,0:T(8,128)(2,1)S(1)} %get-tuple-element.33.refs_1_), custom_call_target="tpu_custom_call" | custom-call | flops 4831838208 | bytes 4194304 | tf_op jit(solution)/shard_map/pallas_call | solution.py:309
  158.7 0.7 copy.19
  (70 shorter events, 5.1 us)
Async XLA Ops:
  2.2 7.7 %collective-permute-start.2 = (bf16[4,64,128]{2,1,0:T(8,128)(2,1)S(1)}, bf16[4,64,128]{2,1,0:T(8,128)(2,1)S(1)}, u32[]{:S(2)}, u32[]{:S(2)}) collective-permute-start(bf16[4,64,128]{2,1,0:T(8,128)(2,1)S(1)} %get-tuple-element.47), channel_id=1, source_target_pairs={{0,24},{4,28},{8,16},{12,20},{16,8},{20,12},{24,0},{28,4},{1,25},{... | collective-permute-start | bytes 196616 | tf_op jit(solution)/shard_map/ppermute | solution.py:322
  7.3 5.6 %collective-permute-start.1 = (bf16[4,64,128]{2,1,0:T(8,128)(2,1)S(1)}, bf16[4,64,128]{2,1,0:T(8,128)(2,1)S(1)}, u32[]{:S(2)}, u32[]{:S(2)}) collective-permute-start(bf16[4,64,128]{2,1,0:T(8,128)(2,1)S(1)} %get-tuple-element.47), channel_id=1, source_target_pairs={{0,16},{4,20},{8,24},{12,28},{16,0},{20,4},{24,8},{28,12},{1,17},{... | collective-permute-start | bytes 196616 | tf_op jit(solution)/shard_map/ppermute | solution.py:322
  7.3 5.6 %collective-permute-start = (bf16[4,64,128]{2,1,0:T(8,128)(2,1)S(1)}, bf16[4,64,128]{2,1,0:T(8,128)(2,1)S(1)}, u32[]{:S(2)}, u32[]{:S(2)}) collective-permute-start(bf16[4,64,128]{2,1,0:T(8,128)(2,1)S(1)} %get-tuple-element.47), channel_id=1, source_target_pairs={{0,8},{4,12},{8,0},{12,4},{16,24},{20,28},{24,16},{28,20},{1,9},{5... | collective-permute-start | bytes 196616 | tf_op jit(solution)/shard_map/ppermute | solution.py:322
  8.0 93.7 %collective-permute-start.17 = (bf16[3,3,1024,256]{3,2,1,0:T(8,128)(2,1)}, bf16[3,3,1024,256]{3,2,1,0:T(8,128)(2,1)S(1)}, u32[]{:S(2)}, u32[]{:S(2)}) collective-permute-start(bf16[3,3,1024,256]{3,2,1,0:T(8,128)(2,1)} %weight.8), channel_id=1, source_target_pairs={{0,1},{1,0},{2,3},{3,2},{4,5},{5,4},{6,7},{7,6},{8,9},{9,8},{10,11... | collective-permute-start | bytes 14155784 | tf_op jit(solution)/shard_map/ppermute | solution.py:322
  13.0 9.3 %collective-permute-start.3 = (bf16[4,4,64,128]{3,2,1,0:T(8,128)(2,1)S(1)}, bf16[4,4,64,128]{3,2,1,0:T(8,128)(2,1)S(1)}, u32[]{:S(2)}, u32[]{:S(2)}) collective-permute-start(bf16[4,4,64,128]{3,2,1,0:T(8,128)(2,1)S(1)} %pad_maximum_fusion.refs_0_), channel_id=1, source_target_pairs={{0,4},{4,0},{8,12},{12,8},{16,20},{20,16},{24,28},{28,24},{1,5},{5... | collective-permute-start | bytes 786440 | tf_op jit(solution)/shard_map/ppermute | solution.py:322
  14.5 13.4 %collective-permute-start.4 = (bf16[4,4,64,128]{3,2,1,0:T(8,128)(2,1)S(1)}, bf16[4,4,64,128]{3,2,1,0:T(8,128)(2,1)S(1)}, u32[]{:S(2)}, u32[]{:S(2)}) collective-permute-start(bf16[4,4,64,128]{3,2,1,0:T(8,128)(2,1)S(1)} %pad_maximum_fusion.refs_0_), channel_id=1, source_target_pairs={{0,2},{1,3},{2,0},{3,1},{4,6},{5,7},{6,4},{7,5},{8,10},{9,11},{10,... | collective-permute-start | bytes 786440 | tf_op jit(solution)/shard_map/ppermute | solution.py:322
  16.1 11.9 %collective-permute-start.5 = (bf16[4,4,64,128]{3,2,1,0:T(8,128)(2,1)S(1)}, bf16[4,4,64,128]{3,2,1,0:T(8,128)(2,1)S(1)}, u32[]{:S(2)}, u32[]{:S(2)}) collective-permute-start(bf16[4,4,64,128]{3,2,1,0:T(8,128)(2,1)S(1)} %pad_maximum_fusion.refs_0_), channel_id=1, source_target_pairs={{0,6},{1,7},{2,4},{3,5},{4,2},{5,3},{6,0},{7,1},{8,14},{9,15},{10,... | collective-permute-start | bytes 786440 | tf_op jit(solution)/shard_map/ppermute | solution.py:332
  16.5 11.9 %collective-permute-start.6 = (bf16[4,4,64,128]{3,2,1,0:T(8,128)(2,1)S(1)}, bf16[4,4,64,128]{3,2,1,0:T(8,128)(2,1)S(1)}, u32[]{:S(2)}, u32[]{:S(2)}) collective-permute-start(bf16[4,4,64,128]{3,2,1,0:T(8,128)(2,1)S(1)} %pad_maximum_fusion.refs_0_), channel_id=1, source_target_pairs={{0,1},{1,0},{2,3},{3,2},{4,5},{5,4},{6,7},{7,6},{8,9},{9,8},{10,11... | collective-permute-start | bytes 786440 | tf_op jit(solution)/shard_map/ppermute | solution.py:322
  22.3 6.2 %collective-permute-start.7 = (bf16[4,4,64,128]{3,2,1,0:T(8,128)(2,1)S(1)}, bf16[4,4,64,128]{3,2,1,0:T(8,128)(2,1)S(1)}, u32[]{:S(2)}, u32[]{:S(2)}) collective-permute-start(bf16[4,4,64,128]{3,2,1,0:T(8,128)(2,1)S(1)} %collective-permute-done.3.refs_1_), channel_id=1, source_target_pairs={{0,1},{1,0},{2,3},{3,2},{4,5},{5,4},{6,7},{7,6},{8,9},{9,8},{10,11... | collective-permute-start | bytes 786440 | tf_op jit(solution)/shard_map/ppermute | solution.py:322
  27.9 1.5 collective-permute-start.8
  27.9 1.9 %collective-permute-start.9 = (bf16[4,4,64,128]{3,2,1,0:T(8,128)(2,1)S(1)}, bf16[4,4,64,128]{3,2,1,0:T(8,128)(2,1)S(1)}, u32[]{:S(2)}, u32[]{:S(2)}) collective-permute-start(bf16[4,4,64,128]{3,2,1,0:T(8,128)(2,1)S(1)} %collective-permute-done.5.refs_3_), channel_id=1, source_target_pairs={{0,1},{1,0},{2,3},{3,2},{4,5},{5,4},{6,7},{7,6},{8,9},{9,8},{10,11... | collective-permute-start | bytes 786440 | tf_op jit(solution)/shard_map/ppermute | solution.py:322
  33.5 33.4 %copy-start.19 = (f32[32,256]{1,0:T(8,128)S(1)}, f32[32,256]{1,0:T(8,128)}, u32[]{:S(2)}) copy-start(f32[32,256]{1,0:T(8,128)} %param.19) | copy-start | bytes 98308
  33.5 48.8 %copy-start.8 = (bf16[3,3,1024,256]{3,2,1,0:T(8,128)(2,1)S(1)}, bf16[3,3,1024,256]{3,2,1,0:T(8,128)(2,1)}, u32[]{:S(2)}) copy-start(bf16[3,3,1024,256]{3,2,1,0:T(8,128)(2,1)} %weight.8) | copy-start | bytes 14155780
  41.6 46.3 %copy-start.9 = (bf16[4,512,256]{2,1,0:T(8,128)(2,1)}, bf16[4,512,256]{2,1,0:T(8,128)(2,1)S(1)}, u32[]{:S(2)}) copy-start(bf16[4,512,256]{2,1,0:T(8,128)(2,1)S(1)} %get-tuple-element.23.one.refs_0_) | copy-start | bytes 3145732
  41.7 46.3 %copy-start.17 = (bf16[4,512,512]{2,1,0:T(8,128)(2,1)}, bf16[4,512,512]{2,1,0:T(8,128)(2,1)S(1)}, u32[]{:S(2)}) copy-start(bf16[4,512,512]{2,1,0:T(8,128)(2,1)S(1)} %get-tuple-element.32.refs_0_) | copy-start | bytes 6291460
  41.7 25.3 %collective-permute-start.10 = (bf16[4,512,256]{2,1,0:T(8,128)(2,1)S(1)}, bf16[4,512,256]{2,1,0:T(8,128)(2,1)S(1)}, u32[]{:S(2)}, u32[]{:S(2)}) collective-permute-start(bf16[4,512,256]{2,1,0:T(8,128)(2,1)S(1)} %get-tuple-element.23.one.refs_0_), channel_id=1, source_target_pairs={{0,2},{1,3},{2,0},{3,1},{4,6},{5,7},{6,4},{7,5},{8,10},{9,11},{10,... | collective-permute-start | bytes 3145736 | tf_op jit(solution)/shard_map/ppermute | solution.py:322
  43.2 39.1 %collective-permute-start.12 = (bf16[4,512,256]{2,1,0:T(8,128)(2,1)S(1)}, bf16[4,512,256]{2,1,0:T(8,128)(2,1)S(1)}, u32[]{:S(2)}, u32[]{:S(2)}) collective-permute-start(bf16[4,512,256]{2,1,0:T(8,128)(2,1)S(1)} %get-tuple-element.23.one.refs_0_), channel_id=1, source_target_pairs={{0,1},{1,0},{2,3},{3,2},{4,5},{5,4},{6,7},{7,6},{8,9},{9,8},{10,11... | collective-permute-start | bytes 3145736 | tf_op jit(solution)/shard_map/ppermute | solution.py:322
  66.9 21.1 %copy-start.11 = (bf16[4,512,256]{2,1,0:T(8,128)(2,1)}, bf16[4,512,256]{2,1,0:T(8,128)(2,1)S(1)}, u32[]{:S(2)}) copy-start(bf16[4,512,256]{2,1,0:T(8,128)(2,1)S(1)} %collective-permute-done.10.one.refs_2_) | copy-start | bytes 3145732
  66.9 21.0 %collective-permute-start.11 = (bf16[4,512,256]{2,1,0:T(8,128)(2,1)S(1)}, bf16[4,512,256]{2,1,0:T(8,128)(2,1)S(1)}, u32[]{:S(2)}, u32[]{:S(2)}) collective-permute-start(bf16[4,512,256]{2,1,0:T(8,128)(2,1)S(1)} %collective-permute-done.10.one.refs_2_), channel_id=1, source_target_pairs={{0,1},{1,0},{2,3},{3,2},{4,5},{5,4},{6,7},{7,6},{8,9},{9,8},{10,11... | collective-permute-start | bytes 3145736 | tf_op jit(solution)/shard_map/ppermute | solution.py:322
  66.9 4.0 %collective-permute-start.13 = (f32[1,32,256]{2,1,0:T(8,128)S(1)}, f32[1,32,256]{2,1,0:T(8,128)S(1)}, u32[]{:S(2)}, u32[]{:S(2)}) collective-permute-start(f32[1,32,256]{2,1,0:T(8,128)S(1)} %bitcast.28), channel_id=1, source_target_pairs={{0,4},{4,0},{8,12},{12,8},{16,20},{20,16},{24,28},{28,24},{1,5},{5... | collective-permute-start | bytes 98312 | tf_op jit(solution)/shard_map/ppermute | solution.py:322
  70.9 4.3 %collective-permute-start.14 = (f32[2,32,256]{2,1,0:T(8,128)S(1)}, f32[2,32,256]{2,1,0:T(8,128)S(1)}, u32[]{:S(2)}, u32[]{:S(2)}) collective-permute-start(f32[2,32,256]{2,1,0:T(8,128)S(1)} %pad_maximum_fusion.3), channel_id=1, source_target_pairs={{0,8},{4,12},{8,0},{12,4},{16,24},{20,28},{24,16},{28,20},{1,9},{5... | collective-permute-start | bytes 196616 | tf_op jit(solution)/shard_map/ppermute | solution.py:322
  75.2 7.0 %collective-permute-start.15 = (f32[4,32,256]{2,1,0:T(8,128)S(1)}, f32[4,32,256]{2,1,0:T(8,128)S(1)}, u32[]{:S(2)}, u32[]{:S(2)}) collective-permute-start(f32[4,32,256]{2,1,0:T(8,128)S(1)} %pad_maximum_fusion.2), channel_id=1, source_target_pairs={{0,16},{4,20},{8,24},{12,28},{16,0},{20,4},{24,8},{28,12},{1,17},{... | collective-permute-start | bytes 393224 | tf_op jit(solution)/shard_map/ppermute | solution.py:322
  88.0 10.9 %copy-start.13 = (bf16[4,512,256]{2,1,0:T(8,128)(2,1)}, bf16[4,512,256]{2,1,0:T(8,128)(2,1)S(1)}, u32[]{:S(2)}) copy-start(bf16[4,512,256]{2,1,0:T(8,128)(2,1)S(1)} %collective-permute-done.11.two.refs_3_) | copy-start | bytes 3145732
  88.0 11.0 %copy-start.1 = (bf16[3,3,512,256]{3,2,1,0:T(8,128)(2,1)S(1)}, bf16[3,3,512,256]{3,2,1,0:T(8,128)(2,1)}, u32[]{:S(2)}) copy-start(bf16[3,3,512,256]{3,2,1,0:T(8,128)(2,1)} %weight.9) | copy-start | bytes 7077892
  99.0 2.7 %collective-permute-start.16 = (bf16[4,512,256]{2,1,0:T(8,128)(2,1)S(1)}, bf16[4,512,256]{2,1,0:T(8,128)(2,1)S(1)}, u32[]{:S(2)}, u32[]{:S(2)}) collective-permute-start(bf16[4,512,256]{2,1,0:T(8,128)(2,1)S(1)} %get-tuple-element.26.one.refs_4_), channel_id=1, source_target_pairs={{0,1},{1,0},{2,3},{3,2},{4,5},{5,4},{6,7},{7,6},{8,9},{9,8},{10,11... | collective-permute-start | bytes 3145736 | tf_op jit(solution)/shard_map/ppermute | solution.py:322
  99.0 47.4 %collective-permute-start.20 = (bf16[3,3,512,256]{3,2,1,0:T(8,128)(2,1)S(1)}, bf16[3,3,512,256]{3,2,1,0:T(8,128)(2,1)S(1)}, u32[]{:S(2)}, u32[]{:S(2)}) collective-permute-start(bf16[3,3,512,256]{3,2,1,0:T(8,128)(2,1)S(1)} %copy-done.1), channel_id=1, source_target_pairs={{0,1},{1,0},{2,3},{3,2},{4,5},{5,4},{6,7},{7,6},{8,9},{9,8},{10,11... | collective-permute-start | bytes 7077896 | tf_op jit(solution)/shard_map/ppermute | solution.py:322
  107.3 25.3 %collective-permute-start.18 = (bf16[4,512,256]{2,1,0:T(8,128)(2,1)S(1)}, bf16[4,512,256]{2,1,0:T(8,128)(2,1)S(1)}, u32[]{:S(2)}, u32[]{:S(2)}) collective-permute-start(bf16[4,512,256]{2,1,0:T(8,128)(2,1)S(1)} %shard_map.165), channel_id=1, source_target_pairs={{0,2},{1,3},{2,0},{3,1},{4,6},{5,7},{6,4},{7,5},{8,10},{9,11},{10,... | collective-permute-start | bytes 3145736 | tf_op jit(solution)/shard_map/ppermute | solution.py:322
  115.6 18.9 %copy-start.10 = (bf16[4,512,256]{2,1,0:T(8,128)(2,1)S(1)}, bf16[4,512,256]{2,1,0:T(8,128)(2,1)}, u32[]{:S(2)}) copy-start(bf16[4,512,256]{2,1,0:T(8,128)(2,1)} %copy-done.9) | copy-start | bytes 3145732
  115.6 18.9 %copy-start.12 = (bf16[4,512,256]{2,1,0:T(8,128)(2,1)S(1)}, bf16[4,512,256]{2,1,0:T(8,128)(2,1)}, u32[]{:S(2)}) copy-start(bf16[4,512,256]{2,1,0:T(8,128)(2,1)} %copy-done.11) | copy-start | bytes 3145732
  115.6 18.9 %copy-start.14 = (bf16[4,512,256]{2,1,0:T(8,128)(2,1)S(1)}, bf16[4,512,256]{2,1,0:T(8,128)(2,1)}, u32[]{:S(2)}) copy-start(bf16[4,512,256]{2,1,0:T(8,128)(2,1)} %copy-done.13) | copy-start | bytes 3145732
  134.5 12.0 %collective-permute-start.19 = (bf16[4,96,256]{2,1,0:T(8,128)(2,1)S(1)}, bf16[4,96,256]{2,1,0:T(8,128)(2,1)S(1)}, u32[]{:S(2)}, u32[]{:S(2)}) collective-permute-start(bf16[4,96,256]{2,1,0:T(8,128)(2,1)S(1)} %get-tuple-element.29.one), channel_id=1, source_target_pairs={{0,1},{1,0},{2,3},{3,2},{4,5},{5,4},{6,7},{7,6},{8,9},{9,8},{10,11... | collective-permute-start | bytes 589832 | tf_op jit(solution)/shard_map/ppermute | solution.py:322
  149.7 8.9 %collective-permute-start.21 = (f32[4,64,128]{2,1,0:T(8,128)S(1)}, f32[4,64,128]{2,1,0:T(8,128)S(1)}, u32[]{:S(2)}, u32[]{:S(2)}) collective-permute-start(f32[4,64,128]{2,1,0:T(8,128)S(1)} %get-tuple-element.31), channel_id=1, source_target_pairs={{0,2},{1,3},{2,0},{3,1},{4,6},{5,7},{6,4},{7,5},{8,10},{9,11},{10,... | collective-permute-start | bytes 393224 | tf_op jit(solution)/shard_map/ppermute | solution.py:322
  (10 other events, 45.5 us)

commit v2 on v1

--- a/solution.py
+++ b/solution.py
@@ -439,9 +439,9 @@
 
 
 def first_kernel(starts, *refs):
-    blocks, (weight_in, gain, shift) = refs[:8], refs[8:11]
-    hidden, field_out, pre_out, keep, stats = refs[11:16]
-    field, weight, lower, middle, upper, sems = refs[16:]
+    blocks, (weight_in, scales) = refs[:8], refs[8:10]
+    hidden, field_out, pre_out, keep, stats = refs[10:15]
+    field, weight, lower, middle, upper, sems = refs[15:]
     mel_count, total, width = field.shape
     out_width = middle.shape[2]
     place, column = lax.axis_index("tm"), lax.axis_index("chan")
@@ -507,8 +507,8 @@
     stats[0:1] = center
     stats[1:2] = inverse
     stats[2:3] = pixels
-    scale = gain[...] * inverse
-    offset = shift[...] - center * scale
+    scale = scales[0:1] * inverse
+    offset = scales[1:2] - center * scale
 
     def activate(at, carry):
         mask = widen(keep[pl.ds(at, ROWS)], out_width)
@@ -522,14 +522,14 @@
     save_pre.wait()
 
 
-def first_block(blocks, weight, gain, shift, starts, total):
+def first_block(blocks, weight, scales, starts, total):
     count, mel_count, frames, lanes = blocks[0].shape
     width, out_width = weight.shape[2], weight.shape[3]
     padded = (mel_count, total + 2 * TILE, out_width)
     return call(
         first_kernel,
-        (starts, *blocks, weight, gain, shift),
-        [scalar_spec()] + [place_spec()] * 9 + [whole_spec()] * 2,
+        (starts, *blocks, weight, scales),
+        [scalar_spec()] + [place_spec()] * 9 + [whole_spec()],
         [
             ((mel_count, total, out_width), bf16),
             ((mel_count, total, width), bf16),
@@ -547,15 +547,15 @@
             pltpu.SemaphoreType.DMA((1 + 8 * count,)),
         ],
         2 * 9 * mel_count * total * width * out_width,
-        32,
-    )
-
-
-def slope_kernel(pre, stats, gain, shift, keep, slope):
+        16,
+    )
+
+
+def slope_kernel(pre, stats, scales, keep, slope):
     mel_count, total, width = pre.shape
     center, inverse = stats[0:1], stats[1:2]
-    scale = gain[...] * inverse
-    offset = shift[...] - center * scale
+    scale = scales[0:1] * inverse
+    offset = scales[1:2] - center * scale
 
     def rows(at, carry):
         mask = widen(keep[pl.ds(at, ROWS)], width)
@@ -567,16 +567,16 @@
     by_rows(total, rows, 0)
 
 
-def first_slope(pre, stats, gain, shift, keep):
+def first_slope(pre, stats, scales, keep):
     return call(
         slope_kernel,
-        (pre, stats, gain, shift, keep),
-        [whole_spec()] * 5,
+        (pre, stats, scales, keep),
+        [whole_spec()] * 4,
         [(pre.shape, f32)],
         [whole_spec()],
         [],
         2**28,
-        10,
+        6,
     )[0]
 
 
@@ -619,11 +619,11 @@
         [whole_spec()],
         [pltpu.VMEM(padded, f32)] * 2,
         2 * 18 * mel_count * total * width * width,
-        20,
+        14,
     )[0]
 
 
-def second_kernel(starts, one, two, weight, middle_in, keep, gain, shift, cotangents, *refs):
+def second_kernel(starts, one, two, weight, middle_in, keep, scales, cotangents, *refs):
     readout, grad, gain_grad, shift_grad = refs[:4]
     middle, slope, lower, upper, hold, wide, full, sems = refs[4:]
     mel_count, total, width = one.shape
@@ -669,8 +669,8 @@
     first, second, num = by_rows(total, combine, (blank, blank, blank))
     pixels = column_sum(num) * mel_count
     center, inverse = moments((first, second), keep, pixels)
-    scale = gain[...] * inverse
-    offset = shift[...] - center * scale
+    scale = scales[2:3] * inverse
+    offset = scales[3:4] - center * scale
 
     def activate(at, carry):
         mask = widen(keep[pl.ds(at, ROWS)], width)
@@ -749,14 +749,14 @@
     by_rows(total, finish, 0)
 
 
-def second_block(one, two, weight, partial, keep, gain, shift, starts, cotangents, own):
+def second_block(one, two, weight, partial, keep, scales, starts, cotangents, own):
     mel_count, total, width = one.shape
     padded = (mel_count, total + 2 * TILE, width)
     full = (mel_count, total, width)
     return call(
         second_kernel,
-        (starts, one, two, weight, partial, keep, gain, shift, cotangents),
-        [scalar_spec()] + [whole_spec()] * 7 + [place_spec()],
+        (starts, one, two, weight, partial, keep, scales, cotangents),
+        [scalar_spec()] + [whole_spec()] * 6 + [place_spec()],
         [((own, width), f32), (full, bf16), ((1, width), f32), ((1, width), f32)],
         [whole_spec()] * 4,
         [
@@ -770,7 +770,7 @@
             pltpu.SemaphoreType.DMA((cotangents.shape[0],)),
         ],
         2 * 18 * mel_count * total * width * width,
-        40,
+        22,
     )
 
 
@@ -816,11 +816,11 @@
             pltpu.VMEM(padded, f32),
         ],
         2 * 18 * mel_count * total * width * width,
-        28,
+        14,
     )[0]
 
 
-def norm_kernel(mine, other, slope, pre, stats, gain, keep, *refs):
+def norm_kernel(mine, other, slope, pre, stats, scales, keep, *refs):
     grad, window, gain_grad, shift_grad, padded = refs
     mel_count, total, width = mine.shape
     center, inverse, pixels = stats[0:1], stats[1:2], stats[2:3]
@@ -845,7 +845,7 @@
     shift_grad[...] = plain
     gain_grad[...] = along
     plain, along = plain / pixels, along / pixels
-    scale = gain[...] * inverse
+    scale = scales[0:1] * inverse
     for m in range(mel_count):
         padded[m, :edge] = jnp.zeros((edge, width), bf16)
         padded[m, edge + total :] = jnp.zeros((edge, width), bf16)
@@ -865,12 +865,12 @@
         window[m] = padded[m, pl.ds(pl.multiple_of(place * frames, frames), reach)]
 
 
-def norm_back_first(mine, other, slope, pre, stats, gain, keep, frames):
+def norm_back_first(mine, other, slope, pre, stats, scales, keep, frames):
     mel_count, total, width = mine.shape
     edge = 16
     return call(
         norm_kernel,
-        (mine, other, slope, pre, stats, gain, keep),
+        (mine, other, slope, pre, stats, scales, keep),
         [whole_spec()] * 7,
         [
             ((mel_count, total, width), bf16),
@@ -881,7 +881,7 @@
         [whole_spec()] * 4,
         [pltpu.VMEM((mel_count, total + 2 * edge, width), bf16)],
         2**28,
-        20,
+        12,
     )
 
 
@@ -969,7 +969,7 @@
             pltpu.SemaphoreType.DMA((2,)),
         ],
         2 * 9 * mel_count * total * in_width * out_width,
-        24,
+        14,
     )[0]
     return out.reshape(3, 3, in_width, out_width)
 
@@ -1019,7 +1019,7 @@
             pltpu.VMEM((mel_count, reach + 2 * TILE, lanes), f32),
         ],
         2**28,
-        20,
+        8,
     )
 
 
@@ -1038,8 +1038,7 @@
     frames, mel_count, lanes = features.shape
     places = lax.axis_size("tm")
     total = frames * places
-    gain1, shift1 = norm1_gain[None], norm1_bias[None]
-    gain2, shift2 = norm2_gain[None], norm2_bias[None]
+    scales = jnp.stack([norm1_gain, norm1_bias, norm2_gain, norm2_bias])
 
     marked = jnp.where(valid[:, None, None] > 0, features, jnp.asarray(ABSENT, bf16))
     own = jnp.transpose(marked, (1, 0, 2))
@@ -1051,21 +1050,29 @@
         swap_both(along, "tm", 1, "chan", 2),
     ]
     blocks = near + [swap(block, "chan", 1) for block in near]
-    other_conv2 = swap(conv2_weight, "chan", 1)
-    other_conv1 = swap(conv1_weight, "chan", 1)
+
+    hidden, field, pre, keep, stats = first_block(
+        blocks, conv1_weight, scales, clip_starts, total
+    )
+    hidden_near = swap(hidden, "chan", 1)
+    hidden_far = swap(hidden, "chan", 2)
+
+    conv2_weight, conv1_weight, readout_grad, hidden_near = lax.optimization_barrier(
+        (conv2_weight, conv1_weight, readout_grad, hidden_near)
+    )
+    partial = second_partial(hidden, hidden_near, conv2_weight, clip_starts)
+    slope = first_slope(pre, stats, scales, keep)
     cotangent = readout_grad[None]
     bit = 1
     while bit < places:
         cotangent = jnp.concatenate([cotangent, swap(cotangent, "tm", bit)])
         bit *= 2
-
-    hidden, field, pre, keep, stats = first_block(
-        blocks, conv1_weight, gain1, shift1, clip_starts, total
-    )
-    hidden_far = swap(hidden, "chan", 2)
-    hidden_near = swap(hidden, "chan", 1)
-    slope = first_slope(pre, stats, gain1, shift1, keep)
-    partial = second_partial(hidden, hidden_near, conv2_weight, clip_starts)
+    other_conv2 = swap(conv2_weight, "chan", 1)
+    other_conv1 = swap(conv1_weight, "chan", 1)
+    hidden_far, partial, slope, cotangent, other_conv2, other_conv1 = lax.optimization_barrier(
+        (hidden_far, partial, slope, cotangent, other_conv2, other_conv1)
+    )
+
     hidden_last = swap(hidden_far, "chan", 1)
     readout, grad2, gain2_grad, shift2_grad = second_block(
         hidden_far,
@@ -1073,8 +1080,7 @@
         conv2_weight,
         partial,
         keep,
-        gain2,
-        shift2,
+        scales,
         clip_starts,
         cotangent,
         readout_grad.shape[0],
@@ -1082,12 +1088,15 @@
     grad2_near = swap(grad2, "chan", 1)
     away = hidden_back(2, grad2, grad2_near, conv2_weight, other_conv2, clip_starts, bf16)
     came = swap(away, "chan", 2)
+
     mine = hidden_back(0, grad2, grad2_near, conv2_weight, other_conv2, clip_starts, f32)
     weight2_grad = weight_back(
         [hidden, hidden_near, hidden_far, hidden_last], grad2, clip_starts
     )
+    came, mine, weight2_grad = lax.optimization_barrier((came, mine, weight2_grad))
+
     grad1, window, gain1_grad, shift1_grad = norm_back_first(
-        mine, came, slope, pre, stats, gain1, keep, frames
+        mine, came, slope, pre, stats, scales, keep, frames
     )
     window_near = swap(window, "chan", 1)
     input_mine, input_away = input_back(
@@ -1095,6 +1104,7 @@
     )
     input_came = swap(input_away, "chan", 2)
     weight1_grad = weight_back([field], grad1, clip_starts)
+    input_came, weight1_grad = lax.optimization_barrier((input_came, weight1_grad))
     live = (valid > 0).astype(f32)[None, :, None]
     input_grad = jnp.transpose((input_mine + input_came) * live, (1, 0, 2))
     return (

time: 160 us -> 132 us (0.82)
  waiting for transfers between devices: 74.7 us -> 43.7 us
  starting transfers between devices: 16.3 us -> 19.9 us
  local copies, waits for them, and re-layouts: 4.51 us -> 1.41 us
  Pallas kernels: 61.3 us -> 63.6 us
    ppermute x21, waiting for transfers between devices: 74.7 us -> 37 us  [swap(): return lax.ppermute(shard, axis, [(i, i ^ bit) for i in range(count)])]
    ppermute x1, waiting for transfers between devices: 0.01 us -> 6.66 us  [swap_both(): return lax.ppermute(shard, (first, second), pairs)]
    unnamed x41 -> x9, local copies, waits for them, and re-layouts: 4.51 us -> 1.41 us
    pallas_call x10, Pallas kernels: 61.3 us -> 63.6 us  [call(): pl.pallas_call(body, out_shape=tuple((jax.ShapeDtypeStruct(s, d) for s, d...]
    ppermute x1, starting transfers between devices: 0.48 us -> 2.51 us  [swap_both(): return lax.ppermute(shard, (first, second), pairs)]
    ppermute x21, starting transfers between devices: 15.8 us -> 17.4 us  [swap(): return lax.ppermute(shard, axis, [(i, i ^ bit) for i in range(count)])]
  transfers between devices with their start and end apart: 22 -> 22, of which waited for: 12 -> 16; matrix products, arithmetic and copies ran while one was open for 0% -> 1% of each run, Pallas kernels for 36% -> 24%
where the time goes in v2:
time: 132 us
  Pallas kernels  63.6 us (48%)
  waiting for transfers between devices  43.7 us (33%)
  starting transfers between devices  19.9 us (15%)
  other arithmetic  2.47 us (2%)
  local copies, waits for them, and re-layouts  1.41 us (1%)
    pallas_call x10, Pallas kernels, call(): pl.pallas_call(body, out_shape=tuple((jax.ShapeDtypeStruct(s, d) for s, d...  63.6 us
    ppermute x21, waiting for transfers between devices, swap(): return lax.ppermute(shard, axis, [(i, i ^ bit) for i in range(count)])  37 us
    ppermute x21, starting transfers between devices, swap(): return lax.ppermute(shard, axis, [(i, i ^ bit) for i in range(count)])  17.4 us
    ppermute x1, waiting for transfers between devices, swap_both(): return lax.ppermute(shard, (first, second), pairs)  6.66 us
  transfers between devices with their start and end apart: 22, of which 16 were waited for; matrix products, arithmetic and copies ran while one was open for 1% of the time, Pallas kernels for 24%

profile of v2, /device:TPU:0, one launch (start us, length us, event | category | flops | bytes accessed | tf_op | source)
XLA Modules:
  0.0 131.9 jit_solution(7705018556611470324)
XLA Ops:
  1.3 0.9 fusion
  2.2 4.1 %collective-permute-start.1 = (bf16[4,64,128]{2,1,0:T(8,128)(2,1)S(1)}, bf16[4,64,128]{2,1,0:T(8,128)(2,1)S(1)}, u32[]{:S(2)}, u32[]{:S(2)}) collective-permute-start(bf16[4,64,128]{2,1,0:T(8,128)(2,1)S(1)} %get-tuple-element.77), channel_id=1, source_target_pairs={{0,16},{4,20},{8,24},{12,28},{16,0},{20,4},{24,8},{28,12},{1,17},{... | collective-permute-start | bytes 196616 | tf_op jit(solution)/shard_map/ppermute | solution.py:322
  6.3 1.6 %collective-permute-start = (bf16[4,64,128]{2,1,0:T(8,128)(2,1)S(1)}, bf16[4,64,128]{2,1,0:T(8,128)(2,1)S(1)}, u32[]{:S(2)}, u32[]{:S(2)}) collective-permute-start(bf16[4,64,128]{2,1,0:T(8,128)(2,1)S(1)} %get-tuple-element.77), channel_id=1, source_target_pairs={{0,8},{4,12},{8,0},{12,4},{16,24},{20,28},{24,16},{28,20},{1,9},{5... | collective-permute-start | bytes 196616 | tf_op jit(solution)/shard_map/ppermute | solution.py:322
  7.9 1.5 %collective-permute-done.1 = bf16[4,64,128]{2,1,0:T(8,128)(2,1)S(1)} collective-permute-done((bf16[4,64,128]{2,1,0:T(8,128)(2,1)S(1)}, bf16[4,64,128]{2,1,0:T(8,128)(2,1)S(1)}, u32[]{:S(2)}, u32[]{:S(2)}) %collective-permute-start.1) | collective-permute-done | bytes 65568 | tf_op jit(solution)/shard_map/ppermute | solution.py:322
  9.4 1.2 collective-permute-done
  10.6 3.4 %collective-permute-done.2 = bf16[4,64,128]{2,1,0:T(8,128)(2,1)S(1)} collective-permute-done((bf16[4,64,128]{2,1,0:T(8,128)(2,1)S(1)}, bf16[4,64,128]{2,1,0:T(8,128)(2,1)S(1)}, u32[]{:S(2)}, u32[]{:S(2)}) %collective-permute-start.2) | collective-permute-done | bytes 65568 | tf_op jit(solution)/shard_map/ppermute | solution.py:322
  14.0 2.5 %collective-permute-start.5 = (bf16[4,4,64,128]{3,2,1,0:T(8,128)(2,1)S(1)}, bf16[4,4,64,128]{3,2,1,0:T(8,128)(2,1)S(1)}, u32[]{:S(2)}, u32[]{:S(2)}) collective-permute-start(bf16[4,4,64,128]{3,2,1,0:T(8,128)(2,1)S(1)} %pad_maximum_fusion.refs_0_), channel_id=1, source_target_pairs={{0,6},{1,7},{2,4},{3,5},{4,2},{5,3},{6,0},{7,1},{8,14},{9,15},{10,... | collective-permute-start | bytes 786440 | tf_op jit(solution)/shard_map/ppermute | solution.py:332
  17.6 6.7 %collective-permute-done.5.refs_3_ = bf16[4,4,64,128]{3,2,1,0:T(8,128)(2,1)S(1)} collective-permute-done((bf16[4,4,64,128]{3,2,1,0:T(8,128)(2,1)S(1)}, bf16[4,4,64,128]{3,2,1,0:T(8,128)(2,1)S(1)}, u32[]{:S(2)}, u32[]{:S(2)}) %collective-permute-start.5) | collective-permute-done | bytes 262176 | tf_op jit(solution)/shard_map/ppermute | solution.py:332
  24.2 2.8 %collective-permute-done.4.refs_2_ = bf16[4,4,64,128]{3,2,1,0:T(8,128)(2,1)S(1)} collective-permute-done((bf16[4,4,64,128]{3,2,1,0:T(8,128)(2,1)S(1)}, bf16[4,4,64,128]{3,2,1,0:T(8,128)(2,1)S(1)}, u32[]{:S(2)}, u32[]{:S(2)}) %collective-permute-start.4) | collective-permute-done | bytes 262176 | tf_op jit(solution)/shard_map/ppermute | solution.py:322
  29.6 9.5 %shard_map.161 = (bf16[4,512,256]{2,1,0:T(8,128)(2,1)S(1)}, bf16[4,512,512]{2,1,0:T(8,128)(2,1)S(1)}, f32[4,512,256]{2,1,0:T(8,128)S(1)}, f32[512,128]{1,0:T(8,128)S(1)}, f32[8,256]{1,0:T(8,128)S(1)}) custom-call(s32[3]{0:T(128)S(1)} %copy-done, bf16[4,4,64,128]{3,2,1,0:T(8,128)(2,1)S(1)} %pad_maximum_fusion.refs_0_, ...), custom_call_target="tpu_custom_call" | custom-call | flops 4831838208 | bytes 4194304 | tf_op jit(solution)/shard_map/pallas_call | solution.py:309
  39.3 2.5 %collective-permute-done.11.two.refs_1_ = bf16[4,512,256]{2,1,0:T(8,128)(2,1)S(1)} collective-permute-done((bf16[4,512,256]{2,1,0:T(8,128)(2,1)S(1)}, bf16[4,512,256]{2,1,0:T(8,128)(2,1)S(1)}, u32[]{:S(2)}, u32[]{:S(2)}) %collective-permute-start.11) | collective-permute-done | bytes 1048608 | tf_op jit(solution)/shard_map/ppermute | solution.py:322
  42.3 1.5 %collective-permute-start.10 = (bf16[4,512,256]{2,1,0:T(8,128)(2,1)S(1)}, bf16[4,512,256]{2,1,0:T(8,128)(2,1)S(1)}, u32[]{:S(2)}, u32[]{:S(2)}) collective-permute-start(bf16[4,512,256]{2,1,0:T(8,128)(2,1)S(1)} %get-tuple-element.38.one.refs_0_), channel_id=1, source_target_pairs={{0,2},{1,3},{2,0},{3,1},{4,6},{5,7},{6,4},{7,5},{8,10},{9,11},{10,... | collective-permute-start | bytes 3145736 | tf_op jit(solution)/shard_map/ppermute | solution.py:322
  43.8 0.8 collective-permute-start.12
  44.6 3.1 %collective-permute-done.12 = f32[1,32,256]{2,1,0:T(8,128)S(1)} collective-permute-done((f32[1,32,256]{2,1,0:T(8,128)S(1)}, f32[1,32,256]{2,1,0:T(8,128)S(1)}, u32[]{:S(2)}, u32[]{:S(2)}) %collective-permute-start.12) | collective-permute-done | bytes 32800 | tf_op jit(solution)/shard_map/ppermute | solution.py:322
  48.4 1.1 shard_map.163.slope
  49.6 2.5 %collective-permute-done.13 = f32[2,32,256]{2,1,0:T(8,128)S(1)} collective-permute-done((f32[2,32,256]{2,1,0:T(8,128)S(1)}, f32[2,32,256]{2,1,0:T(8,128)S(1)}, u32[]{:S(2)}, u32[]{:S(2)}) %collective-permute-start.13) | collective-permute-done | bytes 65568 | tf_op jit(solution)/shard_map/ppermute | solution.py:322
  52.0 3.2 %collective-permute-start.14 = (f32[4,32,256]{2,1,0:T(8,128)S(1)}, f32[4,32,256]{2,1,0:T(8,128)S(1)}, u32[]{:S(2)}, u32[]{:S(2)}) collective-permute-start(f32[4,32,256]{2,1,0:T(8,128)S(1)} %pad_maximum_fusion.2), channel_id=1, source_target_pairs={{0,16},{4,20},{8,24},{12,28},{16,0},{20,4},{24,8},{28,12},{1,17},{... | collective-permute-start | bytes 393224 | tf_op jit(solution)/shard_map/ppermute | solution.py:322
  55.3 5.6 %shard_map.162.middle_in = f32[4,512,256]{2,1,0:T(8,128)S(1)} custom-call(s32[3]{0:T(128)S(1)} %copy-done.1, bf16[4,512,256]{2,1,0:T(8,128)(2,1)S(1)} %get-tuple-element.38.one.refs_0_, bf16[4,512,256]{2,1,0:T(8,128)(2,1)S(1)} %collective-permute-done.11.two.refs_1_, bf16[3,3,1024,256]{3,2,1,0:T(8,128)(2,1)S(1)} %copy-done.2), custom_call_target="tpu_custom_call" | custom-call | flops 4831838208 | bytes 4194304 | tf_op jit(solution)/shard_map/pallas_call | solution.py:309
  60.9 6.6 %collective-permute-done.10.one.refs_2_ = bf16[4,512,256]{2,1,0:T(8,128)(2,1)S(1)} collective-permute-done((bf16[4,512,256]{2,1,0:T(8,128)(2,1)S(1)}, bf16[4,512,256]{2,1,0:T(8,128)(2,1)S(1)}, u32[]{:S(2)}, u32[]{:S(2)}) %collective-permute-start.10) | collective-permute-done | bytes 1048608 | tf_op jit(solution)/shard_map/ppermute | solution.py:322
  67.5 2.7 %collective-permute-done.17.two.refs_3_ = bf16[4,512,256]{2,1,0:T(8,128)(2,1)S(1)} collective-permute-done((bf16[4,512,256]{2,1,0:T(8,128)(2,1)S(1)}, bf16[4,512,256]{2,1,0:T(8,128)(2,1)S(1)}, u32[]{:S(2)}, u32[]{:S(2)}) %collective-permute-start.17) | collective-permute-done | bytes 1048608 | tf_op jit(solution)/shard_map/ppermute | solution.py:322
  70.2 10.9 %shard_map.164 = (f32[32,256]{1,0:T(8,128)}, bf16[4,512,256]{2,1,0:T(8,128)(2,1)S(1)}, f32[1,256]{1,0:T(1,128)}, f32[1,256]{1,0:T(1,128)}) custom-call(s32[3]{0:T(128)S(1)} %copy-done.1, bf16[4,512,256]{2,1,0:T(8,128)(2,1)S(1)} %collective-permute-done.10.one.refs_2_, bf16[4,512,256]{2,1,0:T(8,128)(2,1)S(1)} %collective-permute-done.17.two.refs_3_, ...), custom_call_target="tpu_custom_call" | custom-call | flops 4831838208 | bytes 4194304 | tf_op jit(solution)/shard_map/pallas_call | solution.py:309
  81.3 2.5 %collective-permute-done.18.two = bf16[4,512,256]{2,1,0:T(8,128)(2,1)S(1)} collective-permute-done((bf16[4,512,256]{2,1,0:T(8,128)(2,1)S(1)}, bf16[4,512,256]{2,1,0:T(8,128)(2,1)S(1)}, u32[]{:S(2)}, u32[]{:S(2)}) %collective-permute-start.18) | collective-permute-done | bytes 1048608 | tf_op jit(solution)/shard_map/ppermute | solution.py:322
  83.8 5.6 %shard_map.165 = bf16[4,512,256]{2,1,0:T(8,128)(2,1)S(1)} custom-call(s32[3]{0:T(128)S(1)} %copy-done.1, bf16[4,512,256]{2,1,0:T(8,128)(2,1)S(1)} %get-tuple-element.50.one.refs_4_, bf16[4,512,256]{2,1,0:T(8,128)(2,1)S(1)} %collective-permute-done.18.two, bf16[3,3,1024,256]{3,2,1,0:T(8,128)(2,1)S(1)} %copy-done.2, ...), custom_call_target="tpu_custom_call" | custom-call | flops 4831838208 | bytes 4194304 | tf_op jit(solution)/shard_map/pallas_call | solution.py:309
  89.4 1.6 %collective-permute-start.19 = (bf16[4,512,256]{2,1,0:T(8,128)(2,1)S(1)}, bf16[4,512,256]{2,1,0:T(8,128)(2,1)S(1)}, u32[]{:S(2)}, u32[]{:S(2)}) collective-permute-start(bf16[4,512,256]{2,1,0:T(8,128)(2,1)S(1)} %shard_map.165), channel_id=1, source_target_pairs={{0,2},{1,3},{2,0},{3,1},{4,6},{5,7},{6,4},{7,5},{8,10},{9,11},{10,... | collective-permute-start | bytes 3145736 | tf_op jit(solution)/shard_map/ppermute | solution.py:322
  91.0 12.0 %shard_map.167 = f32[9,1024,256]{2,1,0:T(8,128)} custom-call(s32[3]{0:T(128)S(1)} %copy-done.1, bf16[4,512,256]{2,1,0:T(8,128)(2,1)S(1)} %get-tuple-element.38.one.refs_0_, bf16[4,512,256]{2,1,0:T(8,128)(2,1)S(1)} %collective-permute-done.11.two.refs_1_, bf16[4,512,256]{2,1,0:T(8,128)(2,1)S(1)} %collective-permute-done.10.one.refs_2_, ...), custom_call_target="tpu_custom_call" | custom-call | flops 9663676416 | bytes 4194304 | tf_op jit(solution)/shard_map/pallas_call | solution.py:309
  103.0 5.5 %shard_map.166.mine = f32[4,512,256]{2,1,0:T(8,128)S(1)} custom-call(s32[3]{0:T(128)S(1)} %copy-done.1, bf16[4,512,256]{2,1,0:T(8,128)(2,1)S(1)} %get-tuple-element.50.one.refs_4_, bf16[4,512,256]{2,1,0:T(8,128)(2,1)S(1)} %collective-permute-done.18.two, bf16[3,3,1024,256]{3,2,1,0:T(8,128)(2,1)S(1)} %copy-done.2, ...), custom_call_target="tpu_custom_call" | custom-call | flops 4831838208 | bytes 4194304 | tf_op jit(solution)/shard_map/pallas_call | solution.py:309
  108.6 6.1 %collective-permute-done.19.other = bf16[4,512,256]{2,1,0:T(8,128)(2,1)S(1)} collective-permute-done((bf16[4,512,256]{2,1,0:T(8,128)(2,1)S(1)}, bf16[4,512,256]{2,1,0:T(8,128)(2,1)S(1)}, u32[]{:S(2)}, u32[]{:S(2)}) %collective-permute-start.19) | collective-permute-done | bytes 1048608 | tf_op jit(solution)/shard_map/ppermute | solution.py:322
  114.6 1.9 %shard_map.168 = (bf16[4,512,256]{2,1,0:T(8,128)(2,1)S(1)}, bf16[4,96,256]{2,1,0:T(8,128)(2,1)S(1)}, f32[1,256]{1,0:T(1,128)}, f32[1,256]{1,0:T(1,128)}) custom-call(f32[4,512,256]{2,1,0:T(8,128)S(1)} %shard_map.166.mine, bf16[4,512,256]{2,1,0:T(8,128)(2,1)S(1)} %collective-permute-done.19.other, f32[4,512,256]{2,1,0:T(8,128)S(1)} %shard_map.163.slope, ...), custom_call_target="tpu_custom_call" | custom-call | flops 268435456 | bytes 4194304 | tf_op jit(solution)/shard_map/pallas_call | solution.py:309
  116.6 1.4 %collective-permute-done.20.two = bf16[4,96,256]{2,1,0:T(8,128)(2,1)S(1)} collective-permute-done((bf16[4,96,256]{2,1,0:T(8,128)(2,1)S(1)}, bf16[4,96,256]{2,1,0:T(8,128)(2,1)S(1)}, u32[]{:S(2)}, u32[]{:S(2)}) %collective-permute-start.20) | collective-permute-done | bytes 196640 | tf_op jit(solution)/shard_map/ppermute | solution.py:322
  118.0 4.3 %shard_map.169 = (f32[4,64,128]{2,1,0:T(8,128)S(1)}, f32[4,64,128]{2,1,0:T(8,128)S(1)}) custom-call(s32[3]{0:T(128)S(1)} %copy-done.1, bf16[4,96,256]{2,1,0:T(8,128)(2,1)S(1)} %get-tuple-element.55.one, bf16[4,96,256]{2,1,0:T(8,128)(2,1)S(1)} %collective-permute-done.20.two, bf16[3,3,512,256]{3,2,1,0:T(8,128)(2,1)} %weight.4, ...), custom_call_target="tpu_custom_call" | custom-call | flops 268435456 | bytes 4194304 | tf_op jit(solution)/shard_map/pallas_call | solution.py:309
  122.4 1.6 %collective-permute-start.21 = (f32[4,64,128]{2,1,0:T(8,128)S(1)}, f32[4,64,128]{2,1,0:T(8,128)S(1)}, u32[]{:S(2)}, u32[]{:S(2)}) collective-permute-start(f32[4,64,128]{2,1,0:T(8,128)S(1)} %get-tuple-element.58), channel_id=1, source_target_pairs={{0,2},{1,3},{2,0},{3,1},{4,6},{5,7},{6,4},{7,5},{8,10},{9,11},{10,... | collective-permute-start | bytes 393224 | tf_op jit(solution)/shard_map/ppermute | solution.py:322
  123.9 7.1 %shard_map.170 = f32[9,512,256]{2,1,0:T(8,128)} custom-call(s32[3]{0:T(128)S(1)} %copy-done.1, bf16[4,512,512]{2,1,0:T(8,128)(2,1)S(1)} %get-tuple-element.59.refs_0_, bf16[4,512,256]{2,1,0:T(8,128)(2,1)S(1)} %get-tuple-element.60.refs_1_), custom_call_target="tpu_custom_call" | custom-call | flops 4831838208 | bytes 4194304 | tf_op jit(solution)/shard_map/pallas_call | solution.py:309
  (39 shorter events, 6.8 us)
Async XLA Ops:
  2.2 7.2 %collective-permute-start.1 = (bf16[4,64,128]{2,1,0:T(8,128)(2,1)S(1)}, bf16[4,64,128]{2,1,0:T(8,128)(2,1)S(1)}, u32[]{:S(2)}, u32[]{:S(2)}) collective-permute-start(bf16[4,64,128]{2,1,0:T(8,128)(2,1)S(1)} %get-tuple-element.77), channel_id=1, source_target_pairs={{0,16},{4,20},{8,24},{12,28},{16,0},{20,4},{24,8},{28,12},{1,17},{... | collective-permute-start | bytes 196616 | tf_op jit(solution)/shard_map/ppermute | solution.py:322
  6.3 4.3 %collective-permute-start = (bf16[4,64,128]{2,1,0:T(8,128)(2,1)S(1)}, bf16[4,64,128]{2,1,0:T(8,128)(2,1)S(1)}, u32[]{:S(2)}, u32[]{:S(2)}) collective-permute-start(bf16[4,64,128]{2,1,0:T(8,128)(2,1)S(1)} %get-tuple-element.77), channel_id=1, source_target_pairs={{0,8},{4,12},{8,0},{12,4},{16,24},{20,28},{24,16},{28,20},{1,9},{5... | collective-permute-start | bytes 196616 | tf_op jit(solution)/shard_map/ppermute | solution.py:322
  7.9 6.1 %collective-permute-start.2 = (bf16[4,64,128]{2,1,0:T(8,128)(2,1)S(1)}, bf16[4,64,128]{2,1,0:T(8,128)(2,1)S(1)}, u32[]{:S(2)}, u32[]{:S(2)}) collective-permute-start(bf16[4,64,128]{2,1,0:T(8,128)(2,1)S(1)} %get-tuple-element.77), channel_id=1, source_target_pairs={{0,24},{4,28},{8,16},{12,20},{16,8},{20,12},{24,0},{28,4},{1,25},{... | collective-permute-start | bytes 196616 | tf_op jit(solution)/shard_map/ppermute | solution.py:322
  14.0 10.2 %collective-permute-start.5 = (bf16[4,4,64,128]{3,2,1,0:T(8,128)(2,1)S(1)}, bf16[4,4,64,128]{3,2,1,0:T(8,128)(2,1)S(1)}, u32[]{:S(2)}, u32[]{:S(2)}) collective-permute-start(bf16[4,4,64,128]{3,2,1,0:T(8,128)(2,1)S(1)} %pad_maximum_fusion.refs_0_), channel_id=1, source_target_pairs={{0,6},{1,7},{2,4},{3,5},{4,2},{5,3},{6,0},{7,1},{8,14},{9,15},{10,... | collective-permute-start | bytes 786440 | tf_op jit(solution)/shard_map/ppermute | solution.py:332
  16.5 10.5 %collective-permute-start.4 = (bf16[4,4,64,128]{3,2,1,0:T(8,128)(2,1)S(1)}, bf16[4,4,64,128]{3,2,1,0:T(8,128)(2,1)S(1)}, u32[]{:S(2)}, u32[]{:S(2)}) collective-permute-start(bf16[4,4,64,128]{3,2,1,0:T(8,128)(2,1)S(1)} %pad_maximum_fusion.refs_0_), channel_id=1, source_target_pairs={{0,2},{1,3},{2,0},{3,1},{4,6},{5,7},{6,4},{7,5},{8,10},{9,11},{10,... | collective-permute-start | bytes 786440 | tf_op jit(solution)/shard_map/ppermute | solution.py:322
  17.0 10.1 %collective-permute-start.3 = (bf16[4,4,64,128]{3,2,1,0:T(8,128)(2,1)S(1)}, bf16[4,4,64,128]{3,2,1,0:T(8,128)(2,1)S(1)}, u32[]{:S(2)}, u32[]{:S(2)}) collective-permute-start(bf16[4,4,64,128]{3,2,1,0:T(8,128)(2,1)S(1)} %pad_maximum_fusion.refs_0_), channel_id=1, source_target_pairs={{0,4},{4,0},{8,12},{12,8},{16,20},{20,16},{24,28},{28,24},{1,5},{5... | collective-permute-start | bytes 786440 | tf_op jit(solution)/shard_map/ppermute | solution.py:322
  17.6 10.7 %collective-permute-start.6 = (bf16[4,4,64,128]{3,2,1,0:T(8,128)(2,1)S(1)}, bf16[4,4,64,128]{3,2,1,0:T(8,128)(2,1)S(1)}, u32[]{:S(2)}, u32[]{:S(2)}) collective-permute-start(bf16[4,4,64,128]{3,2,1,0:T(8,128)(2,1)S(1)} %pad_maximum_fusion.refs_0_), channel_id=1, source_target_pairs={{0,1},{1,0},{2,3},{3,2},{4,5},{5,4},{6,7},{7,6},{8,9},{9,8},{10,11... | collective-permute-start | bytes 786440 | tf_op jit(solution)/shard_map/ppermute | solution.py:322
  24.2 4.1 %collective-permute-start.9 = (bf16[4,4,64,128]{3,2,1,0:T(8,128)(2,1)S(1)}, bf16[4,4,64,128]{3,2,1,0:T(8,128)(2,1)S(1)}, u32[]{:S(2)}, u32[]{:S(2)}) collective-permute-start(bf16[4,4,64,128]{3,2,1,0:T(8,128)(2,1)S(1)} %collective-permute-done.5.refs_3_), channel_id=1, source_target_pairs={{0,1},{1,0},{2,3},{3,2},{4,5},{5,4},{6,7},{7,6},{8,9},{9,8},{10,11... | collective-permute-start | bytes 786440 | tf_op jit(solution)/shard_map/ppermute | solution.py:322
  27.0 1.5 %collective-permute-start.8 = (bf16[4,4,64,128]{3,2,1,0:T(8,128)(2,1)S(1)}, bf16[4,4,64,128]{3,2,1,0:T(8,128)(2,1)S(1)}, u32[]{:S(2)}, u32[]{:S(2)}) collective-permute-start(bf16[4,4,64,128]{3,2,1,0:T(8,128)(2,1)S(1)} %collective-permute-done.4.refs_2_), channel_id=1, source_target_pairs={{0,1},{1,0},{2,3},{3,2},{4,5},{5,4},{6,7},{7,6},{8,9},{9,8},{10,11... | collective-permute-start | bytes 786440 | tf_op jit(solution)/shard_map/ppermute | solution.py:322
  27.1 1.8 %collective-permute-start.7 = (bf16[4,4,64,128]{3,2,1,0:T(8,128)(2,1)S(1)}, bf16[4,4,64,128]{3,2,1,0:T(8,128)(2,1)S(1)}, u32[]{:S(2)}, u32[]{:S(2)}) collective-permute-start(bf16[4,4,64,128]{3,2,1,0:T(8,128)(2,1)S(1)} %collective-permute-done.3.refs_1_), channel_id=1, source_target_pairs={{0,1},{1,0},{2,3},{3,2},{4,5},{5,4},{6,7},{7,6},{8,9},{9,8},{10,11... | collective-permute-start | bytes 786440 | tf_op jit(solution)/shard_map/ppermute | solution.py:322
  28.9 0.7 copy-start
  29.6 12.2 %copy-start.2 = (bf16[3,3,1024,256]{3,2,1,0:T(8,128)(2,1)S(1)}, bf16[3,3,1024,256]{3,2,1,0:T(8,128)(2,1)}, u32[]{:S(2)}) copy-start(bf16[3,3,1024,256]{3,2,1,0:T(8,128)(2,1)} %weight.3) | copy-start | bytes 14155780
  29.6 14.2 %copy-start.3 = (f32[32,256]{1,0:T(8,128)S(1)}, f32[32,256]{1,0:T(8,128)}, u32[]{:S(2)}) copy-start(f32[32,256]{1,0:T(8,128)} %param.19) | copy-start | bytes 98308
  39.1 2.7 %collective-permute-start.11 = (bf16[4,512,256]{2,1,0:T(8,128)(2,1)S(1)}, bf16[4,512,256]{2,1,0:T(8,128)(2,1)S(1)}, u32[]{:S(2)}, u32[]{:S(2)}) collective-permute-start(bf16[4,512,256]{2,1,0:T(8,128)(2,1)S(1)} %get-tuple-element.38.one.refs_0_), channel_id=1, source_target_pairs={{0,1},{1,0},{2,3},{3,2},{4,5},{5,4},{6,7},{7,6},{8,9},{9,8},{10,11... | collective-permute-start | bytes 3145736 | tf_op jit(solution)/shard_map/ppermute | solution.py:322
  41.8 25.7 %collective-permute-start.15 = (bf16[3,3,1024,256]{3,2,1,0:T(8,128)(2,1)S(1)}, bf16[3,3,1024,256]{3,2,1,0:T(8,128)(2,1)S(1)}, u32[]{:S(2)}, u32[]{:S(2)}) collective-permute-start(bf16[3,3,1024,256]{3,2,1,0:T(8,128)(2,1)S(1)} %copy-done.2), channel_id=1, source_target_pairs={{0,1},{1,0},{2,3},{3,2},{4,5},{5,4},{6,7},{7,6},{8,9},{9,8},{10,11... | collective-permute-start | bytes 14155784 | tf_op jit(solution)/shard_map/ppermute | solution.py:322
  41.9 25.6 %collective-permute-start.16 = (bf16[3,3,512,256]{3,2,1,0:T(8,128)(2,1)}, bf16[3,3,512,256]{3,2,1,0:T(8,128)(2,1)S(1)}, u32[]{:S(2)}, u32[]{:S(2)}) collective-permute-start(bf16[3,3,512,256]{3,2,1,0:T(8,128)(2,1)} %weight.4), channel_id=1, source_target_pairs={{0,1},{1,0},{2,3},{3,2},{4,5},{5,4},{6,7},{7,6},{8,9},{9,8},{10,11... | collective-permute-start | bytes 7077896 | tf_op jit(solution)/shard_map/ppermute | solution.py:322
  42.3 25.2 %collective-permute-start.10 = (bf16[4,512,256]{2,1,0:T(8,128)(2,1)S(1)}, bf16[4,512,256]{2,1,0:T(8,128)(2,1)S(1)}, u32[]{:S(2)}, u32[]{:S(2)}) collective-permute-start(bf16[4,512,256]{2,1,0:T(8,128)(2,1)S(1)} %get-tuple-element.38.one.refs_0_), channel_id=1, source_target_pairs={{0,2},{1,3},{2,0},{3,1},{4,6},{5,7},{6,4},{7,5},{8,10},{9,11},{10,... | collective-permute-start | bytes 3145736 | tf_op jit(solution)/shard_map/ppermute | solution.py:322
  43.8 3.9 %collective-permute-start.12 = (f32[1,32,256]{2,1,0:T(8,128)S(1)}, f32[1,32,256]{2,1,0:T(8,128)S(1)}, u32[]{:S(2)}, u32[]{:S(2)}) collective-permute-start(f32[1,32,256]{2,1,0:T(8,128)S(1)} %bitcast.21), channel_id=1, source_target_pairs={{0,4},{4,0},{8,12},{12,8},{16,20},{20,16},{24,28},{28,24},{1,5},{5... | collective-permute-start | bytes 98312 | tf_op jit(solution)/shard_map/ppermute | solution.py:322
  47.7 4.3 %collective-permute-start.13 = (f32[2,32,256]{2,1,0:T(8,128)S(1)}, f32[2,32,256]{2,1,0:T(8,128)S(1)}, u32[]{:S(2)}, u32[]{:S(2)}) collective-permute-start(f32[2,32,256]{2,1,0:T(8,128)S(1)} %pad_maximum_fusion.3), channel_id=1, source_target_pairs={{0,8},{4,12},{8,0},{12,4},{16,24},{20,28},{24,16},{28,20},{1,9},{5... | collective-permute-start | bytes 196616 | tf_op jit(solution)/shard_map/ppermute | solution.py:322
  48.4 6.8 %copy-start.1 = (s32[3]{0:T(128)S(1)}, s32[3]{0:T(128)}, u32[]{:S(2)}) copy-start(s32[3]{0:T(128)} %starts.15) | copy-start | bytes 40
  52.0 8.8 %collective-permute-start.14 = (f32[4,32,256]{2,1,0:T(8,128)S(1)}, f32[4,32,256]{2,1,0:T(8,128)S(1)}, u32[]{:S(2)}, u32[]{:S(2)}) collective-permute-start(f32[4,32,256]{2,1,0:T(8,128)S(1)} %pad_maximum_fusion.2), channel_id=1, source_target_pairs={{0,16},{4,20},{8,24},{12,28},{16,0},{20,4},{24,8},{28,12},{1,17},{... | collective-permute-start | bytes 393224 | tf_op jit(solution)/shard_map/ppermute | solution.py:322
  67.5 2.7 %collective-permute-start.17 = (bf16[4,512,256]{2,1,0:T(8,128)(2,1)S(1)}, bf16[4,512,256]{2,1,0:T(8,128)(2,1)S(1)}, u32[]{:S(2)}, u32[]{:S(2)}) collective-permute-start(bf16[4,512,256]{2,1,0:T(8,128)(2,1)S(1)} %collective-permute-done.10.one.refs_2_), channel_id=1, source_target_pairs={{0,1},{1,0},{2,3},{3,2},{4,5},{5,4},{6,7},{7,6},{8,9},{9,8},{10,11... | collective-permute-start | bytes 3145736 | tf_op jit(solution)/shard_map/ppermute | solution.py:322
  81.1 2.7 %collective-permute-start.18 = (bf16[4,512,256]{2,1,0:T(8,128)(2,1)S(1)}, bf16[4,512,256]{2,1,0:T(8,128)(2,1)S(1)}, u32[]{:S(2)}, u32[]{:S(2)}) collective-permute-start(bf16[4,512,256]{2,1,0:T(8,128)(2,1)S(1)} %get-tuple-element.50.one.refs_4_), channel_id=1, source_target_pairs={{0,1},{1,0},{2,3},{3,2},{4,5},{5,4},{6,7},{7,6},{8,9},{9,8},{10,11... | collective-permute-start | bytes 3145736 | tf_op jit(solution)/shard_map/ppermute | solution.py:322
  89.4 25.3 %collective-permute-start.19 = (bf16[4,512,256]{2,1,0:T(8,128)(2,1)S(1)}, bf16[4,512,256]{2,1,0:T(8,128)(2,1)S(1)}, u32[]{:S(2)}, u32[]{:S(2)}) collective-permute-start(bf16[4,512,256]{2,1,0:T(8,128)(2,1)S(1)} %shard_map.165), channel_id=1, source_target_pairs={{0,2},{1,3},{2,0},{3,1},{4,6},{5,7},{6,4},{7,5},{8,10},{9,11},{10,... | collective-permute-start | bytes 3145736 | tf_op jit(solution)/shard_map/ppermute | solution.py:322
  116.6 1.4 %collective-permute-start.20 = (bf16[4,96,256]{2,1,0:T(8,128)(2,1)S(1)}, bf16[4,96,256]{2,1,0:T(8,128)(2,1)S(1)}, u32[]{:S(2)}, u32[]{:S(2)}) collective-permute-start(bf16[4,96,256]{2,1,0:T(8,128)(2,1)S(1)} %get-tuple-element.55.one), channel_id=1, source_target_pairs={{0,1},{1,0},{2,3},{3,2},{4,5},{5,4},{6,7},{7,6},{8,9},{9,8},{10,11... | collective-permute-start | bytes 589832 | tf_op jit(solution)/shard_map/ppermute | solution.py:322
  122.4 8.7 %collective-permute-start.21 = (f32[4,64,128]{2,1,0:T(8,128)S(1)}, f32[4,64,128]{2,1,0:T(8,128)S(1)}, u32[]{:S(2)}, u32[]{:S(2)}) collective-permute-start(f32[4,64,128]{2,1,0:T(8,128)S(1)} %get-tuple-element.58), channel_id=1, source_target_pairs={{0,2},{1,3},{2,0},{3,1},{4,6},{5,7},{6,4},{7,5},{8,10},{9,11},{10,... | collective-permute-start | bytes 393224 | tf_op jit(solution)/shard_map/ppermute | solution.py:322

commit v3 on v2

--- a/solution.py
+++ b/solution.py
@@ -301,6 +301,10 @@
     return pl.BlockSpec(memory_space=pl.ANY)
 
 
+def far_spec():
+    return pl.BlockSpec(memory_space=pltpu.HBM)
+
+
 def scalar_spec():
     return pl.BlockSpec(memory_space=pltpu.SMEM)
 
@@ -313,13 +317,18 @@
         out_specs=tuple(out_specs),
         scratch_shapes=scratch,
         compiler_params=pltpu.CompilerParams(vmem_limit_bytes=megabytes * 2**20),
-        cost_estimate=pl.CostEstimate(flops=flops, bytes_accessed=2**22, transcendentals=0),
+        cost_estimate=pl.CostEstimate(flops=1000, bytes_accessed=1000, transcendentals=0),
     )(*operands)
 
 
 def swap(shard, axis, bit):
     count = lax.axis_size(axis)
     return lax.ppermute(shard, axis, [(i, i ^ bit) for i in range(count)])
+
+
+def gather_bits(places):
+    bits = [1 << k for k in range(places.bit_length() - 1)]
+    return bits[2:][::-1] + bits[:2] if len(bits) > 2 else bits
 
 
 def swap_both(shard, first, first_bit, second, second_bit):
@@ -438,14 +447,40 @@
     return 0.3989422804014327 * jnp.exp(-0.5 * value * value)
 
 
-def first_kernel(starts, *refs):
-    blocks, (weight_in, scales) = refs[:8], refs[8:10]
-    hidden, field_out, pre_out, keep, stats = refs[10:15]
-    field, weight, lower, middle, upper, sems = refs[15:]
+def bring_kernel(starts_in, weight_in, *refs):
+    vectors, (starts, weight, scales, sems) = refs[:4], refs[4:]
+    copies = [pltpu.make_async_copy(weight_in, weight, sems.at[0])]
+    for k, vector in enumerate(vectors):
+        copies.append(pltpu.make_async_copy(vector, scales.at[k : k + 1], sems.at[1 + k]))
+    for copy in copies:
+        copy.start()
+    for k in range(starts.shape[0]):
+        starts[k] = starts_in[k]
+    for copy in copies:
+        copy.wait()
+
+
+def bring(starts, weight, vectors):
+    return call(
+        bring_kernel,
+        (starts, weight, *[v[None] for v in vectors]),
+        [scalar_spec()] + [far_spec()] * 5,
+        [(starts.shape, jnp.int32), (weight.shape, bf16), ((TILE, vectors[0].shape[0]), f32)],
+        [scalar_spec(), whole_spec(), whole_spec()],
+        [pltpu.SemaphoreType.DMA((5,))],
+        0,
+        4,
+    )
+
+
+def first_kernel(*refs):
+    starts, blocks, (weight, scales) = refs[0], refs[1:9], refs[9:11]
+    low, high, picked, field_out, pre_out, keep, stats = refs[11:18]
+    field, lower, middle, upper, sems = refs[18:]
     mel_count, total, width = field.shape
     out_width = middle.shape[2]
     place, column = lax.axis_index("tm"), lax.axis_index("chan")
-    copies = [pltpu.make_async_copy(weight_in, weight, sems.at[0])]
+    copies = []
     frames, lanes = blocks[0].shape[2], blocks[0].shape[3]
     count = blocks[0].shape[0]
     for i, block in enumerate(blocks):
@@ -461,7 +496,7 @@
                         pl.ds(pl.multiple_of(from_place * frames, frames), frames),
                         pl.ds(pl.multiple_of(from_column * lanes, lanes), lanes),
                     ],
-                    sems.at[1 + i * count + k],
+                    sems.at[len(copies)],
                 )
             )
     for copy in copies:
@@ -514,10 +549,17 @@
         mask = widen(keep[pl.ds(at, ROWS)], out_width)
         for m in range(mel_count):
             value = middle[m, pl.ds(at, ROWS)] * scale + offset
-            hidden[m, pl.ds(at, ROWS)] = (value * phi_parts(value) * mask).astype(bf16)
+            rows = (value * phi_parts(value) * mask).astype(bf16)
+            if m < mel_count // 2:
+                low[m, pl.ds(at, ROWS)] = rows
+            else:
+                high[m - mel_count // 2, pl.ds(at, ROWS)] = rows
         return carry
 
     by_rows(total, activate, 0)
+    reach = picked.shape[1]
+    for m in range(picked.shape[0]):
+        picked[m] = high[m, pl.ds(pl.multiple_of((place % 2) * reach, reach), reach)]
     save.wait()
     save_pre.wait()
 
@@ -529,22 +571,23 @@
     return call(
         first_kernel,
         (starts, *blocks, weight, scales),
-        [scalar_spec()] + [place_spec()] * 9 + [whole_spec()],
+        [scalar_spec()] + [place_spec()] * 8 + [whole_spec()] * 2,
         [
-            ((mel_count, total, out_width), bf16),
+            ((mel_count // 2, total, out_width), bf16),
+            ((mel_count // 2, total, out_width), bf16),
+            ((mel_count // 2, total // 2, out_width), bf16),
             ((mel_count, total, width), bf16),
             ((mel_count, total, out_width), f32),
             ((total, LANES), f32),
             ((TILE, out_width), f32),
         ],
-        [whole_spec(), place_spec(), place_spec(), whole_spec(), whole_spec()],
+        [whole_spec()] * 3 + [place_spec()] * 2 + [whole_spec()] * 2,
         [
             pltpu.VMEM((mel_count, total, width), bf16),
-            pltpu.VMEM(weight.shape, bf16),
             pltpu.VMEM(padded, f32),
             pltpu.VMEM((mel_count, total, out_width), f32),
             pltpu.VMEM(padded, f32),
-            pltpu.SemaphoreType.DMA((1 + 8 * count,)),
+            pltpu.SemaphoreType.DMA((8 * count,)),
         ],
         2 * 9 * mel_count * total * width * out_width,
         16,
@@ -580,24 +623,47 @@
     )[0]
 
 
-def partial_kernel(places, starts, one, two, weight, out, lower, upper):
+def gather_taps(parts, groups, weight, lower, middle, upper, outputs, first=None):
+    total, width = middle.shape[1], middle.shape[2]
+    for k, m in enumerate(outputs):
+        for a in range(3):
+            acc = None
+            for mels, arrays in parts:
+                for j, n in enumerate(mels):
+                    b = n - m + 1
+                    if 0 <= b < 3:
+                        for array, start in zip(arrays, groups):
+                            piece = jnp.dot(
+                                array[j],
+                                weight[a, b, pl.ds(start, width)],
+                                preferred_element_type=f32,
+                            )
+                            acc = piece if acc is None else acc + piece
+            target, shift = ((lower, TILE), (middle, 0), (upper, TILE))[a]
+            rows = total
+            if first is not None:
+                rows = total // 2
+                empty = pl.ds(pl.multiple_of(total // 2 - first + shift, TILE), rows)
+                target[k, empty] = jnp.zeros((rows, width), f32)
+                target[k, pl.ds(pl.multiple_of(first + shift, TILE), rows)] = acc
+            elif acc is None:
+                target[k, shift : shift + rows] = jnp.zeros((rows, width), f32)
+            else:
+                target[k, shift : shift + rows] = acc
+
+
+def group_starts(bits, width):
+    column = lax.axis_index("chan")
+    return [pl.multiple_of((column ^ bit) * width, width) for bit in bits]
+
+
+def near_kernel(starts, low, high, low_two, high_two, weight, out, lower, upper):
     mel_count, total, width = out.shape
-    column = lax.axis_index("chan")
-
-    def group(place):
-        start = pl.multiple_of((column ^ place) * width, width)
-        return lambda a, b: weight[a, b, pl.ds(start, width)]
-
+    half = mel_count // 2
     clear_edges(lower, upper, total)
-    convolve(
-        [lambda m: one[m], lambda m: two[m]],
-        [group(p) for p in places],
-        lower,
-        out,
-        upper,
-        total,
-        False,
-    )
+    parts = [(range(half), (low, low_two)), (range(half, mel_count), (high, high_two))]
+    groups = group_starts((0, 1), width)
+    gather_taps(parts, groups, weight, lower, out, upper, range(mel_count))
 
     def combine(at, carry):
         before, after = same_clip(starts, at, (ROWS, width), total)
@@ -608,48 +674,107 @@
     by_rows(total, combine, 0)
 
 
-def second_partial(one, two, weight, starts):
-    mel_count, total, width = one.shape
-    padded = (mel_count, total + 2 * TILE, width)
+def near_part(low, high, low_two, high_two, weight, starts):
+    half, total, width = low.shape
+    padded = (2 * half, total + 2 * TILE, width)
     return call(
-        functools.partial(partial_kernel, (0, 1)),
-        (starts, one, two, weight),
-        [scalar_spec()] + [whole_spec()] * 3,
-        [((mel_count, total, width), f32)],
+        near_kernel,
+        (starts, low, high, low_two, high_two, weight),
+        [scalar_spec()] + [whole_spec()] * 5,
+        [((2 * half, total, width), f32)],
         [whole_spec()],
         [pltpu.VMEM(padded, f32)] * 2,
-        2 * 18 * mel_count * total * width * width,
+        0,
         14,
     )[0]
 
 
-def second_kernel(starts, one, two, weight, middle_in, keep, scales, cotangents, *refs):
-    readout, grad, gain_grad, shift_grad = refs[:4]
-    middle, slope, lower, upper, hold, wide, full, sems = refs[4:]
-    mel_count, total, width = one.shape
-    place, column = lax.axis_index("tm"), lax.axis_index("chan")
+def early_kernel(starts, picked, picked_two, weight, early, lower, upper):
+    outputs, total, width = early.shape
+    mel_count = picked.shape[0] + outputs - 1
+    half = mel_count - picked.shape[0]
+    begin = (lax.axis_index("tm") % 2) * (total // 2)
+    clear_edges(lower, upper, total)
+    parts = [(range(half, mel_count), (picked, picked_two))]
+    groups = group_starts((2, 3), width)
+    mels = range(half - 1, mel_count)
+    gather_taps(parts, groups, weight, lower, early, upper, mels, begin)
+
+    def combine(at, carry):
+        before, after = same_clip(starts, at, (ROWS, width), total)
+        for k in range(outputs):
+            early[k, pl.ds(at, ROWS)] = joined(lower, early, upper, k, at, before, after)
+        return carry
+
+    by_rows(total, combine, 0)
+
+
+def early_part(picked, picked_two, weight, starts):
+    half, rows, width = picked.shape
+    total = 2 * rows
+    shape = (half + 1, total, width)
+    return call(
+        early_kernel,
+        (starts, picked, picked_two, weight),
+        [scalar_spec()] + [whole_spec()] * 3,
+        [(shape, f32)],
+        [whole_spec()],
+        [pltpu.VMEM((half + 1, total + 2 * TILE, width), f32)] * 2,
+        0,
+        12,
+    )[0]
+
+
+def run_sums(mask, plain, values):
+    width = (plain + values)[0].shape[1]
+    terms = list(plain)
+    for value in values:
+        for _ in range(3):
+            term = value.astype(bf16)
+            terms.append(term)
+            value = value - term.astype(f32)
+    out = jnp.dot(mask, jnp.concatenate(terms, axis=1), preferred_element_type=f32)
+    parts = [out[:, k * width : (k + 1) * width] for k in range(len(terms))]
+    results = parts[: len(plain)]
+    for k in range(len(plain), len(parts), 3):
+        results.append(parts[k] + (parts[k + 1] + parts[k + 2]))
+    return results
+
+
+def second_kernel(
+    starts, near, early, far, rest, far_two, rest_two, weight, keep, scales, *refs
+):
+    cotangents, (readout, grad, gain_grad, shift_grad) = refs[:-15], refs[-15:-11]
+    middle, slope, lower, upper, late, late_lower, late_upper, hold, wide, full, sems = refs[-11:]
+    mel_count, total, width = middle.shape
+    half = mel_count // 2
+    place = lax.axis_index("tm")
     pooled_total = total // 2
     own = readout.shape[0]
     copies = []
-    for k in range(cotangents.shape[0]):
+    pieces = [(part, i) for part in cotangents for i in range(part.shape[0])]
+    bits = gather_bits(len(pieces))
+    for k, (part, i) in enumerate(pieces):
+        source = place ^ sum(bit for j, bit in enumerate(bits) if k >> j & 1)
         copies.append(
             pltpu.make_async_copy(
-                cotangents.at[k],
-                full.at[pl.ds(pl.multiple_of((place ^ k) * own, own), own)],
+                part.at[i],
+                full.at[pl.ds(pl.multiple_of(source * own, own), own)],
                 sems.at[k],
             )
         )
     for copy in copies:
         copy.start()
 
-    def group(bit):
-        start = pl.multiple_of((column ^ bit) * width, width)
-        return lambda a, b: weight[a, b, pl.ds(start, width)]
-
+    groups = group_starts((2, 3), width)
     clear_edges(lower, upper, total)
-    convolve(
-        [lambda m: one[m], lambda m: two[m]], [group(2), group(3)], lower, middle, upper, total, False
-    )
+    clear_edges(late_lower, late_upper, total)
+    parts = [(range(half), (far, far_two))]
+    gather_taps(parts, groups, weight, lower, middle, upper, range(half + 1))
+    parts = [(range(half, mel_count), (rest, rest_two))]
+    begin = (1 - place % 2) * (total // 2)
+    outputs = range(half - 1, mel_count)
+    gather_taps(parts, groups, weight, late_lower, late, late_upper, outputs, begin)
     blank = jnp.zeros((TILE, width), f32)
 
     def combine(at, sums):
@@ -658,8 +783,13 @@
         first, second, num = sums
         num = num + fold(mask)
         for m in range(mel_count):
-            rows = joined(lower, middle, upper, m, at, before, after)
-            rows = rows + middle_in[m, pl.ds(at, ROWS)]
+            rows = near[m, pl.ds(at, ROWS)]
+            if m <= half:
+                rows = rows + joined(lower, middle, upper, m, at, before, after)
+            if m in outputs:
+                k = m - outputs[0]
+                new = joined(late_lower, late, late_upper, k, at, before, after)
+                rows = rows + (early[k, pl.ds(at, ROWS)] + new)
             middle[m, pl.ds(at, ROWS)] = rows
             kept = rows * mask
             first = first + fold(kept)
@@ -702,19 +832,17 @@
         crossed = (2 * row < starts[k]) != (2 * col < starts[k])
         same = same & ~crossed
         back = back & ~crossed
-    ahead, behind = same.astype(f32), back.astype(f32)
-    exact = functools.partial(jnp.dot, precision=highest, preferred_element_type=f32)
+    ahead, behind = same.astype(f32).astype(bf16), back.astype(f32).astype(bf16)
     exponent = jnp.exp(pooled)
-    counts = jnp.dot(ahead, present, preferred_element_type=f32)
-    totals = exact(ahead, present * pooled)
-    sums = exact(ahead, present * exponent)
+    counts, totals, sums = run_sums(
+        ahead, (present.astype(bf16),), (present * pooled, present * exponent)
+    )
     wide[...] = totals / counts + jnp.log(sums)
     readout[...] = wide[pl.ds(pl.multiple_of(place * own, own), own)]
     for copy in copies:
         copy.wait()
     cotangent = full[...]
-    by_count = exact(behind, cotangent / counts)
-    by_sum = exact(behind, cotangent / sums)
+    by_count, by_sum = run_sums(behind, (), (cotangent / counts, cotangent / sums))
     down = present * (by_count + exponent * by_sum) * (0.5 / mel_count)
     for c in range(width // LANES):
         hold[c, even] = down[:, c * LANES : (c + 1) * LANES]
@@ -749,14 +877,15 @@
     by_rows(total, finish, 0)
 
 
-def second_block(one, two, weight, partial, keep, scales, starts, cotangents, own):
-    mel_count, total, width = one.shape
+def second_block(near, early, arrays, weight, keep, scales, starts, cotangents, own):
+    mel_count, total, width = near.shape
+    outputs = early.shape[0]
     padded = (mel_count, total + 2 * TILE, width)
     full = (mel_count, total, width)
     return call(
         second_kernel,
-        (starts, one, two, weight, partial, keep, scales, cotangents),
-        [scalar_spec()] + [whole_spec()] * 6 + [place_spec()],
+        (starts, near, early, *arrays, weight, keep, scales, *cotangents),
+        [scalar_spec()] + [whole_spec()] * (len(arrays) + 5) + [place_spec()] * len(cotangents),
         [((own, width), f32), (full, bf16), ((1, width), f32), ((1, width), f32)],
         [whole_spec()] * 4,
         [
@@ -764,63 +893,87 @@
             pltpu.VMEM(full, f32),
             pltpu.VMEM(padded, f32),
             pltpu.VMEM(padded, f32),
+            pltpu.VMEM((outputs, total, width), f32),
+            pltpu.VMEM((outputs, total + 2 * TILE, width), f32),
+            pltpu.VMEM((outputs, total + 2 * TILE, width), f32),
             pltpu.VMEM((width // LANES, total, LANES), f32),
             pltpu.VMEM((total // 2, width), f32),
             pltpu.VMEM((total // 2, width), f32),
-            pltpu.SemaphoreType.DMA((cotangents.shape[0],)),
+            pltpu.SemaphoreType.DMA((sum(part.shape[0] for part in cotangents),)),
         ],
-        2 * 18 * mel_count * total * width * width,
-        22,
-    )
-
-
-def back_kernel(bit, starts, one, two, weight, weight_two, out, lower, middle, upper):
+        0,
+        26,
+    )
+
+
+def back_kernel(bit, mels, halved, starts, one, two, weight, weight_two, out, lower, middle, upper):
     mel_count, total, width = one.shape
-    column = lax.axis_index("chan")
-    start = pl.multiple_of((column ^ bit) * width, width)
-    clear_edges(lower, upper, total)
-    convolve_back(
-        [lambda m: one[m], lambda m: two[m]],
-        [
-            lambda a, b: weight[a, b, pl.ds(start, width)],
-            lambda a, b: weight_two[a, b, pl.ds(start, width)],
-        ],
-        lower,
-        middle,
-        upper,
-        total,
-    )
+    reach, rows_out = middle.shape[1], out.shape[1]
+    side = lax.axis_index("tm") % 2 if halved else 0
+    edge = reach - rows_out
+    first = side * (total - reach)
+    skip = side * edge
+    if halved:
+        first, skip = pl.multiple_of(first, 16), pl.multiple_of(skip, 16)
+    (start,) = group_starts((bit,), width)
+    for k in range(len(mels)):
+        for ref in (lower, upper):
+            ref[k, :TILE] = jnp.zeros((TILE, width), f32)
+            ref[k, TILE + reach :] = jnp.zeros((TILE, width), f32)
+    for k, n in enumerate(mels):
+        for a in range(3):
+            acc = None
+            for field, matrix in ((one, weight), (two, weight_two)):
+                for b in range(3):
+                    if 0 <= n - b + 1 < mel_count:
+                        part = lax.dot_general(
+                            field[n - b + 1, pl.ds(first, reach)],
+                            matrix[a, b, pl.ds(start, width)],
+                            (((1,), (1,)), ((), ())),
+                            preferred_element_type=f32,
+                        )
+                        acc = part if acc is None else acc + part
+            if a == 2:
+                lower[k, TILE : TILE + reach] = acc
+            elif a == 1:
+                middle[k] = acc
+            else:
+                upper[k, TILE : TILE + reach] = acc
 
     def combine(at, carry):
-        before, after = same_clip(starts, at, (ROWS, width), total)
-        for m in range(mel_count):
-            rows = joined(lower, middle, upper, m, at, before, after)
-            out[m, pl.ds(at, ROWS)] = rows.astype(out.dtype)
+        near = pl.multiple_of(at + skip, TILE)
+        before, after = same_clip(starts, first + near, (ROWS, width), total)
+        for k in range(len(mels)):
+            rows = joined(lower, middle, upper, k, near, before, after)
+            out[k, pl.ds(at, ROWS)] = rows.astype(out.dtype)
         return carry
 
-    by_rows(total, combine, 0)
-
-
-def hidden_back(bit, one, two, weight, weight_two, starts, kind):
-    mel_count, total, width = one.shape
-    padded = (mel_count, total + 2 * TILE, width)
+    by_rows(rows_out, combine, 0)
+
+
+def hidden_back(bit, mels, halved, one, two, weight, weight_two, starts, kind):
+    _, total, width = one.shape
+    rows = total // 2 if halved else total
+    reach = rows + 16 if halved else total
+    count = len(mels)
+    padded = (count, reach + 2 * TILE, width)
     return call(
-        functools.partial(back_kernel, bit),
+        functools.partial(back_kernel, bit, mels, halved),
         (starts, one, two, weight, weight_two),
         [scalar_spec()] + [whole_spec()] * 4,
-        [((mel_count, total, width), kind)],
+        [((count, rows, width), kind)],
         [whole_spec()],
         [
             pltpu.VMEM(padded, f32),
-            pltpu.VMEM((mel_count, total, width), f32),
+            pltpu.VMEM((count, reach, width), f32),
             pltpu.VMEM(padded, f32),
         ],
-        2 * 18 * mel_count * total * width * width,
+        0,
         14,
     )[0]
 
 
-def norm_kernel(mine, other, slope, pre, stats, scales, keep, *refs):
+def norm_kernel(mine, other, picked, rest, slope, pre, stats, scales, keep, *refs):
     grad, window, gain_grad, shift_grad, padded = refs
     mel_count, total, width = mine.shape
     center, inverse, pixels = stats[0:1], stats[1:2], stats[2:3]
@@ -830,17 +983,31 @@
     frames = reach - 2 * edge
     place = lax.axis_index("tm")
 
-    def slopes(at, sums):
-        plain, along = sums
-        for m in range(mel_count):
-            rows = mine[m, pl.ds(at, ROWS)] + other[m, pl.ds(at, ROWS)].astype(f32)
-            step = rows * slope[m, pl.ds(at, ROWS)]
-            mine[m, pl.ds(at, ROWS)] = step
-            plain = plain + fold(step)
-            along = along + fold(step * ((pre[m, pl.ds(at, ROWS)] - center) * inverse))
-        return plain, along
-
-    plain, along = by_rows(total, slopes, (blank, blank))
+    half = mel_count // 2
+
+    def add(field, base, mels):
+        def slopes(at, sums):
+            plain, along = sums
+            place_rows = pl.ds(pl.multiple_of(base + at, ROWS), ROWS)
+            for k, m in enumerate(mels):
+                rows = mine[m, place_rows] + field[k, pl.ds(at, ROWS)].astype(f32)
+                step = rows * slope[m, place_rows]
+                mine[m, place_rows] = step
+                plain = plain + fold(step)
+                along = along + fold(step * ((pre[m, place_rows] - center) * inverse))
+            return plain, along
+
+        return slopes
+
+    side = place % 2
+    sums = by_rows(total, add(other, 0, range(half)), (blank, blank))
+    upper = range(half, mel_count)
+    parts = []
+    for field, base in ((picked, side), (rest, 1 - side)):
+        parts.append(by_rows(total // 2, add(field, base * (total // 2), upper), (blank, blank)))
+    plain, along = [
+        a + jnp.where(side == 0, b + c, c + b) for a, b, c in zip(sums, parts[0], parts[1])
+    ]
     plain, along = column_sum(plain), column_sum(along)
     shift_grad[...] = plain
     gain_grad[...] = along
@@ -865,13 +1032,13 @@
         window[m] = padded[m, pl.ds(pl.multiple_of(place * frames, frames), reach)]
 
 
-def norm_back_first(mine, other, slope, pre, stats, scales, keep, frames):
+def norm_back_first(mine, other, picked, rest, slope, pre, stats, scales, keep, frames):
     mel_count, total, width = mine.shape
     edge = 16
     return call(
         norm_kernel,
-        (mine, other, slope, pre, stats, scales, keep),
-        [whole_spec()] * 7,
+        (mine, other, picked, rest, slope, pre, stats, scales, keep),
+        [whole_spec()] * 9,
         [
             ((mel_count, total, width), bf16),
             ((mel_count, frames + 2 * edge, width), bf16),
@@ -885,27 +1052,22 @@
     )
 
 
-def weight_kernel(group_count, starts, *refs):
-    fields = refs[:group_count]
-    grad, out = refs[group_count : group_count + 2]
-    spaced, steps, results, sems = refs[group_count + 2 :]
-    mel_count, total, out_width = grad.shape
-    column = lax.axis_index("chan")
+def spread_kernel(starts, grad, steps, spaced):
+    mel_count, total, width = grad.shape
     for m in range(mel_count):
-        spaced[m, :TILE] = jnp.zeros((TILE, out_width), f32)
-        spaced[m, TILE + total :] = jnp.zeros((TILE, out_width), f32)
+        spaced[m, :TILE] = jnp.zeros((TILE, width), f32)
+        spaced[m, TILE + total :] = jnp.zeros((TILE, width), f32)
 
     def expand(at, carry):
         for m in range(mel_count):
-            spaced[m, pl.ds(pl.multiple_of(at + TILE, TILE), ROWS)] = grad[
-                m, pl.ds(at, ROWS)
-            ].astype(f32)
+            rows = grad[m, pl.ds(at, ROWS)].astype(f32)
+            spaced[m, pl.ds(pl.multiple_of(at + TILE, TILE), ROWS)] = rows
         return carry
 
     by_rows(total, expand, 0)
 
     def shift(at, carry):
-        before, after = same_clip(starts, at, (ROWS, out_width), total)
+        before, after = same_clip(starts, at, (ROWS, width), total)
         for m in range(mel_count):
             rows = spaced[m, pl.ds(at, ROWS + 2 * TILE)]
             ahead = jnp.where(after, rows[TILE + 1 : TILE + 1 + ROWS], 0.0)
@@ -915,61 +1077,92 @@
         return carry
 
     by_rows(total, shift, 0)
-    width = results.shape[3]
+
+
+def spread(grad, starts):
+    mel_count, total, width = grad.shape
+    return call(
+        spread_kernel,
+        (starts, grad),
+        [scalar_spec(), whole_spec()],
+        [((2, mel_count, total, width), bf16)],
+        [whole_spec()],
+        [pltpu.VMEM((mel_count, total + 2 * TILE, width), f32)],
+        0,
+        6,
+    )[0]
+
+
+def weight_kernel(layout, halves, *refs):
+    count = len(refs) - 6
+    fields, grad, steps = list(refs[:count]), refs[count], refs[count + 1]
+    out, results, joint, sems = refs[count + 2 :]
+    mel_count, total, out_width = grad.shape
+    width = results.shape[2]
+    side = lax.axis_index("tm") % 2
+    column = lax.axis_index("chan")
+    moves = []
+    for i, pair in enumerate(halves):
+        for index, begin in zip(pair, (side, 1 - side)):
+            rows = pl.ds(pl.multiple_of(begin * (total // 2), total // 2), total // 2)
+            moves.append(
+                pltpu.make_async_copy(fields[index], joint.at[i, :, rows], sems.at[2 + len(moves)])
+            )
+            moves[-1].start()
+        fields.append(joint.at[i])
     copies = [None, None]
-    count = 0
-    for i, field in enumerate(fields):
-        for part in range(field.shape[2] // width):
-            slot = count % 2
-            if copies[slot] is not None:
-                copies[slot].wait()
-            for a in range(3):
-                for b in range(3):
-                    acc = None
-                    for m in range(mel_count):
-                        if 0 <= m + b - 1 < mel_count:
-                            right = grad[m] if a == 1 else steps[a // 2, m]
-                            left = field[m + b - 1, :, part * width : (part + 1) * width]
-                            piece = lax.dot_general(
-                                left,
-                                right,
-                                (((0,), (0,)), ((), ())),
-                                preferred_element_type=f32,
-                            )
-                            acc = piece if acc is None else acc + piece
-                    results[slot, 3 * a + b] = acc
-            if group_count > 1:
-                start = pl.multiple_of((column ^ i) * width, width)
-            else:
-                start = part * width
-            copies[slot] = pltpu.make_async_copy(
-                results.at[slot], out.at[:, pl.ds(start, width)], sems.at[slot]
-            )
-            copies[slot].start()
-            count += 1
+    for i, (place, pieces) in enumerate(layout):
+        slot = i % 2
+        if copies[slot] is not None:
+            copies[slot].wait()
+        if any(piece[0] >= count for piece in pieces):
+            while moves:
+                moves.pop().wait()
+        for a in range(3):
+            for b in range(3):
+                right = grad if a == 1 else steps.at[a // 2]
+                acc = None
+                for m in range(mel_count):
+                    if 0 <= m + b - 1 < mel_count:
+                        index, k, lane = pieces[m + b - 1]
+                        part = lax.dot_general(
+                            fields[index][k, :, lane : lane + width],
+                            right[m],
+                            (((0,), (0,)), ((), ())),
+                            preferred_element_type=f32,
+                        )
+                        acc = part if acc is None else acc + part
+                results[slot, 3 * a + b] = acc
+        if place is None:
+            start = i * width
+        else:
+            start = pl.multiple_of((column ^ place) * width, width)
+        copies[slot] = pltpu.make_async_copy(
+            results.at[slot], out.at[:, pl.ds(start, width)], sems.at[slot]
+        )
+        copies[slot].start()
     for copy in copies:
         if copy is not None:
             copy.wait()
 
 
-def weight_back(fields, grad, starts):
+def weight_back(layout, halves, fields, grad, steps, in_width):
     mel_count, total, out_width = grad.shape
-    in_width = sum(f.shape[2] for f in fields)
-    width = 256
+    width = in_width // len(layout)
+    joint = (max(len(halves), 1), mel_count // 2, total, width)
     out = call(
-        functools.partial(weight_kernel, len(fields)),
-        (starts, *fields, grad),
-        [scalar_spec()] + [whole_spec()] * (len(fields) + 1),
+        functools.partial(weight_kernel, layout, halves),
+        (*fields, grad, steps),
+        [whole_spec()] * (len(fields) + 2),
         [((9, in_width, out_width), f32)],
         [place_spec()],
         [
-            pltpu.VMEM((mel_count, total + 2 * TILE, out_width), f32),
-            pltpu.VMEM((2, mel_count, total, out_width), bf16),
             pltpu.VMEM((2, 9, width, out_width), f32),
-            pltpu.SemaphoreType.DMA((2,)),
+            pltpu.VMEM(joint, bf16),
+            pltpu.SemaphoreType.DMA((2 + 2 * len(halves),)),
         ],
-        2 * 9 * mel_count * total * in_width * out_width,
-        14,
+        0,
+        12,
     )[0]
     return out.reshape(3, 3, in_width, out_width)
 
@@ -979,29 +1172,38 @@
     frames, lanes = mine.shape[1], mine.shape[2]
     edge = (reach - frames) // 2
     total = frames * lax.axis_size("tm")
-    place, column = lax.axis_index("tm"), lax.axis_index("chan")
-    for bit, out in ((2, other), (0, mine)):
-        start = pl.multiple_of((column ^ bit) * lanes, lanes)
-        convolve_back(
-            [lambda m: one[m], lambda m: two[m]],
-            [
-                lambda a, b: weight[a, b, pl.ds(start, lanes)],
-                lambda a, b: weight_two[a, b, pl.ds(start, lanes)],
-            ],
-            lower,
-            middle,
-            upper,
-            reach,
+    place = lax.axis_index("tm")
+    groups = group_starts((2, 0), lanes)
+    for a in range(3):
+        target, shift = ((upper, TILE), (middle, 0), (lower, TILE))[a]
+        for b in (1, 0, 2):
+            low, count = ((1, mel_count - 1), (0, mel_count), (0, mel_count - 1))[b]
+            acc = None
+            for field, matrix in ((one, weight), (two, weight_two)):
+                rows = field[low : low + count].reshape(count * reach, width)
+                wing = jnp.concatenate([matrix[a, b, pl.ds(g, lanes)] for g in groups])
+                part = lax.dot_general(
+                    rows, wing, (((1,), (1,)), ((), ())), preferred_element_type=f32
+                )
+                acc = part if acc is None else acc + part
+            acc = acc.reshape(count, reach, 2 * lanes)
+            for k in range(count):
+                n = low + k + b - 1
+                if b == 1:
+                    target[n, shift : shift + reach] = acc[k]
+                else:
+                    target[n, shift : shift + reach] += acc[k]
+    before, after = same_clip(starts, place * frames, (frames, 2 * lanes), total)
+    for m in range(mel_count):
+        low = lower[m, TILE + edge - 1 : TILE + edge - 1 + frames]
+        high = upper[m, TILE + edge + 1 : TILE + edge + 1 + frames]
+        rows = (
+            middle[m, edge : edge + frames]
+            + jnp.where(before, low, 0.0)
+            + jnp.where(after, high, 0.0)
         )
-        before, after = same_clip(starts, place * frames, (frames, lanes), total)
-        for m in range(mel_count):
-            low = lower[m, TILE + edge - 1 : TILE + edge - 1 + frames]
-            high = upper[m, TILE + edge + 1 : TILE + edge + 1 + frames]
-            out[m] = (
-                middle[m, edge : edge + frames]
-                + jnp.where(before, low, 0.0)
-                + jnp.where(after, high, 0.0)
-            )
+        other[m] = rows[:, :lanes]
+        mine[m] = rows[:, lanes:]
 
 
 def input_back(one, two, weight, weight_two, starts, frames, lanes):
@@ -1014,13 +1216,35 @@
         [(shape, f32), (shape, f32)],
         [whole_spec()] * 2,
         [
-            pltpu.VMEM((mel_count, reach + 2 * TILE, lanes), f32),
-            pltpu.VMEM((mel_count, reach, lanes), f32),
-            pltpu.VMEM((mel_count, reach + 2 * TILE, lanes), f32),
+            pltpu.VMEM((mel_count, reach + 2 * TILE, 2 * lanes), f32),
+            pltpu.VMEM((mel_count, reach, 2 * lanes), f32),
+            pltpu.VMEM((mel_count, reach + 2 * TILE, 2 * lanes), f32),
         ],
-        2**28,
-        8,
-    )
+        0,
+        10,
+    )
+
+
+def close_kernel(mine, other, keep, out):
+    mel_count, frames, lanes = mine.shape
+    begin = pl.multiple_of(lax.axis_index("tm") * frames, frames)
+    mask = keep[pl.ds(begin, frames)]
+    for m in range(mel_count):
+        out[:, m, :] = (mine[m] + other[m]) * mask
+
+
+def close(mine, other, keep):
+    mel_count, frames, lanes = mine.shape
+    return call(
+        close_kernel,
+        (mine, other, keep),
+        [whole_spec()] * 3,
+        [((frames, mel_count, lanes), f32)],
+        [whole_spec()],
+        [],
+        0,
+        4,
+    )[0]
 
 
 def whole_frames(
@@ -1038,7 +1262,9 @@
     frames, mel_count, lanes = features.shape
     places = lax.axis_size("tm")
     total = frames * places
-    scales = jnp.stack([norm1_gain, norm1_bias, norm2_gain, norm2_bias])
+    clip_starts, conv1_weight, scales = bring(
+        clip_starts, conv1_weight, (norm1_gain, norm1_bias, norm2_gain, norm2_bias)
+    )
 
     marked = jnp.where(valid[:, None, None] > 0, features, jnp.asarray(ABSENT, bf16))
     own = jnp.transpose(marked, (1, 0, 2))
@@ -1049,67 +1275,100 @@
         swap(along, "chan", 2),
         swap_both(along, "tm", 1, "chan", 2),
     ]
+    near[3], clip_starts, conv1_weight, scales = lax.optimization_barrier(
+        (near[3], clip_starts, conv1_weight, scales)
+    )
     blocks = near + [swap(block, "chan", 1) for block in near]
-
-    hidden, field, pre, keep, stats = first_block(
+    other_conv2 = swap(conv2_weight, "chan", 1)
+    readout_grad, own = lax.optimization_barrier((readout_grad, own))
+    cotangents = [readout_grad[None]]
+    for bit in gather_bits(places):
+        cotangents.append(swap(jnp.concatenate(cotangents), "tm", bit))
+    blocks, other_conv2, cotangents = lax.optimization_barrier((blocks, other_conv2, cotangents))
+
+    low, high, picked, field, pre, keep, stats = first_block(
         blocks, conv1_weight, scales, clip_starts, total
     )
-    hidden_near = swap(hidden, "chan", 1)
-    hidden_far = swap(hidden, "chan", 2)
-
-    conv2_weight, conv1_weight, readout_grad, hidden_near = lax.optimization_barrier(
-        (conv2_weight, conv1_weight, readout_grad, hidden_near)
-    )
-    partial = second_partial(hidden, hidden_near, conv2_weight, clip_starts)
+
+    far_picked = swap(picked, "chan", 2)
+    far = swap(low, "chan", 2)
+    far_rest = swap(far_picked, "tm", 1)
+
+    low_two, high_two = swap(low, "chan", 1), swap(high, "chan", 1)
+    near = near_part(low, high, low_two, high_two, conv2_weight, clip_starts)
+    far_picked, near = lax.optimization_barrier((far_picked, near))
+    picked_two = swap(far_picked, "chan", 1)
+    early = early_part(far_picked, picked_two, conv2_weight, clip_starts)
+    early, pre = lax.optimization_barrier((early, pre))
     slope = first_slope(pre, stats, scales, keep)
-    cotangent = readout_grad[None]
-    bit = 1
-    while bit < places:
-        cotangent = jnp.concatenate([cotangent, swap(cotangent, "tm", bit)])
-        bit *= 2
-    other_conv2 = swap(conv2_weight, "chan", 1)
-    other_conv1 = swap(conv1_weight, "chan", 1)
-    hidden_far, partial, slope, cotangent, other_conv2, other_conv1 = lax.optimization_barrier(
-        (hidden_far, partial, slope, cotangent, other_conv2, other_conv1)
-    )
-
-    hidden_last = swap(hidden_far, "chan", 1)
+    far, far_rest, slope = lax.optimization_barrier((far, far_rest, slope))
+    far_two, rest_two = swap(far, "chan", 1), swap(far_rest, "chan", 1)
+
     readout, grad2, gain2_grad, shift2_grad = second_block(
-        hidden_far,
-        hidden_last,
+        near,
+        early,
+        (far, far_rest, far_two, rest_two),
         conv2_weight,
-        partial,
         keep,
         scales,
         clip_starts,
-        cotangent,
+        cotangents,
         readout_grad.shape[0],
     )
     grad2_near = swap(grad2, "chan", 1)
-    away = hidden_back(2, grad2, grad2_near, conv2_weight, other_conv2, clip_starts, bf16)
-    came = swap(away, "chan", 2)
-
-    mine = hidden_back(0, grad2, grad2_near, conv2_weight, other_conv2, clip_starts, f32)
+    steps2 = spread(grad2, clip_starts)
+    grad2_near, steps2 = lax.optimization_barrier((grad2_near, steps2))
+    back = functools.partial(
+        hidden_back,
+        one=grad2,
+        two=grad2_near,
+        weight=conv2_weight,
+        weight_two=other_conv2,
+        starts=clip_starts,
+    )
+    came_picked = swap(back(2, (2, 3), True, kind=bf16), "chan", 2)
+    away_low = back(2, (0, 1), False, kind=bf16)
+    came_low = swap(away_low, "chan", 2)
+
+    away_low, other_conv2 = lax.optimization_barrier((away_low, other_conv2))
+    mine = back(0, (0, 1, 2, 3), False, weight_two=other_conv2, kind=f32)
+    came_picked, mine, conv1_weight = lax.optimization_barrier((came_picked, mine, conv1_weight))
+    came_rest = swap(came_picked, "tm", 1)
+    other_conv1 = swap(conv1_weight, "chan", 1)
+    fields = (low, high, low_two, high_two)
+    fields += (far, far_picked, far_rest, far_two, picked_two, rest_two)
+    layout = [
+        (0, [(0, 0, 0), (0, 1, 0), (1, 0, 0), (1, 1, 0)]),
+        (1, [(2, 0, 0), (2, 1, 0), (3, 0, 0), (3, 1, 0)]),
+        (2, [(4, 0, 0), (4, 1, 0), (10, 0, 0), (10, 1, 0)]),
+        (3, [(7, 0, 0), (7, 1, 0), (11, 0, 0), (11, 1, 0)]),
+    ]
     weight2_grad = weight_back(
-        [hidden, hidden_near, hidden_far, hidden_last], grad2, clip_starts
-    )
-    came, mine, weight2_grad = lax.optimization_barrier((came, mine, weight2_grad))
+        layout, ((5, 6), (8, 9)), fields, grad2, steps2, conv2_weight.shape[2]
+    )
+    came_low, came_rest, mine, weight2_grad, other_conv1 = lax.optimization_barrier(
+        (came_low, came_rest, mine, weight2_grad, other_conv1)
+    )
 
     grad1, window, gain1_grad, shift1_grad = norm_back_first(
-        mine, came, slope, pre, stats, scales, keep, frames
+        mine, came_low, came_picked, came_rest, slope, pre, stats, scales, keep, frames
     )
     window_near = swap(window, "chan", 1)
+    steps1 = spread(grad1, clip_starts)
+    window_near, steps1 = lax.optimization_barrier((window_near, steps1))
     input_mine, input_away = input_back(
         window, window_near, conv1_weight, other_conv1, clip_starts, frames, lanes
     )
     input_came = swap(input_away, "chan", 2)
-    weight1_grad = weight_back([field], grad1, clip_starts)
+    layout = [
+        (None, [(0, m, lane) for m in range(mel_count)])
+        for lane in range(0, field.shape[2], LANES)
+    ]
+    weight1_grad = weight_back(layout, (), (field,), grad1, steps1, field.shape[2])
     input_came, weight1_grad = lax.optimization_barrier((input_came, weight1_grad))
-    live = (valid > 0).astype(f32)[None, :, None]
-    input_grad = jnp.transpose((input_mine + input_came) * live, (1, 0, 2))
     return (
         readout,
-        input_grad,
+        close(input_mine, input_came, keep),
         weight1_grad,
         gain1_grad[0],
         shift1_grad[0],
@@ -1119,13 +1378,14 @@
     )
 
 
-def fits_whole(frames, places, columns, widths):
+def fits_whole(frames, mels, places, columns, widths):
     return (
         places > 1
         and places & (places - 1) == 0
         and columns == 4
         and frames % 32 == 0
         and frames * places <= 512
+        and mels == 4
         and all(w % (columns * LANES) == 0 for w in widths)
         and widths[1] == columns * 256
     )
@@ -1135,6 +1395,7 @@
     features, conv1_weight, conv2_weight = arrays[0], arrays[1], arrays[4]
     if fits_whole(
         features.shape[0],
+        features.shape[1],
         lax.axis_size("tm"),
         lax.axis_size("chan"),
         (conv1_weight.shape[2], conv2_weight.shape[2]),

time: 132 us -> 116 us (0.88)
  waiting for transfers between devices: 43.7 us -> 19.1 us
  local copies, waits for them, and re-layouts: 1.41 us -> 5.04 us
  starting transfers between devices: 19.9 us -> 23.4 us
    ppermute x21 -> x28, waiting for transfers between devices: 37 us -> 19.1 us  [swap(): return lax.ppermute(shard, axis, [(i, i ^ bit) for i in range(count)])]
    ppermute x1, waiting for transfers between devices: 6.66 us -> 0.01 us  [swap_both(): return lax.ppermute(shard, (first, second), pairs)]
    unnamed x9 -> x16, local copies, waits for them, and re-layouts: 1.41 us -> 5.04 us
    ppermute x21 -> x28, starting transfers between devices: 17.4 us -> 20.9 us  [swap(): return lax.ppermute(shard, axis, [(i, i ^ bit) for i in range(count)])]
    concatenate x3 -> x2, other arithmetic: 0.03 us -> 1.53 us  [whole_frames(): cotangents.append(swap(jnp.concatenate(cotangents), 'tm', bit))]
    pallas_call x10 -> x16, Pallas kernels: 63.6 us -> 63.7 us  [call(): pl.pallas_call(body, out_shape=tuple((jax.ShapeDtypeStruct(s, d) for s, d...]
  transfers between devices with their start and end apart: 22 -> 29, of which waited for: 16 -> 13; matrix products, arithmetic and copies ran while one was open for 1% -> 3% of each run, Pallas kernels for 24% -> 34%
where the time goes in v3:
time: 116 us; the launch traced here: 115 us
  Pallas kernels  63.7 us (55%)
  starting transfers between devices  23.4 us (20%)
  waiting for transfers between devices  19.1 us (16%)
  local copies, waits for them, and re-layouts  5.04 us (4%)
  other arithmetic  3.15 us (3%)
    pallas_call x16, Pallas kernels, call(): pl.pallas_call(body, out_shape=tuple((jax.ShapeDtypeStruct(s, d) for s, d...  63.7 us
    ppermute x28, starting transfers between devices, swap(): return lax.ppermute(shard, axis, [(i, i ^ bit) for i in range(count)])  20.9 us
    ppermute x28, waiting for transfers between devices, swap(): return lax.ppermute(shard, axis, [(i, i ^ bit) for i in range(count)])  19.1 us
    unnamed x16, local copies, waits for them, and re-layouts  5.04 us
    ppermute x1, starting transfers between devices, swap_both(): return lax.ppermute(shard, (first, second), pairs)  2.51 us
  transfers between devices with their start and end apart: 29, of which 13 were waited for; matrix products, arithmetic and copies ran while one was open for 3% of the time, Pallas kernels for 34%

profile of v3, /device:TPU:0, one launch (start us, length us, event | category | flops | bytes accessed | tf_op | source)
XLA Modules:
  0.0 115.2 jit_solution(12203363048028473795)
XLA Ops:
  2.7 3.7 %collective-permute-start.11 = (f32[1,32,256]{2,1,0:T(8,128)}, f32[1,32,256]{2,1,0:T(8,128)S(1)}, u32[]{:S(2)}, u32[]{:S(2)}) collective-permute-start(f32[1,32,256]{2,1,0:T(8,128)} %bitcast.19), channel_id=1, source_target_pairs={{0,16},{4,20},{8,24},{12,28},{16,0},{20,4},{24,8},{28,12},{1,17},{... | collective-permute-start | bytes 98312 | tf_op jit(solution)/shard_map/ppermute | solution.py:326
  6.4 1.3 %collective-permute-start.2 = (bf16[4,64,128]{2,1,0:T(8,128)(2,1)S(1)}, bf16[4,64,128]{2,1,0:T(8,128)(2,1)S(1)}, u32[]{:S(2)}, u32[]{:S(2)}) collective-permute-start(bf16[4,64,128]{2,1,0:T(8,128)(2,1)S(1)} %get-tuple-element.129), channel_id=1, source_target_pairs={{0,24},{4,28},{8,16},{12,20},{16,8},{20,12},{24,0},{28,4},{1,25},{... | collective-permute-start | bytes 196616 | tf_op jit(solution)/shard_map/ppermute | solution.py:326
  7.8 1.7 %collective-permute-start.1 = (bf16[4,64,128]{2,1,0:T(8,128)(2,1)S(1)}, bf16[4,64,128]{2,1,0:T(8,128)(2,1)S(1)}, u32[]{:S(2)}, u32[]{:S(2)}) collective-permute-start(bf16[4,64,128]{2,1,0:T(8,128)(2,1)S(1)} %get-tuple-element.129), channel_id=1, source_target_pairs={{0,16},{4,20},{8,24},{12,28},{16,0},{20,4},{24,8},{28,12},{1,17},{... | collective-permute-start | bytes 196616 | tf_op jit(solution)/shard_map/ppermute | solution.py:326
  9.4 1.3 %collective-permute-start = (bf16[4,64,128]{2,1,0:T(8,128)(2,1)S(1)}, bf16[4,64,128]{2,1,0:T(8,128)(2,1)S(1)}, u32[]{:S(2)}, u32[]{:S(2)}) collective-permute-start(bf16[4,64,128]{2,1,0:T(8,128)(2,1)S(1)} %get-tuple-element.129), channel_id=1, source_target_pairs={{0,8},{4,12},{8,0},{12,4},{16,24},{20,28},{24,16},{28,20},{1,9},{5... | collective-permute-start | bytes 196616 | tf_op jit(solution)/shard_map/ppermute | solution.py:326
  11.6 1.5 %collective-permute-start.12 = (f32[2,32,256]{2,1,0:T(8,128)S(1)}, f32[2,32,256]{2,1,0:T(8,128)S(1)}, u32[]{:S(2)}, u32[]{:S(2)}) collective-permute-start(f32[2,32,256]{2,1,0:T(8,128)S(1)} %pad_maximum_fusion.2), channel_id=1, source_target_pairs={{0,4},{4,0},{8,12},{12,8},{16,20},{20,16},{24,28},{28,24},{1,5},{5... | collective-permute-start | bytes 196616 | tf_op jit(solution)/shard_map/ppermute | solution.py:326
  13.2 2.7 %collective-permute-done.1 = bf16[4,64,128]{2,1,0:T(8,128)(2,1)S(1)} collective-permute-done((bf16[4,64,128]{2,1,0:T(8,128)(2,1)S(1)}, bf16[4,64,128]{2,1,0:T(8,128)(2,1)S(1)}, u32[]{:S(2)}, u32[]{:S(2)}) %collective-permute-start.1) | collective-permute-done | bytes 65568 | tf_op jit(solution)/shard_map/ppermute | solution.py:326
  15.9 2.5 %collective-permute-start.3 = (bf16[4,4,64,128]{3,2,1,0:T(8,128)(2,1)S(1)}, bf16[4,4,64,128]{3,2,1,0:T(8,128)(2,1)S(1)}, u32[]{:S(2)}, u32[]{:S(2)}) collective-permute-start(bf16[4,4,64,128]{3,2,1,0:T(8,128)(2,1)S(1)} %pad_maximum_fusion.refs_1_), channel_id=1, source_target_pairs={{0,6},{1,7},{2,4},{3,5},{4,2},{5,3},{6,0},{7,1},{8,14},{9,15},{10,... | collective-permute-start | bytes 786440 | tf_op jit(solution)/shard_map/ppermute | solution.py:341
  20.4 1.7 %copy-done.1 = bf16[3,3,512,256]{3,2,1,0:T(8,128)(2,1)S(1)} copy-done((bf16[3,3,512,256]{3,2,1,0:T(8,128)(2,1)S(1)}, bf16[3,3,512,256]{3,2,1,0:T(8,128)(2,1)}, u32[]{:S(2)}) %copy-start.1) | copy-done | bytes 2359320
  25.4 1.4 %shard_map.161 = (s32[3]{0:T(128)S(1)}, bf16[3,3,512,256]{3,2,1,0:T(8,128)(2,1)S(1)}, f32[8,256]{1,0:T(8,128)S(1)}) custom-call(s32[3]{0:T(128)S(1)} %copy-done.7, bf16[3,3,512,256]{3,2,1,0:T(8,128)(2,1)S(1)} %copy-done.1, f32[1,256]{1,0:T(1,128)S(1)} %bitcast.23, f32[1,256]{1,0:T(1,128)S(1)} %bitcast.24, f32[1,256]{1,0:T(1,128)S(1)} %bitcast.25, ...), custom_call_target="tpu_custom_call" | custom-call | flops 1000 | bytes 1000 | tf_op jit(solution)/shard_map/pallas_call | solution.py:313
  26.8 3.4 %collective-permute-done.5.refs_3_ = bf16[4,4,64,128]{3,2,1,0:T(8,128)(2,1)S(1)} collective-permute-done((bf16[4,4,64,128]{3,2,1,0:T(8,128)(2,1)S(1)}, bf16[4,4,64,128]{3,2,1,0:T(8,128)(2,1)S(1)}, u32[]{:S(2)}, u32[]{:S(2)}) %collective-permute-start.5) | collective-permute-done | bytes 262176 | tf_op jit(solution)/shard_map/ppermute | solution.py:326
  32.6 8.0 %shard_map.162 = (bf16[2,512,256]{2,1,0:T(8,128)(2,1)S(1)}, bf16[2,512,256]{2,1,0:T(8,128)(2,1)S(1)}, bf16[2,256,256]{2,1,0:T(8,128)(2,1)S(1)}, bf16[4,512,512]{...) custom-call(s32[3]{0:T(128)S(1)} %get-tuple-element.71.refs_0_.starts, ...), custom_call_target="tpu_custom_call" | custom-call | flops 1000 | bytes 1000 | tf_op jit(solution)/shard_map/pallas_call | solution.py:313
  41.1 1.5 %collective-permute-start.14 = (bf16[2,256,256]{2,1,0:T(8,128)(2,1)S(1)}, bf16[2,256,256]{2,1,0:T(8,128)(2,1)S(1)}, u32[]{:S(2)}, u32[]{:S(2)}) collective-permute-start(bf16[2,256,256]{2,1,0:T(8,128)(2,1)S(1)} %get-tuple-element.84), channel_id=1, source_target_pairs={{0,2},{1,3},{2,0},{3,1},{4,6},{5,7},{6,4},{7,5},{8,10},{9,11},{10,... | collective-permute-start | bytes 786440 | tf_op jit(solution)/shard_map/ppermute | solution.py:326
  43.3 5.6 %shard_map.163.near = f32[4,512,256]{2,1,0:T(8,128)S(1)} custom-call(s32[3]{0:T(128)S(1)} %get-tuple-element.71.refs_0_.starts, bf16[2,512,256]{2,1,0:T(8,128)(2,1)S(1)} %get-tuple-element.85.low.refs_0_, bf16[2,512,256]{2,1,0:T(8,128)(2,1)S(1)} %get-tuple-element.86.high.refs_1_, bf16[2,512,256]{2,1,0:T(8,128)(2,1)S(1)} %collective-permute-done.15.low_two.refs_2_, ...), custom_call_target="tpu_custom_call" | custom-call | flops 1000 | bytes 1000 | tf_op jit(solution)/shard_map/pallas_call | solution.py:313
  48.9 1.4 %collective-permute-done.14.picked.refs_5_ = bf16[2,256,256]{2,1,0:T(8,128)(2,1)S(1)} collective-permute-done((bf16[2,256,256]{2,1,0:T(8,128)(2,1)S(1)}, bf16[2,256,256]{2,1,0:T(8,128)(2,1)S(1)}, u32[]{:S(2)}, u32[]{:S(2)}) %collective-permute-start.14) | collective-permute-done | bytes 262176 | tf_op jit(solution)/shard_map/ppermute | solution.py:326
  50.3 1.5 %collective-permute-start.19 = (bf16[2,256,256]{2,1,0:T(8,128)(2,1)S(1)}, bf16[2,256,256]{2,1,0:T(8,128)(2,1)S(1)}, u32[]{:S(2)}, u32[]{:S(2)}) collective-permute-start(bf16[2,256,256]{2,1,0:T(8,128)(2,1)S(1)} %collective-permute-done.14.picked.refs_5_), channel_id=1, source_target_pairs={{0,4},{4,0},{8,12},{12,8},{16,20},{20,16},{24,28},{28,24},{1,5},{5... | collective-permute-start | bytes 786440 | tf_op jit(solution)/shard_map/ppermute | solution.py:326
  51.8 2.4 %shard_map.164.early = f32[3,512,256]{2,1,0:T(8,128)S(1)} custom-call(s32[3]{0:T(128)S(1)} %get-tuple-element.71.refs_0_.starts, bf16[2,256,256]{2,1,0:T(8,128)(2,1)S(1)} %collective-permute-done.14.picked.refs_5_, bf16[2,256,256]{2,1,0:T(8,128)(2,1)S(1)} %collective-permute-done.17.picked_two.refs_8_, bf16[3,3,1024,256]{3,2,1,0:T(8,128)(2,1)S(1)} %copy-done), custom_call_target="tpu_custom_call" | custom-call | flops 1000 | bytes 1000 | tf_op jit(solution)/shard_map/pallas_call | solution.py:313
  55.4 5.3 %collective-permute-done.18.far.refs_4_ = bf16[2,512,256]{2,1,0:T(8,128)(2,1)S(1)} collective-permute-done((bf16[2,512,256]{2,1,0:T(8,128)(2,1)S(1)}, bf16[2,512,256]{2,1,0:T(8,128)(2,1)S(1)}, u32[]{:S(2)}, u32[]{:S(2)}) %collective-permute-start.18) | collective-permute-done | bytes 524320 | tf_op jit(solution)/shard_map/ppermute | solution.py:326
  61.2 1.8 %collective-permute-done.21.rest_two.refs_9_ = bf16[2,256,256]{2,1,0:T(8,128)(2,1)S(1)} collective-permute-done((bf16[2,256,256]{2,1,0:T(8,128)(2,1)S(1)}, bf16[2,256,256]{2,1,0:T(8,128)(2,1)S(1)}, u32[]{:S(2)}, u32[]{:S(2)}) %collective-permute-start.21) | collective-permute-done | bytes 262176 | tf_op jit(solution)/shard_map/ppermute | solution.py:326
  63.0 10.1 %shard_map.166 = (f32[32,256]{1,0:T(8,128)}, bf16[4,512,256]{2,1,0:T(8,128)(2,1)S(1)}, f32[1,256]{1,0:T(1,128)}, f32[1,256]{1,0:T(1,128)}) custom-call(s32[3]{0:T(128)S(1)} %get-tuple-element.71.refs_0_.starts, f32[4,512,256]{2,1,0:T(8,128)S(1)} %shard_map.163.near, f32[3,512,256]{2,1,0:T(8,128)S(1)} %shard_map.164.early, ...), custom_call_target="tpu_custom_call" | custom-call | flops 1000 | bytes 1000 | tf_op jit(solution)/shard_map/pallas_call | solution.py:313
  73.3 1.4 %shard_map.167.refs_11_ = bf16[2,4,512,256]{3,2,1,0:T(8,128)(2,1)S(1)} custom-call(s32[3]{0:T(128)S(1)} %get-tuple-element.71.refs_0_.starts, bf16[4,512,256]{2,1,0:T(8,128)(2,1)S(1)} %get-tuple-element.101.grad.one.refs_10_), custom_call_target="tpu_custom_call" | custom-call | flops 1000 | bytes 1000 | tf_op jit(solution)/shard_map/pallas_call | solution.py:313
  74.7 1.1 collective-permute-done.22.two
  75.8 2.1 %shard_map.169 = bf16[2,256,256]{2,1,0:T(8,128)(2,1)S(1)} custom-call(s32[3]{0:T(128)S(1)} %get-tuple-element.71.refs_0_.starts, bf16[4,512,256]{2,1,0:T(8,128)(2,1)S(1)} %get-tuple-element.101.grad.one.refs_10_, bf16[4,512,256]{2,1,0:T(8,128)(2,1)S(1)} %collective-permute-done.22.two, bf16[3,3,1024,256]{3,2,1,0:T(8,128)(2,1)S(1)} %copy-done, ...), custom_call_target="tpu_custom_call" | custom-call | flops 1000 | bytes 1000 | tf_op jit(solution)/shard_map/pallas_call | solution.py:313
  77.9 1.6 %collective-permute-start.24 = (bf16[2,256,256]{2,1,0:T(8,128)(2,1)S(1)}, bf16[2,256,256]{2,1,0:T(8,128)(2,1)S(1)}, u32[]{:S(2)}, u32[]{:S(2)}) collective-permute-start(bf16[2,256,256]{2,1,0:T(8,128)(2,1)S(1)} %shard_map.169), channel_id=1, source_target_pairs={{0,2},{1,3},{2,0},{3,1},{4,6},{5,7},{6,4},{7,5},{8,10},{9,11},{10,... | collective-permute-start | bytes 786440 | tf_op jit(solution)/shard_map/ppermute | solution.py:326
  79.5 3.2 %shard_map.168 = bf16[2,512,256]{2,1,0:T(8,128)(2,1)S(1)} custom-call(s32[3]{0:T(128)S(1)} %get-tuple-element.71.refs_0_.starts, bf16[4,512,256]{2,1,0:T(8,128)(2,1)S(1)} %get-tuple-element.101.grad.one.refs_10_, bf16[4,512,256]{2,1,0:T(8,128)(2,1)S(1)} %collective-permute-done.22.two, bf16[3,3,1024,256]{3,2,1,0:T(8,128)(2,1)S(1)} %copy-done, ...), custom_call_target="tpu_custom_call" | custom-call | flops 1000 | bytes 1000 | tf_op jit(solution)/shard_map/pallas_call | solution.py:313
  82.7 5.5 %shard_map.170.mine = f32[4,512,256]{2,1,0:T(8,128)S(1)} custom-call(s32[3]{0:T(128)S(1)} %get-tuple-element.71.refs_0_.starts, bf16[4,512,256]{2,1,0:T(8,128)(2,1)S(1)} %get-tuple-element.101.grad.one.refs_10_, bf16[4,512,256]{2,1,0:T(8,128)(2,1)S(1)} %collective-permute-done.22.two, bf16[3,3,1024,256]{3,2,1,0:T(8,128)(2,1)S(1)} %copy-done, ...), custom_call_target="tpu_custom_call" | custom-call | flops 1000 | bytes 1000 | tf_op jit(solution)/shard_map/pallas_call | solution.py:313
  88.9 1.5 %collective-permute-start.25 = (bf16[2,256,256]{2,1,0:T(8,128)(2,1)S(1)}, bf16[2,256,256]{2,1,0:T(8,128)(2,1)S(1)}, u32[]{:S(2)}, u32[]{:S(2)}) collective-permute-start(bf16[2,256,256]{2,1,0:T(8,128)(2,1)S(1)} %collective-permute-done.24.picked), channel_id=1, source_target_pairs={{0,4},{4,0},{8,12},{12,8},{16,20},{20,16},{24,28},{28,24},{1,5},{5... | collective-permute-start | bytes 786440 | tf_op jit(solution)/shard_map/ppermute | solution.py:326
  90.4 11.0 %shard_map.171 = f32[9,1024,256]{2,1,0:T(8,128)} custom-call(bf16[2,512,256]{2,1,0:T(8,128)(2,1)S(1)} %get-tuple-element.85.low.refs_0_, bf16[2,512,256]{2,1,0:T(8,128)(2,1)S(1)} %get-tuple-element.86.high.refs_1_, bf16[2,512,256]{2,1,0:T(8,128)(2,1)S(1)} %collective-permute-done.15.low_two.refs_2_, ...), custom_call_target="tpu_custom_call" | custom-call | flops 1000 | bytes 1000 | tf_op jit(solution)/shard_map/pallas_call | solution.py:313
  101.5 1.3 %collective-permute-done.23.other = bf16[2,512,256]{2,1,0:T(8,128)(2,1)S(1)} collective-permute-done((bf16[2,512,256]{2,1,0:T(8,128)(2,1)S(1)}, bf16[2,512,256]{2,1,0:T(8,128)(2,1)S(1)}, u32[]{:S(2)}, u32[]{:S(2)}) %collective-permute-start.23) | collective-permute-done | bytes 524320 | tf_op jit(solution)/shard_map/ppermute | solution.py:326
  102.7 2.0 %shard_map.172 = (bf16[4,512,256]{2,1,0:T(8,128)(2,1)S(1)}, bf16[4,96,256]{2,1,0:T(8,128)(2,1)S(1)}, f32[1,256]{1,0:T(1,128)}, f32[1,256]{1,0:T(1,128)}) custom-call(f32[4,512,256]{2,1,0:T(8,128)S(1)} %shard_map.170.mine, bf16[2,512,256]{2,1,0:T(8,128)(2,1)S(1)} %collective-permute-done.23.other, bf16[2,256,256]{2,1,0:T(8,128)(2,1)S(1)} %collective-permute-done.24.picked, ...), custom_call_target="tpu_custom_call" | custom-call | flops 1000 | bytes 1000 | tf_op jit(solution)/shard_map/pallas_call | solution.py:313
  104.8 1.6 %shard_map.173.refs_2_ = bf16[2,4,512,256]{3,2,1,0:T(8,128)(2,1)S(1)} custom-call(s32[3]{0:T(128)S(1)} %get-tuple-element.71.refs_0_.starts, bf16[4,512,256]{2,1,0:T(8,128)(2,1)S(1)} %get-tuple-element.114.grad.refs_1_), custom_call_target="tpu_custom_call" | custom-call | flops 1000 | bytes 1000 | tf_op jit(solution)/shard_map/pallas_call | solution.py:313
  106.4 1.5 %shard_map.174 = (f32[4,64,128]{2,1,0:T(8,128)S(1)}, f32[4,64,128]{2,1,0:T(8,128)S(1)}) custom-call(s32[3]{0:T(128)S(1)} %get-tuple-element.71.refs_0_.starts, bf16[4,96,256]{2,1,0:T(8,128)(2,1)S(1)} %get-tuple-element.113.one, bf16[4,96,256]{2,1,0:T(8,128)(2,1)S(1)} %collective-permute-done.27.two, ...), custom_call_target="tpu_custom_call" | custom-call | flops 1000 | bytes 1000 | tf_op jit(solution)/shard_map/pallas_call | solution.py:313
  108.5 5.9 %shard_map.175 = f32[9,512,256]{2,1,0:T(8,128)} custom-call(bf16[4,512,512]{2,1,0:T(8,128)(2,1)S(1)} %get-tuple-element.119.refs_0_, bf16[4,512,256]{2,1,0:T(8,128)(2,1)S(1)} %get-tuple-element.114.grad.refs_1_, bf16[2,4,512,256]{3,2,1,0:T(8,128)(2,1)S(1)} %shard_map.173.refs_2_), custom_call_target="tpu_custom_call" | custom-call | flops 1000 | bytes 1000 | tf_op jit(solution)/shard_map/pallas_call | solution.py:313
  (63 shorter events, 15.7 us)
Async XLA Ops:
  0.6 31.9 %collective-permute-start.10 = (bf16[3,3,1024,256]{3,2,1,0:T(8,128)(2,1)}, bf16[3,3,1024,256]{3,2,1,0:T(8,128)(2,1)S(1)}, u32[]{:S(2)}, u32[]{:S(2)}) collective-permute-start(bf16[3,3,1024,256]{3,2,1,0:T(8,128)(2,1)} %weight.11), channel_id=1, source_target_pairs={{0,1},{1,0},{2,3},{3,2},{4,5},{5,4},{6,7},{7,6},{8,9},{9,8},{10,11... | collective-permute-start | bytes 14155784 | tf_op jit(solution)/shard_map/ppermute | solution.py:326
  2.7 8.1 %collective-permute-start.11 = (f32[1,32,256]{2,1,0:T(8,128)}, f32[1,32,256]{2,1,0:T(8,128)S(1)}, u32[]{:S(2)}, u32[]{:S(2)}) collective-permute-start(f32[1,32,256]{2,1,0:T(8,128)} %bitcast.19), channel_id=1, source_target_pairs={{0,16},{4,20},{8,24},{12,28},{16,0},{20,4},{24,8},{28,12},{1,17},{... | collective-permute-start | bytes 98312 | tf_op jit(solution)/shard_map/ppermute | solution.py:326
  6.4 6.8 %collective-permute-start.2 = (bf16[4,64,128]{2,1,0:T(8,128)(2,1)S(1)}, bf16[4,64,128]{2,1,0:T(8,128)(2,1)S(1)}, u32[]{:S(2)}, u32[]{:S(2)}) collective-permute-start(bf16[4,64,128]{2,1,0:T(8,128)(2,1)S(1)} %get-tuple-element.129), channel_id=1, source_target_pairs={{0,24},{4,28},{8,16},{12,20},{16,8},{20,12},{24,0},{28,4},{1,25},{... | collective-permute-start | bytes 196616 | tf_op jit(solution)/shard_map/ppermute | solution.py:326
  7.8 8.1 %collective-permute-start.1 = (bf16[4,64,128]{2,1,0:T(8,128)(2,1)S(1)}, bf16[4,64,128]{2,1,0:T(8,128)(2,1)S(1)}, u32[]{:S(2)}, u32[]{:S(2)}) collective-permute-start(bf16[4,64,128]{2,1,0:T(8,128)(2,1)S(1)} %get-tuple-element.129), channel_id=1, source_target_pairs={{0,16},{4,20},{8,24},{12,28},{16,0},{20,4},{24,8},{28,12},{1,17},{... | collective-permute-start | bytes 196616 | tf_op jit(solution)/shard_map/ppermute | solution.py:326
  9.4 6.5 %collective-permute-start = (bf16[4,64,128]{2,1,0:T(8,128)(2,1)S(1)}, bf16[4,64,128]{2,1,0:T(8,128)(2,1)S(1)}, u32[]{:S(2)}, u32[]{:S(2)}) collective-permute-start(bf16[4,64,128]{2,1,0:T(8,128)(2,1)S(1)} %get-tuple-element.129), channel_id=1, source_target_pairs={{0,8},{4,12},{8,0},{12,4},{16,24},{20,28},{24,16},{28,20},{1,9},{5... | collective-permute-start | bytes 196616 | tf_op jit(solution)/shard_map/ppermute | solution.py:326
  11.6 7.9 %collective-permute-start.12 = (f32[2,32,256]{2,1,0:T(8,128)S(1)}, f32[2,32,256]{2,1,0:T(8,128)S(1)}, u32[]{:S(2)}, u32[]{:S(2)}) collective-permute-start(f32[2,32,256]{2,1,0:T(8,128)S(1)} %pad_maximum_fusion.2), channel_id=1, source_target_pairs={{0,4},{4,0},{8,12},{12,8},{16,20},{20,16},{24,28},{28,24},{1,5},{5... | collective-permute-start | bytes 196616 | tf_op jit(solution)/shard_map/ppermute | solution.py:326
  15.9 10.8 %collective-permute-start.3 = (bf16[4,4,64,128]{3,2,1,0:T(8,128)(2,1)S(1)}, bf16[4,4,64,128]{3,2,1,0:T(8,128)(2,1)S(1)}, u32[]{:S(2)}, u32[]{:S(2)}) collective-permute-start(bf16[4,4,64,128]{3,2,1,0:T(8,128)(2,1)S(1)} %pad_maximum_fusion.refs_1_), channel_id=1, source_target_pairs={{0,6},{1,7},{2,4},{3,5},{4,2},{5,3},{6,0},{7,1},{8,14},{9,15},{10,... | collective-permute-start | bytes 786440 | tf_op jit(solution)/shard_map/ppermute | solution.py:341
  18.4 11.8 %collective-permute-start.5 = (bf16[4,4,64,128]{3,2,1,0:T(8,128)(2,1)S(1)}, bf16[4,4,64,128]{3,2,1,0:T(8,128)(2,1)S(1)}, u32[]{:S(2)}, u32[]{:S(2)}) collective-permute-start(bf16[4,4,64,128]{3,2,1,0:T(8,128)(2,1)S(1)} %pad_maximum_fusion.refs_1_), channel_id=1, source_target_pairs={{0,2},{1,3},{2,0},{3,1},{4,6},{5,7},{6,4},{7,5},{8,10},{9,11},{10,... | collective-permute-start | bytes 786440 | tf_op jit(solution)/shard_map/ppermute | solution.py:326
  19.0 11.4 %collective-permute-start.4 = (bf16[4,4,64,128]{3,2,1,0:T(8,128)(2,1)S(1)}, bf16[4,4,64,128]{3,2,1,0:T(8,128)(2,1)S(1)}, u32[]{:S(2)}, u32[]{:S(2)}) collective-permute-start(bf16[4,4,64,128]{3,2,1,0:T(8,128)(2,1)S(1)} %pad_maximum_fusion.refs_1_), channel_id=1, source_target_pairs={{0,4},{4,0},{8,12},{12,8},{16,20},{20,16},{24,28},{28,24},{1,5},{5... | collective-permute-start | bytes 786440 | tf_op jit(solution)/shard_map/ppermute | solution.py:326
  20.3 10.5 %collective-permute-start.13 = (f32[4,32,256]{2,1,0:T(8,128)S(1)}, f32[4,32,256]{2,1,0:T(8,128)S(1)}, u32[]{:S(2)}, u32[]{:S(2)}) collective-permute-start(f32[4,32,256]{2,1,0:T(8,128)S(1)} %pad_maximum_fusion.1), channel_id=1, source_target_pairs={{0,8},{4,12},{8,0},{12,4},{16,24},{20,28},{24,16},{28,20},{1,9},{5... | collective-permute-start | bytes 393224 | tf_op jit(solution)/shard_map/ppermute | solution.py:326
  20.3 1.7 %copy-start.1 = (bf16[3,3,512,256]{3,2,1,0:T(8,128)(2,1)S(1)}, bf16[3,3,512,256]{3,2,1,0:T(8,128)(2,1)}, u32[]{:S(2)}) copy-start(bf16[3,3,512,256]{3,2,1,0:T(8,128)(2,1)} %weight_in.1) | copy-start | bytes 7077892
  25.4 17.9 %copy-start = (bf16[3,3,1024,256]{3,2,1,0:T(8,128)(2,1)S(1)}, bf16[3,3,1024,256]{3,2,1,0:T(8,128)(2,1)}, u32[]{:S(2)}) copy-start(bf16[3,3,1024,256]{3,2,1,0:T(8,128)(2,1)} %weight.11) | copy-start | bytes 14155780
  26.8 4.1 %collective-permute-start.6 = (bf16[4,4,64,128]{3,2,1,0:T(8,128)(2,1)S(1)}, bf16[4,4,64,128]{3,2,1,0:T(8,128)(2,1)S(1)}, u32[]{:S(2)}, u32[]{:S(2)}) collective-permute-start(bf16[4,4,64,128]{3,2,1,0:T(8,128)(2,1)S(1)} %pad_maximum_fusion.refs_1_), channel_id=1, source_target_pairs={{0,1},{1,0},{2,3},{3,2},{4,5},{5,4},{6,7},{7,6},{8,9},{9,8},{10,11... | collective-permute-start | bytes 786440 | tf_op jit(solution)/shard_map/ppermute | solution.py:326
  30.3 1.5 %collective-permute-start.8 = (bf16[4,4,64,128]{3,2,1,0:T(8,128)(2,1)S(1)}, bf16[4,4,64,128]{3,2,1,0:T(8,128)(2,1)S(1)}, u32[]{:S(2)}, u32[]{:S(2)}) collective-permute-start(bf16[4,4,64,128]{3,2,1,0:T(8,128)(2,1)S(1)} %collective-permute-done.5.refs_3_), channel_id=1, source_target_pairs={{0,1},{1,0},{2,3},{3,2},{4,5},{5,4},{6,7},{7,6},{8,9},{9,8},{10,11... | collective-permute-start | bytes 786440 | tf_op jit(solution)/shard_map/ppermute | solution.py:326
  30.4 1.8 %collective-permute-start.7 = (bf16[4,4,64,128]{3,2,1,0:T(8,128)(2,1)S(1)}, bf16[4,4,64,128]{3,2,1,0:T(8,128)(2,1)S(1)}, u32[]{:S(2)}, u32[]{:S(2)}) collective-permute-start(bf16[4,4,64,128]{3,2,1,0:T(8,128)(2,1)S(1)} %collective-permute-done.4.refs_2_), channel_id=1, source_target_pairs={{0,1},{1,0},{2,3},{3,2},{4,5},{5,4},{6,7},{7,6},{8,9},{9,8},{10,11... | collective-permute-start | bytes 786440 | tf_op jit(solution)/shard_map/ppermute | solution.py:326
  30.8 1.8 %collective-permute-start.9 = (bf16[4,4,64,128]{3,2,1,0:T(8,128)(2,1)S(1)}, bf16[4,4,64,128]{3,2,1,0:T(8,128)(2,1)S(1)}, u32[]{:S(2)}, u32[]{:S(2)}) collective-permute-start(bf16[4,4,64,128]{3,2,1,0:T(8,128)(2,1)S(1)} %collective-permute-done.3.refs_4_), channel_id=1, source_target_pairs={{0,1},{1,0},{2,3},{3,2},{4,5},{5,4},{6,7},{7,6},{8,9},{9,8},{10,11... | collective-permute-start | bytes 786440 | tf_op jit(solution)/shard_map/ppermute | solution.py:326
  40.5 2.6 %collective-permute-start.16 = (bf16[2,512,256]{2,1,0:T(8,128)(2,1)S(1)}, bf16[2,512,256]{2,1,0:T(8,128)(2,1)S(1)}, u32[]{:S(2)}, u32[]{:S(2)}) collective-permute-start(bf16[2,512,256]{2,1,0:T(8,128)(2,1)S(1)} %get-tuple-element.86.high.refs_1_), channel_id=1, source_target_pairs={{0,1},{1,0},{2,3},{3,2},{4,5},{5,4},{6,7},{7,6},{8,9},{9,8},{10,11... | collective-permute-start | bytes 1572872 | tf_op jit(solution)/shard_map/ppermute | solution.py:326
  40.7 2.5 %collective-permute-start.15 = (bf16[2,512,256]{2,1,0:T(8,128)(2,1)S(1)}, bf16[2,512,256]{2,1,0:T(8,128)(2,1)S(1)}, u32[]{:S(2)}, u32[]{:S(2)}) collective-permute-start(bf16[2,512,256]{2,1,0:T(8,128)(2,1)S(1)} %get-tuple-element.85.low.refs_0_), channel_id=1, source_target_pairs={{0,1},{1,0},{2,3},{3,2},{4,5},{5,4},{6,7},{7,6},{8,9},{9,8},{10,11... | collective-permute-start | bytes 1572872 | tf_op jit(solution)/shard_map/ppermute | solution.py:326
  41.1 9.2 %collective-permute-start.14 = (bf16[2,256,256]{2,1,0:T(8,128)(2,1)S(1)}, bf16[2,256,256]{2,1,0:T(8,128)(2,1)S(1)}, u32[]{:S(2)}, u32[]{:S(2)}) collective-permute-start(bf16[2,256,256]{2,1,0:T(8,128)(2,1)S(1)} %get-tuple-element.84), channel_id=1, source_target_pairs={{0,2},{1,3},{2,0},{3,1},{4,6},{5,7},{6,4},{7,5},{8,10},{9,11},{10,... | collective-permute-start | bytes 786440 | tf_op jit(solution)/shard_map/ppermute | solution.py:326
  42.6 18.1 %collective-permute-start.18 = (bf16[2,512,256]{2,1,0:T(8,128)(2,1)S(1)}, bf16[2,512,256]{2,1,0:T(8,128)(2,1)S(1)}, u32[]{:S(2)}, u32[]{:S(2)}) collective-permute-start(bf16[2,512,256]{2,1,0:T(8,128)(2,1)S(1)} %get-tuple-element.85.low.refs_0_), channel_id=1, source_target_pairs={{0,2},{1,3},{2,0},{3,1},{4,6},{5,7},{6,4},{7,5},{8,10},{9,11},{10,... | collective-permute-start | bytes 1572872 | tf_op jit(solution)/shard_map/ppermute | solution.py:326
  50.3 1.5 %collective-permute-start.17 = (bf16[2,256,256]{2,1,0:T(8,128)(2,1)S(1)}, bf16[2,256,256]{2,1,0:T(8,128)(2,1)S(1)}, u32[]{:S(2)}, u32[]{:S(2)}) collective-permute-start(bf16[2,256,256]{2,1,0:T(8,128)(2,1)S(1)} %collective-permute-done.14.picked.refs_5_), channel_id=1, source_target_pairs={{0,1},{1,0},{2,3},{3,2},{4,5},{5,4},{6,7},{7,6},{8,9},{9,8},{10,11... | collective-permute-start | bytes 786440 | tf_op jit(solution)/shard_map/ppermute | solution.py:326
  50.3 10.4 %collective-permute-start.19 = (bf16[2,256,256]{2,1,0:T(8,128)(2,1)S(1)}, bf16[2,256,256]{2,1,0:T(8,128)(2,1)S(1)}, u32[]{:S(2)}, u32[]{:S(2)}) collective-permute-start(bf16[2,256,256]{2,1,0:T(8,128)(2,1)S(1)} %collective-permute-done.14.picked.refs_5_), channel_id=1, source_target_pairs={{0,4},{4,0},{8,12},{12,8},{16,20},{20,16},{24,28},{28,24},{1,5},{5... | collective-permute-start | bytes 786440 | tf_op jit(solution)/shard_map/ppermute | solution.py:326
  54.2 8.8 %copy-start.2 = (f32[32,256]{1,0:T(8,128)S(1)}, f32[32,256]{1,0:T(8,128)}, u32[]{:S(2)}) copy-start(f32[32,256]{1,0:T(8,128)} %param.19) | copy-start | bytes 98308
  60.7 2.3 %collective-permute-start.20 = (bf16[2,512,256]{2,1,0:T(8,128)(2,1)S(1)}, bf16[2,512,256]{2,1,0:T(8,128)(2,1)S(1)}, u32[]{:S(2)}, u32[]{:S(2)}) collective-permute-start(bf16[2,512,256]{2,1,0:T(8,128)(2,1)S(1)} %collective-permute-done.18.far.refs_4_), channel_id=1, source_target_pairs={{0,1},{1,0},{2,3},{3,2},{4,5},{5,4},{6,7},{7,6},{8,9},{9,8},{10,11... | collective-permute-start | bytes 1572872 | tf_op jit(solution)/shard_map/ppermute | solution.py:326
  60.7 2.3 %collective-permute-start.21 = (bf16[2,256,256]{2,1,0:T(8,128)(2,1)S(1)}, bf16[2,256,256]{2,1,0:T(8,128)(2,1)S(1)}, u32[]{:S(2)}, u32[]{:S(2)}) collective-permute-start(bf16[2,256,256]{2,1,0:T(8,128)(2,1)S(1)} %collective-permute-done.19.rest.refs_6_), channel_id=1, source_target_pairs={{0,1},{1,0},{2,3},{3,2},{4,5},{5,4},{6,7},{7,6},{8,9},{9,8},{10,11... | collective-permute-start | bytes 786440 | tf_op jit(solution)/shard_map/ppermute | solution.py:326
  73.1 2.7 %collective-permute-start.22 = (bf16[4,512,256]{2,1,0:T(8,128)(2,1)S(1)}, bf16[4,512,256]{2,1,0:T(8,128)(2,1)S(1)}, u32[]{:S(2)}, u32[]{:S(2)}) collective-permute-start(bf16[4,512,256]{2,1,0:T(8,128)(2,1)S(1)} %get-tuple-element.101.grad.one.refs_10_), channel_id=1, source_target_pairs={{0,1},{1,0},{2,3},{3,2},{4,5},{5,4},{6,7},{7,6},{8,9},{9,8},{10,11... | collective-permute-start | bytes 3145736 | tf_op jit(solution)/shard_map/ppermute | solution.py:326
  77.9 10.4 %collective-permute-start.24 = (bf16[2,256,256]{2,1,0:T(8,128)(2,1)S(1)}, bf16[2,256,256]{2,1,0:T(8,128)(2,1)S(1)}, u32[]{:S(2)}, u32[]{:S(2)}) collective-permute-start(bf16[2,256,256]{2,1,0:T(8,128)(2,1)S(1)} %shard_map.169), channel_id=1, source_target_pairs={{0,2},{1,3},{2,0},{3,1},{4,6},{5,7},{6,4},{7,5},{8,10},{9,11},{10,... | collective-permute-start | bytes 786440 | tf_op jit(solution)/shard_map/ppermute | solution.py:326
  88.3 14.4 %collective-permute-start.26 = (bf16[3,3,512,256]{3,2,1,0:T(8,128)(2,1)S(1)}, bf16[3,3,512,256]{3,2,1,0:T(8,128)(2,1)S(1)}, u32[]{:S(2)}, u32[]{:S(2)}) collective-permute-start(bf16[3,3,512,256]{3,2,1,0:T(8,128)(2,1)S(1)} %get-tuple-element.108.refs_9_.weight), channel_id=1, source_target_pairs={{0,1},{1,0},{2,3},{3,2},{4,5},{5,4},{6,7},{7,6},{8,9},{9,8},{10,11... | collective-permute-start | bytes 7077896 | tf_op jit(solution)/shard_map/ppermute | solution.py:326
  88.4 14.3 %collective-permute-start.23 = (bf16[2,512,256]{2,1,0:T(8,128)(2,1)S(1)}, bf16[2,512,256]{2,1,0:T(8,128)(2,1)S(1)}, u32[]{:S(2)}, u32[]{:S(2)}) collective-permute-start(bf16[2,512,256]{2,1,0:T(8,128)(2,1)S(1)} %shard_map.168), channel_id=1, source_target_pairs={{0,2},{1,3},{2,0},{3,1},{4,6},{5,7},{6,4},{7,5},{8,10},{9,11},{10,... | collective-permute-start | bytes 1572872 | tf_op jit(solution)/shard_map/ppermute | solution.py:326
  88.9 12.5 %collective-permute-start.25 = (bf16[2,256,256]{2,1,0:T(8,128)(2,1)S(1)}, bf16[2,256,256]{2,1,0:T(8,128)(2,1)S(1)}, u32[]{:S(2)}, u32[]{:S(2)}) collective-permute-start(bf16[2,256,256]{2,1,0:T(8,128)(2,1)S(1)} %collective-permute-done.24.picked), channel_id=1, source_target_pairs={{0,4},{4,0},{8,12},{12,8},{16,20},{20,16},{24,28},{28,24},{1,5},{5... | collective-permute-start | bytes 786440 | tf_op jit(solution)/shard_map/ppermute | solution.py:326
  104.8 1.7 %collective-permute-start.27 = (bf16[4,96,256]{2,1,0:T(8,128)(2,1)S(1)}, bf16[4,96,256]{2,1,0:T(8,128)(2,1)S(1)}, u32[]{:S(2)}, u32[]{:S(2)}) collective-permute-start(bf16[4,96,256]{2,1,0:T(8,128)(2,1)S(1)} %get-tuple-element.113.one), channel_id=1, source_target_pairs={{0,1},{1,0},{2,3},{3,2},{4,5},{5,4},{6,7},{7,6},{8,9},{9,8},{10,11... | collective-permute-start | bytes 589832 | tf_op jit(solution)/shard_map/ppermute | solution.py:326
  108.0 6.5 %collective-permute-start.28 = (f32[4,64,128]{2,1,0:T(8,128)S(1)}, f32[4,64,128]{2,1,0:T(8,128)S(1)}, u32[]{:S(2)}, u32[]{:S(2)}) collective-permute-start(f32[4,64,128]{2,1,0:T(8,128)S(1)} %get-tuple-element.118), channel_id=1, source_target_pairs={{0,2},{1,3},{2,0},{3,1},{4,6},{5,7},{6,4},{7,5},{8,10},{9,11},{10,... | collective-permute-start | bytes 393224 | tf_op jit(solution)/shard_map/ppermute | solution.py:326
  (5 other events, 3.4 us)

commit v4 on v3

--- a/solution.py
+++ b/solution.py
@@ -288,7 +288,7 @@
 
 
 ABSENT = 1024.0
-ROWS = 32
+ROWS = 64
 TILE = 8
 LANES = 128
 
@@ -447,75 +447,48 @@
     return 0.3989422804014327 * jnp.exp(-0.5 * value * value)
 
 
-def bring_kernel(starts_in, weight_in, *refs):
-    vectors, (starts, weight, scales, sems) = refs[:4], refs[4:]
-    copies = [pltpu.make_async_copy(weight_in, weight, sems.at[0])]
-    for k, vector in enumerate(vectors):
-        copies.append(pltpu.make_async_copy(vector, scales.at[k : k + 1], sems.at[1 + k]))
-    for copy in copies:
-        copy.start()
+def bring_kernel(starts_in, weight_in, starts, weight, sem):
+    copy = pltpu.make_async_copy(weight_in, weight, sem)
+    copy.start()
     for k in range(starts.shape[0]):
         starts[k] = starts_in[k]
-    for copy in copies:
-        copy.wait()
-
-
-def bring(starts, weight, vectors):
+    copy.wait()
+
+
+def bring(starts, weight):
     return call(
         bring_kernel,
-        (starts, weight, *[v[None] for v in vectors]),
-        [scalar_spec()] + [far_spec()] * 5,
-        [(starts.shape, jnp.int32), (weight.shape, bf16), ((TILE, vectors[0].shape[0]), f32)],
-        [scalar_spec(), whole_spec(), whole_spec()],
-        [pltpu.SemaphoreType.DMA((5,))],
+        (starts, weight),
+        [scalar_spec(), place_spec()],
+        [(starts.shape, jnp.int32), (weight.shape, bf16)],
+        [scalar_spec(), whole_spec()],
+        [pltpu.SemaphoreType.DMA],
         0,
         4,
     )
 
 
-def first_kernel(*refs):
-    starts, blocks, (weight, scales) = refs[0], refs[1:9], refs[9:11]
-    low, high, picked, field_out, pre_out, keep, stats = refs[11:18]
-    field, lower, middle, upper, sems = refs[18:]
+def first_kernel(starts, *refs):
+    blocks, (weight, scales) = refs[:8], refs[8:10]
+    low, high, picked, field, middle, keep, stats = refs[10:17]
+    lower, upper = refs[17:]
     mel_count, total, width = field.shape
     out_width = middle.shape[2]
     place, column = lax.axis_index("tm"), lax.axis_index("chan")
-    copies = []
     frames, lanes = blocks[0].shape[2], blocks[0].shape[3]
-    count = blocks[0].shape[0]
+    clear_edges(lower, upper, total)
     for i, block in enumerate(blocks):
         core, row, side = i // 4, (i // 2) % 2, i % 2
-        from_column = column ^ (2 * row + core)
-        for k in range(count):
-            from_place = place ^ (2 * k + side)
-            copies.append(
-                pltpu.make_async_copy(
-                    block.at[k],
-                    field.at[
-                        :,
-                        pl.ds(pl.multiple_of(from_place * frames, frames), frames),
-                        pl.ds(pl.multiple_of(from_column * lanes, lanes), lanes),
-                    ],
-                    sems.at[len(copies)],
+        to_columns = pl.ds(pl.multiple_of((column ^ (2 * row + core)) * lanes, lanes), lanes)
+        for k in range(block.shape[0]):
+            to_rows = pl.ds(pl.multiple_of((place ^ (2 * k + side)) * frames, frames), frames)
+            for m in range(mel_count):
+                rows = block[k, m]
+                if m == 0 and i < 2:
+                    keep[to_rows] = (rows.astype(f32) < ABSENT / 2).astype(f32)
+                field[m, to_rows, to_columns] = jnp.where(
+                    rows < ABSENT / 2, rows, jnp.zeros_like(rows)
                 )
-            )
-    for copy in copies:
-        copy.start()
-    clear_edges(lower, upper, total)
-    for copy in copies:
-        copy.wait()
-
-    def decode(at, carry):
-        for m in range(mel_count):
-            rows = field[m, pl.ds(at, ROWS)]
-            if m == 0:
-                keep[pl.ds(at, ROWS)] = (rows[:, :LANES].astype(f32) < ABSENT / 2).astype(f32)
-            field[m, pl.ds(at, ROWS)] = jnp.where(rows < ABSENT / 2, rows, jnp.zeros_like(rows))
-        return carry
-
-    by_rows(total, decode, 0)
-    save = pltpu.make_async_copy(field, field_out, sems.at[1])
-    save.start()
     convolve(
         [lambda m: field[m]], [lambda a, b: weight[a, b]], lower, middle, upper, total, False
     )
@@ -535,8 +508,6 @@
 
     blank = jnp.zeros((TILE, out_width), f32)
     one, two, num = by_rows(total, combine, (blank, blank, blank))
-    save_pre = pltpu.make_async_copy(middle, pre_out, sems.at[0])
-    save_pre.start()
     pixels = column_sum(num) * mel_count
     center, inverse = moments((one, two), keep, pixels)
     stats[0:1] = center
@@ -560,36 +531,29 @@
     reach = picked.shape[1]
     for m in range(picked.shape[0]):
         picked[m] = high[m, pl.ds(pl.multiple_of((place % 2) * reach, reach), reach)]
-    save.wait()
-    save_pre.wait()
 
 
 def first_block(blocks, weight, scales, starts, total):
-    count, mel_count, frames, lanes = blocks[0].shape
+    _, mel_count, frames, lanes = blocks[0].shape
     width, out_width = weight.shape[2], weight.shape[3]
     padded = (mel_count, total + 2 * TILE, out_width)
+    half = (mel_count // 2, total, out_width)
     return call(
         first_kernel,
         (starts, *blocks, weight, scales),
-        [scalar_spec()] + [place_spec()] * 8 + [whole_spec()] * 2,
+        [scalar_spec()] + [whole_spec()] * 10,
         [
-            ((mel_count // 2, total, out_width), bf16),
-            ((mel_count // 2, total, out_width), bf16),
+            (half, bf16),
+            (half, bf16),
             ((mel_count // 2, total // 2, out_width), bf16),
             ((mel_count, total, width), bf16),
             ((mel_count, total, out_width), f32),
             ((total, LANES), f32),
             ((TILE, out_width), f32),
         ],
-        [whole_spec()] * 3 + [place_spec()] * 2 + [whole_spec()] * 2,
-        [
-            pltpu.VMEM((mel_count, total, width), bf16),
-            pltpu.VMEM(padded, f32),
-            pltpu.VMEM((mel_count, total, out_width), f32),
-            pltpu.VMEM(padded, f32),
-            pltpu.SemaphoreType.DMA((8 * count,)),
-        ],
-        2 * 9 * mel_count * total * width * out_width,
+        [whole_spec()] * 7,
+        [pltpu.VMEM(padded, f32), pltpu.VMEM(padded, f32)],
+        0,
         16,
     )
 
@@ -1262,29 +1226,29 @@
     frames, mel_count, lanes = features.shape
     places = lax.axis_size("tm")
     total = frames * places
-    clip_starts, conv1_weight, scales = bring(
-        clip_starts, conv1_weight, (norm1_gain, norm1_bias, norm2_gain, norm2_bias)
-    )
+    clip_starts, conv1_weight = bring(clip_starts, conv1_weight)
+    scales = jnp.stack([norm1_gain, norm1_bias, norm2_gain, norm2_bias])
 
     marked = jnp.where(valid[:, None, None] > 0, features, jnp.asarray(ABSENT, bf16))
     own = jnp.transpose(marked, (1, 0, 2))
-    along = jnp.stack([own] + [swap(own, "tm", 2 * k) for k in range(1, places // 2)])
+    pieces = [swap(own, "tm", 2 * k) for k in range(1, places // 2)]
+    along = jnp.stack([own] + pieces)
     near = [
         along,
         swap(along, "tm", 1),
         swap(along, "chan", 2),
         swap_both(along, "tm", 1, "chan", 2),
     ]
-    near[3], clip_starts, conv1_weight, scales = lax.optimization_barrier(
-        (near[3], clip_starts, conv1_weight, scales)
+    readout_grad, _ = lax.optimization_barrier((readout_grad, pieces[0]))
+    bits = gather_bits(places)
+    cotangents = [readout_grad[None]]
+    cotangents.append(swap(cotangents[0], "tm", bits[0]))
+    near[3], clip_starts, conv1_weight, scales, cotangents = lax.optimization_barrier(
+        (near[3], clip_starts, conv1_weight, scales, cotangents)
     )
     blocks = near + [swap(block, "chan", 1) for block in near]
     other_conv2 = swap(conv2_weight, "chan", 1)
-    readout_grad, own = lax.optimization_barrier((readout_grad, own))
-    cotangents = [readout_grad[None]]
-    for bit in gather_bits(places):
-        cotangents.append(swap(jnp.concatenate(cotangents), "tm", bit))
-    blocks, other_conv2, cotangents = lax.optimization_barrier((blocks, other_conv2, cotangents))
+    blocks, other_conv2 = lax.optimization_barrier((blocks, other_conv2))
 
     low, high, picked, field, pre, keep, stats = first_block(
         blocks, conv1_weight, scales, clip_starts, total
@@ -1296,12 +1260,15 @@
 
     low_two, high_two = swap(low, "chan", 1), swap(high, "chan", 1)
     near = near_part(low, high, low_two, high_two, conv2_weight, clip_starts)
-    far_picked, near = lax.optimization_barrier((far_picked, near))
+    far_picked, near, cotangents = lax.optimization_barrier((far_picked, near, cotangents))
     picked_two = swap(far_picked, "chan", 1)
+    for bit in bits[1:-1]:
+        cotangents.append(swap(jnp.concatenate(cotangents), "tm", bit))
     early = early_part(far_picked, picked_two, conv2_weight, clip_starts)
-    early, pre = lax.optimization_barrier((early, pre))
+    early, pre, cotangents = lax.optimization_barrier((early, pre, cotangents))
+    cotangents.append(swap(jnp.concatenate(cotangents), "tm", bits[-1]))
     slope = first_slope(pre, stats, scales, keep)
-    far, far_rest, slope = lax.optimization_barrier((far, far_rest, slope))
+    far, far_rest, slope, cotangents = lax.optimization_barrier((far, far_rest, slope, cotangents))
     far_two, rest_two = swap(far, "chan", 1), swap(far_rest, "chan", 1)
 
     readout, grad2, gain2_grad, shift2_grad = second_block(
@@ -1362,7 +1329,7 @@
     input_came = swap(input_away, "chan", 2)
     layout = [
         (None, [(0, m, lane) for m in range(mel_count)])
-        for lane in range(0, field.shape[2], LANES)
+        for lane in range(0, field.shape[2], 256)
     ]
     weight1_grad = weight_back(layout, (), (field,), grad1, steps1, field.shape[2])
     input_came, weight1_grad = lax.optimization_barrier((input_came, weight1_grad))
@@ -1383,7 +1350,7 @@
         places > 1
         and places & (places - 1) == 0
         and columns == 4
-        and frames % 32 == 0
+        and frames % ROWS == 0
         and frames * places <= 512
         and mels == 4
         and all(w % (columns * LANES) == 0 for w in widths)

time: 116 us -> 111 us (0.957)
  local copies, waits for them, and re-layouts: 5.04 us -> 2.32 us
  Pallas kernels: 63.7 us -> 61.9 us
  waiting for transfers between devices: 19.1 us -> 20.7 us
    unnamed x16 -> x8, local copies, waits for them, and re-layouts: 5.04 us -> 2.32 us
    pallas_call x16, Pallas kernels: 63.7 us -> 61.9 us  [call(): pl.pallas_call(body, out_shape=tuple((jax.ShapeDtypeStruct(s, d) for s, d...]
    concatenate x2 -> x1, other arithmetic: 1.53 us -> 0.01 us  [whole_frames(): cotangents.append(swap(jnp.concatenate(cotangents), 'tm', bit))]
    ppermute x28, waiting for transfers between devices: 19.1 us -> 20.4 us  [swap(): return lax.ppermute(shard, axis, [(i, i ^ bit) for i in range(count)])]
  transfers between devices with their start and end apart: 29 -> 29, of which waited for: 13 -> 16; matrix products, arithmetic and copies ran while one was open for 3% -> 2% of each run, Pallas kernels for 34% -> 35%
where the time goes in v4:
time: 111 us
  Pallas kernels  61.9 us (56%)
  starting transfers between devices  23 us (21%)
  waiting for transfers between devices  20.7 us (19%)
  other arithmetic  2.37 us (2%)
  local copies, waits for them, and re-layouts  2.32 us (2%)
    pallas_call x16, Pallas kernels, call(): pl.pallas_call(body, out_shape=tuple((jax.ShapeDtypeStruct(s, d) for s, d...  61.9 us
    ppermute x28, starting transfers between devices, swap(): return lax.ppermute(shard, axis, [(i, i ^ bit) for i in range(count)])  20.5 us
    ppermute x28, waiting for transfers between devices, swap(): return lax.ppermute(shard, axis, [(i, i ^ bit) for i in range(count)])  20.4 us
    ppermute x1, starting transfers between devices, swap_both(): return lax.ppermute(shard, (first, second), pairs)  2.51 us
    unnamed x8, local copies, waits for them, and re-layouts  2.32 us
  transfers between devices with their start and end apart: 29, of which 16 were waited for; matrix products, arithmetic and copies ran while one was open for 2% of the time, Pallas kernels for 35%

profile of v4, /device:TPU:0, one launch (start us, length us, event | category | flops | bytes accessed | tf_op | source)
XLA Modules:
  0.0 111.1 jit_solution(14543843718360597388)
XLA Ops:
  2.7 3.7 %collective-permute-start.1 = (bf16[4,64,128]{2,1,0:T(8,128)(2,1)S(1)}, bf16[4,64,128]{2,1,0:T(8,128)(2,1)S(1)}, u32[]{:S(2)}, u32[]{:S(2)}) collective-permute-start(bf16[4,64,128]{2,1,0:T(8,128)(2,1)S(1)} %get-tuple-element.141), channel_id=1, source_target_pairs={{0,16},{4,20},{8,24},{12,28},{16,0},{20,4},{24,8},{28,12},{1,17},{... | collective-permute-start | bytes 196616 | tf_op jit(solution)/shard_map/ppermute | solution.py:326
  6.4 1.6 %collective-permute-start = (bf16[4,64,128]{2,1,0:T(8,128)(2,1)S(1)}, bf16[4,64,128]{2,1,0:T(8,128)(2,1)S(1)}, u32[]{:S(2)}, u32[]{:S(2)}) collective-permute-start(bf16[4,64,128]{2,1,0:T(8,128)(2,1)S(1)} %get-tuple-element.141), channel_id=1, source_target_pairs={{0,8},{4,12},{8,0},{12,4},{16,24},{20,28},{24,16},{28,20},{1,9},{5... | collective-permute-start | bytes 196616 | tf_op jit(solution)/shard_map/ppermute | solution.py:326
  8.0 2.5 %collective-permute-done.1 = bf16[4,64,128]{2,1,0:T(8,128)(2,1)S(1)} collective-permute-done((bf16[4,64,128]{2,1,0:T(8,128)(2,1)S(1)}, bf16[4,64,128]{2,1,0:T(8,128)(2,1)S(1)}, u32[]{:S(2)}, u32[]{:S(2)}) %collective-permute-start.1) | collective-permute-done | bytes 65568 | tf_op jit(solution)/shard_map/ppermute | solution.py:326
  10.9 3.1 %collective-permute-done.2 = bf16[4,64,128]{2,1,0:T(8,128)(2,1)S(1)} collective-permute-done((bf16[4,64,128]{2,1,0:T(8,128)(2,1)S(1)}, bf16[4,64,128]{2,1,0:T(8,128)(2,1)S(1)}, u32[]{:S(2)}, u32[]{:S(2)}) %collective-permute-start.2) | collective-permute-done | bytes 65568 | tf_op jit(solution)/shard_map/ppermute | solution.py:326
  14.1 2.5 %collective-permute-start.3 = (bf16[4,4,64,128]{3,2,1,0:T(8,128)(2,1)S(1)}, bf16[4,4,64,128]{3,2,1,0:T(8,128)(2,1)S(1)}, u32[]{:S(2)}, u32[]{:S(2)}) collective-permute-start(bf16[4,4,64,128]{3,2,1,0:T(8,128)(2,1)S(1)} %pad_maximum_fusion.refs_0_), channel_id=1, source_target_pairs={{0,6},{1,7},{2,4},{3,5},{4,2},{5,3},{6,0},{7,1},{8,14},{9,15},{10,... | collective-permute-start | bytes 786440 | tf_op jit(solution)/shard_map/ppermute | solution.py:341
  17.6 2.0 %collective-permute-start.4 = (f32[1,32,256]{2,1,0:T(8,128)}, f32[1,32,256]{2,1,0:T(8,128)S(1)}, u32[]{:S(2)}, u32[]{:S(2)}) collective-permute-start(f32[1,32,256]{2,1,0:T(8,128)} %bitcast.19), channel_id=1, source_target_pairs={{0,16},{4,20},{8,24},{12,28},{16,0},{20,4},{24,8},{28,12},{1,17},{... | collective-permute-start | bytes 98312 | tf_op jit(solution)/shard_map/ppermute | solution.py:326
  20.4 1.7 %copy-done.1 = bf16[3,3,512,256]{3,2,1,0:T(8,128)(2,1)S(1)} copy-done((bf16[3,3,512,256]{3,2,1,0:T(8,128)(2,1)S(1)}, bf16[3,3,512,256]{3,2,1,0:T(8,128)(2,1)}, u32[]{:S(2)}) %copy-start.1) | copy-done | bytes 2359320
  22.7 1.3 %shard_map.161 = (s32[3]{0:T(128)S(1)}, bf16[3,3,512,256]{3,2,1,0:T(8,128)(2,1)S(1)}) custom-call(s32[3]{0:T(128)S(1)} %copy-done.3, bf16[3,3,512,256]{3,2,1,0:T(8,128)(2,1)S(1)} %copy-done.1), custom_call_target="tpu_custom_call" | custom-call | flops 1000 | bytes 1000 | tf_op jit(solution)/shard_map/pallas_call | solution.py:313
  24.3 3.3 %collective-permute-done.6.refs_2_ = bf16[4,4,64,128]{3,2,1,0:T(8,128)(2,1)S(1)} collective-permute-done((bf16[4,4,64,128]{3,2,1,0:T(8,128)(2,1)S(1)}, bf16[4,4,64,128]{3,2,1,0:T(8,128)(2,1)S(1)}, u32[]{:S(2)}, u32[]{:S(2)}) %collective-permute-start.6) | collective-permute-done | bytes 262176 | tf_op jit(solution)/shard_map/ppermute | solution.py:326
  29.9 7.1 %shard_map.162 = (bf16[2,512,256]{2,1,0:T(8,128)(2,1)S(1)}, bf16[2,512,256]{2,1,0:T(8,128)(2,1)S(1)}, bf16[2,256,256]{2,1,0:T(8,128)(2,1)S(1)}, bf16[4,512,512]{...) custom-call(s32[3]{0:T(128)S(1)} %get-tuple-element.77.starts, ...), custom_call_target="tpu_custom_call" | custom-call | flops 1000 | bytes 1000 | tf_op jit(solution)/shard_map/pallas_call | solution.py:313
  37.7 1.5 %collective-permute-start.12 = (bf16[2,256,256]{2,1,0:T(8,128)(2,1)S(1)}, bf16[2,256,256]{2,1,0:T(8,128)(2,1)S(1)}, u32[]{:S(2)}, u32[]{:S(2)}) collective-permute-start(bf16[2,256,256]{2,1,0:T(8,128)(2,1)S(1)} %get-tuple-element.89), channel_id=1, source_target_pairs={{0,2},{1,3},{2,0},{3,1},{4,6},{5,7},{6,4},{7,5},{8,10},{9,11},{10,... | collective-permute-start | bytes 786440 | tf_op jit(solution)/shard_map/ppermute | solution.py:326
  39.8 5.6 %shard_map.163.near = f32[4,512,256]{2,1,0:T(8,128)S(1)} custom-call(s32[3]{0:T(128)S(1)} %get-tuple-element.77.starts, bf16[2,512,256]{2,1,0:T(8,128)(2,1)S(1)} %get-tuple-element.90.low.refs_0_, bf16[2,512,256]{2,1,0:T(8,128)(2,1)S(1)} %get-tuple-element.91.high.refs_1_, bf16[2,512,256]{2,1,0:T(8,128)(2,1)S(1)} %collective-permute-done.13.low_two.refs_2_, ...), custom_call_target="tpu_custom_call" | custom-call | flops 1000 | bytes 1000 | tf_op jit(solution)/shard_map/pallas_call | solution.py:313
  45.4 1.4 %collective-permute-done.12.picked.refs_5_ = bf16[2,256,256]{2,1,0:T(8,128)(2,1)S(1)} collective-permute-done((bf16[2,256,256]{2,1,0:T(8,128)(2,1)S(1)}, bf16[2,256,256]{2,1,0:T(8,128)(2,1)S(1)}, u32[]{:S(2)}, u32[]{:S(2)}) %collective-permute-start.12) | collective-permute-done | bytes 262176 | tf_op jit(solution)/shard_map/ppermute | solution.py:326
  46.8 1.6 %collective-permute-start.16 = (f32[2,32,256]{2,1,0:T(8,128)S(1)}, f32[2,32,256]{2,1,0:T(8,128)S(1)}, u32[]{:S(2)}, u32[]{:S(2)}) collective-permute-start(f32[2,32,256]{2,1,0:T(8,128)S(1)} %pad_maximum_fusion.2), channel_id=1, source_target_pairs={{0,4},{4,0},{8,12},{12,8},{16,20},{20,16},{24,28},{28,24},{1,5},{5... | collective-permute-start | bytes 196616 | tf_op jit(solution)/shard_map/ppermute | solution.py:326
  48.9 2.3 %shard_map.164.early = f32[3,512,256]{2,1,0:T(8,128)S(1)} custom-call(s32[3]{0:T(128)S(1)} %get-tuple-element.77.starts, bf16[2,256,256]{2,1,0:T(8,128)(2,1)S(1)} %collective-permute-done.12.picked.refs_5_, bf16[2,256,256]{2,1,0:T(8,128)(2,1)S(1)} %collective-permute-done.15.picked_two.refs_8_, bf16[3,3,1024,256]{3,2,1,0:T(8,128)(2,1)S(1)} %copy-done), custom_call_target="tpu_custom_call" | custom-call | flops 1000 | bytes 1000 | tf_op jit(solution)/shard_map/pallas_call | solution.py:313
  51.7 1.4 %collective-permute-start.19 = (f32[4,32,256]{2,1,0:T(8,128)S(1)}, f32[4,32,256]{2,1,0:T(8,128)S(1)}, u32[]{:S(2)}, u32[]{:S(2)}) collective-permute-start(f32[4,32,256]{2,1,0:T(8,128)S(1)} %pad_maximum_fusion.1), channel_id=1, source_target_pairs={{0,8},{4,12},{8,0},{12,4},{16,24},{20,28},{24,16},{28,20},{1,9},{5... | collective-permute-start | bytes 393224 | tf_op jit(solution)/shard_map/ppermute | solution.py:326
  54.1 3.2 %collective-permute-done.17.far.refs_4_ = bf16[2,512,256]{2,1,0:T(8,128)(2,1)S(1)} collective-permute-done((bf16[2,512,256]{2,1,0:T(8,128)(2,1)S(1)}, bf16[2,512,256]{2,1,0:T(8,128)(2,1)S(1)}, u32[]{:S(2)}, u32[]{:S(2)}) %collective-permute-start.17) | collective-permute-done | bytes 524320 | tf_op jit(solution)/shard_map/ppermute | solution.py:326
  57.8 1.8 %collective-permute-done.21.rest_two.refs_9_ = bf16[2,256,256]{2,1,0:T(8,128)(2,1)S(1)} collective-permute-done((bf16[2,256,256]{2,1,0:T(8,128)(2,1)S(1)}, bf16[2,256,256]{2,1,0:T(8,128)(2,1)S(1)}, u32[]{:S(2)}, u32[]{:S(2)}) %collective-permute-start.21) | collective-permute-done | bytes 262176 | tf_op jit(solution)/shard_map/ppermute | solution.py:326
  59.6 9.8 %shard_map.166 = (f32[32,256]{1,0:T(8,128)}, bf16[4,512,256]{2,1,0:T(8,128)(2,1)S(1)}, f32[1,256]{1,0:T(1,128)}, f32[1,256]{1,0:T(1,128)}) custom-call(s32[3]{0:T(128)S(1)} %get-tuple-element.77.starts, f32[4,512,256]{2,1,0:T(8,128)S(1)} %shard_map.163.near, f32[3,512,256]{2,1,0:T(8,128)S(1)} %shard_map.164.early, ...), custom_call_target="tpu_custom_call" | custom-call | flops 1000 | bytes 1000 | tf_op jit(solution)/shard_map/pallas_call | solution.py:313
  69.6 1.4 %shard_map.167.refs_11_ = bf16[2,4,512,256]{3,2,1,0:T(8,128)(2,1)S(1)} custom-call(s32[3]{0:T(128)S(1)} %get-tuple-element.77.starts, bf16[4,512,256]{2,1,0:T(8,128)(2,1)S(1)} %get-tuple-element.113.grad.one.refs_10_), custom_call_target="tpu_custom_call" | custom-call | flops 1000 | bytes 1000 | tf_op jit(solution)/shard_map/pallas_call | solution.py:313
  71.0 1.2 %collective-permute-done.22.two = bf16[4,512,256]{2,1,0:T(8,128)(2,1)S(1)} collective-permute-done((bf16[4,512,256]{2,1,0:T(8,128)(2,1)S(1)}, bf16[4,512,256]{2,1,0:T(8,128)(2,1)S(1)}, u32[]{:S(2)}, u32[]{:S(2)}) %collective-permute-start.22) | collective-permute-done | bytes 1048608 | tf_op jit(solution)/shard_map/ppermute | solution.py:326
  72.1 2.1 %shard_map.169 = bf16[2,256,256]{2,1,0:T(8,128)(2,1)S(1)} custom-call(s32[3]{0:T(128)S(1)} %get-tuple-element.77.starts, bf16[4,512,256]{2,1,0:T(8,128)(2,1)S(1)} %get-tuple-element.113.grad.one.refs_10_, bf16[4,512,256]{2,1,0:T(8,128)(2,1)S(1)} %collective-permute-done.22.two, bf16[3,3,1024,256]{3,2,1,0:T(8,128)(2,1)S(1)} %copy-done, ...), custom_call_target="tpu_custom_call" | custom-call | flops 1000 | bytes 1000 | tf_op jit(solution)/shard_map/pallas_call | solution.py:313
  74.2 1.6 %collective-permute-start.24 = (bf16[2,256,256]{2,1,0:T(8,128)(2,1)S(1)}, bf16[2,256,256]{2,1,0:T(8,128)(2,1)S(1)}, u32[]{:S(2)}, u32[]{:S(2)}) collective-permute-start(bf16[2,256,256]{2,1,0:T(8,128)(2,1)S(1)} %shard_map.169), channel_id=1, source_target_pairs={{0,2},{1,3},{2,0},{3,1},{4,6},{5,7},{6,4},{7,5},{8,10},{9,11},{10,... | collective-permute-start | bytes 786440 | tf_op jit(solution)/shard_map/ppermute | solution.py:326
  75.8 3.2 %shard_map.168 = bf16[2,512,256]{2,1,0:T(8,128)(2,1)S(1)} custom-call(s32[3]{0:T(128)S(1)} %get-tuple-element.77.starts, bf16[4,512,256]{2,1,0:T(8,128)(2,1)S(1)} %get-tuple-element.113.grad.one.refs_10_, bf16[4,512,256]{2,1,0:T(8,128)(2,1)S(1)} %collective-permute-done.22.two, bf16[3,3,1024,256]{3,2,1,0:T(8,128)(2,1)S(1)} %copy-done, ...), custom_call_target="tpu_custom_call" | custom-call | flops 1000 | bytes 1000 | tf_op jit(solution)/shard_map/pallas_call | solution.py:313
  79.0 5.5 %shard_map.170.mine = f32[4,512,256]{2,1,0:T(8,128)S(1)} custom-call(s32[3]{0:T(128)S(1)} %get-tuple-element.77.starts, bf16[4,512,256]{2,1,0:T(8,128)(2,1)S(1)} %get-tuple-element.113.grad.one.refs_10_, bf16[4,512,256]{2,1,0:T(8,128)(2,1)S(1)} %collective-permute-done.22.two, bf16[3,3,1024,256]{3,2,1,0:T(8,128)(2,1)S(1)} %copy-done, ...), custom_call_target="tpu_custom_call" | custom-call | flops 1000 | bytes 1000 | tf_op jit(solution)/shard_map/pallas_call | solution.py:313
  85.2 1.5 %collective-permute-start.25 = (bf16[2,256,256]{2,1,0:T(8,128)(2,1)S(1)}, bf16[2,256,256]{2,1,0:T(8,128)(2,1)S(1)}, u32[]{:S(2)}, u32[]{:S(2)}) collective-permute-start(bf16[2,256,256]{2,1,0:T(8,128)(2,1)S(1)} %collective-permute-done.24.picked), channel_id=1, source_target_pairs={{0,4},{4,0},{8,12},{12,8},{16,20},{20,16},{24,28},{28,24},{1,5},{5... | collective-permute-start | bytes 786440 | tf_op jit(solution)/shard_map/ppermute | solution.py:326
  86.7 11.0 %shard_map.171 = f32[9,1024,256]{2,1,0:T(8,128)} custom-call(bf16[2,512,256]{2,1,0:T(8,128)(2,1)S(1)} %get-tuple-element.90.low.refs_0_, bf16[2,512,256]{2,1,0:T(8,128)(2,1)S(1)} %get-tuple-element.91.high.refs_1_, bf16[2,512,256]{2,1,0:T(8,128)(2,1)S(1)} %collective-permute-done.13.low_two.refs_2_, ...), custom_call_target="tpu_custom_call" | custom-call | flops 1000 | bytes 1000 | tf_op jit(solution)/shard_map/pallas_call | solution.py:313
  97.7 1.2 %collective-permute-done.23.other = bf16[2,512,256]{2,1,0:T(8,128)(2,1)S(1)} collective-permute-done((bf16[2,512,256]{2,1,0:T(8,128)(2,1)S(1)}, bf16[2,512,256]{2,1,0:T(8,128)(2,1)S(1)}, u32[]{:S(2)}, u32[]{:S(2)}) %collective-permute-start.23) | collective-permute-done | bytes 524320 | tf_op jit(solution)/shard_map/ppermute | solution.py:326
  99.0 1.8 %shard_map.172 = (bf16[4,512,256]{2,1,0:T(8,128)(2,1)S(1)}, bf16[4,96,256]{2,1,0:T(8,128)(2,1)S(1)}, f32[1,256]{1,0:T(1,128)}, f32[1,256]{1,0:T(1,128)}) custom-call(f32[4,512,256]{2,1,0:T(8,128)S(1)} %shard_map.170.mine, bf16[2,512,256]{2,1,0:T(8,128)(2,1)S(1)} %collective-permute-done.23.other, bf16[2,256,256]{2,1,0:T(8,128)(2,1)S(1)} %collective-permute-done.24.picked, ...), custom_call_target="tpu_custom_call" | custom-call | flops 1000 | bytes 1000 | tf_op jit(solution)/shard_map/pallas_call | solution.py:313
  100.8 1.6 %shard_map.173.refs_2_ = bf16[2,4,512,256]{3,2,1,0:T(8,128)(2,1)S(1)} custom-call(s32[3]{0:T(128)S(1)} %get-tuple-element.77.starts, bf16[4,512,256]{2,1,0:T(8,128)(2,1)S(1)} %get-tuple-element.126.grad.refs_1_), custom_call_target="tpu_custom_call" | custom-call | flops 1000 | bytes 1000 | tf_op jit(solution)/shard_map/pallas_call | solution.py:313
  102.5 1.5 %shard_map.174 = (f32[4,64,128]{2,1,0:T(8,128)S(1)}, f32[4,64,128]{2,1,0:T(8,128)S(1)}) custom-call(s32[3]{0:T(128)S(1)} %get-tuple-element.77.starts, bf16[4,96,256]{2,1,0:T(8,128)(2,1)S(1)} %get-tuple-element.125.one, bf16[4,96,256]{2,1,0:T(8,128)(2,1)S(1)} %collective-permute-done.27.two, bf16[3,3,512,256]{3,2,1,0:T(8,128)(2,1)S(1)} %get-tuple-element.120.refs_8_.weight, ...), custom_call_target="tpu_custom_call" | custom-call | flops 1000 | bytes 1000 | tf_op jit(solution)/shard_map/pallas_call | solution.py:313
  104.6 5.7 %shard_map.175 = f32[9,512,256]{2,1,0:T(8,128)} custom-call(bf16[4,512,512]{2,1,0:T(8,128)(2,1)S(1)} %get-tuple-element.131.refs_0_, bf16[4,512,256]{2,1,0:T(8,128)(2,1)S(1)} %get-tuple-element.126.grad.refs_1_, bf16[2,4,512,256]{3,2,1,0:T(8,128)(2,1)S(1)} %shard_map.173.refs_2_), custom_call_target="tpu_custom_call" | custom-call | flops 1000 | bytes 1000 | tf_op jit(solution)/shard_map/pallas_call | solution.py:313
  (56 shorter events, 13.5 us)
Async XLA Ops:
  0.6 29.3 %collective-permute-start.11 = (bf16[3,3,1024,256]{3,2,1,0:T(8,128)(2,1)}, bf16[3,3,1024,256]{3,2,1,0:T(8,128)(2,1)S(1)}, u32[]{:S(2)}, u32[]{:S(2)}) collective-permute-start(bf16[3,3,1024,256]{3,2,1,0:T(8,128)(2,1)} %weight.11), channel_id=1, source_target_pairs={{0,1},{1,0},{2,3},{3,2},{4,5},{5,4},{6,7},{7,6},{8,9},{9,8},{10,11... | collective-permute-start | bytes 14155784 | tf_op jit(solution)/shard_map/ppermute | solution.py:326
  2.7 7.7 %collective-permute-start.1 = (bf16[4,64,128]{2,1,0:T(8,128)(2,1)S(1)}, bf16[4,64,128]{2,1,0:T(8,128)(2,1)S(1)}, u32[]{:S(2)}, u32[]{:S(2)}) collective-permute-start(bf16[4,64,128]{2,1,0:T(8,128)(2,1)S(1)} %get-tuple-element.141), channel_id=1, source_target_pairs={{0,16},{4,20},{8,24},{12,28},{16,0},{20,4},{24,8},{28,12},{1,17},{... | collective-permute-start | bytes 196616 | tf_op jit(solution)/shard_map/ppermute | solution.py:326
  6.4 4.5 %collective-permute-start = (bf16[4,64,128]{2,1,0:T(8,128)(2,1)S(1)}, bf16[4,64,128]{2,1,0:T(8,128)(2,1)S(1)}, u32[]{:S(2)}, u32[]{:S(2)}) collective-permute-start(bf16[4,64,128]{2,1,0:T(8,128)(2,1)S(1)} %get-tuple-element.141), channel_id=1, source_target_pairs={{0,8},{4,12},{8,0},{12,4},{16,24},{20,28},{24,16},{28,20},{1,9},{5... | collective-permute-start | bytes 196616 | tf_op jit(solution)/shard_map/ppermute | solution.py:326
  8.0 6.1 %collective-permute-start.2 = (bf16[4,64,128]{2,1,0:T(8,128)(2,1)S(1)}, bf16[4,64,128]{2,1,0:T(8,128)(2,1)S(1)}, u32[]{:S(2)}, u32[]{:S(2)}) collective-permute-start(bf16[4,64,128]{2,1,0:T(8,128)(2,1)S(1)} %get-tuple-element.141), channel_id=1, source_target_pairs={{0,24},{4,28},{8,16},{12,20},{16,8},{20,12},{24,0},{28,4},{1,25},{... | collective-permute-start | bytes 196616 | tf_op jit(solution)/shard_map/ppermute | solution.py:326
  14.1 10.3 %collective-permute-start.3 = (bf16[4,4,64,128]{3,2,1,0:T(8,128)(2,1)S(1)}, bf16[4,4,64,128]{3,2,1,0:T(8,128)(2,1)S(1)}, u32[]{:S(2)}, u32[]{:S(2)}) collective-permute-start(bf16[4,4,64,128]{3,2,1,0:T(8,128)(2,1)S(1)} %pad_maximum_fusion.refs_0_), channel_id=1, source_target_pairs={{0,6},{1,7},{2,4},{3,5},{4,2},{5,3},{6,0},{7,1},{8,14},{9,15},{10,... | collective-permute-start | bytes 786440 | tf_op jit(solution)/shard_map/ppermute | solution.py:341
  16.6 11.1 %collective-permute-start.6 = (bf16[4,4,64,128]{3,2,1,0:T(8,128)(2,1)S(1)}, bf16[4,4,64,128]{3,2,1,0:T(8,128)(2,1)S(1)}, u32[]{:S(2)}, u32[]{:S(2)}) collective-permute-start(bf16[4,4,64,128]{3,2,1,0:T(8,128)(2,1)S(1)} %pad_maximum_fusion.refs_0_), channel_id=1, source_target_pairs={{0,2},{1,3},{2,0},{3,1},{4,6},{5,7},{6,4},{7,5},{8,10},{9,11},{10,... | collective-permute-start | bytes 786440 | tf_op jit(solution)/shard_map/ppermute | solution.py:326
  17.1 10.7 %collective-permute-start.5 = (bf16[4,4,64,128]{3,2,1,0:T(8,128)(2,1)S(1)}, bf16[4,4,64,128]{3,2,1,0:T(8,128)(2,1)S(1)}, u32[]{:S(2)}, u32[]{:S(2)}) collective-permute-start(bf16[4,4,64,128]{3,2,1,0:T(8,128)(2,1)S(1)} %pad_maximum_fusion.refs_0_), channel_id=1, source_target_pairs={{0,4},{4,0},{8,12},{12,8},{16,20},{20,16},{24,28},{28,24},{1,5},{5... | collective-permute-start | bytes 786440 | tf_op jit(solution)/shard_map/ppermute | solution.py:326
  17.6 6.3 %collective-permute-start.4 = (f32[1,32,256]{2,1,0:T(8,128)}, f32[1,32,256]{2,1,0:T(8,128)S(1)}, u32[]{:S(2)}, u32[]{:S(2)}) collective-permute-start(f32[1,32,256]{2,1,0:T(8,128)} %bitcast.19), channel_id=1, source_target_pairs={{0,16},{4,20},{8,24},{12,28},{16,0},{20,4},{24,8},{28,12},{1,17},{... | collective-permute-start | bytes 98312 | tf_op jit(solution)/shard_map/ppermute | solution.py:326
  20.3 1.7 %copy-start.1 = (bf16[3,3,512,256]{3,2,1,0:T(8,128)(2,1)S(1)}, bf16[3,3,512,256]{3,2,1,0:T(8,128)(2,1)}, u32[]{:S(2)}) copy-start(bf16[3,3,512,256]{3,2,1,0:T(8,128)(2,1)} %weight_in.1) | copy-start | bytes 7077892
  22.7 17.2 %copy-start = (bf16[3,3,1024,256]{3,2,1,0:T(8,128)(2,1)S(1)}, bf16[3,3,1024,256]{3,2,1,0:T(8,128)(2,1)}, u32[]{:S(2)}) copy-start(bf16[3,3,1024,256]{3,2,1,0:T(8,128)(2,1)} %weight.11) | copy-start | bytes 14155780
  24.0 4.3 %collective-permute-start.7 = (bf16[4,4,64,128]{3,2,1,0:T(8,128)(2,1)S(1)}, bf16[4,4,64,128]{3,2,1,0:T(8,128)(2,1)S(1)}, u32[]{:S(2)}, u32[]{:S(2)}) collective-permute-start(bf16[4,4,64,128]{3,2,1,0:T(8,128)(2,1)S(1)} %pad_maximum_fusion.refs_0_), channel_id=1, source_target_pairs={{0,1},{1,0},{2,3},{3,2},{4,5},{5,4},{6,7},{7,6},{8,9},{9,8},{10,11... | collective-permute-start | bytes 786440 | tf_op jit(solution)/shard_map/ppermute | solution.py:326
  27.7 1.5 %collective-permute-start.9 = (bf16[4,4,64,128]{3,2,1,0:T(8,128)(2,1)S(1)}, bf16[4,4,64,128]{3,2,1,0:T(8,128)(2,1)S(1)}, u32[]{:S(2)}, u32[]{:S(2)}) collective-permute-start(bf16[4,4,64,128]{3,2,1,0:T(8,128)(2,1)S(1)} %collective-permute-done.6.refs_2_), channel_id=1, source_target_pairs={{0,1},{1,0},{2,3},{3,2},{4,5},{5,4},{6,7},{7,6},{8,9},{9,8},{10,11... | collective-permute-start | bytes 786440 | tf_op jit(solution)/shard_map/ppermute | solution.py:326
  27.8 1.8 %collective-permute-start.8 = (bf16[4,4,64,128]{3,2,1,0:T(8,128)(2,1)S(1)}, bf16[4,4,64,128]{3,2,1,0:T(8,128)(2,1)S(1)}, u32[]{:S(2)}, u32[]{:S(2)}) collective-permute-start(bf16[4,4,64,128]{3,2,1,0:T(8,128)(2,1)S(1)} %collective-permute-done.5.refs_1_), channel_id=1, source_target_pairs={{0,1},{1,0},{2,3},{3,2},{4,5},{5,4},{6,7},{7,6},{8,9},{9,8},{10,11... | collective-permute-start | bytes 786440 | tf_op jit(solution)/shard_map/ppermute | solution.py:326
  28.2 1.8 %collective-permute-start.10 = (bf16[4,4,64,128]{3,2,1,0:T(8,128)(2,1)S(1)}, bf16[4,4,64,128]{3,2,1,0:T(8,128)(2,1)S(1)}, u32[]{:S(2)}, u32[]{:S(2)}) collective-permute-start(bf16[4,4,64,128]{3,2,1,0:T(8,128)(2,1)S(1)} %collective-permute-done.3.refs_3_), channel_id=1, source_target_pairs={{0,1},{1,0},{2,3},{3,2},{4,5},{5,4},{6,7},{7,6},{8,9},{9,8},{10,11... | collective-permute-start | bytes 786440 | tf_op jit(solution)/shard_map/ppermute | solution.py:326
  37.1 2.6 %collective-permute-start.14 = (bf16[2,512,256]{2,1,0:T(8,128)(2,1)S(1)}, bf16[2,512,256]{2,1,0:T(8,128)(2,1)S(1)}, u32[]{:S(2)}, u32[]{:S(2)}) collective-permute-start(bf16[2,512,256]{2,1,0:T(8,128)(2,1)S(1)} %get-tuple-element.91.high.refs_1_), channel_id=1, source_target_pairs={{0,1},{1,0},{2,3},{3,2},{4,5},{5,4},{6,7},{7,6},{8,9},{9,8},{10,11... | collective-permute-start | bytes 1572872 | tf_op jit(solution)/shard_map/ppermute | solution.py:326
  37.3 2.5 %collective-permute-start.13 = (bf16[2,512,256]{2,1,0:T(8,128)(2,1)S(1)}, bf16[2,512,256]{2,1,0:T(8,128)(2,1)S(1)}, u32[]{:S(2)}, u32[]{:S(2)}) collective-permute-start(bf16[2,512,256]{2,1,0:T(8,128)(2,1)S(1)} %get-tuple-element.90.low.refs_0_), channel_id=1, source_target_pairs={{0,1},{1,0},{2,3},{3,2},{4,5},{5,4},{6,7},{7,6},{8,9},{9,8},{10,11... | collective-permute-start | bytes 1572872 | tf_op jit(solution)/shard_map/ppermute | solution.py:326
  37.7 9.2 %copy-start.2 = (f32[32,256]{1,0:T(8,128)S(1)}, f32[32,256]{1,0:T(8,128)}, u32[]{:S(2)}) copy-start(f32[32,256]{1,0:T(8,128)} %param.19) | copy-start | bytes 98308
  37.7 9.2 %collective-permute-start.12 = (bf16[2,256,256]{2,1,0:T(8,128)(2,1)S(1)}, bf16[2,256,256]{2,1,0:T(8,128)(2,1)S(1)}, u32[]{:S(2)}, u32[]{:S(2)}) collective-permute-start(bf16[2,256,256]{2,1,0:T(8,128)(2,1)S(1)} %get-tuple-element.89), channel_id=1, source_target_pairs={{0,2},{1,3},{2,0},{3,1},{4,6},{5,7},{6,4},{7,5},{8,10},{9,11},{10,... | collective-permute-start | bytes 786440 | tf_op jit(solution)/shard_map/ppermute | solution.py:326
  39.2 18.1 %collective-permute-start.17 = (bf16[2,512,256]{2,1,0:T(8,128)(2,1)S(1)}, bf16[2,512,256]{2,1,0:T(8,128)(2,1)S(1)}, u32[]{:S(2)}, u32[]{:S(2)}) collective-permute-start(bf16[2,512,256]{2,1,0:T(8,128)(2,1)S(1)} %get-tuple-element.90.low.refs_0_), channel_id=1, source_target_pairs={{0,2},{1,3},{2,0},{3,1},{4,6},{5,7},{6,4},{7,5},{8,10},{9,11},{10,... | collective-permute-start | bytes 1572872 | tf_op jit(solution)/shard_map/ppermute | solution.py:326
  46.8 2.1 %collective-permute-start.15 = (bf16[2,256,256]{2,1,0:T(8,128)(2,1)S(1)}, bf16[2,256,256]{2,1,0:T(8,128)(2,1)S(1)}, u32[]{:S(2)}, u32[]{:S(2)}) collective-permute-start(bf16[2,256,256]{2,1,0:T(8,128)(2,1)S(1)} %collective-permute-done.12.picked.refs_5_), channel_id=1, source_target_pairs={{0,1},{1,0},{2,3},{3,2},{4,5},{5,4},{6,7},{7,6},{8,9},{9,8},{10,11... | collective-permute-start | bytes 786440 | tf_op jit(solution)/shard_map/ppermute | solution.py:326
  46.8 4.8 %collective-permute-start.16 = (f32[2,32,256]{2,1,0:T(8,128)S(1)}, f32[2,32,256]{2,1,0:T(8,128)S(1)}, u32[]{:S(2)}, u32[]{:S(2)}) collective-permute-start(f32[2,32,256]{2,1,0:T(8,128)S(1)} %pad_maximum_fusion.2), channel_id=1, source_target_pairs={{0,4},{4,0},{8,12},{12,8},{16,20},{20,16},{24,28},{28,24},{1,5},{5... | collective-permute-start | bytes 196616 | tf_op jit(solution)/shard_map/ppermute | solution.py:326
  48.4 8.9 %collective-permute-start.18 = (bf16[2,256,256]{2,1,0:T(8,128)(2,1)S(1)}, bf16[2,256,256]{2,1,0:T(8,128)(2,1)S(1)}, u32[]{:S(2)}, u32[]{:S(2)}) collective-permute-start(bf16[2,256,256]{2,1,0:T(8,128)(2,1)S(1)} %collective-permute-done.12.picked.refs_5_), channel_id=1, source_target_pairs={{0,4},{4,0},{8,12},{12,8},{16,20},{20,16},{24,28},{28,24},{1,5},{5... | collective-permute-start | bytes 786440 | tf_op jit(solution)/shard_map/ppermute | solution.py:326
  51.7 5.6 %collective-permute-start.19 = (f32[4,32,256]{2,1,0:T(8,128)S(1)}, f32[4,32,256]{2,1,0:T(8,128)S(1)}, u32[]{:S(2)}, u32[]{:S(2)}) collective-permute-start(f32[4,32,256]{2,1,0:T(8,128)S(1)} %pad_maximum_fusion.1), channel_id=1, source_target_pairs={{0,8},{4,12},{8,0},{12,4},{16,24},{20,28},{24,16},{28,20},{1,9},{5... | collective-permute-start | bytes 393224 | tf_op jit(solution)/shard_map/ppermute | solution.py:326
  57.3 2.3 %collective-permute-start.20 = (bf16[2,512,256]{2,1,0:T(8,128)(2,1)S(1)}, bf16[2,512,256]{2,1,0:T(8,128)(2,1)S(1)}, u32[]{:S(2)}, u32[]{:S(2)}) collective-permute-start(bf16[2,512,256]{2,1,0:T(8,128)(2,1)S(1)} %collective-permute-done.17.far.refs_4_), channel_id=1, source_target_pairs={{0,1},{1,0},{2,3},{3,2},{4,5},{5,4},{6,7},{7,6},{8,9},{9,8},{10,11... | collective-permute-start | bytes 1572872 | tf_op jit(solution)/shard_map/ppermute | solution.py:326
  57.3 2.3 %collective-permute-start.21 = (bf16[2,256,256]{2,1,0:T(8,128)(2,1)S(1)}, bf16[2,256,256]{2,1,0:T(8,128)(2,1)S(1)}, u32[]{:S(2)}, u32[]{:S(2)}) collective-permute-start(bf16[2,256,256]{2,1,0:T(8,128)(2,1)S(1)} %collective-permute-done.18.rest.refs_6_), channel_id=1, source_target_pairs={{0,1},{1,0},{2,3},{3,2},{4,5},{5,4},{6,7},{7,6},{8,9},{9,8},{10,11... | collective-permute-start | bytes 786440 | tf_op jit(solution)/shard_map/ppermute | solution.py:326
  69.4 2.7 %collective-permute-start.22 = (bf16[4,512,256]{2,1,0:T(8,128)(2,1)S(1)}, bf16[4,512,256]{2,1,0:T(8,128)(2,1)S(1)}, u32[]{:S(2)}, u32[]{:S(2)}) collective-permute-start(bf16[4,512,256]{2,1,0:T(8,128)(2,1)S(1)} %get-tuple-element.113.grad.one.refs_10_), channel_id=1, source_target_pairs={{0,1},{1,0},{2,3},{3,2},{4,5},{5,4},{6,7},{7,6},{8,9},{9,8},{10,11... | collective-permute-start | bytes 3145736 | tf_op jit(solution)/shard_map/ppermute | solution.py:326
  74.2 10.3 %collective-permute-start.24 = (bf16[2,256,256]{2,1,0:T(8,128)(2,1)S(1)}, bf16[2,256,256]{2,1,0:T(8,128)(2,1)S(1)}, u32[]{:S(2)}, u32[]{:S(2)}) collective-permute-start(bf16[2,256,256]{2,1,0:T(8,128)(2,1)S(1)} %shard_map.169), channel_id=1, source_target_pairs={{0,2},{1,3},{2,0},{3,1},{4,6},{5,7},{6,4},{7,5},{8,10},{9,11},{10,... | collective-permute-start | bytes 786440 | tf_op jit(solution)/shard_map/ppermute | solution.py:326
  84.6 14.4 %collective-permute-start.26 = (bf16[3,3,512,256]{3,2,1,0:T(8,128)(2,1)S(1)}, bf16[3,3,512,256]{3,2,1,0:T(8,128)(2,1)S(1)}, u32[]{:S(2)}, u32[]{:S(2)}) collective-permute-start(bf16[3,3,512,256]{3,2,1,0:T(8,128)(2,1)S(1)} %get-tuple-element.120.refs_8_.weight), channel_id=1, source_target_pairs={{0,1},{1,0},{2,3},{3,2},{4,5},{5,4},{6,7},{7,6},{8,9},{9,8},{10,11... | collective-permute-start | bytes 7077896 | tf_op jit(solution)/shard_map/ppermute | solution.py:326
  84.6 14.3 %collective-permute-start.23 = (bf16[2,512,256]{2,1,0:T(8,128)(2,1)S(1)}, bf16[2,512,256]{2,1,0:T(8,128)(2,1)S(1)}, u32[]{:S(2)}, u32[]{:S(2)}) collective-permute-start(bf16[2,512,256]{2,1,0:T(8,128)(2,1)S(1)} %shard_map.168), channel_id=1, source_target_pairs={{0,2},{1,3},{2,0},{3,1},{4,6},{5,7},{6,4},{7,5},{8,10},{9,11},{10,... | collective-permute-start | bytes 1572872 | tf_op jit(solution)/shard_map/ppermute | solution.py:326
  85.2 12.5 %collective-permute-start.25 = (bf16[2,256,256]{2,1,0:T(8,128)(2,1)S(1)}, bf16[2,256,256]{2,1,0:T(8,128)(2,1)S(1)}, u32[]{:S(2)}, u32[]{:S(2)}) collective-permute-start(bf16[2,256,256]{2,1,0:T(8,128)(2,1)S(1)} %collective-permute-done.24.picked), channel_id=1, source_target_pairs={{0,4},{4,0},{8,12},{12,8},{16,20},{20,16},{24,28},{28,24},{1,5},{5... | collective-permute-start | bytes 786440 | tf_op jit(solution)/shard_map/ppermute | solution.py:326
  100.8 1.6 %collective-permute-start.27 = (bf16[4,96,256]{2,1,0:T(8,128)(2,1)S(1)}, bf16[4,96,256]{2,1,0:T(8,128)(2,1)S(1)}, u32[]{:S(2)}, u32[]{:S(2)}) collective-permute-start(bf16[4,96,256]{2,1,0:T(8,128)(2,1)S(1)} %get-tuple-element.125.one), channel_id=1, source_target_pairs={{0,1},{1,0},{2,3},{3,2},{4,5},{5,4},{6,7},{7,6},{8,9},{9,8},{10,11... | collective-permute-start | bytes 589832 | tf_op jit(solution)/shard_map/ppermute | solution.py:326
  104.0 6.3 %collective-permute-start.28 = (f32[4,64,128]{2,1,0:T(8,128)S(1)}, f32[4,64,128]{2,1,0:T(8,128)S(1)}, u32[]{:S(2)}, u32[]{:S(2)}) collective-permute-start(f32[4,64,128]{2,1,0:T(8,128)S(1)} %get-tuple-element.130), channel_id=1, source_target_pairs={{0,2},{1,3},{2,0},{3,1},{4,6},{5,7},{6,4},{7,5},{8,10},{9,11},{10,... | collective-permute-start | bytes 393224 | tf_op jit(solution)/shard_map/ppermute | solution.py:326
  (1 other events, 0.7 us)

commit v5 on v4

--- a/solution.py
+++ b/solution.py
@@ -366,50 +366,6 @@
     return jnp.sum(value, axis=0, keepdims=True)
 
 
-def taps(mel, mel_count):
-    return [b for b in range(3) if 0 <= mel + b - 1 < mel_count]
-
-
-def convolve(fields, weights, lower, middle, upper, total, add):
-    mel_count = middle.shape[0]
-    for m in range(mel_count):
-        for a in range(3):
-            acc = None
-            for field, weight in zip(fields, weights):
-                for b in taps(m, mel_count):
-                    part = jnp.dot(field(m + b - 1), weight(a, b), preferred_element_type=f32)
-                    acc = part if acc is None else acc + part
-            if a == 0:
-                lower[m, TILE : TILE + total] = acc
-            elif a == 1:
-                middle[m] = middle[m] + acc if add else acc
-            else:
-                upper[m, TILE : TILE + total] = acc
-
-
-def convolve_back(fields, weights, lower, middle, upper, total):
-    mel_count = middle.shape[0]
-    for n in range(mel_count):
-        for a in range(3):
-            acc = None
-            for field, weight in zip(fields, weights):
-                for b in range(3):
-                    if 0 <= n - b + 1 < mel_count:
-                        part = lax.dot_general(
-                            field(n - b + 1),
-                            weight(a, b),
-                            (((1,), (1,)), ((), ())),
-                            preferred_element_type=f32,
-                        )
-                        acc = part if acc is None else acc + part
-            if a == 2:
-                lower[n, TILE : TILE + total] = acc
-            elif a == 1:
-                middle[n] = acc
-            else:
-                upper[n, TILE : TILE + total] = acc
-
-
 def joined(lower, middle, upper, m, at, before, after):
     low = lower[m, pl.ds(at, ROWS + 2 * TILE)]
     high = upper[m, pl.ds(at, ROWS + 2 * TILE)]
@@ -468,30 +424,82 @@
     )
 
 
-def first_kernel(starts, *refs):
-    blocks, (weight, scales) = refs[:8], refs[8:10]
-    low, high, picked, field, middle, keep, stats = refs[10:17]
-    lower, upper = refs[17:]
-    mel_count, total, width = field.shape
-    out_width = middle.shape[2]
-    place, column = lax.axis_index("tm"), lax.axis_index("chan")
+def settle(blocks, field, keep):
+    mel_count = field.shape[0]
+    place = lax.axis_index("tm")
     frames, lanes = blocks[0].shape[2], blocks[0].shape[3]
-    clear_edges(lower, upper, total)
     for i, block in enumerate(blocks):
-        core, row, side = i // 4, (i // 2) % 2, i % 2
-        to_columns = pl.ds(pl.multiple_of((column ^ (2 * row + core)) * lanes, lanes), lanes)
+        row, side = i // 2, i % 2
+        to_columns = slice(row * lanes, (row + 1) * lanes)
         for k in range(block.shape[0]):
             to_rows = pl.ds(pl.multiple_of((place ^ (2 * k + side)) * frames, frames), frames)
             for m in range(mel_count):
                 rows = block[k, m]
-                if m == 0 and i < 2:
+                if m == 0 and row == 0 and keep is not None:
                     keep[to_rows] = (rows.astype(f32) < ABSENT / 2).astype(f32)
                 field[m, to_rows, to_columns] = jnp.where(
                     rows < ABSENT / 2, rows, jnp.zeros_like(rows)
                 )
-    convolve(
-        [lambda m: field[m]], [lambda a, b: weight[a, b]], lower, middle, upper, total, False
-    )
+
+
+def products(field, weight, bits, targets, sources=None):
+    mel_count, total, width = field.shape
+    lanes = width // len(bits)
+    groups = group_starts(bits, lanes)
+    for m in range(mel_count):
+        for a in range(3):
+            target, at = targets[a]
+            acc = None
+            for b in range(3):
+                if 0 <= m + b - 1 < mel_count:
+                    wing = jnp.concatenate([weight[a, b, pl.ds(g, lanes)] for g in groups])
+                    part = jnp.dot(field[m + b - 1], wing, preferred_element_type=f32)
+                    acc = part if acc is None else acc + part
+            if sources is not None:
+                acc = acc + sources[a][m, at : at + total]
+            target[m, at : at + total] = acc
+
+
+def column_kernel(*refs):
+    blocks, weight, (field, keep, lower, middle, upper) = refs[:4], refs[4], refs[5:]
+    clear_edges(lower, upper, middle.shape[1])
+    settle(blocks, field, keep)
+    products(field, weight, (0, 2), ((lower, TILE), (middle, 0), (upper, TILE)))
+
+
+def column_part(blocks, weight, total):
+    _, mel_count, frames, lanes = blocks[0].shape
+    out_width = weight.shape[3]
+    padded = (mel_count, total + 2 * TILE, out_width)
+    return call(
+        column_kernel,
+        (*blocks, weight),
+        [whole_spec()] * 5,
+        [
+            ((mel_count, total, 2 * lanes), bf16),
+            ((total, LANES), f32),
+            (padded, f32),
+            ((mel_count, total, out_width), f32),
+            (padded, f32),
+        ],
+        [whole_spec()] * 5,
+        [],
+        0,
+        8,
+    )
+
+
+def first_kernel(starts, *refs):
+    blocks, (weight, scales, keep), sources = refs[:4], refs[4:7], refs[7:10]
+    low, high, picked, field, middle, stats = refs[10:16]
+    lower, upper = refs[16:]
+    mel_count, total, _ = field.shape
+    out_width = middle.shape[2]
+    place = lax.axis_index("tm")
+    clear_edges(lower, upper, total)
+    settle(blocks, field, None)
+    targets = ((lower, TILE), (middle, 0), (upper, TILE))
+    products(field, weight, (1, 3), targets, sources)
 
     def combine(at, sums):
         before, after = same_clip(starts, at, (ROWS, out_width), total)
@@ -533,25 +541,24 @@
         picked[m] = high[m, pl.ds(pl.multiple_of((place % 2) * reach, reach), reach)]
 
 
-def first_block(blocks, weight, scales, starts, total):
+def first_block(blocks, weight, scales, keep, sources, starts, total):
     _, mel_count, frames, lanes = blocks[0].shape
-    width, out_width = weight.shape[2], weight.shape[3]
+    out_width = weight.shape[3]
     padded = (mel_count, total + 2 * TILE, out_width)
     half = (mel_count // 2, total, out_width)
     return call(
         first_kernel,
-        (starts, *blocks, weight, scales),
+        (starts, *blocks, weight, scales, keep, *sources),
         [scalar_spec()] + [whole_spec()] * 10,
         [
             (half, bf16),
             (half, bf16),
             ((mel_count // 2, total // 2, out_width), bf16),
-            ((mel_count, total, width), bf16),
+            ((mel_count, total, 2 * lanes), bf16),
             ((mel_count, total, out_width), f32),
-            ((total, LANES), f32),
             ((TILE, out_width), f32),
         ],
-        [whole_spec()] * 7,
+        [whole_spec()] * 6,
         [pltpu.VMEM(padded, f32), pltpu.VMEM(padded, f32)],
         0,
         16,
@@ -587,33 +594,35 @@
     )[0]
 
 
-def gather_taps(parts, groups, weight, lower, middle, upper, outputs, first=None):
-    total, width = middle.shape[1], middle.shape[2]
-    for k, m in enumerate(outputs):
+def group_sums(fields, weight, starts, targets, sources=None):
+    mel_count, (_, total, width) = len(fields[0]), targets[1][0].shape
+    for m in range(mel_count):
         for a in range(3):
             acc = None
-            for mels, arrays in parts:
-                for j, n in enumerate(mels):
-                    b = n - m + 1
-                    if 0 <= b < 3:
-                        for array, start in zip(arrays, groups):
-                            piece = jnp.dot(
-                                array[j],
-                                weight[a, b, pl.ds(start, width)],
-                                preferred_element_type=f32,
-                            )
-                            acc = piece if acc is None else acc + piece
-            target, shift = ((lower, TILE), (middle, 0), (upper, TILE))[a]
-            rows = total
-            if first is not None:
-                rows = total // 2
-                empty = pl.ds(pl.multiple_of(total // 2 - first + shift, TILE), rows)
-                target[k, empty] = jnp.zeros((rows, width), f32)
-                target[k, pl.ds(pl.multiple_of(first + shift, TILE), rows)] = acc
-            elif acc is None:
-                target[k, shift : shift + rows] = jnp.zeros((rows, width), f32)
-            else:
-                target[k, shift : shift + rows] = acc
+            for mels, start in zip(fields, starts):
+                for b in range(3):
+                    if 0 <= m + b - 1 < mel_count:
+                        part = jnp.dot(
+                            mels[m + b - 1][...],
+                            weight[a, b, pl.ds(start, width)],
+                            preferred_element_type=f32,
+                        )
+                        acc = part if acc is None else acc + part
+            if sources is not None:
+                acc = acc + sources[a, m]
+            target, at = targets[a]
+            target[m, at : at + total] = acc
+
+
+def join_halves(pair, joint, sems):
+    side = lax.axis_index("tm") % 2
+    half = pair[0].shape[1]
+    copies = []
+    for i, (part, begin) in enumerate(zip(pair, (side, 1 - side))):
+        rows = pl.ds(pl.multiple_of(begin * half, half), half)
+        copies.append(pltpu.make_async_copy(part, joint.at[:, rows], sems.at[i]))
+        copies[-1].start()
+    return copies
 
 
 def group_starts(bits, width):
@@ -621,71 +630,49 @@
     return [pl.multiple_of((column ^ bit) * width, width) for bit in bits]
 
 
-def near_kernel(starts, low, high, low_two, high_two, weight, out, lower, upper):
-    mel_count, total, width = out.shape
-    half = mel_count // 2
-    clear_edges(lower, upper, total)
-    parts = [(range(half), (low, low_two)), (range(half, mel_count), (high, high_two))]
-    groups = group_starts((0, 1), width)
-    gather_taps(parts, groups, weight, lower, out, upper, range(mel_count))
-
-    def combine(at, carry):
-        before, after = same_clip(starts, at, (ROWS, width), total)
-        for m in range(mel_count):
-            out[m, pl.ds(at, ROWS)] = joined(lower, out, upper, m, at, before, after)
-        return carry
-
-    by_rows(total, combine, 0)
-
-
-def near_part(low, high, low_two, high_two, weight, starts):
+def near_kernel(low, high, low_two, high_two, weight, sums):
+    half, _, width = low.shape
+    fields = [
+        [a.at[k] for a in pair for k in range(half)] for pair in ((low, high), (low_two, high_two))
+    ]
+    targets = [(sums.at[a], 0) for a in range(3)]
+    group_sums(fields, weight, group_starts((0, 1), width), targets)
+
+
+def near_part(low, high, low_two, high_two, weight):
     half, total, width = low.shape
-    padded = (2 * half, total + 2 * TILE, width)
     return call(
         near_kernel,
-        (starts, low, high, low_two, high_two, weight),
-        [scalar_spec()] + [whole_spec()] * 5,
-        [((2 * half, total, width), f32)],
+        (low, high, low_two, high_two, weight),
+        [whole_spec()] * 5,
+        [((3, 2 * half, total, width), f32)],
         [whole_spec()],
-        [pltpu.VMEM(padded, f32)] * 2,
+        [],
         0,
-        14,
+        6,
     )[0]
 
 
-def early_kernel(starts, picked, picked_two, weight, early, lower, upper):
-    outputs, total, width = early.shape
-    mel_count = picked.shape[0] + outputs - 1
-    half = mel_count - picked.shape[0]
-    begin = (lax.axis_index("tm") % 2) * (total // 2)
-    clear_edges(lower, upper, total)
-    parts = [(range(half, mel_count), (picked, picked_two))]
-    groups = group_starts((2, 3), width)
-    mels = range(half - 1, mel_count)
-    gather_taps(parts, groups, weight, lower, early, upper, mels, begin)
-
-    def combine(at, carry):
-        before, after = same_clip(starts, at, (ROWS, width), total)
-        for k in range(outputs):
-            early[k, pl.ds(at, ROWS)] = joined(lower, early, upper, k, at, before, after)
-        return carry
-
-    by_rows(total, combine, 0)
-
-
-def early_part(picked, picked_two, weight, starts):
-    half, rows, width = picked.shape
-    total = 2 * rows
-    shape = (half + 1, total, width)
+def far_kernel(far, picked, rest, weight, near, sums, joint, sems):
+    half, _, width = far.shape
+    copies = join_halves((picked, rest), joint, sems)
+    for copy in copies:
+        copy.wait()
+    fields = [[a.at[k] for a in (far, joint) for k in range(half)]]
+    targets = [(sums.at[a], 0) for a in range(3)]
+    group_sums(fields, weight, group_starts((2,), width), targets, near)
+
+
+def far_part(far, picked, rest, weight, near):
     return call(
-        early_kernel,
-        (starts, picked, picked_two, weight),
-        [scalar_spec()] + [whole_spec()] * 3,
-        [(shape, f32)],
+        far_kernel,
+        (far, picked, rest, weight, near),
+        [whole_spec()] * 5,
+        [(near.shape, f32)],
         [whole_spec()],
-        [pltpu.VMEM((half + 1, total + 2 * TILE, width), f32)] * 2,
+        [pltpu.VMEM(far.shape, bf16), pltpu.SemaphoreType.DMA((2,))],
         0,
-        12,
+        8,
     )[0]
 
 
@@ -706,10 +693,10 @@
 
 
 def second_kernel(
-    starts, near, early, far, rest, far_two, rest_two, weight, keep, scales, *refs
+    starts, sums, far_two, picked_two, rest_two, weight, keep, scales, *refs
 ):
-    cotangents, (readout, grad, gain_grad, shift_grad) = refs[:-15], refs[-15:-11]
-    middle, slope, lower, upper, late, late_lower, late_upper, hold, wide, full, sems = refs[-11:]
+    cotangents, (readout, grad, gain_grad, shift_grad) = refs[:-14], refs[-14:-10]
+    middle, slope, lower, upper, joint, hold, wide, full, sems, joint_sems = refs[-10:]
     mel_count, total, width = middle.shape
     half = mel_count // 2
     place = lax.axis_index("tm")
@@ -730,15 +717,13 @@
     for copy in copies:
         copy.start()
 
-    groups = group_starts((2, 3), width)
+    halves = join_halves((picked_two, rest_two), joint, joint_sems)
     clear_edges(lower, upper, total)
-    clear_edges(late_lower, late_upper, total)
-    parts = [(range(half), (far, far_two))]
-    gather_taps(parts, groups, weight, lower, middle, upper, range(half + 1))
-    parts = [(range(half, mel_count), (rest, rest_two))]
-    begin = (1 - place % 2) * (total // 2)
-    outputs = range(half - 1, mel_count)
-    gather_taps(parts, groups, weight, late_lower, late, late_upper, outputs, begin)
+    for copy in halves:
+        copy.wait()
+    fields = [[a.at[k] for a in (far_two, joint) for k in range(half)]]
+    targets = ((lower, TILE), (middle, 0), (upper, TILE))
+    group_sums(fields, weight, group_starts((3,), width), targets, sums)
     blank = jnp.zeros((TILE, width), f32)
 
     def combine(at, sums):
@@ -747,13 +732,7 @@
         first, second, num = sums
         num = num + fold(mask)
         for m in range(mel_count):
-            rows = near[m, pl.ds(at, ROWS)]
-            if m <= half:
-                rows = rows + joined(lower, middle, upper, m, at, before, after)
-            if m in outputs:
-                k = m - outputs[0]
-                new = joined(late_lower, late, late_upper, k, at, before, after)
-                rows = rows + (early[k, pl.ds(at, ROWS)] + new)
+            rows = joined(lower, middle, upper, m, at, before, after)
             middle[m, pl.ds(at, ROWS)] = rows
             kept = rows * mask
             first = first + fold(kept)
@@ -841,15 +820,14 @@
     by_rows(total, finish, 0)
 
 
-def second_block(near, early, arrays, weight, keep, scales, starts, cotangents, own):
-    mel_count, total, width = near.shape
-    outputs = early.shape[0]
+def second_block(sums, arrays, weight, keep, scales, starts, cotangents, own):
+    _, mel_count, total, width = sums.shape
     padded = (mel_count, total + 2 * TILE, width)
     full = (mel_count, total, width)
     return call(
         second_kernel,
-        (starts, near, early, *arrays, weight, keep, scales, *cotangents),
-        [scalar_spec()] + [whole_spec()] * (len(arrays) + 5) + [place_spec()] * len(cotangents),
+        (starts, sums, *arrays, weight, keep, scales, *cotangents),
+        [scalar_spec()] + [whole_spec()] * (len(arrays) + 4) + [place_spec()] * len(cotangents),
         [((own, width), f32), (full, bf16), ((1, width), f32), ((1, width), f32)],
         [whole_spec()] * 4,
         [
@@ -857,16 +835,15 @@
             pltpu.VMEM(full, f32),
             pltpu.VMEM(padded, f32),
             pltpu.VMEM(padded, f32),
-            pltpu.VMEM((outputs, total, width), f32),
-            pltpu.VMEM((outputs, total + 2 * TILE, width), f32),
-            pltpu.VMEM((outputs, total + 2 * TILE, width), f32),
+            pltpu.VMEM(arrays[0].shape, bf16),
             pltpu.VMEM((width // LANES, total, LANES), f32),
             pltpu.VMEM((total // 2, width), f32),
             pltpu.VMEM((total // 2, width), f32),
             pltpu.SemaphoreType.DMA((sum(part.shape[0] for part in cotangents),)),
+            pltpu.SemaphoreType.DMA((2,)),
         ],
         0,
-        26,
+        20,
     )
 
 
@@ -934,10 +911,10 @@
         ],
         0,
         14,
-    )[0]
-
-
-def norm_kernel(mine, other, picked, rest, slope, pre, stats, scales, keep, *refs):
+    )
+
+
+def norm_kernel(mine, low, picked, rest, slope, pre, stats, scales, keep, *refs):
     grad, window, gain_grad, shift_grad, padded = refs
     mel_count, total, width = mine.shape
     center, inverse, pixels = stats[0:1], stats[1:2], stats[2:3]
@@ -964,7 +941,7 @@
         return slopes
 
     side = place % 2
-    sums = by_rows(total, add(other, 0, range(half)), (blank, blank))
+    sums = by_rows(total, add(low, 0, range(half)), (blank, blank))
     upper = range(half, mel_count)
     parts = []
     for field, base in ((picked, side), (rest, 1 - side)):
@@ -996,12 +973,12 @@
         window[m] = padded[m, pl.ds(pl.multiple_of(place * frames, frames), reach)]
 
 
-def norm_back_first(mine, other, picked, rest, slope, pre, stats, scales, keep, frames):
+def norm_back_first(mine, low, picked, rest, slope, pre, stats, scales, keep, frames):
     mel_count, total, width = mine.shape
     edge = 16
     return call(
         norm_kernel,
-        (mine, other, picked, rest, slope, pre, stats, scales, keep),
+        (mine, low, picked, rest, slope, pre, stats, scales, keep),
         [whole_spec()] * 9,
         [
             ((mel_count, total, width), bf16),
@@ -1058,9 +1035,9 @@
 
 
 def weight_kernel(layout, halves, *refs):
-    count = len(refs) - 6
+    count = len(refs) - 7
     fields, grad, steps = list(refs[:count]), refs[count], refs[count + 1]
-    out, results, joint, sems = refs[count + 2 :]
+    out, results, joint, sems, move_sems = refs[count + 2 :]
     mel_count, total, out_width = grad.shape
     width = results.shape[2]
     side = lax.axis_index("tm") % 2
@@ -1070,15 +1047,15 @@
         for index, begin in zip(pair, (side, 1 - side)):
             rows = pl.ds(pl.multiple_of(begin * (total // 2), total // 2), total // 2)
             moves.append(
-                pltpu.make_async_copy(fields[index], joint.at[i, :, rows], sems.at[2 + len(moves)])
+                pltpu.make_async_copy(fields[index], joint.at[i, :, rows], move_sems.at[len(moves)])
             )
             moves[-1].start()
         fields.append(joint.at[i])
-    copies = [None, None]
-    for i, (place, pieces) in enumerate(layout):
+    copies = [[], []]
+    for i, (places, pieces) in enumerate(layout):
         slot = i % 2
-        if copies[slot] is not None:
-            copies[slot].wait()
+        for copy in copies[slot]:
+            copy.wait()
         if any(piece[0] >= count for piece in pieces):
             while moves:
                 moves.pop().wait()
@@ -1097,17 +1074,20 @@
                         )
                         acc = part if acc is None else acc + part
                 results[slot, 3 * a + b] = acc
-        if place is None:
-            start = i * width
-        else:
-            start = pl.multiple_of((column ^ place) * width, width)
-        copies[slot] = pltpu.make_async_copy(
-            results.at[slot], out.at[:, pl.ds(start, width)], sems.at[slot]
-        )
-        copies[slot].start()
-    for copy in copies:
-        if copy is not None:
-            copy.wait()
+        each = width // len(places)
+        copies[slot] = []
+        for j, bit in enumerate(places):
+            start = pl.multiple_of((column ^ bit) * each, each)
+            copies[slot].append(
+                pltpu.make_async_copy(
+                    results.at[slot, :, j * each : (j + 1) * each],
+                    out.at[:, pl.ds(start, each)],
+                    sems.at[slot, j],
+                )
+            )
+            copies[slot][-1].start()
+    for copy in copies[0] + copies[1]:
+        copy.wait()
 
 
 def weight_back(layout, halves, fields, grad, steps, in_width):
@@ -1123,7 +1103,8 @@
         [
             pltpu.VMEM((2, 9, width, out_width), f32),
             pltpu.VMEM(joint, bf16),
-            pltpu.SemaphoreType.DMA((2 + 2 * len(halves),)),
+            pltpu.SemaphoreType.DMA((2, 2)),
+            pltpu.SemaphoreType.DMA((max(2 * len(halves), 1),)),
         ],
         0,
         12,
@@ -1246,35 +1227,38 @@
     near[3], clip_starts, conv1_weight, scales, cotangents = lax.optimization_barrier(
         (near[3], clip_starts, conv1_weight, scales, cotangents)
     )
-    blocks = near + [swap(block, "chan", 1) for block in near]
+    others = [swap(block, "chan", 1) for block in near]
+    column, keep, *sources = column_part(near, conv1_weight, total)
+    column, others = lax.optimization_barrier((column, others))
     other_conv2 = swap(conv2_weight, "chan", 1)
-    blocks, other_conv2 = lax.optimization_barrier((blocks, other_conv2))
-
-    low, high, picked, field, pre, keep, stats = first_block(
-        blocks, conv1_weight, scales, clip_starts, total
-    )
+    others, other_conv2 = lax.optimization_barrier((others, other_conv2))
+
+    low, high, picked, other_column, pre, stats = first_block(
+        others, conv1_weight, scales, keep, sources, clip_starts, total
+    )
+    fields1 = (column, other_column)
 
     far_picked = swap(picked, "chan", 2)
     far = swap(low, "chan", 2)
     far_rest = swap(far_picked, "tm", 1)
 
     low_two, high_two = swap(low, "chan", 1), swap(high, "chan", 1)
-    near = near_part(low, high, low_two, high_two, conv2_weight, clip_starts)
+    near = near_part(low, high, low_two, high_two, conv2_weight)
     far_picked, near, cotangents = lax.optimization_barrier((far_picked, near, cotangents))
     picked_two = swap(far_picked, "chan", 1)
     for bit in bits[1:-1]:
         cotangents.append(swap(jnp.concatenate(cotangents), "tm", bit))
-    early = early_part(far_picked, picked_two, conv2_weight, clip_starts)
-    early, pre, cotangents = lax.optimization_barrier((early, pre, cotangents))
+    picked_two, pre, cotangents = lax.optimization_barrier((picked_two, pre, cotangents))
     cotangents.append(swap(jnp.concatenate(cotangents), "tm", bits[-1]))
     slope = first_slope(pre, stats, scales, keep)
     far, far_rest, slope, cotangents = lax.optimization_barrier((far, far_rest, slope, cotangents))
     far_two, rest_two = swap(far, "chan", 1), swap(far_rest, "chan", 1)
+    sums = far_part(far, far_picked, far_rest, conv2_weight, near)
+    far_two, rest_two, sums = lax.optimization_barrier((far_two, rest_two, sums))
 
     readout, grad2, gain2_grad, shift2_grad = second_block(
-        near,
-        early,
-        (far, far_rest, far_two, rest_two),
+        sums,
+        (far_two, picked_two, rest_two),
         conv2_weight,
         keep,
         scales,
@@ -1293,22 +1277,22 @@
         weight_two=other_conv2,
         starts=clip_starts,
     )
-    came_picked = swap(back(2, (2, 3), True, kind=bf16), "chan", 2)
-    away_low = back(2, (0, 1), False, kind=bf16)
+    came_picked = swap(back(2, (2, 3), True, kind=bf16)[0], "chan", 2)
+    (away_low,) = back(2, (0, 1), False, kind=bf16)
     came_low = swap(away_low, "chan", 2)
 
     away_low, other_conv2 = lax.optimization_barrier((away_low, other_conv2))
-    mine = back(0, (0, 1, 2, 3), False, weight_two=other_conv2, kind=f32)
+    (mine,) = back(0, (0, 1, 2, 3), False, weight_two=other_conv2, kind=f32)
     came_picked, mine, conv1_weight = lax.optimization_barrier((came_picked, mine, conv1_weight))
     came_rest = swap(came_picked, "tm", 1)
     other_conv1 = swap(conv1_weight, "chan", 1)
     fields = (low, high, low_two, high_two)
     fields += (far, far_picked, far_rest, far_two, picked_two, rest_two)
     layout = [
-        (0, [(0, 0, 0), (0, 1, 0), (1, 0, 0), (1, 1, 0)]),
-        (1, [(2, 0, 0), (2, 1, 0), (3, 0, 0), (3, 1, 0)]),
-        (2, [(4, 0, 0), (4, 1, 0), (10, 0, 0), (10, 1, 0)]),
-        (3, [(7, 0, 0), (7, 1, 0), (11, 0, 0), (11, 1, 0)]),
+        ((0,), [(0, 0, 0), (0, 1, 0), (1, 0, 0), (1, 1, 0)]),
+        ((1,), [(2, 0, 0), (2, 1, 0), (3, 0, 0), (3, 1, 0)]),
+        ((2,), [(4, 0, 0), (4, 1, 0), (10, 0, 0), (10, 1, 0)]),
+        ((3,), [(7, 0, 0), (7, 1, 0), (11, 0, 0), (11, 1, 0)]),
     ]
     weight2_grad = weight_back(
         layout, ((5, 6), (8, 9)), fields, grad2, steps2, conv2_weight.shape[2]
@@ -1327,11 +1311,8 @@
         window, window_near, conv1_weight, other_conv1, clip_starts, frames, lanes
     )
     input_came = swap(input_away, "chan", 2)
-    layout = [
-        (None, [(0, m, lane) for m in range(mel_count)])
-        for lane in range(0, field.shape[2], 256)
-    ]
-    weight1_grad = weight_back(layout, (), (field,), grad1, steps1, field.shape[2])
+    layout = [(bits, [(i, m, 0) for m in range(mel_count)]) for i, bits in enumerate(((0, 2), (1, 3)))]
+    weight1_grad = weight_back(layout, (), fields1, grad1, steps1, conv1_weight.shape[2])
     input_came, weight1_grad = lax.optimization_barrier((input_came, weight1_grad))
     return (
         readout,

time: 111 us -> 109 us (0.982)
  Pallas kernels: 61.9 us -> 59.3 us
    pallas_call x16 -> x17, Pallas kernels: 61.9 us -> 59.3 us  [call(): pl.pallas_call(body, out_shape=tuple((jax.ShapeDtypeStruct(s, d) for s, d...]
    unnamed x8 -> x10, local copies, waits for them, and re-layouts: 2.32 us -> 2.33 us
  transfers between devices with their start and end apart: 29 -> 29, of which waited for: 16 -> 12; matrix products, arithmetic and copies ran while one was open for 2% -> 2% of each run, Pallas kernels for 35% -> 37%
where the time goes in v5:
time: 109 us
  Pallas kernels  59.3 us (54%)
  starting transfers between devices  22.9 us (21%)
  waiting for transfers between devices  21.4 us (20%)
  other arithmetic  2.37 us (2%)
  local copies, waits for them, and re-layouts  2.33 us (2%)
    pallas_call x17, Pallas kernels, call(): pl.pallas_call(body, out_shape=tuple((jax.ShapeDtypeStruct(s, d) for s, d...  59.3 us
    ppermute x28, waiting for transfers between devices, swap(): return lax.ppermute(shard, axis, [(i, i ^ bit) for i in range(count)])  21.1 us
    ppermute x28, starting transfers between devices, swap(): return lax.ppermute(shard, axis, [(i, i ^ bit) for i in range(count)])  20.4 us
    ppermute x1, starting transfers between devices, swap_both(): return lax.ppermute(shard, (first, second), pairs)  2.51 us
    unnamed x10, local copies, waits for them, and re-layouts  2.33 us
  transfers between devices with their start and end apart: 29, of which 12 were waited for; matrix products, arithmetic and copies ran while one was open for 2% of the time, Pallas kernels for 37%

profile of v5, /device:TPU:0, one launch (start us, length us, event | category | flops | bytes accessed | tf_op | source)
XLA Modules:
  0.0 109.2 jit_solution(1045615231479838363)
XLA Ops:
  2.7 3.7 %collective-permute-start.1 = (bf16[4,64,128]{2,1,0:T(8,128)(2,1)S(1)}, bf16[4,64,128]{2,1,0:T(8,128)(2,1)S(1)}, u32[]{:S(2)}, u32[]{:S(2)}) collective-permute-start(bf16[4,64,128]{2,1,0:T(8,128)(2,1)S(1)} %get-tuple-element.157), channel_id=1, source_target_pairs={{0,16},{4,20},{8,24},{12,28},{16,0},{20,4},{24,8},{28,12},{1,17},{... | collective-permute-start | bytes 196616 | tf_op jit(solution)/shard_map/ppermute | solution.py:326
  6.4 1.6 %collective-permute-start = (bf16[4,64,128]{2,1,0:T(8,128)(2,1)S(1)}, bf16[4,64,128]{2,1,0:T(8,128)(2,1)S(1)}, u32[]{:S(2)}, u32[]{:S(2)}) collective-permute-start(bf16[4,64,128]{2,1,0:T(8,128)(2,1)S(1)} %get-tuple-element.157), channel_id=1, source_target_pairs={{0,8},{4,12},{8,0},{12,4},{16,24},{20,28},{24,16},{28,20},{1,9},{5... | collective-permute-start | bytes 196616 | tf_op jit(solution)/shard_map/ppermute | solution.py:326
  8.0 2.5 %collective-permute-done.1 = bf16[4,64,128]{2,1,0:T(8,128)(2,1)S(1)} collective-permute-done((bf16[4,64,128]{2,1,0:T(8,128)(2,1)S(1)}, bf16[4,64,128]{2,1,0:T(8,128)(2,1)S(1)}, u32[]{:S(2)}, u32[]{:S(2)}) %collective-permute-start.1) | collective-permute-done | bytes 65568 | tf_op jit(solution)/shard_map/ppermute | solution.py:326
  10.9 3.1 %collective-permute-done.2 = bf16[4,64,128]{2,1,0:T(8,128)(2,1)S(1)} collective-permute-done((bf16[4,64,128]{2,1,0:T(8,128)(2,1)S(1)}, bf16[4,64,128]{2,1,0:T(8,128)(2,1)S(1)}, u32[]{:S(2)}, u32[]{:S(2)}) %collective-permute-start.2) | collective-permute-done | bytes 65568 | tf_op jit(solution)/shard_map/ppermute | solution.py:326
  14.1 2.5 %collective-permute-start.3 = (bf16[4,4,64,128]{3,2,1,0:T(8,128)(2,1)S(1)}, bf16[4,4,64,128]{3,2,1,0:T(8,128)(2,1)S(1)}, u32[]{:S(2)}, u32[]{:S(2)}) collective-permute-start(bf16[4,4,64,128]{3,2,1,0:T(8,128)(2,1)S(1)} %pad_maximum_fusion.refs_0_), channel_id=1, source_target_pairs={{0,6},{1,7},{2,4},{3,5},{4,2},{5,3},{6,0},{7,1},{8,14},{9,15},{10,... | collective-permute-start | bytes 786440 | tf_op jit(solution)/shard_map/ppermute | solution.py:341
  17.6 2.0 %collective-permute-start.4 = (f32[1,32,256]{2,1,0:T(8,128)}, f32[1,32,256]{2,1,0:T(8,128)S(1)}, u32[]{:S(2)}, u32[]{:S(2)}) collective-permute-start(f32[1,32,256]{2,1,0:T(8,128)} %bitcast.21), channel_id=1, source_target_pairs={{0,16},{4,20},{8,24},{12,28},{16,0},{20,4},{24,8},{28,12},{1,17},{... | collective-permute-start | bytes 98312 | tf_op jit(solution)/shard_map/ppermute | solution.py:326
  20.4 1.7 %copy-done = bf16[3,3,512,256]{3,2,1,0:T(8,128)(2,1)S(1)} copy-done((bf16[3,3,512,256]{3,2,1,0:T(8,128)(2,1)S(1)}, bf16[3,3,512,256]{3,2,1,0:T(8,128)(2,1)}, u32[]{:S(2)}) %copy-start) | copy-done | bytes 2359320
  22.7 1.3 %shard_map.161 = (s32[3]{0:T(128)S(1)}, bf16[3,3,512,256]{3,2,1,0:T(8,128)(2,1)S(1)}) custom-call(s32[3]{0:T(128)S(1)} %copy-done.2, bf16[3,3,512,256]{3,2,1,0:T(8,128)(2,1)S(1)} %copy-done), custom_call_target="tpu_custom_call" | custom-call | flops 1000 | bytes 1000 | tf_op jit(solution)/shard_map/pallas_call | solution.py:313
  24.3 3.3 %collective-permute-done.6.refs_2_ = bf16[4,4,64,128]{3,2,1,0:T(8,128)(2,1)S(1)} collective-permute-done((bf16[4,4,64,128]{3,2,1,0:T(8,128)(2,1)S(1)}, bf16[4,4,64,128]{3,2,1,0:T(8,128)(2,1)S(1)}, u32[]{:S(2)}, u32[]{:S(2)}) %collective-permute-start.6) | collective-permute-done | bytes 262176 | tf_op jit(solution)/shard_map/ppermute | solution.py:326
  28.3 2.5 %shard_map.162 = (bf16[4,512,256]{2,1,0:T(8,128)(2,1)S(1)}, f32[512,128]{1,0:T(8,128)S(1)}, f32[4,528,256]{2,1,0:T(8,128)S(1)}, f32[4,512,256]{2,1,0:T(8,128)S(1)}, f32[4,528,256]{2,1,0:T(8,128)S(1)}) custom-call(bf16[4,4,64,128]{3,2,1,0:T(8,128)(2,1)S(1)} %pad_maximum_fusion.refs_0_, bf16[4,4,64,128]{3,2,1,0:T(8,128)(2,1)S(1)} %collective-permute-done.5.refs_1_, ...), custom_call_target="tpu_custom_call" | custom-call | flops 1000 | bytes 1000 | tf_op jit(solution)/shard_map/pallas_call | solution.py:313
  30.9 4.9 %shard_map.163 = (bf16[2,512,256]{2,1,0:T(8,128)(2,1)S(1)}, bf16[2,512,256]{2,1,0:T(8,128)(2,1)S(1)}, bf16[2,256,256]{2,1,0:T(8,128)(2,1)S(1)}, bf16[4,512,256]{...) custom-call(s32[3]{0:T(128)S(1)} %get-tuple-element.85.starts, ...), custom_call_target="tpu_custom_call" | custom-call | flops 1000 | bytes 1000 | tf_op jit(solution)/shard_map/pallas_call | solution.py:313
  36.3 1.5 %collective-permute-start.13 = (bf16[2,256,256]{2,1,0:T(8,128)(2,1)S(1)}, bf16[2,256,256]{2,1,0:T(8,128)(2,1)S(1)}, u32[]{:S(2)}, u32[]{:S(2)}) collective-permute-start(bf16[2,256,256]{2,1,0:T(8,128)(2,1)S(1)} %get-tuple-element.103), channel_id=1, source_target_pairs={{0,2},{1,3},{2,0},{3,1},{4,6},{5,7},{6,4},{7,5},{8,10},{9,11},{10,... | collective-permute-start | bytes 786440 | tf_op jit(solution)/shard_map/ppermute | solution.py:326
  38.5 4.2 %shard_map.164.near = f32[3,4,512,256]{3,2,1,0:T(8,128)S(1)} custom-call(bf16[2,512,256]{2,1,0:T(8,128)(2,1)S(1)} %get-tuple-element.102.low.refs_0_, bf16[2,512,256]{2,1,0:T(8,128)(2,1)S(1)} %get-tuple-element.104.high.refs_1_, bf16[2,512,256]{2,1,0:T(8,128)(2,1)S(1)} %collective-permute-done.15.low_two.refs_2_, ...), custom_call_target="tpu_custom_call" | custom-call | flops 1000 | bytes 1000 | tf_op jit(solution)/shard_map/pallas_call | solution.py:313
  42.8 2.7 %collective-permute-done.13.picked.refs_5_ = bf16[2,256,256]{2,1,0:T(8,128)(2,1)S(1)} collective-permute-done((bf16[2,256,256]{2,1,0:T(8,128)(2,1)S(1)}, bf16[2,256,256]{2,1,0:T(8,128)(2,1)S(1)}, u32[]{:S(2)}, u32[]{:S(2)}) %collective-permute-start.13) | collective-permute-done | bytes 262176 | tf_op jit(solution)/shard_map/ppermute | solution.py:326
  45.5 1.6 %collective-permute-start.18 = (f32[2,32,256]{2,1,0:T(8,128)S(1)}, f32[2,32,256]{2,1,0:T(8,128)S(1)}, u32[]{:S(2)}, u32[]{:S(2)}) collective-permute-start(f32[2,32,256]{2,1,0:T(8,128)S(1)} %pad_maximum_fusion.2), channel_id=1, source_target_pairs={{0,4},{4,0},{8,12},{12,8},{16,20},{20,16},{24,28},{28,24},{1,5},{5... | collective-permute-start | bytes 196616 | tf_op jit(solution)/shard_map/ppermute | solution.py:326
  47.6 2.7 %collective-permute-done.18.refs_2_ = f32[2,32,256]{2,1,0:T(8,128)S(1)} collective-permute-done((f32[2,32,256]{2,1,0:T(8,128)S(1)}, f32[2,32,256]{2,1,0:T(8,128)S(1)}, u32[]{:S(2)}, u32[]{:S(2)}) %collective-permute-start.18) | collective-permute-done | bytes 65568 | tf_op jit(solution)/shard_map/ppermute | solution.py:326
  50.3 1.4 %collective-permute-start.19 = (f32[4,32,256]{2,1,0:T(8,128)S(1)}, f32[4,32,256]{2,1,0:T(8,128)S(1)}, u32[]{:S(2)}, u32[]{:S(2)}) collective-permute-start(f32[4,32,256]{2,1,0:T(8,128)S(1)} %pad_maximum_fusion.1), channel_id=1, source_target_pairs={{0,8},{4,12},{8,0},{12,4},{16,24},{20,28},{24,16},{28,20},{1,9},{5... | collective-permute-start | bytes 393224 | tf_op jit(solution)/shard_map/ppermute | solution.py:326
  52.7 3.5 %collective-permute-done.12.far.refs_4_ = bf16[2,512,256]{2,1,0:T(8,128)(2,1)S(1)} collective-permute-done((bf16[2,512,256]{2,1,0:T(8,128)(2,1)S(1)}, bf16[2,512,256]{2,1,0:T(8,128)(2,1)S(1)}, u32[]{:S(2)}, u32[]{:S(2)}) %collective-permute-start.12) | collective-permute-done | bytes 524320 | tf_op jit(solution)/shard_map/ppermute | solution.py:326
  56.7 2.4 %shard_map.166.sums = f32[3,4,512,256]{3,2,1,0:T(8,128)S(1)} custom-call(bf16[2,512,256]{2,1,0:T(8,128)(2,1)S(1)} %collective-permute-done.12.far.refs_4_, bf16[2,256,256]{2,1,0:T(8,128)(2,1)S(1)} %collective-permute-done.13.picked.refs_5_, bf16[2,256,256]{2,1,0:T(8,128)(2,1)S(1)} %collective-permute-done.14.rest.refs_6_, ...), custom_call_target="tpu_custom_call" | custom-call | flops 1000 | bytes 1000 | tf_op jit(solution)/shard_map/pallas_call | solution.py:313
  59.1 8.3 %shard_map.167 = (f32[32,256]{1,0:T(8,128)}, bf16[4,512,256]{2,1,0:T(8,128)(2,1)S(1)}, f32[1,256]{1,0:T(1,128)}, f32[1,256]{1,0:T(1,128)}) custom-call(s32[3]{0:T(128)S(1)} %get-tuple-element.85.starts, f32[3,4,512,256]{3,2,1,0:T(8,128)S(1)} %shard_map.166.sums, bf16[2,512,256]{2,1,0:T(8,128)(2,1)S(1)} %collective-permute-done.20.far_two.refs_7_, ...), custom_call_target="tpu_custom_call" | custom-call | flops 1000 | bytes 1000 | tf_op jit(solution)/shard_map/pallas_call | solution.py:313
  67.6 1.4 %shard_map.168.refs_11_ = bf16[2,4,512,256]{3,2,1,0:T(8,128)(2,1)S(1)} custom-call(s32[3]{0:T(128)S(1)} %get-tuple-element.85.starts, bf16[4,512,256]{2,1,0:T(8,128)(2,1)S(1)} %get-tuple-element.128.grad.one.refs_10_), custom_call_target="tpu_custom_call" | custom-call | flops 1000 | bytes 1000 | tf_op jit(solution)/shard_map/pallas_call | solution.py:313
  70.2 2.1 %shard_map.170 = bf16[2,256,256]{2,1,0:T(8,128)(2,1)S(1)} custom-call(s32[3]{0:T(128)S(1)} %get-tuple-element.85.starts, bf16[4,512,256]{2,1,0:T(8,128)(2,1)S(1)} %get-tuple-element.128.grad.one.refs_10_, bf16[4,512,256]{2,1,0:T(8,128)(2,1)S(1)} %collective-permute-done.22.two, bf16[3,3,1024,256]{3,2,1,0:T(8,128)(2,1)S(1)} %bitcast.20, ...), custom_call_target="tpu_custom_call" | custom-call | flops 1000 | bytes 1000 | tf_op jit(solution)/shard_map/pallas_call | solution.py:313
  72.2 1.6 %collective-permute-start.24 = (bf16[2,256,256]{2,1,0:T(8,128)(2,1)S(1)}, bf16[2,256,256]{2,1,0:T(8,128)(2,1)S(1)}, u32[]{:S(2)}, u32[]{:S(2)}) collective-permute-start(bf16[2,256,256]{2,1,0:T(8,128)(2,1)S(1)} %shard_map.170), channel_id=1, source_target_pairs={{0,2},{1,3},{2,0},{3,1},{4,6},{5,7},{6,4},{7,5},{8,10},{9,11},{10,... | collective-permute-start | bytes 786440 | tf_op jit(solution)/shard_map/ppermute | solution.py:326
  73.8 3.2 %shard_map.169 = bf16[2,512,256]{2,1,0:T(8,128)(2,1)S(1)} custom-call(s32[3]{0:T(128)S(1)} %get-tuple-element.85.starts, bf16[4,512,256]{2,1,0:T(8,128)(2,1)S(1)} %get-tuple-element.128.grad.one.refs_10_, bf16[4,512,256]{2,1,0:T(8,128)(2,1)S(1)} %collective-permute-done.22.two, bf16[3,3,1024,256]{3,2,1,0:T(8,128)(2,1)S(1)} %bitcast.20, ...), custom_call_target="tpu_custom_call" | custom-call | flops 1000 | bytes 1000 | tf_op jit(solution)/shard_map/pallas_call | solution.py:313
  77.1 5.5 %shard_map.171.mine = f32[4,512,256]{2,1,0:T(8,128)S(1)} custom-call(s32[3]{0:T(128)S(1)} %get-tuple-element.85.starts, bf16[4,512,256]{2,1,0:T(8,128)(2,1)S(1)} %get-tuple-element.128.grad.one.refs_10_, bf16[4,512,256]{2,1,0:T(8,128)(2,1)S(1)} %collective-permute-done.22.two, bf16[3,3,1024,256]{3,2,1,0:T(8,128)(2,1)S(1)} %bitcast.20, ...), custom_call_target="tpu_custom_call" | custom-call | flops 1000 | bytes 1000 | tf_op jit(solution)/shard_map/pallas_call | solution.py:313
  83.3 1.5 %collective-permute-start.25 = (bf16[2,256,256]{2,1,0:T(8,128)(2,1)S(1)}, bf16[2,256,256]{2,1,0:T(8,128)(2,1)S(1)}, u32[]{:S(2)}, u32[]{:S(2)}) collective-permute-start(bf16[2,256,256]{2,1,0:T(8,128)(2,1)S(1)} %collective-permute-done.24.picked), channel_id=1, source_target_pairs={{0,4},{4,0},{8,12},{12,8},{16,20},{20,16},{24,28},{28,24},{1,5},{5... | collective-permute-start | bytes 786440 | tf_op jit(solution)/shard_map/ppermute | solution.py:326
  84.8 10.9 %shard_map.172 = f32[9,1024,256]{2,1,0:T(8,128)} custom-call(bf16[2,512,256]{2,1,0:T(8,128)(2,1)S(1)} %get-tuple-element.102.low.refs_0_, bf16[2,512,256]{2,1,0:T(8,128)(2,1)S(1)} %get-tuple-element.104.high.refs_1_, bf16[2,512,256]{2,1,0:T(8,128)(2,1)S(1)} %collective-permute-done.15.low_two.refs_2_, ...), custom_call_target="tpu_custom_call" | custom-call | flops 1000 | bytes 1000 | tf_op jit(solution)/shard_map/pallas_call | solution.py:313
  95.7 1.3 %collective-permute-done.23.low = bf16[2,512,256]{2,1,0:T(8,128)(2,1)S(1)} collective-permute-done((bf16[2,512,256]{2,1,0:T(8,128)(2,1)S(1)}, bf16[2,512,256]{2,1,0:T(8,128)(2,1)S(1)}, u32[]{:S(2)}, u32[]{:S(2)}) %collective-permute-start.23) | collective-permute-done | bytes 524320 | tf_op jit(solution)/shard_map/ppermute | solution.py:326
  97.0 1.8 %shard_map.173 = (bf16[4,512,256]{2,1,0:T(8,128)(2,1)S(1)}, bf16[4,96,256]{2,1,0:T(8,128)(2,1)S(1)}, f32[1,256]{1,0:T(1,128)}, f32[1,256]{1,0:T(1,128)}) custom-call(f32[4,512,256]{2,1,0:T(8,128)S(1)} %shard_map.171.mine, bf16[2,512,256]{2,1,0:T(8,128)(2,1)S(1)} %collective-permute-done.23.low, bf16[2,256,256]{2,1,0:T(8,128)(2,1)S(1)} %collective-permute-done.24.picked, ...), custom_call_target="tpu_custom_call" | custom-call | flops 1000 | bytes 1000 | tf_op jit(solution)/shard_map/pallas_call | solution.py:313
  98.8 1.6 %shard_map.174.refs_3_ = bf16[2,4,512,256]{3,2,1,0:T(8,128)(2,1)S(1)} custom-call(s32[3]{0:T(128)S(1)} %get-tuple-element.85.starts, bf16[4,512,256]{2,1,0:T(8,128)(2,1)S(1)} %get-tuple-element.141.grad.refs_2_), custom_call_target="tpu_custom_call" | custom-call | flops 1000 | bytes 1000 | tf_op jit(solution)/shard_map/pallas_call | solution.py:313
  100.4 1.5 %shard_map.175 = (f32[4,64,128]{2,1,0:T(8,128)S(1)}, f32[4,64,128]{2,1,0:T(8,128)S(1)}) custom-call(s32[3]{0:T(128)S(1)} %get-tuple-element.85.starts, bf16[4,96,256]{2,1,0:T(8,128)(2,1)S(1)} %get-tuple-element.140.one, bf16[4,96,256]{2,1,0:T(8,128)(2,1)S(1)} %collective-permute-done.27.two, bf16[3,3,512,256]{3,2,1,0:T(8,128)(2,1)S(1)} %get-tuple-element.135.refs_4_.weight, ...), custom_call_target="tpu_custom_call" | custom-call | flops 1000 | bytes 1000 | tf_op jit(solution)/shard_map/pallas_call | solution.py:313
  102.5 5.9 %shard_map.176 = f32[9,512,256]{2,1,0:T(8,128)} custom-call(bf16[4,512,256]{2,1,0:T(8,128)(2,1)S(1)} %get-tuple-element.146.refs_0_, bf16[4,512,256]{2,1,0:T(8,128)(2,1)S(1)} %get-tuple-element.147.refs_1_, bf16[4,512,256]{2,1,0:T(8,128)(2,1)S(1)} %get-tuple-element.141.grad.refs_2_, bf16[2,4,512,256]{3,2,1,0:T(8,128)(2,1)S(1)} %shard_map.174.refs_3_), custom_call_target="tpu_custom_call" | custom-call | flops 1000 | bytes 1000 | tf_op jit(solution)/shard_map/pallas_call | solution.py:313
  (60 shorter events, 12.7 us)
Async XLA Ops:
  0.6 30.2 %collective-permute-start.11 = (bf16[3,3,1024,256]{3,2,1,0:T(8,128)(2,1)}, bf16[3,3,1024,256]{3,2,1,0:T(8,128)(2,1)S(1)}, u32[]{:S(2)}, u32[]{:S(2)}) collective-permute-start(bf16[3,3,1024,256]{3,2,1,0:T(8,128)(2,1)} %weight.11), channel_id=1, source_target_pairs={{0,1},{1,0},{2,3},{3,2},{4,5},{5,4},{6,7},{7,6},{8,9},{9,8},{10,11... | collective-permute-start | bytes 14155784 | tf_op jit(solution)/shard_map/ppermute | solution.py:326
  2.7 7.7 %collective-permute-start.1 = (bf16[4,64,128]{2,1,0:T(8,128)(2,1)S(1)}, bf16[4,64,128]{2,1,0:T(8,128)(2,1)S(1)}, u32[]{:S(2)}, u32[]{:S(2)}) collective-permute-start(bf16[4,64,128]{2,1,0:T(8,128)(2,1)S(1)} %get-tuple-element.157), channel_id=1, source_target_pairs={{0,16},{4,20},{8,24},{12,28},{16,0},{20,4},{24,8},{28,12},{1,17},{... | collective-permute-start | bytes 196616 | tf_op jit(solution)/shard_map/ppermute | solution.py:326
  6.4 4.5 %collective-permute-start = (bf16[4,64,128]{2,1,0:T(8,128)(2,1)S(1)}, bf16[4,64,128]{2,1,0:T(8,128)(2,1)S(1)}, u32[]{:S(2)}, u32[]{:S(2)}) collective-permute-start(bf16[4,64,128]{2,1,0:T(8,128)(2,1)S(1)} %get-tuple-element.157), channel_id=1, source_target_pairs={{0,8},{4,12},{8,0},{12,4},{16,24},{20,28},{24,16},{28,20},{1,9},{5... | collective-permute-start | bytes 196616 | tf_op jit(solution)/shard_map/ppermute | solution.py:326
  8.0 6.1 %collective-permute-start.2 = (bf16[4,64,128]{2,1,0:T(8,128)(2,1)S(1)}, bf16[4,64,128]{2,1,0:T(8,128)(2,1)S(1)}, u32[]{:S(2)}, u32[]{:S(2)}) collective-permute-start(bf16[4,64,128]{2,1,0:T(8,128)(2,1)S(1)} %get-tuple-element.157), channel_id=1, source_target_pairs={{0,24},{4,28},{8,16},{12,20},{16,8},{20,12},{24,0},{28,4},{1,25},{... | collective-permute-start | bytes 196616 | tf_op jit(solution)/shard_map/ppermute | solution.py:326
  14.1 10.3 %collective-permute-start.3 = (bf16[4,4,64,128]{3,2,1,0:T(8,128)(2,1)S(1)}, bf16[4,4,64,128]{3,2,1,0:T(8,128)(2,1)S(1)}, u32[]{:S(2)}, u32[]{:S(2)}) collective-permute-start(bf16[4,4,64,128]{3,2,1,0:T(8,128)(2,1)S(1)} %pad_maximum_fusion.refs_0_), channel_id=1, source_target_pairs={{0,6},{1,7},{2,4},{3,5},{4,2},{5,3},{6,0},{7,1},{8,14},{9,15},{10,... | collective-permute-start | bytes 786440 | tf_op jit(solution)/shard_map/ppermute | solution.py:341
  16.6 11.1 %collective-permute-start.6 = (bf16[4,4,64,128]{3,2,1,0:T(8,128)(2,1)S(1)}, bf16[4,4,64,128]{3,2,1,0:T(8,128)(2,1)S(1)}, u32[]{:S(2)}, u32[]{:S(2)}) collective-permute-start(bf16[4,4,64,128]{3,2,1,0:T(8,128)(2,1)S(1)} %pad_maximum_fusion.refs_0_), channel_id=1, source_target_pairs={{0,2},{1,3},{2,0},{3,1},{4,6},{5,7},{6,4},{7,5},{8,10},{9,11},{10,... | collective-permute-start | bytes 786440 | tf_op jit(solution)/shard_map/ppermute | solution.py:326
  17.1 10.7 %collective-permute-start.5 = (bf16[4,4,64,128]{3,2,1,0:T(8,128)(2,1)S(1)}, bf16[4,4,64,128]{3,2,1,0:T(8,128)(2,1)S(1)}, u32[]{:S(2)}, u32[]{:S(2)}) collective-permute-start(bf16[4,4,64,128]{3,2,1,0:T(8,128)(2,1)S(1)} %pad_maximum_fusion.refs_0_), channel_id=1, source_target_pairs={{0,4},{4,0},{8,12},{12,8},{16,20},{20,16},{24,28},{28,24},{1,5},{5... | collective-permute-start | bytes 786440 | tf_op jit(solution)/shard_map/ppermute | solution.py:326
  17.6 6.3 %collective-permute-start.4 = (f32[1,32,256]{2,1,0:T(8,128)}, f32[1,32,256]{2,1,0:T(8,128)S(1)}, u32[]{:S(2)}, u32[]{:S(2)}) collective-permute-start(f32[1,32,256]{2,1,0:T(8,128)} %bitcast.21), channel_id=1, source_target_pairs={{0,16},{4,20},{8,24},{12,28},{16,0},{20,4},{24,8},{28,12},{1,17},{... | collective-permute-start | bytes 98312 | tf_op jit(solution)/shard_map/ppermute | solution.py:326
  24.0 6.8 %collective-permute-start.7 = (bf16[4,4,64,128]{3,2,1,0:T(8,128)(2,1)S(1)}, bf16[4,4,64,128]{3,2,1,0:T(8,128)(2,1)S(1)}, u32[]{:S(2)}, u32[]{:S(2)}) collective-permute-start(bf16[4,4,64,128]{3,2,1,0:T(8,128)(2,1)S(1)} %pad_maximum_fusion.refs_0_), channel_id=1, source_target_pairs={{0,1},{1,0},{2,3},{3,2},{4,5},{5,4},{6,7},{7,6},{8,9},{9,8},{10,11... | collective-permute-start | bytes 786440 | tf_op jit(solution)/shard_map/ppermute | solution.py:326
  27.7 3.2 %collective-permute-start.9 = (bf16[4,4,64,128]{3,2,1,0:T(8,128)(2,1)S(1)}, bf16[4,4,64,128]{3,2,1,0:T(8,128)(2,1)S(1)}, u32[]{:S(2)}, u32[]{:S(2)}) collective-permute-start(bf16[4,4,64,128]{3,2,1,0:T(8,128)(2,1)S(1)} %collective-permute-done.6.refs_2_), channel_id=1, source_target_pairs={{0,1},{1,0},{2,3},{3,2},{4,5},{5,4},{6,7},{7,6},{8,9},{9,8},{10,11... | collective-permute-start | bytes 786440 | tf_op jit(solution)/shard_map/ppermute | solution.py:326
  27.8 3.1 %collective-permute-start.8 = (bf16[4,4,64,128]{3,2,1,0:T(8,128)(2,1)S(1)}, bf16[4,4,64,128]{3,2,1,0:T(8,128)(2,1)S(1)}, u32[]{:S(2)}, u32[]{:S(2)}) collective-permute-start(bf16[4,4,64,128]{3,2,1,0:T(8,128)(2,1)S(1)} %collective-permute-done.5.refs_1_), channel_id=1, source_target_pairs={{0,1},{1,0},{2,3},{3,2},{4,5},{5,4},{6,7},{7,6},{8,9},{9,8},{10,11... | collective-permute-start | bytes 786440 | tf_op jit(solution)/shard_map/ppermute | solution.py:326
  28.2 2.7 %collective-permute-start.10 = (bf16[4,4,64,128]{3,2,1,0:T(8,128)(2,1)S(1)}, bf16[4,4,64,128]{3,2,1,0:T(8,128)(2,1)S(1)}, u32[]{:S(2)}, u32[]{:S(2)}) collective-permute-start(bf16[4,4,64,128]{3,2,1,0:T(8,128)(2,1)S(1)} %collective-permute-done.3.refs_3_), channel_id=1, source_target_pairs={{0,1},{1,0},{2,3},{3,2},{4,5},{5,4},{6,7},{7,6},{8,9},{9,8},{10,11... | collective-permute-start | bytes 786440 | tf_op jit(solution)/shard_map/ppermute | solution.py:326
  30.9 7.7 %slice-start = ((s8[4718592]{0:T(1024)(128)(4,1)}), s8[4194304]{0:T(1024)(128)(4,1)S(1)}, s32[]{:S(2)}) async-start(s8[4718592]{0:T(1024)(128)(4,1)} %bitcast.19), calls=%async_computation | async-start | bytes 8388608
  30.9 7.7 %slice-start.1 = ((s8[4718592]{0:T(1024)(128)(4,1)}), s8[524288]{0:T(1024)(128)(4,1)S(1)}, s32[]{:S(2)}) async-start(s8[4718592]{0:T(1024)(128)(4,1)} %bitcast.19), calls=%async_computation.1 | async-start | bytes 1048576
  35.8 2.6 %collective-permute-start.16 = (bf16[2,512,256]{2,1,0:T(8,128)(2,1)S(1)}, bf16[2,512,256]{2,1,0:T(8,128)(2,1)S(1)}, u32[]{:S(2)}, u32[]{:S(2)}) collective-permute-start(bf16[2,512,256]{2,1,0:T(8,128)(2,1)S(1)} %get-tuple-element.104.high.refs_1_), channel_id=1, source_target_pairs={{0,1},{1,0},{2,3},{3,2},{4,5},{5,4},{6,7},{7,6},{8,9},{9,8},{10,11... | collective-permute-start | bytes 1572872 | tf_op jit(solution)/shard_map/ppermute | solution.py:326
  36.2 2.3 %collective-permute-start.15 = (bf16[2,512,256]{2,1,0:T(8,128)(2,1)S(1)}, bf16[2,512,256]{2,1,0:T(8,128)(2,1)S(1)}, u32[]{:S(2)}, u32[]{:S(2)}) collective-permute-start(bf16[2,512,256]{2,1,0:T(8,128)(2,1)S(1)} %get-tuple-element.102.low.refs_0_), channel_id=1, source_target_pairs={{0,1},{1,0},{2,3},{3,2},{4,5},{5,4},{6,7},{7,6},{8,9},{9,8},{10,11... | collective-permute-start | bytes 1572872 | tf_op jit(solution)/shard_map/ppermute | solution.py:326
  36.3 9.1 %copy-start.1 = (f32[32,256]{1,0:T(8,128)S(1)}, f32[32,256]{1,0:T(8,128)}, u32[]{:S(2)}) copy-start(f32[32,256]{1,0:T(8,128)} %param.19) | copy-start | bytes 98308
  36.3 9.1 %collective-permute-start.13 = (bf16[2,256,256]{2,1,0:T(8,128)(2,1)S(1)}, bf16[2,256,256]{2,1,0:T(8,128)(2,1)S(1)}, u32[]{:S(2)}, u32[]{:S(2)}) collective-permute-start(bf16[2,256,256]{2,1,0:T(8,128)(2,1)S(1)} %get-tuple-element.103), channel_id=1, source_target_pairs={{0,2},{1,3},{2,0},{3,1},{4,6},{5,7},{6,4},{7,5},{8,10},{9,11},{10,... | collective-permute-start | bytes 786440 | tf_op jit(solution)/shard_map/ppermute | solution.py:326
  37.8 18.4 %collective-permute-start.12 = (bf16[2,512,256]{2,1,0:T(8,128)(2,1)S(1)}, bf16[2,512,256]{2,1,0:T(8,128)(2,1)S(1)}, u32[]{:S(2)}, u32[]{:S(2)}) collective-permute-start(bf16[2,512,256]{2,1,0:T(8,128)(2,1)S(1)} %get-tuple-element.102.low.refs_0_), channel_id=1, source_target_pairs={{0,2},{1,3},{2,0},{3,1},{4,6},{5,7},{6,4},{7,5},{8,10},{9,11},{10,... | collective-permute-start | bytes 1572872 | tf_op jit(solution)/shard_map/ppermute | solution.py:326
  45.4 4.8 %collective-permute-start.17 = (bf16[2,256,256]{2,1,0:T(8,128)(2,1)S(1)}, bf16[2,256,256]{2,1,0:T(8,128)(2,1)S(1)}, u32[]{:S(2)}, u32[]{:S(2)}) collective-permute-start(bf16[2,256,256]{2,1,0:T(8,128)(2,1)S(1)} %collective-permute-done.13.picked.refs_5_), channel_id=1, source_target_pairs={{0,1},{1,0},{2,3},{3,2},{4,5},{5,4},{6,7},{7,6},{8,9},{9,8},{10,11... | collective-permute-start | bytes 786440 | tf_op jit(solution)/shard_map/ppermute | solution.py:326
  45.5 4.8 %collective-permute-start.18 = (f32[2,32,256]{2,1,0:T(8,128)S(1)}, f32[2,32,256]{2,1,0:T(8,128)S(1)}, u32[]{:S(2)}, u32[]{:S(2)}) collective-permute-start(f32[2,32,256]{2,1,0:T(8,128)S(1)} %pad_maximum_fusion.2), channel_id=1, source_target_pairs={{0,4},{4,0},{8,12},{12,8},{16,20},{20,16},{24,28},{28,24},{1,5},{5... | collective-permute-start | bytes 196616 | tf_op jit(solution)/shard_map/ppermute | solution.py:326
  47.0 9.2 %collective-permute-start.14 = (bf16[2,256,256]{2,1,0:T(8,128)(2,1)S(1)}, bf16[2,256,256]{2,1,0:T(8,128)(2,1)S(1)}, u32[]{:S(2)}, u32[]{:S(2)}) collective-permute-start(bf16[2,256,256]{2,1,0:T(8,128)(2,1)S(1)} %collective-permute-done.13.picked.refs_5_), channel_id=1, source_target_pairs={{0,4},{4,0},{8,12},{12,8},{16,20},{20,16},{24,28},{28,24},{1,5},{5... | collective-permute-start | bytes 786440 | tf_op jit(solution)/shard_map/ppermute | solution.py:326
  50.3 5.9 %collective-permute-start.19 = (f32[4,32,256]{2,1,0:T(8,128)S(1)}, f32[4,32,256]{2,1,0:T(8,128)S(1)}, u32[]{:S(2)}, u32[]{:S(2)}) collective-permute-start(f32[4,32,256]{2,1,0:T(8,128)S(1)} %pad_maximum_fusion.1), channel_id=1, source_target_pairs={{0,8},{4,12},{8,0},{12,4},{16,24},{20,28},{24,16},{28,20},{1,9},{5... | collective-permute-start | bytes 393224 | tf_op jit(solution)/shard_map/ppermute | solution.py:326
  56.2 2.9 %collective-permute-start.20 = (bf16[2,512,256]{2,1,0:T(8,128)(2,1)S(1)}, bf16[2,512,256]{2,1,0:T(8,128)(2,1)S(1)}, u32[]{:S(2)}, u32[]{:S(2)}) collective-permute-start(bf16[2,512,256]{2,1,0:T(8,128)(2,1)S(1)} %collective-permute-done.12.far.refs_4_), channel_id=1, source_target_pairs={{0,1},{1,0},{2,3},{3,2},{4,5},{5,4},{6,7},{7,6},{8,9},{9,8},{10,11... | collective-permute-start | bytes 1572872 | tf_op jit(solution)/shard_map/ppermute | solution.py:326
  56.2 2.9 %collective-permute-start.21 = (bf16[2,256,256]{2,1,0:T(8,128)(2,1)S(1)}, bf16[2,256,256]{2,1,0:T(8,128)(2,1)S(1)}, u32[]{:S(2)}, u32[]{:S(2)}) collective-permute-start(bf16[2,256,256]{2,1,0:T(8,128)(2,1)S(1)} %collective-permute-done.14.rest.refs_6_), channel_id=1, source_target_pairs={{0,1},{1,0},{2,3},{3,2},{4,5},{5,4},{6,7},{7,6},{8,9},{9,8},{10,11... | collective-permute-start | bytes 786440 | tf_op jit(solution)/shard_map/ppermute | solution.py:326
  67.5 2.7 %collective-permute-start.22 = (bf16[4,512,256]{2,1,0:T(8,128)(2,1)S(1)}, bf16[4,512,256]{2,1,0:T(8,128)(2,1)S(1)}, u32[]{:S(2)}, u32[]{:S(2)}) collective-permute-start(bf16[4,512,256]{2,1,0:T(8,128)(2,1)S(1)} %get-tuple-element.128.grad.one.refs_10_), channel_id=1, source_target_pairs={{0,1},{1,0},{2,3},{3,2},{4,5},{5,4},{6,7},{7,6},{8,9},{9,8},{10,11... | collective-permute-start | bytes 3145736 | tf_op jit(solution)/shard_map/ppermute | solution.py:326
  72.2 10.3 %collective-permute-start.24 = (bf16[2,256,256]{2,1,0:T(8,128)(2,1)S(1)}, bf16[2,256,256]{2,1,0:T(8,128)(2,1)S(1)}, u32[]{:S(2)}, u32[]{:S(2)}) collective-permute-start(bf16[2,256,256]{2,1,0:T(8,128)(2,1)S(1)} %shard_map.170), channel_id=1, source_target_pairs={{0,2},{1,3},{2,0},{3,1},{4,6},{5,7},{6,4},{7,5},{8,10},{9,11},{10,... | collective-permute-start | bytes 786440 | tf_op jit(solution)/shard_map/ppermute | solution.py:326
  82.6 14.4 %collective-permute-start.26 = (bf16[3,3,512,256]{3,2,1,0:T(8,128)(2,1)S(1)}, bf16[3,3,512,256]{3,2,1,0:T(8,128)(2,1)S(1)}, u32[]{:S(2)}, u32[]{:S(2)}) collective-permute-start(bf16[3,3,512,256]{3,2,1,0:T(8,128)(2,1)S(1)} %get-tuple-element.135.refs_4_.weight), channel_id=1, source_target_pairs={{0,1},{1,0},{2,3},{3,2},{4,5},{5,4},{6,7},{7,6},{8,9},{9,8},{10,11... | collective-permute-start | bytes 7077896 | tf_op jit(solution)/shard_map/ppermute | solution.py:326
  82.7 14.3 %collective-permute-start.23 = (bf16[2,512,256]{2,1,0:T(8,128)(2,1)S(1)}, bf16[2,512,256]{2,1,0:T(8,128)(2,1)S(1)}, u32[]{:S(2)}, u32[]{:S(2)}) collective-permute-start(bf16[2,512,256]{2,1,0:T(8,128)(2,1)S(1)} %shard_map.169), channel_id=1, source_target_pairs={{0,2},{1,3},{2,0},{3,1},{4,6},{5,7},{6,4},{7,5},{8,10},{9,11},{10,... | collective-permute-start | bytes 1572872 | tf_op jit(solution)/shard_map/ppermute | solution.py:326
  83.3 12.4 %collective-permute-start.25 = (bf16[2,256,256]{2,1,0:T(8,128)(2,1)S(1)}, bf16[2,256,256]{2,1,0:T(8,128)(2,1)S(1)}, u32[]{:S(2)}, u32[]{:S(2)}) collective-permute-start(bf16[2,256,256]{2,1,0:T(8,128)(2,1)S(1)} %collective-permute-done.24.picked), channel_id=1, source_target_pairs={{0,4},{4,0},{8,12},{12,8},{16,20},{20,16},{24,28},{28,24},{1,5},{5... | collective-permute-start | bytes 786440 | tf_op jit(solution)/shard_map/ppermute | solution.py:326
  98.8 1.6 %collective-permute-start.27 = (bf16[4,96,256]{2,1,0:T(8,128)(2,1)S(1)}, bf16[4,96,256]{2,1,0:T(8,128)(2,1)S(1)}, u32[]{:S(2)}, u32[]{:S(2)}) collective-permute-start(bf16[4,96,256]{2,1,0:T(8,128)(2,1)S(1)} %get-tuple-element.140.one), channel_id=1, source_target_pairs={{0,1},{1,0},{2,3},{3,2},{4,5},{5,4},{6,7},{7,6},{8,9},{9,8},{10,11... | collective-permute-start | bytes 589832 | tf_op jit(solution)/shard_map/ppermute | solution.py:326
  102.0 6.5 %collective-permute-start.28 = (f32[4,64,128]{2,1,0:T(8,128)S(1)}, f32[4,64,128]{2,1,0:T(8,128)S(1)}, u32[]{:S(2)}, u32[]{:S(2)}) collective-permute-start(f32[4,64,128]{2,1,0:T(8,128)S(1)} %get-tuple-element.145), channel_id=1, source_target_pairs={{0,2},{1,3},{2,0},{3,1},{4,6},{5,7},{6,4},{7,5},{8,10},{9,11},{10,... | collective-permute-start | bytes 393224 | tf_op jit(solution)/shard_map/ppermute | solution.py:326
  (2 other events, 2.3 us)

commit v6 on v5

--- a/solution.py
+++ b/solution.py
@@ -290,6 +290,7 @@
 ABSENT = 1024.0
 ROWS = 64
 TILE = 8
+NORMS = 4
 LANES = 128
 
 
@@ -303,10 +304,6 @@
 
 def far_spec():
     return pl.BlockSpec(memory_space=pltpu.HBM)
-
-
-def scalar_spec():
-    return pl.BlockSpec(memory_space=pltpu.SMEM)
 
 
 def call(body, operands, in_specs, outs, out_specs, scratch, flops, megabytes):
@@ -343,12 +340,17 @@
 
 def same_clip(starts, at, shape, total):
     frame = lax.broadcasted_iota(jnp.int32, shape, 0) + at
-    before = frame != starts[0]
+    first, *others = clip_rows(starts)
+    before = frame != first
     after = frame != total - 1
-    for k in range(1, starts.shape[0]):
-        before = before & (frame != starts[k])
-        after = after & (frame != starts[k] - 1)
+    for start in others:
+        before = before & (frame != start)
+        after = after & (frame != start - 1)
     return before, after
+
+
+def clip_rows(table):
+    return [table[k : k + 1].astype(jnp.int32) for k in range(NORMS, table.shape[0])]
 
 
 def widen(mask, width):
@@ -403,25 +405,23 @@
     return 0.3989422804014327 * jnp.exp(-0.5 * value * value)
 
 
-def bring_kernel(starts_in, weight_in, starts, weight, sem):
+def bring_kernel(weight_in, weight, sem):
     copy = pltpu.make_async_copy(weight_in, weight, sem)
     copy.start()
-    for k in range(starts.shape[0]):
-        starts[k] = starts_in[k]
     copy.wait()
 
 
-def bring(starts, weight):
+def bring(weight):
     return call(
         bring_kernel,
-        (starts, weight),
-        [scalar_spec(), place_spec()],
-        [(starts.shape, jnp.int32), (weight.shape, bf16)],
-        [scalar_spec(), whole_spec()],
+        (weight,),
+        [place_spec()],
+        [(weight.shape, bf16)],
+        [whole_spec()],
         [pltpu.SemaphoreType.DMA],
         0,
         4,
-    )
+    )[0]
 
 
 def settle(blocks, field, keep):
@@ -549,7 +549,7 @@
     return call(
         first_kernel,
         (starts, *blocks, weight, scales, keep, *sources),
-        [scalar_spec()] + [whole_spec()] * 10,
+        [whole_spec()] + [whole_spec()] * 10,
         [
             (half, bf16),
             (half, bf16),
@@ -771,8 +771,9 @@
     col = lax.broadcasted_iota(jnp.int32, square, 1)
     same = row >= col
     back = row <= col
-    for k in range(1, starts.shape[0]):
-        crossed = (2 * row < starts[k]) != (2 * col < starts[k])
+    for start in clip_rows(starts)[1:]:
+        start = start[:, :pooled_total]
+        crossed = (2 * row < start) != (2 * col < start)
         same = same & ~crossed
         back = back & ~crossed
     ahead, behind = same.astype(f32).astype(bf16), back.astype(f32).astype(bf16)
@@ -827,7 +828,7 @@
     return call(
         second_kernel,
         (starts, sums, *arrays, weight, keep, scales, *cotangents),
-        [scalar_spec()] + [whole_spec()] * (len(arrays) + 4) + [place_spec()] * len(cotangents),
+        [whole_spec()] + [whole_spec()] * (len(arrays) + 4) + [place_spec()] * len(cotangents),
         [((own, width), f32), (full, bf16), ((1, width), f32), ((1, width), f32)],
         [whole_spec()] * 4,
         [
@@ -847,39 +848,99 @@
     )
 
 
-def back_kernel(bit, mels, halved, starts, one, two, weight, weight_two, out, lower, middle, upper):
-    mel_count, total, width = one.shape
-    reach, rows_out = middle.shape[1], out.shape[1]
-    side = lax.axis_index("tm") % 2 if halved else 0
-    edge = reach - rows_out
-    first = side * (total - reach)
-    skip = side * edge
-    if halved:
-        first, skip = pl.multiple_of(first, 16), pl.multiple_of(skip, 16)
+def wings_kernel(weight, wings, sems):
+    width = wings.shape[3]
+    copies = []
+    for i, start in enumerate(group_starts((2, 0), width)):
+        for a in range(3):
+            for b in range(3):
+                copies.append(
+                    pltpu.make_async_copy(
+                        weight.at[a, b, pl.ds(start, width)], wings.at[i, 3 * a + b], sems.at[len(copies)]
+                    )
+                )
+    for copy in copies:
+        copy.start()
+    for copy in copies:
+        copy.wait()
+
+
+def bring_wings(weight):
+    width = weight.shape[3]
+    return call(
+        wings_kernel,
+        (weight,),
+        [place_spec()],
+        [((2, 9, width, width), bf16)],
+        [whole_spec()],
+        [pltpu.SemaphoreType.DMA((18,))],
+        0,
+        4,
+    )[0]
+
+
+def back_sums(field, wing, mels, reach, first, targets, sources=None):
+    mel_count = field.shape[0]
+    for k, n in enumerate(mels):
+        for a in range(3):
+            acc = None
+            for b in range(3):
+                if 0 <= n - b + 1 < mel_count:
+                    part = lax.dot_general(
+                        field[n - b + 1, pl.ds(first, reach)],
+                        wing(a, b),
+                        (((1,), (1,)), ((), ())),
+                        preferred_element_type=f32,
+                    )
+                    acc = part if acc is None else acc + part
+            if sources is not None:
+                acc = sources[a, k] + acc
+            target, at = targets[a]
+            target[k, at : at + reach] = acc
+
+
+def half_rows(total, reach):
+    side = lax.axis_index("tm") % 2
+    return (
+        pl.multiple_of(side * (total - reach), 16),
+        pl.multiple_of(side * (reach - total // 2), 16),
+    )
+
+
+def ahead_kernel(bit, mels, one, weight, sums):
+    _, total, width = one.shape
+    reach = sums.shape[2]
+    first, _ = half_rows(total, reach)
     (start,) = group_starts((bit,), width)
+    targets = [(sums.at[a], 0) for a in range(3)]
+    back_sums(one, lambda a, b: weight[a, b, pl.ds(start, width)], mels, reach, first, targets)
+
+
+def hidden_ahead(bit, mels, one, weight):
+    _, total, width = one.shape
+    return call(
+        functools.partial(ahead_kernel, bit, mels),
+        (one, weight),
+        [whole_spec()] * 2,
+        [((3, len(mels), total // 2 + 16, width), f32)],
+        [whole_spec()],
+        [],
+        0,
+        4,
+    )[0]
+
+
+def half_kernel(bit, mels, starts, two, wings, sums, out, lower, middle, upper):
+    _, total, width = two.shape
+    reach = sums.shape[2]
+    first, skip = half_rows(total, reach)
     for k in range(len(mels)):
         for ref in (lower, upper):
             ref[k, :TILE] = jnp.zeros((TILE, width), f32)
             ref[k, TILE + reach :] = jnp.zeros((TILE, width), f32)
-    for k, n in enumerate(mels):
-        for a in range(3):
-            acc = None
-            for field, matrix in ((one, weight), (two, weight_two)):
-                for b in range(3):
-                    if 0 <= n - b + 1 < mel_count:
-                        part = lax.dot_general(
-                            field[n - b + 1, pl.ds(first, reach)],
-                            matrix[a, b, pl.ds(start, width)],
-                            (((1,), (1,)), ((), ())),
-                            preferred_element_type=f32,
-                        )
-                        acc = part if acc is None else acc + part
-            if a == 2:
-                lower[k, TILE : TILE + reach] = acc
-            elif a == 1:
-                middle[k] = acc
-            else:
-                upper[k, TILE : TILE + reach] = acc
+    wing = wings.at[0 if bit else 1]
+    targets = ((upper, TILE), (middle, 0), (lower, TILE))
+    back_sums(two, lambda a, b: wing[3 * a + b], mels, reach, first, targets, sums)
 
     def combine(at, carry):
         near = pl.multiple_of(at + skip, TILE)
@@ -889,20 +950,18 @@
             out[k, pl.ds(at, ROWS)] = rows.astype(out.dtype)
         return carry
 
-    by_rows(rows_out, combine, 0)
-
-
-def hidden_back(bit, mels, halved, one, two, weight, weight_two, starts, kind):
-    _, total, width = one.shape
-    rows = total // 2 if halved else total
-    reach = rows + 16 if halved else total
-    count = len(mels)
+    by_rows(total // 2, combine, 0)
+
+
+def hidden_half(bit, mels, two, wings, sums, starts, kind):
+    _, total, width = two.shape
+    reach, count = sums.shape[2], len(mels)
     padded = (count, reach + 2 * TILE, width)
     return call(
-        functools.partial(back_kernel, bit, mels, halved),
-        (starts, one, two, weight, weight_two),
-        [scalar_spec()] + [whole_spec()] * 4,
-        [((count, rows, width), kind)],
+        functools.partial(half_kernel, bit, mels),
+        (starts, two, wings, sums),
+        [whole_spec()] * 4,
+        [((count, total // 2, width), kind)],
         [whole_spec()],
         [
             pltpu.VMEM(padded, f32),
@@ -910,8 +969,61 @@
             pltpu.VMEM(padded, f32),
         ],
         0,
+        8,
+    )[0]
+
+
+def back_kernel(bit, mels, starts, one, two, weight, wings, out, lower, middle, upper):
+    mel_count, total, width = one.shape
+    (start,) = group_starts((bit,), width)
+    wing = wings.at[0 if bit else 1]
+    clear_edges(lower, upper, total)
+    for k, n in enumerate(mels):
+        for a, (target, at) in enumerate(((upper, TILE), (middle, 0), (lower, TILE))):
+            acc = None
+            for field, matrix in (
+                (one, lambda b, a=a: weight[a, b, pl.ds(start, width)]),
+                (two, lambda b, a=a: wing[3 * a + b]),
+            ):
+                for b in range(3):
+                    if 0 <= n - b + 1 < mel_count:
+                        part = lax.dot_general(
+                            field[n - b + 1],
+                            matrix(b),
+                            (((1,), (1,)), ((), ())),
+                            preferred_element_type=f32,
+                        )
+                        acc = part if acc is None else acc + part
+            target[k, at : at + total] = acc
+
+    def combine(at, carry):
+        before, after = same_clip(starts, at, (ROWS, width), total)
+        for k in range(len(mels)):
+            rows = joined(lower, middle, upper, k, at, before, after)
+            out[k, pl.ds(at, ROWS)] = rows.astype(out.dtype)
+        return carry
+
+    by_rows(total, combine, 0)
+
+
+def hidden_back(bit, mels, one, two, weight, wings, starts, kind):
+    _, total, width = one.shape
+    count = len(mels)
+    padded = (count, total + 2 * TILE, width)
+    return call(
+        functools.partial(back_kernel, bit, mels),
+        (starts, one, two, weight, wings),
+        [whole_spec()] * 5,
+        [((count, total, width), kind)],
+        [whole_spec()],
+        [
+            pltpu.VMEM(padded, f32),
+            pltpu.VMEM((count, total, width), f32),
+            pltpu.VMEM(padded, f32),
+        ],
+        0,
         14,
-    )
+    )[0]
 
 
 def norm_kernel(mine, low, picked, rest, slope, pre, stats, scales, keep, *refs):
@@ -1025,7 +1137,7 @@
     return call(
         spread_kernel,
         (starts, grad),
-        [scalar_spec(), whole_spec()],
+        [whole_spec()] * 2,
         [((2, mel_count, total, width), bf16)],
         [whole_spec()],
         [pltpu.VMEM((mel_count, total + 2 * TILE, width), f32)],
@@ -1056,6 +1168,8 @@
         slot = i % 2
         for copy in copies[slot]:
             copy.wait()
+        copies[slot] = []
+        each = width // len(places)
         if any(piece[0] >= count for piece in pieces):
             while moves:
                 moves.pop().wait()
@@ -1073,19 +1187,18 @@
                             preferred_element_type=f32,
                         )
                         acc = part if acc is None else acc + part
-                results[slot, 3 * a + b] = acc
-        each = width // len(places)
-        copies[slot] = []
-        for j, bit in enumerate(places):
-            start = pl.multiple_of((column ^ bit) * each, each)
-            copies[slot].append(
-                pltpu.make_async_copy(
-                    results.at[slot, :, j * each : (j + 1) * each],
-                    out.at[:, pl.ds(start, each)],
-                    sems.at[slot, j],
-                )
-            )
-            copies[slot][-1].start()
+                tap = 3 * a + b
+                results[slot, tap] = acc
+                for j, bit in enumerate(places):
+                    start = pl.multiple_of((column ^ bit) * each, each)
+                    copies[slot].append(
+                        pltpu.make_async_copy(
+                            results.at[slot, tap, j * each : (j + 1) * each],
+                            out.at[tap, pl.ds(start, each)],
+                            sems.at[slot, tap, j],
+                        )
+                    )
+                    copies[slot][-1].start()
     for copy in copies[0] + copies[1]:
         copy.wait()
 
@@ -1103,7 +1216,7 @@
         [
             pltpu.VMEM((2, 9, width, out_width), f32),
             pltpu.VMEM(joint, bf16),
-            pltpu.SemaphoreType.DMA((2, 2)),
+            pltpu.SemaphoreType.DMA((2, 9, 2)),
             pltpu.SemaphoreType.DMA((max(2 * len(halves), 1),)),
         ],
         0,
@@ -1157,7 +1270,7 @@
     return call(
         input_kernel,
         (starts, one, two, weight, weight_two),
-        [scalar_spec()] + [whole_spec()] * 4,
+        [whole_spec()] + [whole_spec()] * 4,
         [(shape, f32), (shape, f32)],
         [whole_spec()] * 2,
         [
@@ -1207,8 +1320,10 @@
     frames, mel_count, lanes = features.shape
     places = lax.axis_size("tm")
     total = frames * places
-    clip_starts, conv1_weight = bring(clip_starts, conv1_weight)
-    scales = jnp.stack([norm1_gain, norm1_bias, norm2_gain, norm2_bias])
+    conv1_weight = bring(conv1_weight)
+    starts = jnp.broadcast_to(clip_starts.astype(f32)[:, None], clip_starts.shape + norm1_gain.shape)
+    norms = jnp.stack([norm1_gain, norm1_bias, norm2_gain, norm2_bias])
+    table = jnp.concatenate([norms, starts])
 
     marked = jnp.where(valid[:, None, None] > 0, features, jnp.asarray(ABSENT, bf16))
     own = jnp.transpose(marked, (1, 0, 2))
@@ -1224,8 +1339,8 @@
     bits = gather_bits(places)
     cotangents = [readout_grad[None]]
     cotangents.append(swap(cotangents[0], "tm", bits[0]))
-    near[3], clip_starts, conv1_weight, scales, cotangents = lax.optimization_barrier(
-        (near[3], clip_starts, conv1_weight, scales, cotangents)
+    near[3], conv1_weight, table, cotangents = lax.optimization_barrier(
+        (near[3], conv1_weight, table, cotangents)
     )
     others = [swap(block, "chan", 1) for block in near]
     column, keep, *sources = column_part(near, conv1_weight, total)
@@ -1234,7 +1349,7 @@
     others, other_conv2 = lax.optimization_barrier((others, other_conv2))
 
     low, high, picked, other_column, pre, stats = first_block(
-        others, conv1_weight, scales, keep, sources, clip_starts, total
+        others, conv1_weight, table, keep, sources, table, total
     )
     fields1 = (column, other_column)
 
@@ -1246,11 +1361,15 @@
     near = near_part(low, high, low_two, high_two, conv2_weight)
     far_picked, near, cotangents = lax.optimization_barrier((far_picked, near, cotangents))
     picked_two = swap(far_picked, "chan", 1)
+    other_conv2, near = lax.optimization_barrier((other_conv2, near))
+    wings = bring_wings(other_conv2)
     for bit in bits[1:-1]:
         cotangents.append(swap(jnp.concatenate(cotangents), "tm", bit))
-    picked_two, pre, cotangents = lax.optimization_barrier((picked_two, pre, cotangents))
+    picked_two, pre, cotangents, wings = lax.optimization_barrier(
+        (picked_two, pre, cotangents, wings)
+    )
     cotangents.append(swap(jnp.concatenate(cotangents), "tm", bits[-1]))
-    slope = first_slope(pre, stats, scales, keep)
+    slope = first_slope(pre, stats, table, keep)
     far, far_rest, slope, cotangents = lax.optimization_barrier((far, far_rest, slope, cotangents))
     far_two, rest_two = swap(far, "chan", 1), swap(far_rest, "chan", 1)
     sums = far_part(far, far_picked, far_rest, conv2_weight, near)
@@ -1261,28 +1380,25 @@
         (far_two, picked_two, rest_two),
         conv2_weight,
         keep,
-        scales,
-        clip_starts,
+        table,
+        table,
         cotangents,
         readout_grad.shape[0],
     )
     grad2_near = swap(grad2, "chan", 1)
-    steps2 = spread(grad2, clip_starts)
-    grad2_near, steps2 = lax.optimization_barrier((grad2_near, steps2))
+    steps2 = spread(grad2, table)
+    ahead = hidden_ahead(2, (2, 3), grad2, conv2_weight)
+    grad2_near, steps2, ahead = lax.optimization_barrier((grad2_near, steps2, ahead))
+    away = hidden_half(2, (2, 3), grad2_near, wings, ahead, table, bf16)
+    came_picked = swap(away, "chan", 2)
     back = functools.partial(
-        hidden_back,
-        one=grad2,
-        two=grad2_near,
-        weight=conv2_weight,
-        weight_two=other_conv2,
-        starts=clip_starts,
-    )
-    came_picked = swap(back(2, (2, 3), True, kind=bf16)[0], "chan", 2)
-    (away_low,) = back(2, (0, 1), False, kind=bf16)
+        hidden_back, one=grad2, two=grad2_near, weight=conv2_weight, starts=table
+    )
+    away_low = back(2, (0, 1), wings=wings, kind=bf16)
     came_low = swap(away_low, "chan", 2)
 
-    away_low, other_conv2 = lax.optimization_barrier((away_low, other_conv2))
-    (mine,) = back(0, (0, 1, 2, 3), False, weight_two=other_conv2, kind=f32)
+    away_low, wings = lax.optimization_barrier((away_low, wings))
+    mine = back(0, (0, 1, 2, 3), wings=wings, kind=f32)
     came_picked, mine, conv1_weight = lax.optimization_barrier((came_picked, mine, conv1_weight))
     came_rest = swap(came_picked, "tm", 1)
     other_conv1 = swap(conv1_weight, "chan", 1)
@@ -1302,13 +1418,13 @@
     )
 
     grad1, window, gain1_grad, shift1_grad = norm_back_first(
-        mine, came_low, came_picked, came_rest, slope, pre, stats, scales, keep, frames
+        mine, came_low, came_picked, came_rest, slope, pre, stats, table, keep, frames
     )
     window_near = swap(window, "chan", 1)
-    steps1 = spread(grad1, clip_starts)
+    steps1 = spread(grad1, table)
     window_near, steps1 = lax.optimization_barrier((window_near, steps1))
     input_mine, input_away = input_back(
-        window, window_near, conv1_weight, other_conv1, clip_starts, frames, lanes
+        window, window_near, conv1_weight, other_conv1, table, frames, lanes
     )
     input_came = swap(input_away, "chan", 2)
     layout = [(bits, [(i, m, 0) for m in range(mel_count)]) for i, bits in enumerate(((0, 2), (1, 3)))]

time: 109 us -> 106 us (0.972)
  Pallas kernels: 59.3 us -> 56.2 us
    pallas_call x17 -> x19, Pallas kernels: 59.3 us -> 56.2 us  [call(): pl.pallas_call(body, out_shape=tuple((jax.ShapeDtypeStruct(s, d) for s, d...]
    ppermute x1, waiting for transfers between devices: 0.27 us -> 1.67 us  [swap_both(): return lax.ppermute(shard, (first, second), pairs)]
    unnamed x10 -> x18, local copies, waits for them, and re-layouts: 2.33 us -> 2.15 us
  transfers between devices with their start and end apart: 29 -> 29, of which waited for: 12 -> 14; matrix products, arithmetic and copies ran while one was open for 2% -> 2% of each run, Pallas kernels for 37% -> 37%
where the time goes in v6:
time: 106 us
  Pallas kernels  56.2 us (53%)
  starting transfers between devices  22.8 us (22%)
  waiting for transfers between devices  21.7 us (20%)
  local copies, waits for them, and re-layouts  2.25 us (2%)
  other arithmetic  1.64 us (2%)
    pallas_call x19, Pallas kernels, call(): pl.pallas_call(body, out_shape=tuple((jax.ShapeDtypeStruct(s, d) for s, d...  56.2 us
    ppermute x28, starting transfers between devices, swap(): return lax.ppermute(shard, axis, [(i, i ^ bit) for i in range(count)])  20.3 us
    ppermute x28, waiting for transfers between devices, swap(): return lax.ppermute(shard, axis, [(i, i ^ bit) for i in range(count)])  20 us
    ppermute x1, starting transfers between devices, swap_both(): return lax.ppermute(shard, (first, second), pairs)  2.51 us
    unnamed x18, local copies, waits for them, and re-layouts  2.15 us
  transfers between devices with their start and end apart: 29, of which 14 were waited for; matrix products, arithmetic and copies ran while one was open for 2% of the time, Pallas kernels for 37%

profile of v6, /device:TPU:0, one launch (start us, length us, event | category | flops | bytes accessed | tf_op | source)
XLA Modules:
  0.0 105.5 jit_solution(1335009520484869090)
XLA Ops:
  2.7 3.7 %collective-permute-start.1 = (bf16[4,64,128]{2,1,0:T(8,128)(2,1)S(1)}, bf16[4,64,128]{2,1,0:T(8,128)(2,1)S(1)}, u32[]{:S(2)}, u32[]{:S(2)}) collective-permute-start(bf16[4,64,128]{2,1,0:T(8,128)(2,1)S(1)} %get-tuple-element.159), channel_id=1, source_target_pairs={{0,16},{4,20},{8,24},{12,28},{16,0},{20,4},{24,8},{28,12},{1,17},{... | collective-permute-start | bytes 196616 | tf_op jit(solution)/shard_map/ppermute | solution.py:323
  6.4 1.6 %collective-permute-start = (bf16[4,64,128]{2,1,0:T(8,128)(2,1)S(1)}, bf16[4,64,128]{2,1,0:T(8,128)(2,1)S(1)}, u32[]{:S(2)}, u32[]{:S(2)}) collective-permute-start(bf16[4,64,128]{2,1,0:T(8,128)(2,1)S(1)} %get-tuple-element.159), channel_id=1, source_target_pairs={{0,8},{4,12},{8,0},{12,4},{16,24},{20,28},{24,16},{28,20},{1,9},{5... | collective-permute-start | bytes 196616 | tf_op jit(solution)/shard_map/ppermute | solution.py:323
  8.0 2.5 %collective-permute-done.1 = bf16[4,64,128]{2,1,0:T(8,128)(2,1)S(1)} collective-permute-done((bf16[4,64,128]{2,1,0:T(8,128)(2,1)S(1)}, bf16[4,64,128]{2,1,0:T(8,128)(2,1)S(1)}, u32[]{:S(2)}, u32[]{:S(2)}) %collective-permute-start.1) | collective-permute-done | bytes 65568 | tf_op jit(solution)/shard_map/ppermute | solution.py:323
  10.9 3.1 %collective-permute-done.2 = bf16[4,64,128]{2,1,0:T(8,128)(2,1)S(1)} collective-permute-done((bf16[4,64,128]{2,1,0:T(8,128)(2,1)S(1)}, bf16[4,64,128]{2,1,0:T(8,128)(2,1)S(1)}, u32[]{:S(2)}, u32[]{:S(2)}) %collective-permute-start.2) | collective-permute-done | bytes 65568 | tf_op jit(solution)/shard_map/ppermute | solution.py:323
  14.1 2.5 %collective-permute-start.3 = (bf16[4,4,64,128]{3,2,1,0:T(8,128)(2,1)S(1)}, bf16[4,4,64,128]{3,2,1,0:T(8,128)(2,1)S(1)}, u32[]{:S(2)}, u32[]{:S(2)}) collective-permute-start(bf16[4,4,64,128]{3,2,1,0:T(8,128)(2,1)S(1)} %pad_maximum_fusion.refs_0_), channel_id=1, source_target_pairs={{0,6},{1,7},{2,4},{3,5},{4,2},{5,3},{6,0},{7,1},{8,14},{9,15},{10,... | collective-permute-start | bytes 786440 | tf_op jit(solution)/shard_map/ppermute | solution.py:338
  17.6 2.0 %collective-permute-start.4 = (f32[1,32,256]{2,1,0:T(8,128)}, f32[1,32,256]{2,1,0:T(8,128)S(1)}, u32[]{:S(2)}, u32[]{:S(2)}) collective-permute-start(f32[1,32,256]{2,1,0:T(8,128)} %bitcast.21), channel_id=1, source_target_pairs={{0,16},{4,20},{8,24},{12,28},{16,0},{20,4},{24,8},{28,12},{1,17},{... | collective-permute-start | bytes 98312 | tf_op jit(solution)/shard_map/ppermute | solution.py:323
  19.6 1.7 %copy-done = bf16[3,3,512,256]{3,2,1,0:T(8,128)(2,1)S(1)} copy-done((bf16[3,3,512,256]{3,2,1,0:T(8,128)(2,1)S(1)}, bf16[3,3,512,256]{3,2,1,0:T(8,128)(2,1)}, u32[]{:S(2)}) %copy-start) | copy-done | bytes 2359320
  22.7 1.7 %collective-permute-done.3.refs_3_ = bf16[4,4,64,128]{3,2,1,0:T(8,128)(2,1)S(1)} collective-permute-done((bf16[4,4,64,128]{3,2,1,0:T(8,128)(2,1)S(1)}, bf16[4,4,64,128]{3,2,1,0:T(8,128)(2,1)S(1)}, u32[]{:S(2)}, u32[]{:S(2)}) %collective-permute-start.3) | collective-permute-done | bytes 262176 | tf_op jit(solution)/shard_map/ppermute | solution.py:338
  24.3 3.3 %collective-permute-done.6.refs_2_ = bf16[4,4,64,128]{3,2,1,0:T(8,128)(2,1)S(1)} collective-permute-done((bf16[4,4,64,128]{3,2,1,0:T(8,128)(2,1)S(1)}, bf16[4,4,64,128]{3,2,1,0:T(8,128)(2,1)S(1)}, u32[]{:S(2)}, u32[]{:S(2)}) %collective-permute-start.6) | collective-permute-done | bytes 262176 | tf_op jit(solution)/shard_map/ppermute | solution.py:323
  28.3 2.5 %shard_map.162 = (bf16[4,512,256]{2,1,0:T(8,128)(2,1)S(1)}, f32[512,128]{1,0:T(8,128)S(1)}, f32[4,528,256]{2,1,0:T(8,128)S(1)}, f32[4,512,256]{2,1,0:T(8,128)S(1)}, f32[4,528,256]{2,1,0:T(8,128)S(1)}) custom-call(bf16[4,4,64,128]{3,2,1,0:T(8,128)(2,1)S(1)} %pad_maximum_fusion.refs_0_, bf16[4,4,64,128]{3,2,1,0:T(8,128)(2,1)S(1)} %collective-permute-done.5.refs_1_, ...), custom_call_target="tpu_custom_call" | custom-call | flops 1000 | bytes 1000 | tf_op jit(solution)/shard_map/pallas_call | solution.py:310
  30.9 4.6 %shard_map.163 = (bf16[2,512,256]{2,1,0:T(8,128)(2,1)S(1)}, bf16[2,512,256]{2,1,0:T(8,128)(2,1)S(1)}, bf16[2,256,256]{2,1,0:T(8,128)(2,1)S(1)}, bf16[4,512,256]{...) custom-call(f32[7,256]{1,0:T(8,128)S(1)} %concatenate.9.starts.refs_5_.scales, ...), custom_call_target="tpu_custom_call" | custom-call | flops 1000 | bytes 1000 | tf_op jit(solution)/shard_map/pallas_call | solution.py:310
  36.0 1.5 %collective-permute-start.13 = (bf16[2,256,256]{2,1,0:T(8,128)(2,1)S(1)}, bf16[2,256,256]{2,1,0:T(8,128)(2,1)S(1)}, u32[]{:S(2)}, u32[]{:S(2)}) collective-permute-start(bf16[2,256,256]{2,1,0:T(8,128)(2,1)S(1)} %get-tuple-element.101), channel_id=1, source_target_pairs={{0,2},{1,3},{2,0},{3,1},{4,6},{5,7},{6,4},{7,5},{8,10},{9,11},{10,... | collective-permute-start | bytes 786440 | tf_op jit(solution)/shard_map/ppermute | solution.py:323
  38.2 4.2 %shard_map.164.near = f32[3,4,512,256]{3,2,1,0:T(8,128)S(1)} custom-call(bf16[2,512,256]{2,1,0:T(8,128)(2,1)S(1)} %get-tuple-element.100.low.refs_0_, bf16[2,512,256]{2,1,0:T(8,128)(2,1)S(1)} %get-tuple-element.102.high.refs_1_, bf16[2,512,256]{2,1,0:T(8,128)(2,1)S(1)} %collective-permute-done.15.low_two.refs_2_, ...), custom_call_target="tpu_custom_call" | custom-call | flops 1000 | bytes 1000 | tf_op jit(solution)/shard_map/pallas_call | solution.py:310
  42.5 2.7 %collective-permute-done.13.picked.refs_5_ = bf16[2,256,256]{2,1,0:T(8,128)(2,1)S(1)} collective-permute-done((bf16[2,256,256]{2,1,0:T(8,128)(2,1)S(1)}, bf16[2,256,256]{2,1,0:T(8,128)(2,1)S(1)}, u32[]{:S(2)}, u32[]{:S(2)}) %collective-permute-start.13) | collective-permute-done | bytes 262176 | tf_op jit(solution)/shard_map/ppermute | solution.py:323
  45.2 1.6 %collective-permute-start.18 = (f32[2,32,256]{2,1,0:T(8,128)S(1)}, f32[2,32,256]{2,1,0:T(8,128)S(1)}, u32[]{:S(2)}, u32[]{:S(2)}) collective-permute-start(f32[2,32,256]{2,1,0:T(8,128)S(1)} %pad_maximum_fusion.2), channel_id=1, source_target_pairs={{0,4},{4,0},{8,12},{12,8},{16,20},{20,16},{24,28},{28,24},{1,5},{5... | collective-permute-start | bytes 196616 | tf_op jit(solution)/shard_map/ppermute | solution.py:323
  47.3 1.8 %shard_map.165.wings = bf16[2,9,256,256]{3,2,1,0:T(8,128)(2,1)S(1)} custom-call(bf16[3,3,1024,256]{3,2,1,0:T(8,128)(2,1)} %collective-permute-done.11.weight), custom_call_target="tpu_custom_call" | custom-call | flops 1000 | bytes 1000 | tf_op jit(solution)/shard_map/pallas_call | solution.py:310
  50.0 1.4 %collective-permute-start.19 = (f32[4,32,256]{2,1,0:T(8,128)S(1)}, f32[4,32,256]{2,1,0:T(8,128)S(1)}, u32[]{:S(2)}, u32[]{:S(2)}) collective-permute-start(f32[4,32,256]{2,1,0:T(8,128)S(1)} %pad_maximum_fusion.1), channel_id=1, source_target_pairs={{0,8},{4,12},{8,0},{12,4},{16,24},{20,28},{24,16},{28,20},{1,9},{5... | collective-permute-start | bytes 393224 | tf_op jit(solution)/shard_map/ppermute | solution.py:323
  51.4 1.0 shard_map.166.slope
  52.4 3.5 %collective-permute-done.12.far.refs_4_ = bf16[2,512,256]{2,1,0:T(8,128)(2,1)S(1)} collective-permute-done((bf16[2,512,256]{2,1,0:T(8,128)(2,1)S(1)}, bf16[2,512,256]{2,1,0:T(8,128)(2,1)S(1)}, u32[]{:S(2)}, u32[]{:S(2)}) %collective-permute-start.12) | collective-permute-done | bytes 524320 | tf_op jit(solution)/shard_map/ppermute | solution.py:323
  56.4 2.4 %shard_map.167.sums = f32[3,4,512,256]{3,2,1,0:T(8,128)S(1)} custom-call(bf16[2,512,256]{2,1,0:T(8,128)(2,1)S(1)} %collective-permute-done.12.far.refs_4_, bf16[2,256,256]{2,1,0:T(8,128)(2,1)S(1)} %collective-permute-done.13.picked.refs_5_, bf16[2,256,256]{2,1,0:T(8,128)(2,1)S(1)} %collective-permute-done.14.rest.refs_6_, ...), custom_call_target="tpu_custom_call" | custom-call | flops 1000 | bytes 1000 | tf_op jit(solution)/shard_map/pallas_call | solution.py:310
  58.8 8.0 %shard_map.168 = (f32[32,256]{1,0:T(8,128)}, bf16[4,512,256]{2,1,0:T(8,128)(2,1)S(1)}, f32[1,256]{1,0:T(1,128)}, f32[1,256]{1,0:T(1,128)}) custom-call(f32[7,256]{1,0:T(8,128)S(1)} %concatenate.9.starts.refs_5_.scales, f32[3,4,512,256]{3,2,1,0:T(8,128)S(1)} %shard_map.167.sums, bf16[2,512,256]{2,1,0:T(8,128)(2,1)S(1)} %collective-permute-done.20.far_two.refs_7_, ...), custom_call_target="tpu_custom_call" | custom-call | flops 1000 | bytes 1000 | tf_op jit(solution)/shard_map/pallas_call | solution.py:310
  67.7 1.0 shard_map.169.refs_11_
  69.5 1.0 shard_map.172
  70.6 1.6 %collective-permute-start.24 = (bf16[2,256,256]{2,1,0:T(8,128)(2,1)S(1)}, bf16[2,256,256]{2,1,0:T(8,128)(2,1)S(1)}, u32[]{:S(2)}, u32[]{:S(2)}) collective-permute-start(bf16[2,256,256]{2,1,0:T(8,128)(2,1)S(1)} %shard_map.172), channel_id=1, source_target_pairs={{0,2},{1,3},{2,0},{3,1},{4,6},{5,7},{6,4},{7,5},{8,10},{9,11},{10,... | collective-permute-start | bytes 786440 | tf_op jit(solution)/shard_map/ppermute | solution.py:323
  72.1 2.8 %shard_map.171 = bf16[2,512,256]{2,1,0:T(8,128)(2,1)S(1)} custom-call(f32[7,256]{1,0:T(8,128)S(1)} %concatenate.9.starts.refs_5_.scales, bf16[4,512,256]{2,1,0:T(8,128)(2,1)S(1)} %get-tuple-element.129.grad.one.refs_10_, bf16[4,512,256]{2,1,0:T(8,128)(2,1)S(1)} %collective-permute-done.22.two, bf16[3,3,1024,256]{3,2,1,0:T(8,128)(2,1)S(1)} %bitcast.20, ...), custom_call_target="tpu_custom_call" | custom-call | flops 1000 | bytes 1000 | tf_op jit(solution)/shard_map/pallas_call | solution.py:310
  74.9 5.1 %shard_map.173.mine = f32[4,512,256]{2,1,0:T(8,128)S(1)} custom-call(f32[7,256]{1,0:T(8,128)S(1)} %concatenate.9.starts.refs_5_.scales, bf16[4,512,256]{2,1,0:T(8,128)(2,1)S(1)} %get-tuple-element.129.grad.one.refs_10_, bf16[4,512,256]{2,1,0:T(8,128)(2,1)S(1)} %collective-permute-done.22.two, bf16[3,3,1024,256]{3,2,1,0:T(8,128)(2,1)S(1)} %bitcast.20, ...), custom_call_target="tpu_custom_call" | custom-call | flops 1000 | bytes 1000 | tf_op jit(solution)/shard_map/pallas_call | solution.py:310
  80.8 1.5 %collective-permute-start.25 = (bf16[2,256,256]{2,1,0:T(8,128)(2,1)S(1)}, bf16[2,256,256]{2,1,0:T(8,128)(2,1)S(1)}, u32[]{:S(2)}, u32[]{:S(2)}) collective-permute-start(bf16[2,256,256]{2,1,0:T(8,128)(2,1)S(1)} %collective-permute-done.24.picked), channel_id=1, source_target_pairs={{0,4},{4,0},{8,12},{12,8},{16,20},{20,16},{24,28},{28,24},{1,5},{5... | collective-permute-start | bytes 786440 | tf_op jit(solution)/shard_map/ppermute | solution.py:323
  82.3 10.6 %shard_map.174 = f32[9,1024,256]{2,1,0:T(8,128)} custom-call(bf16[2,512,256]{2,1,0:T(8,128)(2,1)S(1)} %get-tuple-element.100.low.refs_0_, bf16[2,512,256]{2,1,0:T(8,128)(2,1)S(1)} %get-tuple-element.102.high.refs_1_, bf16[2,512,256]{2,1,0:T(8,128)(2,1)S(1)} %collective-permute-done.15.low_two.refs_2_, ...), custom_call_target="tpu_custom_call" | custom-call | flops 1000 | bytes 1000 | tf_op jit(solution)/shard_map/pallas_call | solution.py:310
  92.8 1.7 %collective-permute-done.23.low = bf16[2,512,256]{2,1,0:T(8,128)(2,1)S(1)} collective-permute-done((bf16[2,512,256]{2,1,0:T(8,128)(2,1)S(1)}, bf16[2,512,256]{2,1,0:T(8,128)(2,1)S(1)}, u32[]{:S(2)}, u32[]{:S(2)}) %collective-permute-start.23) | collective-permute-done | bytes 524320 | tf_op jit(solution)/shard_map/ppermute | solution.py:323
  94.5 1.8 %shard_map.175 = (bf16[4,512,256]{2,1,0:T(8,128)(2,1)S(1)}, bf16[4,96,256]{2,1,0:T(8,128)(2,1)S(1)}, f32[1,256]{1,0:T(1,128)}, f32[1,256]{1,0:T(1,128)}) custom-call(f32[4,512,256]{2,1,0:T(8,128)S(1)} %shard_map.173.mine, bf16[2,512,256]{2,1,0:T(8,128)(2,1)S(1)} %collective-permute-done.23.low, bf16[2,256,256]{2,1,0:T(8,128)(2,1)S(1)} %collective-permute-done.24.picked, ...), custom_call_target="tpu_custom_call" | custom-call | flops 1000 | bytes 1000 | tf_op jit(solution)/shard_map/pallas_call | solution.py:310
  96.3 1.3 %shard_map.176.refs_3_ = bf16[2,4,512,256]{3,2,1,0:T(8,128)(2,1)S(1)} custom-call(f32[7,256]{1,0:T(8,128)S(1)} %concatenate.9.starts.refs_5_.scales, bf16[4,512,256]{2,1,0:T(8,128)(2,1)S(1)} %get-tuple-element.143.grad.refs_2_), custom_call_target="tpu_custom_call" | custom-call | flops 1000 | bytes 1000 | tf_op jit(solution)/shard_map/pallas_call | solution.py:310
  99.4 5.4 %shard_map.178 = f32[9,512,256]{2,1,0:T(8,128)} custom-call(bf16[4,512,256]{2,1,0:T(8,128)(2,1)S(1)} %get-tuple-element.148.refs_0_, bf16[4,512,256]{2,1,0:T(8,128)(2,1)S(1)} %get-tuple-element.149.refs_1_, bf16[4,512,256]{2,1,0:T(8,128)(2,1)S(1)} %get-tuple-element.143.grad.refs_2_, bf16[2,4,512,256]{3,2,1,0:T(8,128)(2,1)S(1)} %shard_map.176.refs_3_), custom_call_target="tpu_custom_call" | custom-call | flops 1000 | bytes 1000 | tf_op jit(solution)/shard_map/pallas_call | solution.py:310
  (72 shorter events, 13.7 us)
Async XLA Ops:
  0.6 30.2 %collective-permute-start.11 = (bf16[3,3,1024,256]{3,2,1,0:T(8,128)(2,1)}, bf16[3,3,1024,256]{3,2,1,0:T(8,128)(2,1)}, u32[]{:S(2)}, u32[]{:S(2)}) collective-permute-start(bf16[3,3,1024,256]{3,2,1,0:T(8,128)(2,1)} %weight.11), channel_id=1, source_target_pairs={{0,1},{1,0},{2,3},{3,2},{4,5},{5,4},{6,7},{7,6},{8,9},{9,8},{10,11... | collective-permute-start | bytes 14155784 | tf_op jit(solution)/shard_map/ppermute | solution.py:323
  2.7 7.7 %collective-permute-start.1 = (bf16[4,64,128]{2,1,0:T(8,128)(2,1)S(1)}, bf16[4,64,128]{2,1,0:T(8,128)(2,1)S(1)}, u32[]{:S(2)}, u32[]{:S(2)}) collective-permute-start(bf16[4,64,128]{2,1,0:T(8,128)(2,1)S(1)} %get-tuple-element.159), channel_id=1, source_target_pairs={{0,16},{4,20},{8,24},{12,28},{16,0},{20,4},{24,8},{28,12},{1,17},{... | collective-permute-start | bytes 196616 | tf_op jit(solution)/shard_map/ppermute | solution.py:323
  6.4 4.5 %collective-permute-start = (bf16[4,64,128]{2,1,0:T(8,128)(2,1)S(1)}, bf16[4,64,128]{2,1,0:T(8,128)(2,1)S(1)}, u32[]{:S(2)}, u32[]{:S(2)}) collective-permute-start(bf16[4,64,128]{2,1,0:T(8,128)(2,1)S(1)} %get-tuple-element.159), channel_id=1, source_target_pairs={{0,8},{4,12},{8,0},{12,4},{16,24},{20,28},{24,16},{28,20},{1,9},{5... | collective-permute-start | bytes 196616 | tf_op jit(solution)/shard_map/ppermute | solution.py:323
  8.0 6.1 %collective-permute-start.2 = (bf16[4,64,128]{2,1,0:T(8,128)(2,1)S(1)}, bf16[4,64,128]{2,1,0:T(8,128)(2,1)S(1)}, u32[]{:S(2)}, u32[]{:S(2)}) collective-permute-start(bf16[4,64,128]{2,1,0:T(8,128)(2,1)S(1)} %get-tuple-element.159), channel_id=1, source_target_pairs={{0,24},{4,28},{8,16},{12,20},{16,8},{20,12},{24,0},{28,4},{1,25},{... | collective-permute-start | bytes 196616 | tf_op jit(solution)/shard_map/ppermute | solution.py:323
  14.1 10.3 %collective-permute-start.3 = (bf16[4,4,64,128]{3,2,1,0:T(8,128)(2,1)S(1)}, bf16[4,4,64,128]{3,2,1,0:T(8,128)(2,1)S(1)}, u32[]{:S(2)}, u32[]{:S(2)}) collective-permute-start(bf16[4,4,64,128]{3,2,1,0:T(8,128)(2,1)S(1)} %pad_maximum_fusion.refs_0_), channel_id=1, source_target_pairs={{0,6},{1,7},{2,4},{3,5},{4,2},{5,3},{6,0},{7,1},{8,14},{9,15},{10,... | collective-permute-start | bytes 786440 | tf_op jit(solution)/shard_map/ppermute | solution.py:338
  16.6 11.1 %collective-permute-start.6 = (bf16[4,4,64,128]{3,2,1,0:T(8,128)(2,1)S(1)}, bf16[4,4,64,128]{3,2,1,0:T(8,128)(2,1)S(1)}, u32[]{:S(2)}, u32[]{:S(2)}) collective-permute-start(bf16[4,4,64,128]{3,2,1,0:T(8,128)(2,1)S(1)} %pad_maximum_fusion.refs_0_), channel_id=1, source_target_pairs={{0,2},{1,3},{2,0},{3,1},{4,6},{5,7},{6,4},{7,5},{8,10},{9,11},{10,... | collective-permute-start | bytes 786440 | tf_op jit(solution)/shard_map/ppermute | solution.py:323
  17.1 10.7 %collective-permute-start.5 = (bf16[4,4,64,128]{3,2,1,0:T(8,128)(2,1)S(1)}, bf16[4,4,64,128]{3,2,1,0:T(8,128)(2,1)S(1)}, u32[]{:S(2)}, u32[]{:S(2)}) collective-permute-start(bf16[4,4,64,128]{3,2,1,0:T(8,128)(2,1)S(1)} %pad_maximum_fusion.refs_0_), channel_id=1, source_target_pairs={{0,4},{4,0},{8,12},{12,8},{16,20},{20,16},{24,28},{28,24},{1,5},{5... | collective-permute-start | bytes 786440 | tf_op jit(solution)/shard_map/ppermute | solution.py:323
  17.6 5.0 %collective-permute-start.4 = (f32[1,32,256]{2,1,0:T(8,128)}, f32[1,32,256]{2,1,0:T(8,128)S(1)}, u32[]{:S(2)}, u32[]{:S(2)}) collective-permute-start(f32[1,32,256]{2,1,0:T(8,128)} %bitcast.21), channel_id=1, source_target_pairs={{0,16},{4,20},{8,24},{12,28},{16,0},{20,4},{24,8},{28,12},{1,17},{... | collective-permute-start | bytes 98312 | tf_op jit(solution)/shard_map/ppermute | solution.py:323
  22.7 8.2 %collective-permute-start.7 = (bf16[4,4,64,128]{3,2,1,0:T(8,128)(2,1)S(1)}, bf16[4,4,64,128]{3,2,1,0:T(8,128)(2,1)S(1)}, u32[]{:S(2)}, u32[]{:S(2)}) collective-permute-start(bf16[4,4,64,128]{3,2,1,0:T(8,128)(2,1)S(1)} %pad_maximum_fusion.refs_0_), channel_id=1, source_target_pairs={{0,1},{1,0},{2,3},{3,2},{4,5},{5,4},{6,7},{7,6},{8,9},{9,8},{10,11... | collective-permute-start | bytes 786440 | tf_op jit(solution)/shard_map/ppermute | solution.py:323
  27.7 3.2 %collective-permute-start.9 = (bf16[4,4,64,128]{3,2,1,0:T(8,128)(2,1)S(1)}, bf16[4,4,64,128]{3,2,1,0:T(8,128)(2,1)S(1)}, u32[]{:S(2)}, u32[]{:S(2)}) collective-permute-start(bf16[4,4,64,128]{3,2,1,0:T(8,128)(2,1)S(1)} %collective-permute-done.6.refs_2_), channel_id=1, source_target_pairs={{0,1},{1,0},{2,3},{3,2},{4,5},{5,4},{6,7},{7,6},{8,9},{9,8},{10,11... | collective-permute-start | bytes 786440 | tf_op jit(solution)/shard_map/ppermute | solution.py:323
  27.8 3.1 %collective-permute-start.8 = (bf16[4,4,64,128]{3,2,1,0:T(8,128)(2,1)S(1)}, bf16[4,4,64,128]{3,2,1,0:T(8,128)(2,1)S(1)}, u32[]{:S(2)}, u32[]{:S(2)}) collective-permute-start(bf16[4,4,64,128]{3,2,1,0:T(8,128)(2,1)S(1)} %collective-permute-done.5.refs_1_), channel_id=1, source_target_pairs={{0,1},{1,0},{2,3},{3,2},{4,5},{5,4},{6,7},{7,6},{8,9},{9,8},{10,11... | collective-permute-start | bytes 786440 | tf_op jit(solution)/shard_map/ppermute | solution.py:323
  28.2 2.7 %collective-permute-start.10 = (bf16[4,4,64,128]{3,2,1,0:T(8,128)(2,1)S(1)}, bf16[4,4,64,128]{3,2,1,0:T(8,128)(2,1)S(1)}, u32[]{:S(2)}, u32[]{:S(2)}) collective-permute-start(bf16[4,4,64,128]{3,2,1,0:T(8,128)(2,1)S(1)} %collective-permute-done.3.refs_3_), channel_id=1, source_target_pairs={{0,1},{1,0},{2,3},{3,2},{4,5},{5,4},{6,7},{7,6},{8,9},{9,8},{10,11... | collective-permute-start | bytes 786440 | tf_op jit(solution)/shard_map/ppermute | solution.py:323
  30.9 7.4 %slice-start = ((s8[4718592]{0:T(1024)(128)(4,1)}), s8[4194304]{0:T(1024)(128)(4,1)S(1)}, s32[]{:S(2)}) async-start(s8[4718592]{0:T(1024)(128)(4,1)} %bitcast.19), calls=%async_computation | async-start | bytes 8388608
  30.9 7.3 %slice-start.1 = ((s8[4718592]{0:T(1024)(128)(4,1)}), s8[524288]{0:T(1024)(128)(4,1)S(1)}, s32[]{:S(2)}) async-start(s8[4718592]{0:T(1024)(128)(4,1)} %bitcast.19), calls=%async_computation.1 | async-start | bytes 1048576
  35.5 2.6 %collective-permute-start.16 = (bf16[2,512,256]{2,1,0:T(8,128)(2,1)S(1)}, bf16[2,512,256]{2,1,0:T(8,128)(2,1)S(1)}, u32[]{:S(2)}, u32[]{:S(2)}) collective-permute-start(bf16[2,512,256]{2,1,0:T(8,128)(2,1)S(1)} %get-tuple-element.102.high.refs_1_), channel_id=1, source_target_pairs={{0,1},{1,0},{2,3},{3,2},{4,5},{5,4},{6,7},{7,6},{8,9},{9,8},{10,11... | collective-permute-start | bytes 1572872 | tf_op jit(solution)/shard_map/ppermute | solution.py:323
  35.9 2.3 %collective-permute-start.15 = (bf16[2,512,256]{2,1,0:T(8,128)(2,1)S(1)}, bf16[2,512,256]{2,1,0:T(8,128)(2,1)S(1)}, u32[]{:S(2)}, u32[]{:S(2)}) collective-permute-start(bf16[2,512,256]{2,1,0:T(8,128)(2,1)S(1)} %get-tuple-element.100.low.refs_0_), channel_id=1, source_target_pairs={{0,1},{1,0},{2,3},{3,2},{4,5},{5,4},{6,7},{7,6},{8,9},{9,8},{10,11... | collective-permute-start | bytes 1572872 | tf_op jit(solution)/shard_map/ppermute | solution.py:323
  36.0 9.1 %copy-start.1 = (f32[32,256]{1,0:T(8,128)S(1)}, f32[32,256]{1,0:T(8,128)}, u32[]{:S(2)}) copy-start(f32[32,256]{1,0:T(8,128)} %param.19) | copy-start | bytes 98308
  36.0 9.1 %collective-permute-start.13 = (bf16[2,256,256]{2,1,0:T(8,128)(2,1)S(1)}, bf16[2,256,256]{2,1,0:T(8,128)(2,1)S(1)}, u32[]{:S(2)}, u32[]{:S(2)}) collective-permute-start(bf16[2,256,256]{2,1,0:T(8,128)(2,1)S(1)} %get-tuple-element.101), channel_id=1, source_target_pairs={{0,2},{1,3},{2,0},{3,1},{4,6},{5,7},{6,4},{7,5},{8,10},{9,11},{10,... | collective-permute-start | bytes 786440 | tf_op jit(solution)/shard_map/ppermute | solution.py:323
  37.5 18.4 %collective-permute-start.12 = (bf16[2,512,256]{2,1,0:T(8,128)(2,1)S(1)}, bf16[2,512,256]{2,1,0:T(8,128)(2,1)S(1)}, u32[]{:S(2)}, u32[]{:S(2)}) collective-permute-start(bf16[2,512,256]{2,1,0:T(8,128)(2,1)S(1)} %get-tuple-element.100.low.refs_0_), channel_id=1, source_target_pairs={{0,2},{1,3},{2,0},{3,1},{4,6},{5,7},{6,4},{7,5},{8,10},{9,11},{10,... | collective-permute-start | bytes 1572872 | tf_op jit(solution)/shard_map/ppermute | solution.py:323
  45.2 4.8 %collective-permute-start.17 = (bf16[2,256,256]{2,1,0:T(8,128)(2,1)S(1)}, bf16[2,256,256]{2,1,0:T(8,128)(2,1)S(1)}, u32[]{:S(2)}, u32[]{:S(2)}) collective-permute-start(bf16[2,256,256]{2,1,0:T(8,128)(2,1)S(1)} %collective-permute-done.13.picked.refs_5_), channel_id=1, source_target_pairs={{0,1},{1,0},{2,3},{3,2},{4,5},{5,4},{6,7},{7,6},{8,9},{9,8},{10,11... | collective-permute-start | bytes 786440 | tf_op jit(solution)/shard_map/ppermute | solution.py:323
  45.2 4.8 %collective-permute-start.18 = (f32[2,32,256]{2,1,0:T(8,128)S(1)}, f32[2,32,256]{2,1,0:T(8,128)S(1)}, u32[]{:S(2)}, u32[]{:S(2)}) collective-permute-start(f32[2,32,256]{2,1,0:T(8,128)S(1)} %pad_maximum_fusion.2), channel_id=1, source_target_pairs={{0,4},{4,0},{8,12},{12,8},{16,20},{20,16},{24,28},{28,24},{1,5},{5... | collective-permute-start | bytes 196616 | tf_op jit(solution)/shard_map/ppermute | solution.py:323
  46.7 9.2 %collective-permute-start.14 = (bf16[2,256,256]{2,1,0:T(8,128)(2,1)S(1)}, bf16[2,256,256]{2,1,0:T(8,128)(2,1)S(1)}, u32[]{:S(2)}, u32[]{:S(2)}) collective-permute-start(bf16[2,256,256]{2,1,0:T(8,128)(2,1)S(1)} %collective-permute-done.13.picked.refs_5_), channel_id=1, source_target_pairs={{0,4},{4,0},{8,12},{12,8},{16,20},{20,16},{24,28},{28,24},{1,5},{5... | collective-permute-start | bytes 786440 | tf_op jit(solution)/shard_map/ppermute | solution.py:323
  50.0 5.9 %collective-permute-start.19 = (f32[4,32,256]{2,1,0:T(8,128)S(1)}, f32[4,32,256]{2,1,0:T(8,128)S(1)}, u32[]{:S(2)}, u32[]{:S(2)}) collective-permute-start(f32[4,32,256]{2,1,0:T(8,128)S(1)} %pad_maximum_fusion.1), channel_id=1, source_target_pairs={{0,8},{4,12},{8,0},{12,4},{16,24},{20,28},{24,16},{28,20},{1,9},{5... | collective-permute-start | bytes 393224 | tf_op jit(solution)/shard_map/ppermute | solution.py:323
  55.9 2.9 %collective-permute-start.20 = (bf16[2,512,256]{2,1,0:T(8,128)(2,1)S(1)}, bf16[2,512,256]{2,1,0:T(8,128)(2,1)S(1)}, u32[]{:S(2)}, u32[]{:S(2)}) collective-permute-start(bf16[2,512,256]{2,1,0:T(8,128)(2,1)S(1)} %collective-permute-done.12.far.refs_4_), channel_id=1, source_target_pairs={{0,1},{1,0},{2,3},{3,2},{4,5},{5,4},{6,7},{7,6},{8,9},{9,8},{10,11... | collective-permute-start | bytes 1572872 | tf_op jit(solution)/shard_map/ppermute | solution.py:323
  55.9 2.9 %collective-permute-start.21 = (bf16[2,256,256]{2,1,0:T(8,128)(2,1)S(1)}, bf16[2,256,256]{2,1,0:T(8,128)(2,1)S(1)}, u32[]{:S(2)}, u32[]{:S(2)}) collective-permute-start(bf16[2,256,256]{2,1,0:T(8,128)(2,1)S(1)} %collective-permute-done.14.rest.refs_6_), channel_id=1, source_target_pairs={{0,1},{1,0},{2,3},{3,2},{4,5},{5,4},{6,7},{7,6},{8,9},{9,8},{10,11... | collective-permute-start | bytes 786440 | tf_op jit(solution)/shard_map/ppermute | solution.py:323
  66.8 2.7 %collective-permute-start.22 = (bf16[4,512,256]{2,1,0:T(8,128)(2,1)S(1)}, bf16[4,512,256]{2,1,0:T(8,128)(2,1)S(1)}, u32[]{:S(2)}, u32[]{:S(2)}) collective-permute-start(bf16[4,512,256]{2,1,0:T(8,128)(2,1)S(1)} %get-tuple-element.129.grad.one.refs_10_), channel_id=1, source_target_pairs={{0,1},{1,0},{2,3},{3,2},{4,5},{5,4},{6,7},{7,6},{8,9},{9,8},{10,11... | collective-permute-start | bytes 3145736 | tf_op jit(solution)/shard_map/ppermute | solution.py:323
  70.6 9.5 %collective-permute-start.24 = (bf16[2,256,256]{2,1,0:T(8,128)(2,1)S(1)}, bf16[2,256,256]{2,1,0:T(8,128)(2,1)S(1)}, u32[]{:S(2)}, u32[]{:S(2)}) collective-permute-start(bf16[2,256,256]{2,1,0:T(8,128)(2,1)S(1)} %shard_map.172), channel_id=1, source_target_pairs={{0,2},{1,3},{2,0},{3,1},{4,6},{5,7},{6,4},{7,5},{8,10},{9,11},{10,... | collective-permute-start | bytes 786440 | tf_op jit(solution)/shard_map/ppermute | solution.py:323
  80.1 14.4 %collective-permute-start.26 = (bf16[3,3,512,256]{3,2,1,0:T(8,128)(2,1)S(1)}, bf16[3,3,512,256]{3,2,1,0:T(8,128)(2,1)S(1)}, u32[]{:S(2)}, u32[]{:S(2)}) collective-permute-start(bf16[3,3,512,256]{3,2,1,0:T(8,128)(2,1)S(1)} %shard_map.161.refs_4_.weight), channel_id=1, source_target_pairs={{0,1},{1,0},{2,3},{3,2},{4,5},{5,4},{6,7},{7,6},{8,9},{9,8},{10,11... | collective-permute-start | bytes 7077896 | tf_op jit(solution)/shard_map/ppermute | solution.py:323
  80.2 14.3 %collective-permute-start.23 = (bf16[2,512,256]{2,1,0:T(8,128)(2,1)S(1)}, bf16[2,512,256]{2,1,0:T(8,128)(2,1)S(1)}, u32[]{:S(2)}, u32[]{:S(2)}) collective-permute-start(bf16[2,512,256]{2,1,0:T(8,128)(2,1)S(1)} %shard_map.171), channel_id=1, source_target_pairs={{0,2},{1,3},{2,0},{3,1},{4,6},{5,7},{6,4},{7,5},{8,10},{9,11},{10,... | collective-permute-start | bytes 1572872 | tf_op jit(solution)/shard_map/ppermute | solution.py:323
  80.8 12.1 %collective-permute-start.25 = (bf16[2,256,256]{2,1,0:T(8,128)(2,1)S(1)}, bf16[2,256,256]{2,1,0:T(8,128)(2,1)S(1)}, u32[]{:S(2)}, u32[]{:S(2)}) collective-permute-start(bf16[2,256,256]{2,1,0:T(8,128)(2,1)S(1)} %collective-permute-done.24.picked), channel_id=1, source_target_pairs={{0,4},{4,0},{8,12},{12,8},{16,20},{20,16},{24,28},{28,24},{1,5},{5... | collective-permute-start | bytes 786440 | tf_op jit(solution)/shard_map/ppermute | solution.py:323
  96.3 1.4 %collective-permute-start.27 = (bf16[4,96,256]{2,1,0:T(8,128)(2,1)S(1)}, bf16[4,96,256]{2,1,0:T(8,128)(2,1)S(1)}, u32[]{:S(2)}, u32[]{:S(2)}) collective-permute-start(bf16[4,96,256]{2,1,0:T(8,128)(2,1)S(1)} %get-tuple-element.142.one), channel_id=1, source_target_pairs={{0,1},{1,0},{2,3},{3,2},{4,5},{5,4},{6,7},{7,6},{8,9},{9,8},{10,11... | collective-permute-start | bytes 589832 | tf_op jit(solution)/shard_map/ppermute | solution.py:323
  98.8 6.0 %collective-permute-start.28 = (f32[4,64,128]{2,1,0:T(8,128)S(1)}, f32[4,64,128]{2,1,0:T(8,128)S(1)}, u32[]{:S(2)}, u32[]{:S(2)}) collective-permute-start(f32[4,64,128]{2,1,0:T(8,128)S(1)} %get-tuple-element.147), channel_id=1, source_target_pairs={{0,2},{1,3},{2,0},{3,1},{4,6},{5,7},{6,4},{7,5},{8,10},{9,11},{10,... | collective-permute-start | bytes 393224 | tf_op jit(solution)/shard_map/ppermute | solution.py:323
  (6 other events, 5.2 us)

commit v7 on v6

--- a/solution.py
+++ b/solution.py
@@ -614,15 +614,11 @@
             target[m, at : at + total] = acc
 
 
-def join_halves(pair, joint, sems):
+def join_halves(pair, joint):
     side = lax.axis_index("tm") % 2
     half = pair[0].shape[1]
-    copies = []
-    for i, (part, begin) in enumerate(zip(pair, (side, 1 - side))):
-        rows = pl.ds(pl.multiple_of(begin * half, half), half)
-        copies.append(pltpu.make_async_copy(part, joint.at[:, rows], sems.at[i]))
-        copies[-1].start()
-    return copies
+    for part, begin in zip(pair, (side, 1 - side)):
+        joint[:, pl.ds(pl.multiple_of(begin * half, half), half)] = part[...]
 
 
 def group_starts(bits, width):
@@ -653,11 +649,9 @@
     )[0]
 
 
-def far_kernel(far, picked, rest, weight, near, sums, joint, sems):
+def far_kernel(far, picked, rest, weight, near, sums, joint):
     half, _, width = far.shape
-    copies = join_halves((picked, rest), joint, sems)
-    for copy in copies:
-        copy.wait()
+    join_halves((picked, rest), joint)
     fields = [[a.at[k] for a in (far, joint) for k in range(half)]]
     targets = [(sums.at[a], 0) for a in range(3)]
     group_sums(fields, weight, group_starts((2,), width), targets, near)
@@ -670,7 +664,7 @@
         [whole_spec()] * 5,
         [(near.shape, f32)],
         [whole_spec()],
-        [pltpu.VMEM(far.shape, bf16), pltpu.SemaphoreType.DMA((2,))],
+        [pltpu.VMEM(far.shape, bf16)],
         0,
         8,
     )[0]
@@ -695,8 +689,8 @@
 def second_kernel(
     starts, sums, far_two, picked_two, rest_two, weight, keep, scales, *refs
 ):
-    cotangents, (readout, grad, gain_grad, shift_grad) = refs[:-14], refs[-14:-10]
-    middle, slope, lower, upper, joint, hold, wide, full, sems, joint_sems = refs[-10:]
+    cotangents, (readout, grad, gain_grad, shift_grad) = refs[:-13], refs[-13:-9]
+    middle, slope, lower, upper, joint, hold, wide, full, sems = refs[-9:]
     mel_count, total, width = middle.shape
     half = mel_count // 2
     place = lax.axis_index("tm")
@@ -717,10 +711,8 @@
     for copy in copies:
         copy.start()
 
-    halves = join_halves((picked_two, rest_two), joint, joint_sems)
+    join_halves((picked_two, rest_two), joint)
     clear_edges(lower, upper, total)
-    for copy in halves:
-        copy.wait()
     fields = [[a.at[k] for a in (far_two, joint) for k in range(half)]]
     targets = ((lower, TILE), (middle, 0), (upper, TILE))
     group_sums(fields, weight, group_starts((3,), width), targets, sums)
@@ -841,7 +833,6 @@
             pltpu.VMEM((total // 2, width), f32),
             pltpu.VMEM((total // 2, width), f32),
             pltpu.SemaphoreType.DMA((sum(part.shape[0] for part in cotangents),)),
-            pltpu.SemaphoreType.DMA((2,)),
         ],
         0,
         20,
@@ -1027,7 +1018,7 @@
 
 
 def norm_kernel(mine, low, picked, rest, slope, pre, stats, scales, keep, *refs):
-    grad, window, gain_grad, shift_grad, padded = refs
+    grad, window, gain_grad, shift_grad, padded, held = refs
     mel_count, total, width = mine.shape
     center, inverse, pixels = stats[0:1], stats[1:2], stats[2:3]
     blank = jnp.zeros((TILE, width), f32)
@@ -1045,7 +1036,7 @@
             for k, m in enumerate(mels):
                 rows = mine[m, place_rows] + field[k, pl.ds(at, ROWS)].astype(f32)
                 step = rows * slope[m, place_rows]
-                mine[m, place_rows] = step
+                held[m, place_rows] = step
                 plain = plain + fold(step)
                 along = along + fold(step * ((pre[m, place_rows] - center) * inverse))
             return plain, along
@@ -1074,7 +1065,7 @@
         mask = widen(keep[pl.ds(at, ROWS)], width)
         for m in range(mel_count):
             normed = (pre[m, pl.ds(at, ROWS)] - center) * inverse
-            rows = mine[m, pl.ds(at, ROWS)] - plain - normed * along
+            rows = held[m, pl.ds(at, ROWS)] - plain - normed * along
             rows = (mask * (scale * rows)).astype(bf16)
             grad[m, pl.ds(at, ROWS)] = rows
             padded[m, pl.ds(pl.multiple_of(at + edge, 16), ROWS)] = rows
@@ -1099,7 +1090,7 @@
             ((1, width), f32),
         ],
         [whole_spec()] * 4,
-        [pltpu.VMEM((mel_count, total + 2 * edge, width), bf16)],
+        [pltpu.VMEM((mel_count, total + 2 * edge, width), bf16), pltpu.VMEM(mine.shape, f32)],
         2**28,
         12,
     )
@@ -1283,26 +1274,30 @@
     )
 
 
-def close_kernel(mine, other, keep, out):
+def close_kernel(mine, other, keep, *refs):
+    count = len(refs) // 2
+    small, out, small_out = refs[:count], refs[count], refs[count + 1 :]
     mel_count, frames, lanes = mine.shape
     begin = pl.multiple_of(lax.axis_index("tm") * frames, frames)
     mask = keep[pl.ds(begin, frames)]
     for m in range(mel_count):
         out[:, m, :] = (mine[m] + other[m]) * mask
-
-
-def close(mine, other, keep):
+    for source, target in zip(small, small_out):
+        target[...] = source[...]
+
+
+def close(mine, other, keep, small):
     mel_count, frames, lanes = mine.shape
     return call(
         close_kernel,
-        (mine, other, keep),
-        [whole_spec()] * 3,
-        [((frames, mel_count, lanes), f32)],
-        [whole_spec()],
+        (mine, other, keep, *small),
+        [whole_spec()] * (3 + len(small)),
+        [((frames, mel_count, lanes), f32)] + [(a.shape, f32) for a in small],
+        [whole_spec()] * (1 + len(small)),
         [],
         0,
         4,
-    )[0]
+    )
 
 
 def whole_frames(
@@ -1430,9 +1425,15 @@
     layout = [(bits, [(i, m, 0) for m in range(mel_count)]) for i, bits in enumerate(((0, 2), (1, 3)))]
     weight1_grad = weight_back(layout, (), fields1, grad1, steps1, conv1_weight.shape[2])
     input_came, weight1_grad = lax.optimization_barrier((input_came, weight1_grad))
+    input_grad, readout, gain1_grad, shift1_grad, gain2_grad, shift2_grad = close(
+        input_mine,
+        input_came,
+        keep,
+        (readout, gain1_grad, shift1_grad, gain2_grad, shift2_grad),
+    )
     return (
         readout,
-        close(input_mine, input_came, keep),
+        input_grad,
         weight1_grad,
         gain1_grad[0],
         shift1_grad[0],

time: 106 us -> 105 us (level)
  Pallas kernels: 56.2 us -> 54.7 us
    pallas_call x19, Pallas kernels: 56.2 us -> 54.7 us  [call(): pl.pallas_call(body, out_shape=tuple((jax.ShapeDtypeStruct(s, d) for s, d...]
where the time goes in v7:
time: 105 us; the launch traced here: 104 us
  Pallas kernels  54.7 us (52%)
  starting transfers between devices  22.9 us (22%)
  waiting for transfers between devices  21.8 us (21%)
  local copies, waits for them, and re-layouts  2.25 us (2%)
  other arithmetic  1.64 us (2%)
    pallas_call x19, Pallas kernels, call(): pl.pallas_call(body, out_shape=tuple((jax.ShapeDtypeStruct(s, d) for s, d...  54.7 us
    ppermute x28, starting transfers between devices, swap(): return lax.ppermute(shard, axis, [(i, i ^ bit) for i in range(count)])  20.4 us
    ppermute x28, waiting for transfers between devices, swap(): return lax.ppermute(shard, axis, [(i, i ^ bit) for i in range(count)])  20.2 us
    ppermute x1, starting transfers between devices, swap_both(): return lax.ppermute(shard, (first, second), pairs)  2.51 us
    unnamed x18, local copies, waits for them, and re-layouts  2.15 us
  transfers between devices with their start and end apart: 29, of which 14 were waited for; matrix products, arithmetic and copies ran while one was open for 2% of the time, Pallas kernels for 37%

profile of v7, /device:TPU:0, one launch (start us, length us, event | category | flops | bytes accessed | tf_op | source)
XLA Modules:
  0.0 104.3 jit_solution(2575442786174428585)
XLA Ops:
  2.7 3.7 %collective-permute-start.1 = (bf16[4,64,128]{2,1,0:T(8,128)(2,1)S(1)}, bf16[4,64,128]{2,1,0:T(8,128)(2,1)S(1)}, u32[]{:S(2)}, u32[]{:S(2)}) collective-permute-start(bf16[4,64,128]{2,1,0:T(8,128)(2,1)S(1)} %get-tuple-element.171), channel_id=1, source_target_pairs={{0,16},{4,20},{8,24},{12,28},{16,0},{20,4},{24,8},{28,12},{1,17},{... | collective-permute-start | bytes 196616 | tf_op jit(solution)/shard_map/ppermute | solution.py:323
  6.4 1.6 %collective-permute-start = (bf16[4,64,128]{2,1,0:T(8,128)(2,1)S(1)}, bf16[4,64,128]{2,1,0:T(8,128)(2,1)S(1)}, u32[]{:S(2)}, u32[]{:S(2)}) collective-permute-start(bf16[4,64,128]{2,1,0:T(8,128)(2,1)S(1)} %get-tuple-element.171), channel_id=1, source_target_pairs={{0,8},{4,12},{8,0},{12,4},{16,24},{20,28},{24,16},{28,20},{1,9},{5... | collective-permute-start | bytes 196616 | tf_op jit(solution)/shard_map/ppermute | solution.py:323
  8.0 2.5 %collective-permute-done.1 = bf16[4,64,128]{2,1,0:T(8,128)(2,1)S(1)} collective-permute-done((bf16[4,64,128]{2,1,0:T(8,128)(2,1)S(1)}, bf16[4,64,128]{2,1,0:T(8,128)(2,1)S(1)}, u32[]{:S(2)}, u32[]{:S(2)}) %collective-permute-start.1) | collective-permute-done | bytes 65568 | tf_op jit(solution)/shard_map/ppermute | solution.py:323
  10.9 3.1 %collective-permute-done.2 = bf16[4,64,128]{2,1,0:T(8,128)(2,1)S(1)} collective-permute-done((bf16[4,64,128]{2,1,0:T(8,128)(2,1)S(1)}, bf16[4,64,128]{2,1,0:T(8,128)(2,1)S(1)}, u32[]{:S(2)}, u32[]{:S(2)}) %collective-permute-start.2) | collective-permute-done | bytes 65568 | tf_op jit(solution)/shard_map/ppermute | solution.py:323
  14.1 2.5 %collective-permute-start.3 = (bf16[4,4,64,128]{3,2,1,0:T(8,128)(2,1)S(1)}, bf16[4,4,64,128]{3,2,1,0:T(8,128)(2,1)S(1)}, u32[]{:S(2)}, u32[]{:S(2)}) collective-permute-start(bf16[4,4,64,128]{3,2,1,0:T(8,128)(2,1)S(1)} %pad_maximum_fusion.refs_0_), channel_id=1, source_target_pairs={{0,6},{1,7},{2,4},{3,5},{4,2},{5,3},{6,0},{7,1},{8,14},{9,15},{10,... | collective-permute-start | bytes 786440 | tf_op jit(solution)/shard_map/ppermute | solution.py:338
  17.6 2.0 %collective-permute-start.4 = (f32[1,32,256]{2,1,0:T(8,128)}, f32[1,32,256]{2,1,0:T(8,128)S(1)}, u32[]{:S(2)}, u32[]{:S(2)}) collective-permute-start(f32[1,32,256]{2,1,0:T(8,128)} %bitcast.21), channel_id=1, source_target_pairs={{0,16},{4,20},{8,24},{12,28},{16,0},{20,4},{24,8},{28,12},{1,17},{... | collective-permute-start | bytes 98312 | tf_op jit(solution)/shard_map/ppermute | solution.py:323
  19.6 1.7 %copy-done = bf16[3,3,512,256]{3,2,1,0:T(8,128)(2,1)S(1)} copy-done((bf16[3,3,512,256]{3,2,1,0:T(8,128)(2,1)S(1)}, bf16[3,3,512,256]{3,2,1,0:T(8,128)(2,1)}, u32[]{:S(2)}) %copy-start) | copy-done | bytes 2359320
  22.7 1.7 %collective-permute-done.3.refs_3_ = bf16[4,4,64,128]{3,2,1,0:T(8,128)(2,1)S(1)} collective-permute-done((bf16[4,4,64,128]{3,2,1,0:T(8,128)(2,1)S(1)}, bf16[4,4,64,128]{3,2,1,0:T(8,128)(2,1)S(1)}, u32[]{:S(2)}, u32[]{:S(2)}) %collective-permute-start.3) | collective-permute-done | bytes 262176 | tf_op jit(solution)/shard_map/ppermute | solution.py:338
  24.3 3.3 %collective-permute-done.6.refs_2_ = bf16[4,4,64,128]{3,2,1,0:T(8,128)(2,1)S(1)} collective-permute-done((bf16[4,4,64,128]{3,2,1,0:T(8,128)(2,1)S(1)}, bf16[4,4,64,128]{3,2,1,0:T(8,128)(2,1)S(1)}, u32[]{:S(2)}, u32[]{:S(2)}) %collective-permute-start.6) | collective-permute-done | bytes 262176 | tf_op jit(solution)/shard_map/ppermute | solution.py:323
  28.3 2.5 %shard_map.162 = (bf16[4,512,256]{2,1,0:T(8,128)(2,1)S(1)}, f32[512,128]{1,0:T(8,128)S(1)}, f32[4,528,256]{2,1,0:T(8,128)S(1)}, f32[4,512,256]{2,1,0:T(8,128)S(1)}, f32[4,528,256]{2,1,0:T(8,128)S(1)}) custom-call(bf16[4,4,64,128]{3,2,1,0:T(8,128)(2,1)S(1)} %pad_maximum_fusion.refs_0_, bf16[4,4,64,128]{3,2,1,0:T(8,128)(2,1)S(1)} %collective-permute-done.5.refs_1_, ...), custom_call_target="tpu_custom_call" | custom-call | flops 1000 | bytes 1000 | tf_op jit(solution)/shard_map/pallas_call | solution.py:310
  30.9 4.5 %shard_map.163 = (bf16[2,512,256]{2,1,0:T(8,128)(2,1)S(1)}, bf16[2,512,256]{2,1,0:T(8,128)(2,1)S(1)}, bf16[2,256,256]{2,1,0:T(8,128)(2,1)S(1)}, bf16[4,512,256]{...) custom-call(f32[7,256]{1,0:T(8,128)S(1)} %concatenate.9.starts.refs_5_.scales, ...), custom_call_target="tpu_custom_call" | custom-call | flops 1000 | bytes 1000 | tf_op jit(solution)/shard_map/pallas_call | solution.py:310
  36.0 1.5 %collective-permute-start.13 = (bf16[2,256,256]{2,1,0:T(8,128)(2,1)S(1)}, bf16[2,256,256]{2,1,0:T(8,128)(2,1)S(1)}, u32[]{:S(2)}, u32[]{:S(2)}) collective-permute-start(bf16[2,256,256]{2,1,0:T(8,128)(2,1)S(1)} %get-tuple-element.107), channel_id=1, source_target_pairs={{0,2},{1,3},{2,0},{3,1},{4,6},{5,7},{6,4},{7,5},{8,10},{9,11},{10,... | collective-permute-start | bytes 786440 | tf_op jit(solution)/shard_map/ppermute | solution.py:323
  38.2 4.2 %shard_map.164.near = f32[3,4,512,256]{3,2,1,0:T(8,128)S(1)} custom-call(bf16[2,512,256]{2,1,0:T(8,128)(2,1)S(1)} %get-tuple-element.106.low.refs_0_, bf16[2,512,256]{2,1,0:T(8,128)(2,1)S(1)} %get-tuple-element.108.high.refs_1_, bf16[2,512,256]{2,1,0:T(8,128)(2,1)S(1)} %collective-permute-done.15.low_two.refs_2_, ...), custom_call_target="tpu_custom_call" | custom-call | flops 1000 | bytes 1000 | tf_op jit(solution)/shard_map/pallas_call | solution.py:310
  42.4 2.7 %collective-permute-done.13.picked.refs_5_ = bf16[2,256,256]{2,1,0:T(8,128)(2,1)S(1)} collective-permute-done((bf16[2,256,256]{2,1,0:T(8,128)(2,1)S(1)}, bf16[2,256,256]{2,1,0:T(8,128)(2,1)S(1)}, u32[]{:S(2)}, u32[]{:S(2)}) %collective-permute-start.13) | collective-permute-done | bytes 262176 | tf_op jit(solution)/shard_map/ppermute | solution.py:323
  45.1 1.6 %collective-permute-start.18 = (f32[2,32,256]{2,1,0:T(8,128)S(1)}, f32[2,32,256]{2,1,0:T(8,128)S(1)}, u32[]{:S(2)}, u32[]{:S(2)}) collective-permute-start(f32[2,32,256]{2,1,0:T(8,128)S(1)} %pad_maximum_fusion.2), channel_id=1, source_target_pairs={{0,4},{4,0},{8,12},{12,8},{16,20},{20,16},{24,28},{28,24},{1,5},{5... | collective-permute-start | bytes 196616 | tf_op jit(solution)/shard_map/ppermute | solution.py:323
  47.2 1.8 %shard_map.165.wings = bf16[2,9,256,256]{3,2,1,0:T(8,128)(2,1)S(1)} custom-call(bf16[3,3,1024,256]{3,2,1,0:T(8,128)(2,1)} %collective-permute-done.11.weight), custom_call_target="tpu_custom_call" | custom-call | flops 1000 | bytes 1000 | tf_op jit(solution)/shard_map/pallas_call | solution.py:310
  49.9 1.4 %collective-permute-start.19 = (f32[4,32,256]{2,1,0:T(8,128)S(1)}, f32[4,32,256]{2,1,0:T(8,128)S(1)}, u32[]{:S(2)}, u32[]{:S(2)}) collective-permute-start(f32[4,32,256]{2,1,0:T(8,128)S(1)} %pad_maximum_fusion.1), channel_id=1, source_target_pairs={{0,8},{4,12},{8,0},{12,4},{16,24},{20,28},{24,16},{28,20},{1,9},{5... | collective-permute-start | bytes 393224 | tf_op jit(solution)/shard_map/ppermute | solution.py:323
  51.3 1.0 shard_map.166.slope
  52.4 3.5 %collective-permute-done.12.far.refs_4_ = bf16[2,512,256]{2,1,0:T(8,128)(2,1)S(1)} collective-permute-done((bf16[2,512,256]{2,1,0:T(8,128)(2,1)S(1)}, bf16[2,512,256]{2,1,0:T(8,128)(2,1)S(1)}, u32[]{:S(2)}, u32[]{:S(2)}) %collective-permute-start.12) | collective-permute-done | bytes 524320 | tf_op jit(solution)/shard_map/ppermute | solution.py:323
  56.4 2.2 %shard_map.167.sums = f32[3,4,512,256]{3,2,1,0:T(8,128)S(1)} custom-call(bf16[2,512,256]{2,1,0:T(8,128)(2,1)S(1)} %collective-permute-done.12.far.refs_4_, bf16[2,256,256]{2,1,0:T(8,128)(2,1)S(1)} %collective-permute-done.13.picked.refs_5_, bf16[2,256,256]{2,1,0:T(8,128)(2,1)S(1)} %collective-permute-done.14.rest.refs_6_, ...), custom_call_target="tpu_custom_call" | custom-call | flops 1000 | bytes 1000 | tf_op jit(solution)/shard_map/pallas_call | solution.py:310
  58.6 7.3 %shard_map.168 = (f32[32,256]{1,0:T(8,128)S(1)}, bf16[4,512,256]{2,1,0:T(8,128)(2,1)S(1)}, f32[1,256]{1,0:T(1,128)S(1)}, f32[1,256]{1,0:T(1,128)S(1)}) custom-call(f32[7,256]{1,0:T(8,128)S(1)} %concatenate.9.starts.refs_5_.scales, f32[3,4,512,256]{3,2,1,0:T(8,128)S(1)} %shard_map.167.sums, bf16[2,512,256]{2,1,0:T(8,128)(2,1)S(1)} %collective-permute-done.20.far_two.refs_7_, ...), custom_call_target="tpu_custom_call" | custom-call | flops 1000 | bytes 1000 | tf_op jit(solution)/shard_map/pallas_call | solution.py:310
  66.8 1.0 shard_map.169.refs_11_
  68.6 1.0 shard_map.172
  69.7 1.6 %collective-permute-start.24 = (bf16[2,256,256]{2,1,0:T(8,128)(2,1)S(1)}, bf16[2,256,256]{2,1,0:T(8,128)(2,1)S(1)}, u32[]{:S(2)}, u32[]{:S(2)}) collective-permute-start(bf16[2,256,256]{2,1,0:T(8,128)(2,1)S(1)} %shard_map.172), channel_id=1, source_target_pairs={{0,2},{1,3},{2,0},{3,1},{4,6},{5,7},{6,4},{7,5},{8,10},{9,11},{10,... | collective-permute-start | bytes 786440 | tf_op jit(solution)/shard_map/ppermute | solution.py:323
  71.2 2.8 %shard_map.171 = bf16[2,512,256]{2,1,0:T(8,128)(2,1)S(1)} custom-call(f32[7,256]{1,0:T(8,128)S(1)} %concatenate.9.starts.refs_5_.scales, bf16[4,512,256]{2,1,0:T(8,128)(2,1)S(1)} %get-tuple-element.134.grad.one.refs_10_, bf16[4,512,256]{2,1,0:T(8,128)(2,1)S(1)} %collective-permute-done.22.two, bf16[3,3,1024,256]{3,2,1,0:T(8,128)(2,1)S(1)} %bitcast.20, ...), custom_call_target="tpu_custom_call" | custom-call | flops 1000 | bytes 1000 | tf_op jit(solution)/shard_map/pallas_call | solution.py:310
  74.0 5.2 %shard_map.173.mine = f32[4,512,256]{2,1,0:T(8,128)S(1)} custom-call(f32[7,256]{1,0:T(8,128)S(1)} %concatenate.9.starts.refs_5_.scales, bf16[4,512,256]{2,1,0:T(8,128)(2,1)S(1)} %get-tuple-element.134.grad.one.refs_10_, bf16[4,512,256]{2,1,0:T(8,128)(2,1)S(1)} %collective-permute-done.22.two, bf16[3,3,1024,256]{3,2,1,0:T(8,128)(2,1)S(1)} %bitcast.20, ...), custom_call_target="tpu_custom_call" | custom-call | flops 1000 | bytes 1000 | tf_op jit(solution)/shard_map/pallas_call | solution.py:310
  79.9 1.5 %collective-permute-start.25 = (bf16[2,256,256]{2,1,0:T(8,128)(2,1)S(1)}, bf16[2,256,256]{2,1,0:T(8,128)(2,1)S(1)}, u32[]{:S(2)}, u32[]{:S(2)}) collective-permute-start(bf16[2,256,256]{2,1,0:T(8,128)(2,1)S(1)} %collective-permute-done.24.picked), channel_id=1, source_target_pairs={{0,4},{4,0},{8,12},{12,8},{16,20},{20,16},{24,28},{28,24},{1,5},{5... | collective-permute-start | bytes 786440 | tf_op jit(solution)/shard_map/ppermute | solution.py:323
  81.4 10.4 %shard_map.174 = f32[9,1024,256]{2,1,0:T(8,128)} custom-call(bf16[2,512,256]{2,1,0:T(8,128)(2,1)S(1)} %get-tuple-element.106.low.refs_0_, bf16[2,512,256]{2,1,0:T(8,128)(2,1)S(1)} %get-tuple-element.108.high.refs_1_, bf16[2,512,256]{2,1,0:T(8,128)(2,1)S(1)} %collective-permute-done.15.low_two.refs_2_, ...), custom_call_target="tpu_custom_call" | custom-call | flops 1000 | bytes 1000 | tf_op jit(solution)/shard_map/pallas_call | solution.py:310
  91.8 1.8 %collective-permute-done.23.low = bf16[2,512,256]{2,1,0:T(8,128)(2,1)S(1)} collective-permute-done((bf16[2,512,256]{2,1,0:T(8,128)(2,1)S(1)}, bf16[2,512,256]{2,1,0:T(8,128)(2,1)S(1)}, u32[]{:S(2)}, u32[]{:S(2)}) %collective-permute-start.23) | collective-permute-done | bytes 524320 | tf_op jit(solution)/shard_map/ppermute | solution.py:323
  93.6 1.3 %shard_map.175 = (bf16[4,512,256]{2,1,0:T(8,128)(2,1)S(1)}, bf16[4,96,256]{2,1,0:T(8,128)(2,1)S(1)}, f32[1,256]{1,0:T(1,128)S(1)}, f32[1,256]{1,0:T(1,128)S(1)}) custom-call(f32[4,512,256]{2,1,0:T(8,128)S(1)} %shard_map.173.mine, bf16[2,512,256]{2,1,0:T(8,128)(2,1)S(1)} %collective-permute-done.23.low, ...), custom_call_target="tpu_custom_call" | custom-call | flops 1000 | bytes 1000 | tf_op jit(solution)/shard_map/pallas_call | solution.py:310
  95.0 1.3 %shard_map.176.refs_3_ = bf16[2,4,512,256]{3,2,1,0:T(8,128)(2,1)S(1)} custom-call(f32[7,256]{1,0:T(8,128)S(1)} %concatenate.9.starts.refs_5_.scales, bf16[4,512,256]{2,1,0:T(8,128)(2,1)S(1)} %get-tuple-element.148.grad.refs_2_), custom_call_target="tpu_custom_call" | custom-call | flops 1000 | bytes 1000 | tf_op jit(solution)/shard_map/pallas_call | solution.py:310
  98.0 5.4 %shard_map.178 = f32[9,512,256]{2,1,0:T(8,128)} custom-call(bf16[4,512,256]{2,1,0:T(8,128)(2,1)S(1)} %get-tuple-element.153.refs_0_, bf16[4,512,256]{2,1,0:T(8,128)(2,1)S(1)} %get-tuple-element.154.refs_1_, bf16[4,512,256]{2,1,0:T(8,128)(2,1)S(1)} %get-tuple-element.148.grad.refs_2_, bf16[2,4,512,256]{3,2,1,0:T(8,128)(2,1)S(1)} %shard_map.176.refs_3_), custom_call_target="tpu_custom_call" | custom-call | flops 1000 | bytes 1000 | tf_op jit(solution)/shard_map/pallas_call | solution.py:310
  (72 shorter events, 13.8 us)
Async XLA Ops:
  0.6 30.2 %collective-permute-start.11 = (bf16[3,3,1024,256]{3,2,1,0:T(8,128)(2,1)}, bf16[3,3,1024,256]{3,2,1,0:T(8,128)(2,1)}, u32[]{:S(2)}, u32[]{:S(2)}) collective-permute-start(bf16[3,3,1024,256]{3,2,1,0:T(8,128)(2,1)} %weight.11), channel_id=1, source_target_pairs={{0,1},{1,0},{2,3},{3,2},{4,5},{5,4},{6,7},{7,6},{8,9},{9,8},{10,11... | collective-permute-start | bytes 14155784 | tf_op jit(solution)/shard_map/ppermute | solution.py:323
  2.7 7.7 %collective-permute-start.1 = (bf16[4,64,128]{2,1,0:T(8,128)(2,1)S(1)}, bf16[4,64,128]{2,1,0:T(8,128)(2,1)S(1)}, u32[]{:S(2)}, u32[]{:S(2)}) collective-permute-start(bf16[4,64,128]{2,1,0:T(8,128)(2,1)S(1)} %get-tuple-element.171), channel_id=1, source_target_pairs={{0,16},{4,20},{8,24},{12,28},{16,0},{20,4},{24,8},{28,12},{1,17},{... | collective-permute-start | bytes 196616 | tf_op jit(solution)/shard_map/ppermute | solution.py:323
  6.4 4.5 %collective-permute-start = (bf16[4,64,128]{2,1,0:T(8,128)(2,1)S(1)}, bf16[4,64,128]{2,1,0:T(8,128)(2,1)S(1)}, u32[]{:S(2)}, u32[]{:S(2)}) collective-permute-start(bf16[4,64,128]{2,1,0:T(8,128)(2,1)S(1)} %get-tuple-element.171), channel_id=1, source_target_pairs={{0,8},{4,12},{8,0},{12,4},{16,24},{20,28},{24,16},{28,20},{1,9},{5... | collective-permute-start | bytes 196616 | tf_op jit(solution)/shard_map/ppermute | solution.py:323
  8.0 6.1 %collective-permute-start.2 = (bf16[4,64,128]{2,1,0:T(8,128)(2,1)S(1)}, bf16[4,64,128]{2,1,0:T(8,128)(2,1)S(1)}, u32[]{:S(2)}, u32[]{:S(2)}) collective-permute-start(bf16[4,64,128]{2,1,0:T(8,128)(2,1)S(1)} %get-tuple-element.171), channel_id=1, source_target_pairs={{0,24},{4,28},{8,16},{12,20},{16,8},{20,12},{24,0},{28,4},{1,25},{... | collective-permute-start | bytes 196616 | tf_op jit(solution)/shard_map/ppermute | solution.py:323
  14.1 10.3 %collective-permute-start.3 = (bf16[4,4,64,128]{3,2,1,0:T(8,128)(2,1)S(1)}, bf16[4,4,64,128]{3,2,1,0:T(8,128)(2,1)S(1)}, u32[]{:S(2)}, u32[]{:S(2)}) collective-permute-start(bf16[4,4,64,128]{3,2,1,0:T(8,128)(2,1)S(1)} %pad_maximum_fusion.refs_0_), channel_id=1, source_target_pairs={{0,6},{1,7},{2,4},{3,5},{4,2},{5,3},{6,0},{7,1},{8,14},{9,15},{10,... | collective-permute-start | bytes 786440 | tf_op jit(solution)/shard_map/ppermute | solution.py:338
  16.6 11.1 %collective-permute-start.6 = (bf16[4,4,64,128]{3,2,1,0:T(8,128)(2,1)S(1)}, bf16[4,4,64,128]{3,2,1,0:T(8,128)(2,1)S(1)}, u32[]{:S(2)}, u32[]{:S(2)}) collective-permute-start(bf16[4,4,64,128]{3,2,1,0:T(8,128)(2,1)S(1)} %pad_maximum_fusion.refs_0_), channel_id=1, source_target_pairs={{0,2},{1,3},{2,0},{3,1},{4,6},{5,7},{6,4},{7,5},{8,10},{9,11},{10,... | collective-permute-start | bytes 786440 | tf_op jit(solution)/shard_map/ppermute | solution.py:323
  17.1 10.7 %collective-permute-start.5 = (bf16[4,4,64,128]{3,2,1,0:T(8,128)(2,1)S(1)}, bf16[4,4,64,128]{3,2,1,0:T(8,128)(2,1)S(1)}, u32[]{:S(2)}, u32[]{:S(2)}) collective-permute-start(bf16[4,4,64,128]{3,2,1,0:T(8,128)(2,1)S(1)} %pad_maximum_fusion.refs_0_), channel_id=1, source_target_pairs={{0,4},{4,0},{8,12},{12,8},{16,20},{20,16},{24,28},{28,24},{1,5},{5... | collective-permute-start | bytes 786440 | tf_op jit(solution)/shard_map/ppermute | solution.py:323
  17.6 5.0 %collective-permute-start.4 = (f32[1,32,256]{2,1,0:T(8,128)}, f32[1,32,256]{2,1,0:T(8,128)S(1)}, u32[]{:S(2)}, u32[]{:S(2)}) collective-permute-start(f32[1,32,256]{2,1,0:T(8,128)} %bitcast.21), channel_id=1, source_target_pairs={{0,16},{4,20},{8,24},{12,28},{16,0},{20,4},{24,8},{28,12},{1,17},{... | collective-permute-start | bytes 98312 | tf_op jit(solution)/shard_map/ppermute | solution.py:323
  22.7 8.1 %collective-permute-start.7 = (bf16[4,4,64,128]{3,2,1,0:T(8,128)(2,1)S(1)}, bf16[4,4,64,128]{3,2,1,0:T(8,128)(2,1)S(1)}, u32[]{:S(2)}, u32[]{:S(2)}) collective-permute-start(bf16[4,4,64,128]{3,2,1,0:T(8,128)(2,1)S(1)} %pad_maximum_fusion.refs_0_), channel_id=1, source_target_pairs={{0,1},{1,0},{2,3},{3,2},{4,5},{5,4},{6,7},{7,6},{8,9},{9,8},{10,11... | collective-permute-start | bytes 786440 | tf_op jit(solution)/shard_map/ppermute | solution.py:323
  27.7 3.2 %collective-permute-start.9 = (bf16[4,4,64,128]{3,2,1,0:T(8,128)(2,1)S(1)}, bf16[4,4,64,128]{3,2,1,0:T(8,128)(2,1)S(1)}, u32[]{:S(2)}, u32[]{:S(2)}) collective-permute-start(bf16[4,4,64,128]{3,2,1,0:T(8,128)(2,1)S(1)} %collective-permute-done.6.refs_2_), channel_id=1, source_target_pairs={{0,1},{1,0},{2,3},{3,2},{4,5},{5,4},{6,7},{7,6},{8,9},{9,8},{10,11... | collective-permute-start | bytes 786440 | tf_op jit(solution)/shard_map/ppermute | solution.py:323
  27.8 3.1 %collective-permute-start.8 = (bf16[4,4,64,128]{3,2,1,0:T(8,128)(2,1)S(1)}, bf16[4,4,64,128]{3,2,1,0:T(8,128)(2,1)S(1)}, u32[]{:S(2)}, u32[]{:S(2)}) collective-permute-start(bf16[4,4,64,128]{3,2,1,0:T(8,128)(2,1)S(1)} %collective-permute-done.5.refs_1_), channel_id=1, source_target_pairs={{0,1},{1,0},{2,3},{3,2},{4,5},{5,4},{6,7},{7,6},{8,9},{9,8},{10,11... | collective-permute-start | bytes 786440 | tf_op jit(solution)/shard_map/ppermute | solution.py:323
  28.2 2.7 %collective-permute-start.10 = (bf16[4,4,64,128]{3,2,1,0:T(8,128)(2,1)S(1)}, bf16[4,4,64,128]{3,2,1,0:T(8,128)(2,1)S(1)}, u32[]{:S(2)}, u32[]{:S(2)}) collective-permute-start(bf16[4,4,64,128]{3,2,1,0:T(8,128)(2,1)S(1)} %collective-permute-done.3.refs_3_), channel_id=1, source_target_pairs={{0,1},{1,0},{2,3},{3,2},{4,5},{5,4},{6,7},{7,6},{8,9},{9,8},{10,11... | collective-permute-start | bytes 786440 | tf_op jit(solution)/shard_map/ppermute | solution.py:323
  30.9 7.3 %slice-start = ((s8[4718592]{0:T(1024)(128)(4,1)}), s8[4194304]{0:T(1024)(128)(4,1)S(1)}, s32[]{:S(2)}) async-start(s8[4718592]{0:T(1024)(128)(4,1)} %bitcast.19), calls=%async_computation | async-start | bytes 8388608
  30.9 7.3 %slice-start.1 = ((s8[4718592]{0:T(1024)(128)(4,1)}), s8[524288]{0:T(1024)(128)(4,1)S(1)}, s32[]{:S(2)}) async-start(s8[4718592]{0:T(1024)(128)(4,1)} %bitcast.19), calls=%async_computation.1 | async-start | bytes 1048576
  35.4 2.6 %collective-permute-start.16 = (bf16[2,512,256]{2,1,0:T(8,128)(2,1)S(1)}, bf16[2,512,256]{2,1,0:T(8,128)(2,1)S(1)}, u32[]{:S(2)}, u32[]{:S(2)}) collective-permute-start(bf16[2,512,256]{2,1,0:T(8,128)(2,1)S(1)} %get-tuple-element.108.high.refs_1_), channel_id=1, source_target_pairs={{0,1},{1,0},{2,3},{3,2},{4,5},{5,4},{6,7},{7,6},{8,9},{9,8},{10,11... | collective-permute-start | bytes 1572872 | tf_op jit(solution)/shard_map/ppermute | solution.py:323
  35.9 2.3 %collective-permute-start.15 = (bf16[2,512,256]{2,1,0:T(8,128)(2,1)S(1)}, bf16[2,512,256]{2,1,0:T(8,128)(2,1)S(1)}, u32[]{:S(2)}, u32[]{:S(2)}) collective-permute-start(bf16[2,512,256]{2,1,0:T(8,128)(2,1)S(1)} %get-tuple-element.106.low.refs_0_), channel_id=1, source_target_pairs={{0,1},{1,0},{2,3},{3,2},{4,5},{5,4},{6,7},{7,6},{8,9},{9,8},{10,11... | collective-permute-start | bytes 1572872 | tf_op jit(solution)/shard_map/ppermute | solution.py:323
  36.0 9.1 %copy-start.1 = (f32[32,256]{1,0:T(8,128)S(1)}, f32[32,256]{1,0:T(8,128)}, u32[]{:S(2)}) copy-start(f32[32,256]{1,0:T(8,128)} %param.19) | copy-start | bytes 98308
  36.0 9.1 %collective-permute-start.13 = (bf16[2,256,256]{2,1,0:T(8,128)(2,1)S(1)}, bf16[2,256,256]{2,1,0:T(8,128)(2,1)S(1)}, u32[]{:S(2)}, u32[]{:S(2)}) collective-permute-start(bf16[2,256,256]{2,1,0:T(8,128)(2,1)S(1)} %get-tuple-element.107), channel_id=1, source_target_pairs={{0,2},{1,3},{2,0},{3,1},{4,6},{5,7},{6,4},{7,5},{8,10},{9,11},{10,... | collective-permute-start | bytes 786440 | tf_op jit(solution)/shard_map/ppermute | solution.py:323
  37.5 18.4 %collective-permute-start.12 = (bf16[2,512,256]{2,1,0:T(8,128)(2,1)S(1)}, bf16[2,512,256]{2,1,0:T(8,128)(2,1)S(1)}, u32[]{:S(2)}, u32[]{:S(2)}) collective-permute-start(bf16[2,512,256]{2,1,0:T(8,128)(2,1)S(1)} %get-tuple-element.106.low.refs_0_), channel_id=1, source_target_pairs={{0,2},{1,3},{2,0},{3,1},{4,6},{5,7},{6,4},{7,5},{8,10},{9,11},{10,... | collective-permute-start | bytes 1572872 | tf_op jit(solution)/shard_map/ppermute | solution.py:323
  45.1 4.8 %collective-permute-start.17 = (bf16[2,256,256]{2,1,0:T(8,128)(2,1)S(1)}, bf16[2,256,256]{2,1,0:T(8,128)(2,1)S(1)}, u32[]{:S(2)}, u32[]{:S(2)}) collective-permute-start(bf16[2,256,256]{2,1,0:T(8,128)(2,1)S(1)} %collective-permute-done.13.picked.refs_5_), channel_id=1, source_target_pairs={{0,1},{1,0},{2,3},{3,2},{4,5},{5,4},{6,7},{7,6},{8,9},{9,8},{10,11... | collective-permute-start | bytes 786440 | tf_op jit(solution)/shard_map/ppermute | solution.py:323
  45.1 4.8 %collective-permute-start.18 = (f32[2,32,256]{2,1,0:T(8,128)S(1)}, f32[2,32,256]{2,1,0:T(8,128)S(1)}, u32[]{:S(2)}, u32[]{:S(2)}) collective-permute-start(f32[2,32,256]{2,1,0:T(8,128)S(1)} %pad_maximum_fusion.2), channel_id=1, source_target_pairs={{0,4},{4,0},{8,12},{12,8},{16,20},{20,16},{24,28},{28,24},{1,5},{5... | collective-permute-start | bytes 196616 | tf_op jit(solution)/shard_map/ppermute | solution.py:323
  46.7 9.2 %collective-permute-start.14 = (bf16[2,256,256]{2,1,0:T(8,128)(2,1)S(1)}, bf16[2,256,256]{2,1,0:T(8,128)(2,1)S(1)}, u32[]{:S(2)}, u32[]{:S(2)}) collective-permute-start(bf16[2,256,256]{2,1,0:T(8,128)(2,1)S(1)} %collective-permute-done.13.picked.refs_5_), channel_id=1, source_target_pairs={{0,4},{4,0},{8,12},{12,8},{16,20},{20,16},{24,28},{28,24},{1,5},{5... | collective-permute-start | bytes 786440 | tf_op jit(solution)/shard_map/ppermute | solution.py:323
  49.9 5.9 %collective-permute-start.19 = (f32[4,32,256]{2,1,0:T(8,128)S(1)}, f32[4,32,256]{2,1,0:T(8,128)S(1)}, u32[]{:S(2)}, u32[]{:S(2)}) collective-permute-start(f32[4,32,256]{2,1,0:T(8,128)S(1)} %pad_maximum_fusion.1), channel_id=1, source_target_pairs={{0,8},{4,12},{8,0},{12,4},{16,24},{20,28},{24,16},{28,20},{1,9},{5... | collective-permute-start | bytes 393224 | tf_op jit(solution)/shard_map/ppermute | solution.py:323
  55.9 2.7 %collective-permute-start.20 = (bf16[2,512,256]{2,1,0:T(8,128)(2,1)S(1)}, bf16[2,512,256]{2,1,0:T(8,128)(2,1)S(1)}, u32[]{:S(2)}, u32[]{:S(2)}) collective-permute-start(bf16[2,512,256]{2,1,0:T(8,128)(2,1)S(1)} %collective-permute-done.12.far.refs_4_), channel_id=1, source_target_pairs={{0,1},{1,0},{2,3},{3,2},{4,5},{5,4},{6,7},{7,6},{8,9},{9,8},{10,11... | collective-permute-start | bytes 1572872 | tf_op jit(solution)/shard_map/ppermute | solution.py:323
  55.9 2.7 %collective-permute-start.21 = (bf16[2,256,256]{2,1,0:T(8,128)(2,1)S(1)}, bf16[2,256,256]{2,1,0:T(8,128)(2,1)S(1)}, u32[]{:S(2)}, u32[]{:S(2)}) collective-permute-start(bf16[2,256,256]{2,1,0:T(8,128)(2,1)S(1)} %collective-permute-done.14.rest.refs_6_), channel_id=1, source_target_pairs={{0,1},{1,0},{2,3},{3,2},{4,5},{5,4},{6,7},{7,6},{8,9},{9,8},{10,11... | collective-permute-start | bytes 786440 | tf_op jit(solution)/shard_map/ppermute | solution.py:323
  65.9 2.7 %collective-permute-start.22 = (bf16[4,512,256]{2,1,0:T(8,128)(2,1)S(1)}, bf16[4,512,256]{2,1,0:T(8,128)(2,1)S(1)}, u32[]{:S(2)}, u32[]{:S(2)}) collective-permute-start(bf16[4,512,256]{2,1,0:T(8,128)(2,1)S(1)} %get-tuple-element.134.grad.one.refs_10_), channel_id=1, source_target_pairs={{0,1},{1,0},{2,3},{3,2},{4,5},{5,4},{6,7},{7,6},{8,9},{9,8},{10,11... | collective-permute-start | bytes 3145736 | tf_op jit(solution)/shard_map/ppermute | solution.py:323
  69.7 9.6 %collective-permute-start.24 = (bf16[2,256,256]{2,1,0:T(8,128)(2,1)S(1)}, bf16[2,256,256]{2,1,0:T(8,128)(2,1)S(1)}, u32[]{:S(2)}, u32[]{:S(2)}) collective-permute-start(bf16[2,256,256]{2,1,0:T(8,128)(2,1)S(1)} %shard_map.172), channel_id=1, source_target_pairs={{0,2},{1,3},{2,0},{3,1},{4,6},{5,7},{6,4},{7,5},{8,10},{9,11},{10,... | collective-permute-start | bytes 786440 | tf_op jit(solution)/shard_map/ppermute | solution.py:323
  79.2 14.4 %collective-permute-start.26 = (bf16[3,3,512,256]{3,2,1,0:T(8,128)(2,1)S(1)}, bf16[3,3,512,256]{3,2,1,0:T(8,128)(2,1)S(1)}, u32[]{:S(2)}, u32[]{:S(2)}) collective-permute-start(bf16[3,3,512,256]{3,2,1,0:T(8,128)(2,1)S(1)} %shard_map.161.refs_4_.weight), channel_id=1, source_target_pairs={{0,1},{1,0},{2,3},{3,2},{4,5},{5,4},{6,7},{7,6},{8,9},{9,8},{10,11... | collective-permute-start | bytes 7077896 | tf_op jit(solution)/shard_map/ppermute | solution.py:323
  79.3 14.3 %collective-permute-start.23 = (bf16[2,512,256]{2,1,0:T(8,128)(2,1)S(1)}, bf16[2,512,256]{2,1,0:T(8,128)(2,1)S(1)}, u32[]{:S(2)}, u32[]{:S(2)}) collective-permute-start(bf16[2,512,256]{2,1,0:T(8,128)(2,1)S(1)} %shard_map.171), channel_id=1, source_target_pairs={{0,2},{1,3},{2,0},{3,1},{4,6},{5,7},{6,4},{7,5},{8,10},{9,11},{10,... | collective-permute-start | bytes 1572872 | tf_op jit(solution)/shard_map/ppermute | solution.py:323
  79.9 11.9 %collective-permute-start.25 = (bf16[2,256,256]{2,1,0:T(8,128)(2,1)S(1)}, bf16[2,256,256]{2,1,0:T(8,128)(2,1)S(1)}, u32[]{:S(2)}, u32[]{:S(2)}) collective-permute-start(bf16[2,256,256]{2,1,0:T(8,128)(2,1)S(1)} %collective-permute-done.24.picked), channel_id=1, source_target_pairs={{0,4},{4,0},{8,12},{12,8},{16,20},{20,16},{24,28},{28,24},{1,5},{5... | collective-permute-start | bytes 786440 | tf_op jit(solution)/shard_map/ppermute | solution.py:323
  94.9 1.5 %collective-permute-start.27 = (bf16[4,96,256]{2,1,0:T(8,128)(2,1)S(1)}, bf16[4,96,256]{2,1,0:T(8,128)(2,1)S(1)}, u32[]{:S(2)}, u32[]{:S(2)}) collective-permute-start(bf16[4,96,256]{2,1,0:T(8,128)(2,1)S(1)} %get-tuple-element.147.one), channel_id=1, source_target_pairs={{0,1},{1,0},{2,3},{3,2},{4,5},{5,4},{6,7},{7,6},{8,9},{9,8},{10,11... | collective-permute-start | bytes 589832 | tf_op jit(solution)/shard_map/ppermute | solution.py:323
  97.5 6.0 %collective-permute-start.28 = (f32[4,64,128]{2,1,0:T(8,128)S(1)}, f32[4,64,128]{2,1,0:T(8,128)S(1)}, u32[]{:S(2)}, u32[]{:S(2)}) collective-permute-start(f32[4,64,128]{2,1,0:T(8,128)S(1)} %get-tuple-element.152), channel_id=1, source_target_pairs={{0,2},{1,3},{2,0},{3,1},{4,6},{5,7},{6,4},{7,5},{8,10},{9,11},{10,... | collective-permute-start | bytes 393224 | tf_op jit(solution)/shard_map/ppermute | solution.py:323
  (6 other events, 5.2 us)

commit v8 on v7

--- a/solution.py
+++ b/solution.py
@@ -565,16 +565,16 @@
     )
 
 
-def slope_kernel(pre, stats, scales, keep, slope):
+def slope_kernel(pre, stats, scales, keep, slope, hats):
     mel_count, total, width = pre.shape
     center, inverse = stats[0:1], stats[1:2]
-    scale = scales[0:1] * inverse
-    offset = scales[1:2] - center * scale
 
     def rows(at, carry):
         mask = widen(keep[pl.ds(at, ROWS)], width)
         for m in range(mel_count):
-            value = pre[m, pl.ds(at, ROWS)] * scale + offset
+            normed = (pre[m, pl.ds(at, ROWS)] - center) * inverse
+            hats[m, pl.ds(at, ROWS)] = normed
+            value = normed * scales[0:1] + scales[1:2]
             slope[m, pl.ds(at, ROWS)] = mask * (phi_parts(value) + value * bell(value))
         return carry
 
@@ -586,12 +586,12 @@
         slope_kernel,
         (pre, stats, scales, keep),
         [whole_spec()] * 4,
-        [(pre.shape, f32)],
-        [whole_spec()],
+        [(pre.shape, f32)] * 2,
+        [whole_spec()] * 2,
         [],
         2**28,
         6,
-    )[0]
+    )
 
 
 def group_sums(fields, weight, starts, targets, sources=None):
@@ -674,15 +674,15 @@
     width = (plain + values)[0].shape[1]
     terms = list(plain)
     for value in values:
-        for _ in range(3):
+        for _ in range(2):
             term = value.astype(bf16)
             terms.append(term)
             value = value - term.astype(f32)
     out = jnp.dot(mask, jnp.concatenate(terms, axis=1), preferred_element_type=f32)
     parts = [out[:, k * width : (k + 1) * width] for k in range(len(terms))]
     results = parts[: len(plain)]
-    for k in range(len(plain), len(parts), 3):
-        results.append(parts[k] + (parts[k + 1] + parts[k + 2]))
+    for k in range(len(plain), len(parts), 2):
+        results.append(parts[k] + parts[k + 1])
     return results
 
 
@@ -735,13 +735,14 @@
     pixels = column_sum(num) * mel_count
     center, inverse = moments((first, second), keep, pixels)
     scale = scales[2:3] * inverse
-    offset = scales[3:4] - center * scale
 
     def activate(at, carry):
         mask = widen(keep[pl.ds(at, ROWS)], width)
         pooled = jnp.zeros((ROWS, width), f32)
         for m in range(mel_count):
-            value = middle[m, pl.ds(at, ROWS)] * scale + offset
+            normed = (middle[m, pl.ds(at, ROWS)] - center) * inverse
+            middle[m, pl.ds(at, ROWS)] = normed
+            value = normed * scales[2:3] + scales[3:4]
             share = phi_parts(value)
             pooled = pooled + value * share
             slope[m, pl.ds(at, ROWS)] = mask * (share + value * bell(value))
@@ -773,8 +774,10 @@
     counts, totals, sums = run_sums(
         ahead, (present.astype(bf16),), (present * pooled, present * exponent)
     )
-    wide[...] = totals / counts + jnp.log(sums)
-    readout[...] = wide[pl.ds(pl.multiple_of(place * own, own), own)]
+    mine = pl.ds(pl.multiple_of(place * own, own), own)
+    for i, value in enumerate((totals, counts, sums)):
+        wide[i] = value
+    readout[...] = wide[0, mine] / wide[1, mine] + jnp.log(wide[2, mine])
     for copy in copies:
         copy.wait()
     cotangent = full[...]
@@ -793,7 +796,7 @@
             step = down_rows * slope[m, pl.ds(at, ROWS)]
             slope[m, pl.ds(at, ROWS)] = step
             plain = plain + fold(step)
-            along = along + fold(step * ((middle[m, pl.ds(at, ROWS)] - center) * inverse))
+            along = along + fold(step * middle[m, pl.ds(at, ROWS)])
         return plain, along
 
     plain, along = by_rows(total, slopes, (blank, blank))
@@ -805,8 +808,7 @@
     def finish(at, carry):
         mask = widen(keep[pl.ds(at, ROWS)], width)
         for m in range(mel_count):
-            normed = (middle[m, pl.ds(at, ROWS)] - center) * inverse
-            rows = slope[m, pl.ds(at, ROWS)] - plain - normed * along
+            rows = slope[m, pl.ds(at, ROWS)] - plain - middle[m, pl.ds(at, ROWS)] * along
             grad[m, pl.ds(at, ROWS)] = (mask * (scale * rows)).astype(bf16)
         return carry
 
@@ -830,7 +832,7 @@
             pltpu.VMEM(padded, f32),
             pltpu.VMEM(arrays[0].shape, bf16),
             pltpu.VMEM((width // LANES, total, LANES), f32),
-            pltpu.VMEM((total // 2, width), f32),
+            pltpu.VMEM((3, total // 2, width), f32),
             pltpu.VMEM((total // 2, width), f32),
             pltpu.SemaphoreType.DMA((sum(part.shape[0] for part in cotangents),)),
         ],
@@ -1017,10 +1019,10 @@
     )[0]
 
 
-def norm_kernel(mine, low, picked, rest, slope, pre, stats, scales, keep, *refs):
+def norm_kernel(mine, low, picked, rest, slope, hats, stats, scales, keep, *refs):
     grad, window, gain_grad, shift_grad, padded, held = refs
     mel_count, total, width = mine.shape
-    center, inverse, pixels = stats[0:1], stats[1:2], stats[2:3]
+    inverse, pixels = stats[1:2], stats[2:3]
     blank = jnp.zeros((TILE, width), f32)
     edge = (padded.shape[1] - total) // 2
     reach = window.shape[1]
@@ -1038,7 +1040,7 @@
                 step = rows * slope[m, place_rows]
                 held[m, place_rows] = step
                 plain = plain + fold(step)
-                along = along + fold(step * ((pre[m, place_rows] - center) * inverse))
+                along = along + fold(step * hats[m, place_rows])
             return plain, along
 
         return slopes
@@ -1064,8 +1066,7 @@
     def finish(at, carry):
         mask = widen(keep[pl.ds(at, ROWS)], width)
         for m in range(mel_count):
-            normed = (pre[m, pl.ds(at, ROWS)] - center) * inverse
-            rows = held[m, pl.ds(at, ROWS)] - plain - normed * along
+            rows = held[m, pl.ds(at, ROWS)] - plain - hats[m, pl.ds(at, ROWS)] * along
             rows = (mask * (scale * rows)).astype(bf16)
             grad[m, pl.ds(at, ROWS)] = rows
             padded[m, pl.ds(pl.multiple_of(at + edge, 16), ROWS)] = rows
@@ -1364,8 +1365,10 @@
         (picked_two, pre, cotangents, wings)
     )
     cotangents.append(swap(jnp.concatenate(cotangents), "tm", bits[-1]))
-    slope = first_slope(pre, stats, table, keep)
-    far, far_rest, slope, cotangents = lax.optimization_barrier((far, far_rest, slope, cotangents))
+    slope, pre = first_slope(pre, stats, table, keep)
+    far, far_rest, slope, pre, cotangents = lax.optimization_barrier(
+        (far, far_rest, slope, pre, cotangents)
+    )
     far_two, rest_two = swap(far, "chan", 1), swap(far_rest, "chan", 1)
     sums = far_part(far, far_picked, far_rest, conv2_weight, near)
     far_two, rest_two, sums = lax.optimization_barrier((far_two, rest_two, sums))

time: 105 us -> 104 us (level)
  transfers between devices with their start and end apart: 29 -> 29, of which waited for: 14 -> 14; matrix products, arithmetic and copies ran while one was open for 2% -> 2% of each run, Pallas kernels for 37% -> 38%
where the time goes in v8:
time: 104 us
  Pallas kernels  54.6 us (52%)
  starting transfers between devices  22.9 us (22%)
  waiting for transfers between devices  21.6 us (21%)
  local copies, waits for them, and re-layouts  2.25 us (2%)
  other arithmetic  1.63 us (2%)
    pallas_call x19, Pallas kernels, call(): pl.pallas_call(body, out_shape=tuple((jax.ShapeDtypeStruct(s, d) for s, d...  54.6 us
    ppermute x28, starting transfers between devices, swap(): return lax.ppermute(shard, axis, [(i, i ^ bit) for i in range(count)])  20.4 us
    ppermute x28, waiting for transfers between devices, swap(): return lax.ppermute(shard, axis, [(i, i ^ bit) for i in range(count)])  19.9 us
    ppermute x1, starting transfers between devices, swap_both(): return lax.ppermute(shard, (first, second), pairs)  2.51 us
    unnamed x18, local copies, waits for them, and re-layouts  2.15 us
  transfers between devices with their start and end apart: 29, of which 14 were waited for; matrix products, arithmetic and copies ran while one was open for 2% of the time, Pallas kernels for 38%

profile of v8, /device:TPU:0, one launch (start us, length us, event | category | flops | bytes accessed | tf_op | source)
XLA Modules:
  0.0 103.9 jit_solution(15968854415666485152)
XLA Ops:
  2.7 3.7 %collective-permute-start.1 = (bf16[4,64,128]{2,1,0:T(8,128)(2,1)S(1)}, bf16[4,64,128]{2,1,0:T(8,128)(2,1)S(1)}, u32[]{:S(2)}, u32[]{:S(2)}) collective-permute-start(bf16[4,64,128]{2,1,0:T(8,128)(2,1)S(1)} %get-tuple-element.177), channel_id=1, source_target_pairs={{0,16},{4,20},{8,24},{12,28},{16,0},{20,4},{24,8},{28,12},{1,17},{... | collective-permute-start | bytes 196616 | tf_op jit(solution)/shard_map/ppermute | solution.py:323
  6.4 1.6 %collective-permute-start = (bf16[4,64,128]{2,1,0:T(8,128)(2,1)S(1)}, bf16[4,64,128]{2,1,0:T(8,128)(2,1)S(1)}, u32[]{:S(2)}, u32[]{:S(2)}) collective-permute-start(bf16[4,64,128]{2,1,0:T(8,128)(2,1)S(1)} %get-tuple-element.177), channel_id=1, source_target_pairs={{0,8},{4,12},{8,0},{12,4},{16,24},{20,28},{24,16},{28,20},{1,9},{5... | collective-permute-start | bytes 196616 | tf_op jit(solution)/shard_map/ppermute | solution.py:323
  8.0 2.5 %collective-permute-done.1 = bf16[4,64,128]{2,1,0:T(8,128)(2,1)S(1)} collective-permute-done((bf16[4,64,128]{2,1,0:T(8,128)(2,1)S(1)}, bf16[4,64,128]{2,1,0:T(8,128)(2,1)S(1)}, u32[]{:S(2)}, u32[]{:S(2)}) %collective-permute-start.1) | collective-permute-done | bytes 65568 | tf_op jit(solution)/shard_map/ppermute | solution.py:323
  10.9 3.1 %collective-permute-done.2 = bf16[4,64,128]{2,1,0:T(8,128)(2,1)S(1)} collective-permute-done((bf16[4,64,128]{2,1,0:T(8,128)(2,1)S(1)}, bf16[4,64,128]{2,1,0:T(8,128)(2,1)S(1)}, u32[]{:S(2)}, u32[]{:S(2)}) %collective-permute-start.2) | collective-permute-done | bytes 65568 | tf_op jit(solution)/shard_map/ppermute | solution.py:323
  14.1 2.5 %collective-permute-start.3 = (bf16[4,4,64,128]{3,2,1,0:T(8,128)(2,1)S(1)}, bf16[4,4,64,128]{3,2,1,0:T(8,128)(2,1)S(1)}, u32[]{:S(2)}, u32[]{:S(2)}) collective-permute-start(bf16[4,4,64,128]{3,2,1,0:T(8,128)(2,1)S(1)} %pad_maximum_fusion.refs_0_), channel_id=1, source_target_pairs={{0,6},{1,7},{2,4},{3,5},{4,2},{5,3},{6,0},{7,1},{8,14},{9,15},{10,... | collective-permute-start | bytes 786440 | tf_op jit(solution)/shard_map/ppermute | solution.py:338
  17.6 2.0 %collective-permute-start.4 = (f32[1,32,256]{2,1,0:T(8,128)}, f32[1,32,256]{2,1,0:T(8,128)S(1)}, u32[]{:S(2)}, u32[]{:S(2)}) collective-permute-start(f32[1,32,256]{2,1,0:T(8,128)} %bitcast.21), channel_id=1, source_target_pairs={{0,16},{4,20},{8,24},{12,28},{16,0},{20,4},{24,8},{28,12},{1,17},{... | collective-permute-start | bytes 98312 | tf_op jit(solution)/shard_map/ppermute | solution.py:323
  19.6 1.7 %copy-done = bf16[3,3,512,256]{3,2,1,0:T(8,128)(2,1)S(1)} copy-done((bf16[3,3,512,256]{3,2,1,0:T(8,128)(2,1)S(1)}, bf16[3,3,512,256]{3,2,1,0:T(8,128)(2,1)}, u32[]{:S(2)}) %copy-start) | copy-done | bytes 2359320
  22.7 1.7 %collective-permute-done.3.refs_3_ = bf16[4,4,64,128]{3,2,1,0:T(8,128)(2,1)S(1)} collective-permute-done((bf16[4,4,64,128]{3,2,1,0:T(8,128)(2,1)S(1)}, bf16[4,4,64,128]{3,2,1,0:T(8,128)(2,1)S(1)}, u32[]{:S(2)}, u32[]{:S(2)}) %collective-permute-start.3) | collective-permute-done | bytes 262176 | tf_op jit(solution)/shard_map/ppermute | solution.py:338
  24.3 3.3 %collective-permute-done.6.refs_2_ = bf16[4,4,64,128]{3,2,1,0:T(8,128)(2,1)S(1)} collective-permute-done((bf16[4,4,64,128]{3,2,1,0:T(8,128)(2,1)S(1)}, bf16[4,4,64,128]{3,2,1,0:T(8,128)(2,1)S(1)}, u32[]{:S(2)}, u32[]{:S(2)}) %collective-permute-start.6) | collective-permute-done | bytes 262176 | tf_op jit(solution)/shard_map/ppermute | solution.py:323
  28.3 2.5 %shard_map.162 = (bf16[4,512,256]{2,1,0:T(8,128)(2,1)S(1)}, f32[512,128]{1,0:T(8,128)S(1)}, f32[4,528,256]{2,1,0:T(8,128)S(1)}, f32[4,512,256]{2,1,0:T(8,128)S(1)}, f32[4,528,256]{2,1,0:T(8,128)S(1)}) custom-call(bf16[4,4,64,128]{3,2,1,0:T(8,128)(2,1)S(1)} %pad_maximum_fusion.refs_0_, bf16[4,4,64,128]{3,2,1,0:T(8,128)(2,1)S(1)} %collective-permute-done.5.refs_1_, ...), custom_call_target="tpu_custom_call" | custom-call | flops 1000 | bytes 1000 | tf_op jit(solution)/shard_map/pallas_call | solution.py:310
  30.9 4.4 %shard_map.163 = (bf16[2,512,256]{2,1,0:T(8,128)(2,1)S(1)}, bf16[2,512,256]{2,1,0:T(8,128)(2,1)S(1)}, bf16[2,256,256]{2,1,0:T(8,128)(2,1)S(1)}, bf16[4,512,256]{...) custom-call(f32[7,256]{1,0:T(8,128)S(1)} %concatenate.9.starts.refs_5_.scales, ...), custom_call_target="tpu_custom_call" | custom-call | flops 1000 | bytes 1000 | tf_op jit(solution)/shard_map/pallas_call | solution.py:310
  35.9 1.5 %collective-permute-start.13 = (bf16[2,256,256]{2,1,0:T(8,128)(2,1)S(1)}, bf16[2,256,256]{2,1,0:T(8,128)(2,1)S(1)}, u32[]{:S(2)}, u32[]{:S(2)}) collective-permute-start(bf16[2,256,256]{2,1,0:T(8,128)(2,1)S(1)} %get-tuple-element.110), channel_id=1, source_target_pairs={{0,2},{1,3},{2,0},{3,1},{4,6},{5,7},{6,4},{7,5},{8,10},{9,11},{10,... | collective-permute-start | bytes 786440 | tf_op jit(solution)/shard_map/ppermute | solution.py:323
  38.1 4.2 %shard_map.164.near = f32[3,4,512,256]{3,2,1,0:T(8,128)S(1)} custom-call(bf16[2,512,256]{2,1,0:T(8,128)(2,1)S(1)} %get-tuple-element.109.low.refs_0_, bf16[2,512,256]{2,1,0:T(8,128)(2,1)S(1)} %get-tuple-element.111.high.refs_1_, bf16[2,512,256]{2,1,0:T(8,128)(2,1)S(1)} %collective-permute-done.15.low_two.refs_2_, ...), custom_call_target="tpu_custom_call" | custom-call | flops 1000 | bytes 1000 | tf_op jit(solution)/shard_map/pallas_call | solution.py:310
  42.3 2.7 %collective-permute-done.13.picked.refs_5_ = bf16[2,256,256]{2,1,0:T(8,128)(2,1)S(1)} collective-permute-done((bf16[2,256,256]{2,1,0:T(8,128)(2,1)S(1)}, bf16[2,256,256]{2,1,0:T(8,128)(2,1)S(1)}, u32[]{:S(2)}, u32[]{:S(2)}) %collective-permute-start.13) | collective-permute-done | bytes 262176 | tf_op jit(solution)/shard_map/ppermute | solution.py:323
  45.0 1.6 %collective-permute-start.18 = (f32[2,32,256]{2,1,0:T(8,128)S(1)}, f32[2,32,256]{2,1,0:T(8,128)S(1)}, u32[]{:S(2)}, u32[]{:S(2)}) collective-permute-start(f32[2,32,256]{2,1,0:T(8,128)S(1)} %pad_maximum_fusion.2), channel_id=1, source_target_pairs={{0,4},{4,0},{8,12},{12,8},{16,20},{20,16},{24,28},{28,24},{1,5},{5... | collective-permute-start | bytes 196616 | tf_op jit(solution)/shard_map/ppermute | solution.py:323
  47.1 1.8 %shard_map.165.wings = bf16[2,9,256,256]{3,2,1,0:T(8,128)(2,1)S(1)} custom-call(bf16[3,3,1024,256]{3,2,1,0:T(8,128)(2,1)} %collective-permute-done.11.weight), custom_call_target="tpu_custom_call" | custom-call | flops 1000 | bytes 1000 | tf_op jit(solution)/shard_map/pallas_call | solution.py:310
  49.8 1.4 %collective-permute-start.19 = (f32[4,32,256]{2,1,0:T(8,128)S(1)}, f32[4,32,256]{2,1,0:T(8,128)S(1)}, u32[]{:S(2)}, u32[]{:S(2)}) collective-permute-start(f32[4,32,256]{2,1,0:T(8,128)S(1)} %pad_maximum_fusion.1), channel_id=1, source_target_pairs={{0,8},{4,12},{8,0},{12,4},{16,24},{20,28},{24,16},{28,20},{1,9},{5... | collective-permute-start | bytes 393224 | tf_op jit(solution)/shard_map/ppermute | solution.py:323
  51.2 1.2 %shard_map.166 = (f32[4,512,256]{2,1,0:T(8,128)S(1)}, f32[4,512,256]{2,1,0:T(8,128)S(1)}) custom-call(f32[4,512,256]{2,1,0:T(8,128)S(1)} %get-tuple-element.121.pre, f32[8,256]{1,0:T(8,128)S(1)} %get-tuple-element.122.stats, f32[7,256]{1,0:T(8,128)S(1)} %concatenate.9.starts.refs_5_.scales, f32[512,128]{1,0:T(8,128)S(1)} %get-tuple-element.105.refs_6_.keep), custom_call_target="tpu_custom_call" | custom-call | flops 1000 | bytes 1000 | tf_op jit(solution)/shard_map/pallas_call | solution.py:310
  52.4 3.4 %collective-permute-done.12.far.refs_4_ = bf16[2,512,256]{2,1,0:T(8,128)(2,1)S(1)} collective-permute-done((bf16[2,512,256]{2,1,0:T(8,128)(2,1)S(1)}, bf16[2,512,256]{2,1,0:T(8,128)(2,1)S(1)}, u32[]{:S(2)}, u32[]{:S(2)}) %collective-permute-start.12) | collective-permute-done | bytes 524320 | tf_op jit(solution)/shard_map/ppermute | solution.py:323
  56.3 2.3 %shard_map.167.sums = f32[3,4,512,256]{3,2,1,0:T(8,128)S(1)} custom-call(bf16[2,512,256]{2,1,0:T(8,128)(2,1)S(1)} %collective-permute-done.12.far.refs_4_, bf16[2,256,256]{2,1,0:T(8,128)(2,1)S(1)} %collective-permute-done.13.picked.refs_5_, bf16[2,256,256]{2,1,0:T(8,128)(2,1)S(1)} %collective-permute-done.14.rest.refs_6_, ...), custom_call_target="tpu_custom_call" | custom-call | flops 1000 | bytes 1000 | tf_op jit(solution)/shard_map/pallas_call | solution.py:310
  58.6 7.1 %shard_map.168 = (f32[32,256]{1,0:T(8,128)S(1)}, bf16[4,512,256]{2,1,0:T(8,128)(2,1)S(1)}, f32[1,256]{1,0:T(1,128)S(1)}, f32[1,256]{1,0:T(1,128)S(1)}) custom-call(f32[7,256]{1,0:T(8,128)S(1)} %concatenate.9.starts.refs_5_.scales, f32[3,4,512,256]{3,2,1,0:T(8,128)S(1)} %shard_map.167.sums, bf16[2,512,256]{2,1,0:T(8,128)(2,1)S(1)} %collective-permute-done.20.far_two.refs_7_, ...), custom_call_target="tpu_custom_call" | custom-call | flops 1000 | bytes 1000 | tf_op jit(solution)/shard_map/pallas_call | solution.py:310
  66.6 1.0 shard_map.169.refs_11_
  68.4 1.0 %shard_map.172 = bf16[2,256,256]{2,1,0:T(8,128)(2,1)S(1)} custom-call(f32[7,256]{1,0:T(8,128)S(1)} %concatenate.9.starts.refs_5_.scales, bf16[4,512,256]{2,1,0:T(8,128)(2,1)S(1)} %collective-permute-done.22.two, bf16[2,9,256,256]{3,2,1,0:T(8,128)(2,1)S(1)} %shard_map.165.wings, f32[3,2,272,256]{3,2,1,0:T(8,128)S(1)} %shard_map.170.sums), custom_call_target="tpu_custom_call" | custom-call | flops 1000 | bytes 1000 | tf_op jit(solution)/shard_map/pallas_call | solution.py:310
  69.5 1.6 %collective-permute-start.24 = (bf16[2,256,256]{2,1,0:T(8,128)(2,1)S(1)}, bf16[2,256,256]{2,1,0:T(8,128)(2,1)S(1)}, u32[]{:S(2)}, u32[]{:S(2)}) collective-permute-start(bf16[2,256,256]{2,1,0:T(8,128)(2,1)S(1)} %shard_map.172), channel_id=1, source_target_pairs={{0,2},{1,3},{2,0},{3,1},{4,6},{5,7},{6,4},{7,5},{8,10},{9,11},{10,... | collective-permute-start | bytes 786440 | tf_op jit(solution)/shard_map/ppermute | solution.py:323
  71.1 2.8 %shard_map.171 = bf16[2,512,256]{2,1,0:T(8,128)(2,1)S(1)} custom-call(f32[7,256]{1,0:T(8,128)S(1)} %concatenate.9.starts.refs_5_.scales, bf16[4,512,256]{2,1,0:T(8,128)(2,1)S(1)} %get-tuple-element.139.grad.one.refs_10_, bf16[4,512,256]{2,1,0:T(8,128)(2,1)S(1)} %collective-permute-done.22.two, bf16[3,3,1024,256]{3,2,1,0:T(8,128)(2,1)S(1)} %bitcast.20, ...), custom_call_target="tpu_custom_call" | custom-call | flops 1000 | bytes 1000 | tf_op jit(solution)/shard_map/pallas_call | solution.py:310
  73.9 5.2 %shard_map.173.mine = f32[4,512,256]{2,1,0:T(8,128)S(1)} custom-call(f32[7,256]{1,0:T(8,128)S(1)} %concatenate.9.starts.refs_5_.scales, bf16[4,512,256]{2,1,0:T(8,128)(2,1)S(1)} %get-tuple-element.139.grad.one.refs_10_, bf16[4,512,256]{2,1,0:T(8,128)(2,1)S(1)} %collective-permute-done.22.two, bf16[3,3,1024,256]{3,2,1,0:T(8,128)(2,1)S(1)} %bitcast.20, ...), custom_call_target="tpu_custom_call" | custom-call | flops 1000 | bytes 1000 | tf_op jit(solution)/shard_map/pallas_call | solution.py:310
  79.7 1.5 %collective-permute-start.25 = (bf16[2,256,256]{2,1,0:T(8,128)(2,1)S(1)}, bf16[2,256,256]{2,1,0:T(8,128)(2,1)S(1)}, u32[]{:S(2)}, u32[]{:S(2)}) collective-permute-start(bf16[2,256,256]{2,1,0:T(8,128)(2,1)S(1)} %collective-permute-done.24.picked), channel_id=1, source_target_pairs={{0,4},{4,0},{8,12},{12,8},{16,20},{20,16},{24,28},{28,24},{1,5},{5... | collective-permute-start | bytes 786440 | tf_op jit(solution)/shard_map/ppermute | solution.py:323
  81.2 10.5 %shard_map.174 = f32[9,1024,256]{2,1,0:T(8,128)} custom-call(bf16[2,512,256]{2,1,0:T(8,128)(2,1)S(1)} %get-tuple-element.109.low.refs_0_, bf16[2,512,256]{2,1,0:T(8,128)(2,1)S(1)} %get-tuple-element.111.high.refs_1_, bf16[2,512,256]{2,1,0:T(8,128)(2,1)S(1)} %collective-permute-done.15.low_two.refs_2_, ...), custom_call_target="tpu_custom_call" | custom-call | flops 1000 | bytes 1000 | tf_op jit(solution)/shard_map/pallas_call | solution.py:310
  91.7 1.7 %collective-permute-done.23.low = bf16[2,512,256]{2,1,0:T(8,128)(2,1)S(1)} collective-permute-done((bf16[2,512,256]{2,1,0:T(8,128)(2,1)S(1)}, bf16[2,512,256]{2,1,0:T(8,128)(2,1)S(1)}, u32[]{:S(2)}, u32[]{:S(2)}) %collective-permute-start.23) | collective-permute-done | bytes 524320 | tf_op jit(solution)/shard_map/ppermute | solution.py:323
  93.5 1.1 %shard_map.175 = (bf16[4,512,256]{2,1,0:T(8,128)(2,1)S(1)}, bf16[4,96,256]{2,1,0:T(8,128)(2,1)S(1)}, f32[1,256]{1,0:T(1,128)S(1)}, f32[1,256]{1,0:T(1,128)S(1)}) custom-call(f32[4,512,256]{2,1,0:T(8,128)S(1)} %shard_map.173.mine, bf16[2,512,256]{2,1,0:T(8,128)(2,1)S(1)} %collective-permute-done.23.low, ...), custom_call_target="tpu_custom_call" | custom-call | flops 1000 | bytes 1000 | tf_op jit(solution)/shard_map/pallas_call | solution.py:310
  94.7 1.3 %shard_map.176.refs_3_ = bf16[2,4,512,256]{3,2,1,0:T(8,128)(2,1)S(1)} custom-call(f32[7,256]{1,0:T(8,128)S(1)} %concatenate.9.starts.refs_5_.scales, bf16[4,512,256]{2,1,0:T(8,128)(2,1)S(1)} %get-tuple-element.154.grad.refs_2_), custom_call_target="tpu_custom_call" | custom-call | flops 1000 | bytes 1000 | tf_op jit(solution)/shard_map/pallas_call | solution.py:310
  97.7 5.4 %shard_map.178 = f32[9,512,256]{2,1,0:T(8,128)} custom-call(bf16[4,512,256]{2,1,0:T(8,128)(2,1)S(1)} %get-tuple-element.159.refs_0_, bf16[4,512,256]{2,1,0:T(8,128)(2,1)S(1)} %get-tuple-element.160.refs_1_, bf16[4,512,256]{2,1,0:T(8,128)(2,1)S(1)} %get-tuple-element.154.grad.refs_2_, bf16[2,4,512,256]{3,2,1,0:T(8,128)(2,1)S(1)} %shard_map.176.refs_3_), custom_call_target="tpu_custom_call" | custom-call | flops 1000 | bytes 1000 | tf_op jit(solution)/shard_map/pallas_call | solution.py:310
  (72 shorter events, 13.8 us)
Async XLA Ops:
  0.6 30.2 %collective-permute-start.11 = (bf16[3,3,1024,256]{3,2,1,0:T(8,128)(2,1)}, bf16[3,3,1024,256]{3,2,1,0:T(8,128)(2,1)}, u32[]{:S(2)}, u32[]{:S(2)}) collective-permute-start(bf16[3,3,1024,256]{3,2,1,0:T(8,128)(2,1)} %weight.11), channel_id=1, source_target_pairs={{0,1},{1,0},{2,3},{3,2},{4,5},{5,4},{6,7},{7,6},{8,9},{9,8},{10,11... | collective-permute-start | bytes 14155784 | tf_op jit(solution)/shard_map/ppermute | solution.py:323
  2.7 7.7 %collective-permute-start.1 = (bf16[4,64,128]{2,1,0:T(8,128)(2,1)S(1)}, bf16[4,64,128]{2,1,0:T(8,128)(2,1)S(1)}, u32[]{:S(2)}, u32[]{:S(2)}) collective-permute-start(bf16[4,64,128]{2,1,0:T(8,128)(2,1)S(1)} %get-tuple-element.177), channel_id=1, source_target_pairs={{0,16},{4,20},{8,24},{12,28},{16,0},{20,4},{24,8},{28,12},{1,17},{... | collective-permute-start | bytes 196616 | tf_op jit(solution)/shard_map/ppermute | solution.py:323
  6.4 4.5 %collective-permute-start = (bf16[4,64,128]{2,1,0:T(8,128)(2,1)S(1)}, bf16[4,64,128]{2,1,0:T(8,128)(2,1)S(1)}, u32[]{:S(2)}, u32[]{:S(2)}) collective-permute-start(bf16[4,64,128]{2,1,0:T(8,128)(2,1)S(1)} %get-tuple-element.177), channel_id=1, source_target_pairs={{0,8},{4,12},{8,0},{12,4},{16,24},{20,28},{24,16},{28,20},{1,9},{5... | collective-permute-start | bytes 196616 | tf_op jit(solution)/shard_map/ppermute | solution.py:323
  8.0 6.1 %collective-permute-start.2 = (bf16[4,64,128]{2,1,0:T(8,128)(2,1)S(1)}, bf16[4,64,128]{2,1,0:T(8,128)(2,1)S(1)}, u32[]{:S(2)}, u32[]{:S(2)}) collective-permute-start(bf16[4,64,128]{2,1,0:T(8,128)(2,1)S(1)} %get-tuple-element.177), channel_id=1, source_target_pairs={{0,24},{4,28},{8,16},{12,20},{16,8},{20,12},{24,0},{28,4},{1,25},{... | collective-permute-start | bytes 196616 | tf_op jit(solution)/shard_map/ppermute | solution.py:323
  14.1 10.3 %collective-permute-start.3 = (bf16[4,4,64,128]{3,2,1,0:T(8,128)(2,1)S(1)}, bf16[4,4,64,128]{3,2,1,0:T(8,128)(2,1)S(1)}, u32[]{:S(2)}, u32[]{:S(2)}) collective-permute-start(bf16[4,4,64,128]{3,2,1,0:T(8,128)(2,1)S(1)} %pad_maximum_fusion.refs_0_), channel_id=1, source_target_pairs={{0,6},{1,7},{2,4},{3,5},{4,2},{5,3},{6,0},{7,1},{8,14},{9,15},{10,... | collective-permute-start | bytes 786440 | tf_op jit(solution)/shard_map/ppermute | solution.py:338
  16.6 11.1 %collective-permute-start.6 = (bf16[4,4,64,128]{3,2,1,0:T(8,128)(2,1)S(1)}, bf16[4,4,64,128]{3,2,1,0:T(8,128)(2,1)S(1)}, u32[]{:S(2)}, u32[]{:S(2)}) collective-permute-start(bf16[4,4,64,128]{3,2,1,0:T(8,128)(2,1)S(1)} %pad_maximum_fusion.refs_0_), channel_id=1, source_target_pairs={{0,2},{1,3},{2,0},{3,1},{4,6},{5,7},{6,4},{7,5},{8,10},{9,11},{10,... | collective-permute-start | bytes 786440 | tf_op jit(solution)/shard_map/ppermute | solution.py:323
  17.1 10.7 %collective-permute-start.5 = (bf16[4,4,64,128]{3,2,1,0:T(8,128)(2,1)S(1)}, bf16[4,4,64,128]{3,2,1,0:T(8,128)(2,1)S(1)}, u32[]{:S(2)}, u32[]{:S(2)}) collective-permute-start(bf16[4,4,64,128]{3,2,1,0:T(8,128)(2,1)S(1)} %pad_maximum_fusion.refs_0_), channel_id=1, source_target_pairs={{0,4},{4,0},{8,12},{12,8},{16,20},{20,16},{24,28},{28,24},{1,5},{5... | collective-permute-start | bytes 786440 | tf_op jit(solution)/shard_map/ppermute | solution.py:323
  17.6 5.0 %collective-permute-start.4 = (f32[1,32,256]{2,1,0:T(8,128)}, f32[1,32,256]{2,1,0:T(8,128)S(1)}, u32[]{:S(2)}, u32[]{:S(2)}) collective-permute-start(f32[1,32,256]{2,1,0:T(8,128)} %bitcast.21), channel_id=1, source_target_pairs={{0,16},{4,20},{8,24},{12,28},{16,0},{20,4},{24,8},{28,12},{1,17},{... | collective-permute-start | bytes 98312 | tf_op jit(solution)/shard_map/ppermute | solution.py:323
  22.7 8.1 %collective-permute-start.7 = (bf16[4,4,64,128]{3,2,1,0:T(8,128)(2,1)S(1)}, bf16[4,4,64,128]{3,2,1,0:T(8,128)(2,1)S(1)}, u32[]{:S(2)}, u32[]{:S(2)}) collective-permute-start(bf16[4,4,64,128]{3,2,1,0:T(8,128)(2,1)S(1)} %pad_maximum_fusion.refs_0_), channel_id=1, source_target_pairs={{0,1},{1,0},{2,3},{3,2},{4,5},{5,4},{6,7},{7,6},{8,9},{9,8},{10,11... | collective-permute-start | bytes 786440 | tf_op jit(solution)/shard_map/ppermute | solution.py:323
  27.7 3.2 %collective-permute-start.9 = (bf16[4,4,64,128]{3,2,1,0:T(8,128)(2,1)S(1)}, bf16[4,4,64,128]{3,2,1,0:T(8,128)(2,1)S(1)}, u32[]{:S(2)}, u32[]{:S(2)}) collective-permute-start(bf16[4,4,64,128]{3,2,1,0:T(8,128)(2,1)S(1)} %collective-permute-done.6.refs_2_), channel_id=1, source_target_pairs={{0,1},{1,0},{2,3},{3,2},{4,5},{5,4},{6,7},{7,6},{8,9},{9,8},{10,11... | collective-permute-start | bytes 786440 | tf_op jit(solution)/shard_map/ppermute | solution.py:323
  27.8 3.1 %collective-permute-start.8 = (bf16[4,4,64,128]{3,2,1,0:T(8,128)(2,1)S(1)}, bf16[4,4,64,128]{3,2,1,0:T(8,128)(2,1)S(1)}, u32[]{:S(2)}, u32[]{:S(2)}) collective-permute-start(bf16[4,4,64,128]{3,2,1,0:T(8,128)(2,1)S(1)} %collective-permute-done.5.refs_1_), channel_id=1, source_target_pairs={{0,1},{1,0},{2,3},{3,2},{4,5},{5,4},{6,7},{7,6},{8,9},{9,8},{10,11... | collective-permute-start | bytes 786440 | tf_op jit(solution)/shard_map/ppermute | solution.py:323
  28.2 2.7 %collective-permute-start.10 = (bf16[4,4,64,128]{3,2,1,0:T(8,128)(2,1)S(1)}, bf16[4,4,64,128]{3,2,1,0:T(8,128)(2,1)S(1)}, u32[]{:S(2)}, u32[]{:S(2)}) collective-permute-start(bf16[4,4,64,128]{3,2,1,0:T(8,128)(2,1)S(1)} %collective-permute-done.3.refs_3_), channel_id=1, source_target_pairs={{0,1},{1,0},{2,3},{3,2},{4,5},{5,4},{6,7},{7,6},{8,9},{9,8},{10,11... | collective-permute-start | bytes 786440 | tf_op jit(solution)/shard_map/ppermute | solution.py:323
  30.9 7.2 %slice-start = ((s8[4718592]{0:T(1024)(128)(4,1)}), s8[4194304]{0:T(1024)(128)(4,1)S(1)}, s32[]{:S(2)}) async-start(s8[4718592]{0:T(1024)(128)(4,1)} %bitcast.19), calls=%async_computation | async-start | bytes 8388608
  30.9 7.2 %slice-start.1 = ((s8[4718592]{0:T(1024)(128)(4,1)}), s8[524288]{0:T(1024)(128)(4,1)S(1)}, s32[]{:S(2)}) async-start(s8[4718592]{0:T(1024)(128)(4,1)} %bitcast.19), calls=%async_computation.1 | async-start | bytes 1048576
  35.3 2.6 %collective-permute-start.16 = (bf16[2,512,256]{2,1,0:T(8,128)(2,1)S(1)}, bf16[2,512,256]{2,1,0:T(8,128)(2,1)S(1)}, u32[]{:S(2)}, u32[]{:S(2)}) collective-permute-start(bf16[2,512,256]{2,1,0:T(8,128)(2,1)S(1)} %get-tuple-element.111.high.refs_1_), channel_id=1, source_target_pairs={{0,1},{1,0},{2,3},{3,2},{4,5},{5,4},{6,7},{7,6},{8,9},{9,8},{10,11... | collective-permute-start | bytes 1572872 | tf_op jit(solution)/shard_map/ppermute | solution.py:323
  35.8 2.3 %collective-permute-start.15 = (bf16[2,512,256]{2,1,0:T(8,128)(2,1)S(1)}, bf16[2,512,256]{2,1,0:T(8,128)(2,1)S(1)}, u32[]{:S(2)}, u32[]{:S(2)}) collective-permute-start(bf16[2,512,256]{2,1,0:T(8,128)(2,1)S(1)} %get-tuple-element.109.low.refs_0_), channel_id=1, source_target_pairs={{0,1},{1,0},{2,3},{3,2},{4,5},{5,4},{6,7},{7,6},{8,9},{9,8},{10,11... | collective-permute-start | bytes 1572872 | tf_op jit(solution)/shard_map/ppermute | solution.py:323
  35.9 9.1 %copy-start.1 = (f32[32,256]{1,0:T(8,128)S(1)}, f32[32,256]{1,0:T(8,128)}, u32[]{:S(2)}) copy-start(f32[32,256]{1,0:T(8,128)} %param.19) | copy-start | bytes 98308
  35.9 9.1 %collective-permute-start.13 = (bf16[2,256,256]{2,1,0:T(8,128)(2,1)S(1)}, bf16[2,256,256]{2,1,0:T(8,128)(2,1)S(1)}, u32[]{:S(2)}, u32[]{:S(2)}) collective-permute-start(bf16[2,256,256]{2,1,0:T(8,128)(2,1)S(1)} %get-tuple-element.110), channel_id=1, source_target_pairs={{0,2},{1,3},{2,0},{3,1},{4,6},{5,7},{6,4},{7,5},{8,10},{9,11},{10,... | collective-permute-start | bytes 786440 | tf_op jit(solution)/shard_map/ppermute | solution.py:323
  37.4 18.4 %collective-permute-start.12 = (bf16[2,512,256]{2,1,0:T(8,128)(2,1)S(1)}, bf16[2,512,256]{2,1,0:T(8,128)(2,1)S(1)}, u32[]{:S(2)}, u32[]{:S(2)}) collective-permute-start(bf16[2,512,256]{2,1,0:T(8,128)(2,1)S(1)} %get-tuple-element.109.low.refs_0_), channel_id=1, source_target_pairs={{0,2},{1,3},{2,0},{3,1},{4,6},{5,7},{6,4},{7,5},{8,10},{9,11},{10,... | collective-permute-start | bytes 1572872 | tf_op jit(solution)/shard_map/ppermute | solution.py:323
  45.0 4.8 %collective-permute-start.17 = (bf16[2,256,256]{2,1,0:T(8,128)(2,1)S(1)}, bf16[2,256,256]{2,1,0:T(8,128)(2,1)S(1)}, u32[]{:S(2)}, u32[]{:S(2)}) collective-permute-start(bf16[2,256,256]{2,1,0:T(8,128)(2,1)S(1)} %collective-permute-done.13.picked.refs_5_), channel_id=1, source_target_pairs={{0,1},{1,0},{2,3},{3,2},{4,5},{5,4},{6,7},{7,6},{8,9},{9,8},{10,11... | collective-permute-start | bytes 786440 | tf_op jit(solution)/shard_map/ppermute | solution.py:323
  45.0 4.8 %collective-permute-start.18 = (f32[2,32,256]{2,1,0:T(8,128)S(1)}, f32[2,32,256]{2,1,0:T(8,128)S(1)}, u32[]{:S(2)}, u32[]{:S(2)}) collective-permute-start(f32[2,32,256]{2,1,0:T(8,128)S(1)} %pad_maximum_fusion.2), channel_id=1, source_target_pairs={{0,4},{4,0},{8,12},{12,8},{16,20},{20,16},{24,28},{28,24},{1,5},{5... | collective-permute-start | bytes 196616 | tf_op jit(solution)/shard_map/ppermute | solution.py:323
  46.6 9.2 %collective-permute-start.14 = (bf16[2,256,256]{2,1,0:T(8,128)(2,1)S(1)}, bf16[2,256,256]{2,1,0:T(8,128)(2,1)S(1)}, u32[]{:S(2)}, u32[]{:S(2)}) collective-permute-start(bf16[2,256,256]{2,1,0:T(8,128)(2,1)S(1)} %collective-permute-done.13.picked.refs_5_), channel_id=1, source_target_pairs={{0,4},{4,0},{8,12},{12,8},{16,20},{20,16},{24,28},{28,24},{1,5},{5... | collective-permute-start | bytes 786440 | tf_op jit(solution)/shard_map/ppermute | solution.py:323
  49.8 5.9 %collective-permute-start.19 = (f32[4,32,256]{2,1,0:T(8,128)S(1)}, f32[4,32,256]{2,1,0:T(8,128)S(1)}, u32[]{:S(2)}, u32[]{:S(2)}) collective-permute-start(f32[4,32,256]{2,1,0:T(8,128)S(1)} %pad_maximum_fusion.1), channel_id=1, source_target_pairs={{0,8},{4,12},{8,0},{12,4},{16,24},{20,28},{24,16},{28,20},{1,9},{5... | collective-permute-start | bytes 393224 | tf_op jit(solution)/shard_map/ppermute | solution.py:323
  55.8 2.8 %collective-permute-start.20 = (bf16[2,512,256]{2,1,0:T(8,128)(2,1)S(1)}, bf16[2,512,256]{2,1,0:T(8,128)(2,1)S(1)}, u32[]{:S(2)}, u32[]{:S(2)}) collective-permute-start(bf16[2,512,256]{2,1,0:T(8,128)(2,1)S(1)} %collective-permute-done.12.far.refs_4_), channel_id=1, source_target_pairs={{0,1},{1,0},{2,3},{3,2},{4,5},{5,4},{6,7},{7,6},{8,9},{9,8},{10,11... | collective-permute-start | bytes 1572872 | tf_op jit(solution)/shard_map/ppermute | solution.py:323
  55.8 2.8 %collective-permute-start.21 = (bf16[2,256,256]{2,1,0:T(8,128)(2,1)S(1)}, bf16[2,256,256]{2,1,0:T(8,128)(2,1)S(1)}, u32[]{:S(2)}, u32[]{:S(2)}) collective-permute-start(bf16[2,256,256]{2,1,0:T(8,128)(2,1)S(1)} %collective-permute-done.14.rest.refs_6_), channel_id=1, source_target_pairs={{0,1},{1,0},{2,3},{3,2},{4,5},{5,4},{6,7},{7,6},{8,9},{9,8},{10,11... | collective-permute-start | bytes 786440 | tf_op jit(solution)/shard_map/ppermute | solution.py:323
  65.7 2.7 %collective-permute-start.22 = (bf16[4,512,256]{2,1,0:T(8,128)(2,1)S(1)}, bf16[4,512,256]{2,1,0:T(8,128)(2,1)S(1)}, u32[]{:S(2)}, u32[]{:S(2)}) collective-permute-start(bf16[4,512,256]{2,1,0:T(8,128)(2,1)S(1)} %get-tuple-element.139.grad.one.refs_10_), channel_id=1, source_target_pairs={{0,1},{1,0},{2,3},{3,2},{4,5},{5,4},{6,7},{7,6},{8,9},{9,8},{10,11... | collective-permute-start | bytes 3145736 | tf_op jit(solution)/shard_map/ppermute | solution.py:323
  69.5 9.6 %collective-permute-start.24 = (bf16[2,256,256]{2,1,0:T(8,128)(2,1)S(1)}, bf16[2,256,256]{2,1,0:T(8,128)(2,1)S(1)}, u32[]{:S(2)}, u32[]{:S(2)}) collective-permute-start(bf16[2,256,256]{2,1,0:T(8,128)(2,1)S(1)} %shard_map.172), channel_id=1, source_target_pairs={{0,2},{1,3},{2,0},{3,1},{4,6},{5,7},{6,4},{7,5},{8,10},{9,11},{10,... | collective-permute-start | bytes 786440 | tf_op jit(solution)/shard_map/ppermute | solution.py:323
  79.0 14.4 %collective-permute-start.26 = (bf16[3,3,512,256]{3,2,1,0:T(8,128)(2,1)S(1)}, bf16[3,3,512,256]{3,2,1,0:T(8,128)(2,1)S(1)}, u32[]{:S(2)}, u32[]{:S(2)}) collective-permute-start(bf16[3,3,512,256]{3,2,1,0:T(8,128)(2,1)S(1)} %shard_map.161.refs_4_.weight), channel_id=1, source_target_pairs={{0,1},{1,0},{2,3},{3,2},{4,5},{5,4},{6,7},{7,6},{8,9},{9,8},{10,11... | collective-permute-start | bytes 7077896 | tf_op jit(solution)/shard_map/ppermute | solution.py:323
  79.1 14.3 %collective-permute-start.23 = (bf16[2,512,256]{2,1,0:T(8,128)(2,1)S(1)}, bf16[2,512,256]{2,1,0:T(8,128)(2,1)S(1)}, u32[]{:S(2)}, u32[]{:S(2)}) collective-permute-start(bf16[2,512,256]{2,1,0:T(8,128)(2,1)S(1)} %shard_map.171), channel_id=1, source_target_pairs={{0,2},{1,3},{2,0},{3,1},{4,6},{5,7},{6,4},{7,5},{8,10},{9,11},{10,... | collective-permute-start | bytes 1572872 | tf_op jit(solution)/shard_map/ppermute | solution.py:323
  79.7 12.0 %collective-permute-start.25 = (bf16[2,256,256]{2,1,0:T(8,128)(2,1)S(1)}, bf16[2,256,256]{2,1,0:T(8,128)(2,1)S(1)}, u32[]{:S(2)}, u32[]{:S(2)}) collective-permute-start(bf16[2,256,256]{2,1,0:T(8,128)(2,1)S(1)} %collective-permute-done.24.picked), channel_id=1, source_target_pairs={{0,4},{4,0},{8,12},{12,8},{16,20},{20,16},{24,28},{28,24},{1,5},{5... | collective-permute-start | bytes 786440 | tf_op jit(solution)/shard_map/ppermute | solution.py:323
  94.6 1.5 %collective-permute-start.27 = (bf16[4,96,256]{2,1,0:T(8,128)(2,1)S(1)}, bf16[4,96,256]{2,1,0:T(8,128)(2,1)S(1)}, u32[]{:S(2)}, u32[]{:S(2)}) collective-permute-start(bf16[4,96,256]{2,1,0:T(8,128)(2,1)S(1)} %get-tuple-element.153.one), channel_id=1, source_target_pairs={{0,1},{1,0},{2,3},{3,2},{4,5},{5,4},{6,7},{7,6},{8,9},{9,8},{10,11... | collective-permute-start | bytes 589832 | tf_op jit(solution)/shard_map/ppermute | solution.py:323
  97.1 6.0 %collective-permute-start.28 = (f32[4,64,128]{2,1,0:T(8,128)S(1)}, f32[4,64,128]{2,1,0:T(8,128)S(1)}, u32[]{:S(2)}, u32[]{:S(2)}) collective-permute-start(f32[4,64,128]{2,1,0:T(8,128)S(1)} %get-tuple-element.158), channel_id=1, source_target_pairs={{0,2},{1,3},{2,0},{3,1},{4,6},{5,7},{6,4},{7,5},{8,10},{9,11},{10,... | collective-permute-start | bytes 393224 | tf_op jit(solution)/shard_map/ppermute | solution.py:323
  (6 other events, 5.2 us)

commit v9 on v8

--- a/solution.py
+++ b/solution.py
@@ -491,8 +491,8 @@
 
 def first_kernel(starts, *refs):
     blocks, (weight, scales, keep), sources = refs[:4], refs[4:7], refs[7:10]
-    low, high, picked, field, middle, stats = refs[10:16]
-    lower, upper = refs[16:]
+    field, middle, stats = refs[10:13]
+    lower, upper = refs[13:]
     mel_count, total, _ = field.shape
     out_width = middle.shape[2]
     place = lax.axis_index("tm")
@@ -521,44 +521,55 @@
     stats[0:1] = center
     stats[1:2] = inverse
     stats[2:3] = pixels
-    scale = scales[0:1] * inverse
-    offset = scales[1:2] - center * scale
+
+def active_kernel(first, pre, stats, scales, keep, out, *picked):
+    mel_count, total, width = out.shape
+    scale = scales[0:1] * stats[1:2]
+    offset = scales[1:2] - stats[0:1] * scale
 
     def activate(at, carry):
-        mask = widen(keep[pl.ds(at, ROWS)], out_width)
+        mask = widen(keep[pl.ds(at, ROWS)], width)
         for m in range(mel_count):
-            value = middle[m, pl.ds(at, ROWS)] * scale + offset
-            rows = (value * phi_parts(value) * mask).astype(bf16)
-            if m < mel_count // 2:
-                low[m, pl.ds(at, ROWS)] = rows
-            else:
-                high[m - mel_count // 2, pl.ds(at, ROWS)] = rows
+            value = pre[first + m, pl.ds(at, ROWS)] * scale + offset
+            out[m, pl.ds(at, ROWS)] = (value * phi_parts(value) * mask).astype(bf16)
         return carry
 
     by_rows(total, activate, 0)
-    reach = picked.shape[1]
-    for m in range(picked.shape[0]):
-        picked[m] = high[m, pl.ds(pl.multiple_of((place % 2) * reach, reach), reach)]
+    for part in picked:
+        reach = part.shape[1]
+        side = lax.axis_index("tm") % 2
+        part[...] = out[:, pl.ds(pl.multiple_of(side * reach, reach), reach)]
+
+
+def active(first, count, pick, pre, stats, scales, keep):
+    _, total, width = pre.shape
+    shapes = [(count, total, width)] + [(count, total // 2, width)] * pick
+    return call(
+        functools.partial(active_kernel, first),
+        (pre, stats, scales, keep),
+        [whole_spec()] * 4,
+        [(shape, bf16) for shape in shapes],
+        [whole_spec()] * len(shapes),
+        [],
+        0,
+        4,
+    )
 
 
 def first_block(blocks, weight, scales, keep, sources, starts, total):
     _, mel_count, frames, lanes = blocks[0].shape
     out_width = weight.shape[3]
     padded = (mel_count, total + 2 * TILE, out_width)
-    half = (mel_count // 2, total, out_width)
     return call(
         first_kernel,
         (starts, *blocks, weight, scales, keep, *sources),
         [whole_spec()] + [whole_spec()] * 10,
         [
-            (half, bf16),
-            (half, bf16),
-            ((mel_count // 2, total // 2, out_width), bf16),
             ((mel_count, total, 2 * lanes), bf16),
             ((mel_count, total, out_width), f32),
             ((TILE, out_width), f32),
         ],
-        [whole_spec()] * 6,
+        [whole_spec()] * 3,
         [pltpu.VMEM(padded, f32), pltpu.VMEM(padded, f32)],
         0,
         16,
@@ -1344,9 +1355,13 @@
     other_conv2 = swap(conv2_weight, "chan", 1)
     others, other_conv2 = lax.optimization_barrier((others, other_conv2))
 
-    low, high, picked, other_column, pre, stats = first_block(
+    other_column, pre, stats = first_block(
         others, conv1_weight, table, keep, sources, table, total
     )
+    half = mel_count // 2
+    high, picked = active(half, half, 1, pre, stats, table, keep)
+    picked, low_pre = lax.optimization_barrier((picked, pre))
+    (low,) = active(0, half, 0, low_pre, stats, table, keep)
     fields1 = (column, other_column)
 
     far_picked = swap(picked, "chan", 2)

time: 104 us -> 104 us (level)
    pallas_call x19 -> x21, Pallas kernels: 54.6 us -> 54.6 us  [call(): pl.pallas_call(body, out_shape=tuple((jax.ShapeDtypeStruct(s, d) for s, d...]
where the time goes in v9:
time: 104 us
  Pallas kernels  54.6 us (52%)
  starting transfers between devices  22.9 us (22%)
  waiting for transfers between devices  21.5 us (21%)
  local copies, waits for them, and re-layouts  2.25 us (2%)
  other arithmetic  1.64 us (2%)
    pallas_call x21, Pallas kernels, call(): pl.pallas_call(body, out_shape=tuple((jax.ShapeDtypeStruct(s, d) for s, d...  54.6 us
    ppermute x28, starting transfers between devices, swap(): return lax.ppermute(shard, axis, [(i, i ^ bit) for i in range(count)])  20.4 us
    ppermute x28, waiting for transfers between devices, swap(): return lax.ppermute(shard, axis, [(i, i ^ bit) for i in range(count)])  19.8 us
    ppermute x1, starting transfers between devices, swap_both(): return lax.ppermute(shard, (first, second), pairs)  2.51 us
    unnamed x18, local copies, waits for them, and re-layouts  2.15 us
  transfers between devices with their start and end apart: 29, of which 14 were waited for; matrix products, arithmetic and copies ran while one was open for 2% of the time, Pallas kernels for 38%

profile of v9, /device:TPU:0, one launch (start us, length us, event | category | flops | bytes accessed | tf_op | source)
XLA Modules:
  0.0 103.8 jit_solution(6214403878968643365)
XLA Ops:
  2.7 3.7 %collective-permute-start.1 = (bf16[4,64,128]{2,1,0:T(8,128)(2,1)S(1)}, bf16[4,64,128]{2,1,0:T(8,128)(2,1)S(1)}, u32[]{:S(2)}, u32[]{:S(2)}) collective-permute-start(bf16[4,64,128]{2,1,0:T(8,128)(2,1)S(1)} %get-tuple-element.179), channel_id=1, source_target_pairs={{0,16},{4,20},{8,24},{12,28},{16,0},{20,4},{24,8},{28,12},{1,17},{... | collective-permute-start | bytes 196616 | tf_op jit(solution)/shard_map/ppermute | solution.py:323
  6.4 1.6 %collective-permute-start = (bf16[4,64,128]{2,1,0:T(8,128)(2,1)S(1)}, bf16[4,64,128]{2,1,0:T(8,128)(2,1)S(1)}, u32[]{:S(2)}, u32[]{:S(2)}) collective-permute-start(bf16[4,64,128]{2,1,0:T(8,128)(2,1)S(1)} %get-tuple-element.179), channel_id=1, source_target_pairs={{0,8},{4,12},{8,0},{12,4},{16,24},{20,28},{24,16},{28,20},{1,9},{5... | collective-permute-start | bytes 196616 | tf_op jit(solution)/shard_map/ppermute | solution.py:323
  8.0 2.5 %collective-permute-done.1 = bf16[4,64,128]{2,1,0:T(8,128)(2,1)S(1)} collective-permute-done((bf16[4,64,128]{2,1,0:T(8,128)(2,1)S(1)}, bf16[4,64,128]{2,1,0:T(8,128)(2,1)S(1)}, u32[]{:S(2)}, u32[]{:S(2)}) %collective-permute-start.1) | collective-permute-done | bytes 65568 | tf_op jit(solution)/shard_map/ppermute | solution.py:323
  10.9 3.1 %collective-permute-done.2 = bf16[4,64,128]{2,1,0:T(8,128)(2,1)S(1)} collective-permute-done((bf16[4,64,128]{2,1,0:T(8,128)(2,1)S(1)}, bf16[4,64,128]{2,1,0:T(8,128)(2,1)S(1)}, u32[]{:S(2)}, u32[]{:S(2)}) %collective-permute-start.2) | collective-permute-done | bytes 65568 | tf_op jit(solution)/shard_map/ppermute | solution.py:323
  14.1 2.5 %collective-permute-start.3 = (bf16[4,4,64,128]{3,2,1,0:T(8,128)(2,1)S(1)}, bf16[4,4,64,128]{3,2,1,0:T(8,128)(2,1)S(1)}, u32[]{:S(2)}, u32[]{:S(2)}) collective-permute-start(bf16[4,4,64,128]{3,2,1,0:T(8,128)(2,1)S(1)} %pad_maximum_fusion.refs_0_), channel_id=1, source_target_pairs={{0,6},{1,7},{2,4},{3,5},{4,2},{5,3},{6,0},{7,1},{8,14},{9,15},{10,... | collective-permute-start | bytes 786440 | tf_op jit(solution)/shard_map/ppermute | solution.py:338
  17.6 2.0 %collective-permute-start.4 = (f32[1,32,256]{2,1,0:T(8,128)}, f32[1,32,256]{2,1,0:T(8,128)S(1)}, u32[]{:S(2)}, u32[]{:S(2)}) collective-permute-start(f32[1,32,256]{2,1,0:T(8,128)} %bitcast.21), channel_id=1, source_target_pairs={{0,16},{4,20},{8,24},{12,28},{16,0},{20,4},{24,8},{28,12},{1,17},{... | collective-permute-start | bytes 98312 | tf_op jit(solution)/shard_map/ppermute | solution.py:323
  19.6 1.7 %copy-done = bf16[3,3,512,256]{3,2,1,0:T(8,128)(2,1)S(1)} copy-done((bf16[3,3,512,256]{3,2,1,0:T(8,128)(2,1)S(1)}, bf16[3,3,512,256]{3,2,1,0:T(8,128)(2,1)}, u32[]{:S(2)}) %copy-start) | copy-done | bytes 2359320
  22.7 1.7 %collective-permute-done.3.refs_3_ = bf16[4,4,64,128]{3,2,1,0:T(8,128)(2,1)S(1)} collective-permute-done((bf16[4,4,64,128]{3,2,1,0:T(8,128)(2,1)S(1)}, bf16[4,4,64,128]{3,2,1,0:T(8,128)(2,1)S(1)}, u32[]{:S(2)}, u32[]{:S(2)}) %collective-permute-start.3) | collective-permute-done | bytes 262176 | tf_op jit(solution)/shard_map/ppermute | solution.py:338
  24.3 3.3 %collective-permute-done.6.refs_2_ = bf16[4,4,64,128]{3,2,1,0:T(8,128)(2,1)S(1)} collective-permute-done((bf16[4,4,64,128]{3,2,1,0:T(8,128)(2,1)S(1)}, bf16[4,4,64,128]{3,2,1,0:T(8,128)(2,1)S(1)}, u32[]{:S(2)}, u32[]{:S(2)}) %collective-permute-start.6) | collective-permute-done | bytes 262176 | tf_op jit(solution)/shard_map/ppermute | solution.py:323
  28.3 2.5 %shard_map.162 = (bf16[4,512,256]{2,1,0:T(8,128)(2,1)S(1)}, f32[512,128]{1,0:T(8,128)S(1)}, f32[4,528,256]{2,1,0:T(8,128)S(1)}, f32[4,512,256]{2,1,0:T(8,128)S(1)}, f32[4,528,256]{2,1,0:T(8,128)S(1)}) custom-call(bf16[4,4,64,128]{3,2,1,0:T(8,128)(2,1)S(1)} %pad_maximum_fusion.refs_0_, bf16[4,4,64,128]{3,2,1,0:T(8,128)(2,1)S(1)} %collective-permute-done.5.refs_1_, ...), custom_call_target="tpu_custom_call" | custom-call | flops 1000 | bytes 1000 | tf_op jit(solution)/shard_map/pallas_call | solution.py:310
  30.9 3.8 %shard_map.163 = (bf16[4,512,256]{2,1,0:T(8,128)(2,1)S(1)}, f32[4,512,256]{2,1,0:T(8,128)S(1)}, f32[8,256]{1,0:T(8,128)S(1)}) custom-call(f32[7,256]{1,0:T(8,128)S(1)} %concatenate.9.starts.refs_5_.scales, bf16[4,4,64,128]{3,2,1,0:T(8,128)(2,1)S(1)} %collective-permute-done.7.refs_0_, bf16[4,4,64,128]{3,2,1,0:T(8,128)(2,1)S(1)} %collective-permute-done.8.refs_1_, ...), custom_call_target="tpu_custom_call" | custom-call | flops 1000 | bytes 1000 | tf_op jit(solution)/shard_map/pallas_call | solution.py:310
  36.0 1.5 %collective-permute-start.13 = (bf16[2,256,256]{2,1,0:T(8,128)(2,1)S(1)}, bf16[2,256,256]{2,1,0:T(8,128)(2,1)S(1)}, u32[]{:S(2)}, u32[]{:S(2)}) collective-permute-start(bf16[2,256,256]{2,1,0:T(8,128)(2,1)S(1)} %get-tuple-element.114), channel_id=1, source_target_pairs={{0,2},{1,3},{2,0},{3,1},{4,6},{5,7},{6,4},{7,5},{8,10},{9,11},{10,... | collective-permute-start | bytes 786440 | tf_op jit(solution)/shard_map/ppermute | solution.py:323
  38.2 4.2 %shard_map.166.near = f32[3,4,512,256]{3,2,1,0:T(8,128)S(1)} custom-call(bf16[2,512,256]{2,1,0:T(8,128)(2,1)S(1)} %shard_map.165.low.refs_0_, bf16[2,512,256]{2,1,0:T(8,128)(2,1)S(1)} %get-tuple-element.115.high.refs_1_, bf16[2,512,256]{2,1,0:T(8,128)(2,1)S(1)} %collective-permute-done.15.low_two.refs_2_, ...), custom_call_target="tpu_custom_call" | custom-call | flops 1000 | bytes 1000 | tf_op jit(solution)/shard_map/pallas_call | solution.py:310
  42.4 2.7 %collective-permute-done.13.picked.refs_5_ = bf16[2,256,256]{2,1,0:T(8,128)(2,1)S(1)} collective-permute-done((bf16[2,256,256]{2,1,0:T(8,128)(2,1)S(1)}, bf16[2,256,256]{2,1,0:T(8,128)(2,1)S(1)}, u32[]{:S(2)}, u32[]{:S(2)}) %collective-permute-start.13) | collective-permute-done | bytes 262176 | tf_op jit(solution)/shard_map/ppermute | solution.py:323
  45.1 1.6 %collective-permute-start.18 = (f32[2,32,256]{2,1,0:T(8,128)S(1)}, f32[2,32,256]{2,1,0:T(8,128)S(1)}, u32[]{:S(2)}, u32[]{:S(2)}) collective-permute-start(f32[2,32,256]{2,1,0:T(8,128)S(1)} %pad_maximum_fusion.2), channel_id=1, source_target_pairs={{0,4},{4,0},{8,12},{12,8},{16,20},{20,16},{24,28},{28,24},{1,5},{5... | collective-permute-start | bytes 196616 | tf_op jit(solution)/shard_map/ppermute | solution.py:323
  47.2 1.8 %shard_map.167.wings = bf16[2,9,256,256]{3,2,1,0:T(8,128)(2,1)S(1)} custom-call(bf16[3,3,1024,256]{3,2,1,0:T(8,128)(2,1)} %collective-permute-done.11.weight), custom_call_target="tpu_custom_call" | custom-call | flops 1000 | bytes 1000 | tf_op jit(solution)/shard_map/pallas_call | solution.py:310
  49.9 1.4 %collective-permute-start.19 = (f32[4,32,256]{2,1,0:T(8,128)S(1)}, f32[4,32,256]{2,1,0:T(8,128)S(1)}, u32[]{:S(2)}, u32[]{:S(2)}) collective-permute-start(f32[4,32,256]{2,1,0:T(8,128)S(1)} %pad_maximum_fusion.1), channel_id=1, source_target_pairs={{0,8},{4,12},{8,0},{12,4},{16,24},{20,28},{24,16},{28,20},{1,9},{5... | collective-permute-start | bytes 393224 | tf_op jit(solution)/shard_map/ppermute | solution.py:323
  51.3 1.2 %shard_map.168 = (f32[4,512,256]{2,1,0:T(8,128)S(1)}, f32[4,512,256]{2,1,0:T(8,128)S(1)}) custom-call(f32[4,512,256]{2,1,0:T(8,128)S(1)} %get-tuple-element.124.pre, f32[8,256]{1,0:T(8,128)S(1)} %get-tuple-element.111.stats, f32[7,256]{1,0:T(8,128)S(1)} %concatenate.9.starts.refs_5_.scales, f32[512,128]{1,0:T(8,128)S(1)} %get-tuple-element.106.refs_6_.keep), custom_call_target="tpu_custom_call" | custom-call | flops 1000 | bytes 1000 | tf_op jit(solution)/shard_map/pallas_call | solution.py:310
  52.5 3.4 %collective-permute-done.12.far.refs_4_ = bf16[2,512,256]{2,1,0:T(8,128)(2,1)S(1)} collective-permute-done((bf16[2,512,256]{2,1,0:T(8,128)(2,1)S(1)}, bf16[2,512,256]{2,1,0:T(8,128)(2,1)S(1)}, u32[]{:S(2)}, u32[]{:S(2)}) %collective-permute-start.12) | collective-permute-done | bytes 524320 | tf_op jit(solution)/shard_map/ppermute | solution.py:323
  56.4 2.2 %shard_map.169.sums = f32[3,4,512,256]{3,2,1,0:T(8,128)S(1)} custom-call(bf16[2,512,256]{2,1,0:T(8,128)(2,1)S(1)} %collective-permute-done.12.far.refs_4_, bf16[2,256,256]{2,1,0:T(8,128)(2,1)S(1)} %collective-permute-done.13.picked.refs_5_, bf16[2,256,256]{2,1,0:T(8,128)(2,1)S(1)} %collective-permute-done.14.rest.refs_6_, ...), custom_call_target="tpu_custom_call" | custom-call | flops 1000 | bytes 1000 | tf_op jit(solution)/shard_map/pallas_call | solution.py:310
  58.6 7.1 %shard_map.170 = (f32[32,256]{1,0:T(8,128)S(1)}, bf16[4,512,256]{2,1,0:T(8,128)(2,1)S(1)}, f32[1,256]{1,0:T(1,128)S(1)}, f32[1,256]{1,0:T(1,128)S(1)}) custom-call(f32[7,256]{1,0:T(8,128)S(1)} %concatenate.9.starts.refs_5_.scales, f32[3,4,512,256]{3,2,1,0:T(8,128)S(1)} %shard_map.169.sums, bf16[2,512,256]{2,1,0:T(8,128)(2,1)S(1)} %collective-permute-done.20.far_two.refs_7_, ...), custom_call_target="tpu_custom_call" | custom-call | flops 1000 | bytes 1000 | tf_op jit(solution)/shard_map/pallas_call | solution.py:310
  66.6 1.0 shard_map.171.refs_11_
  68.5 1.0 shard_map.174
  69.5 1.6 %collective-permute-start.24 = (bf16[2,256,256]{2,1,0:T(8,128)(2,1)S(1)}, bf16[2,256,256]{2,1,0:T(8,128)(2,1)S(1)}, u32[]{:S(2)}, u32[]{:S(2)}) collective-permute-start(bf16[2,256,256]{2,1,0:T(8,128)(2,1)S(1)} %shard_map.174), channel_id=1, source_target_pairs={{0,2},{1,3},{2,0},{3,1},{4,6},{5,7},{6,4},{7,5},{8,10},{9,11},{10,... | collective-permute-start | bytes 786440 | tf_op jit(solution)/shard_map/ppermute | solution.py:323
  71.1 2.8 %shard_map.173 = bf16[2,512,256]{2,1,0:T(8,128)(2,1)S(1)} custom-call(f32[7,256]{1,0:T(8,128)S(1)} %concatenate.9.starts.refs_5_.scales, bf16[4,512,256]{2,1,0:T(8,128)(2,1)S(1)} %get-tuple-element.141.grad.one.refs_10_, bf16[4,512,256]{2,1,0:T(8,128)(2,1)S(1)} %collective-permute-done.22.two, bf16[3,3,1024,256]{3,2,1,0:T(8,128)(2,1)S(1)} %bitcast.20, ...), custom_call_target="tpu_custom_call" | custom-call | flops 1000 | bytes 1000 | tf_op jit(solution)/shard_map/pallas_call | solution.py:310
  73.9 5.2 %shard_map.175.mine = f32[4,512,256]{2,1,0:T(8,128)S(1)} custom-call(f32[7,256]{1,0:T(8,128)S(1)} %concatenate.9.starts.refs_5_.scales, bf16[4,512,256]{2,1,0:T(8,128)(2,1)S(1)} %get-tuple-element.141.grad.one.refs_10_, bf16[4,512,256]{2,1,0:T(8,128)(2,1)S(1)} %collective-permute-done.22.two, bf16[3,3,1024,256]{3,2,1,0:T(8,128)(2,1)S(1)} %bitcast.20, ...), custom_call_target="tpu_custom_call" | custom-call | flops 1000 | bytes 1000 | tf_op jit(solution)/shard_map/pallas_call | solution.py:310
  79.7 1.5 %collective-permute-start.25 = (bf16[2,256,256]{2,1,0:T(8,128)(2,1)S(1)}, bf16[2,256,256]{2,1,0:T(8,128)(2,1)S(1)}, u32[]{:S(2)}, u32[]{:S(2)}) collective-permute-start(bf16[2,256,256]{2,1,0:T(8,128)(2,1)S(1)} %collective-permute-done.24.picked), channel_id=1, source_target_pairs={{0,4},{4,0},{8,12},{12,8},{16,20},{20,16},{24,28},{28,24},{1,5},{5... | collective-permute-start | bytes 786440 | tf_op jit(solution)/shard_map/ppermute | solution.py:323
  81.2 10.6 %shard_map.176 = f32[9,1024,256]{2,1,0:T(8,128)} custom-call(bf16[2,512,256]{2,1,0:T(8,128)(2,1)S(1)} %shard_map.165.low.refs_0_, bf16[2,512,256]{2,1,0:T(8,128)(2,1)S(1)} %get-tuple-element.115.high.refs_1_, bf16[2,512,256]{2,1,0:T(8,128)(2,1)S(1)} %collective-permute-done.15.low_two.refs_2_, ...), custom_call_target="tpu_custom_call" | custom-call | flops 1000 | bytes 1000 | tf_op jit(solution)/shard_map/pallas_call | solution.py:310
  91.9 1.6 %collective-permute-done.23.low = bf16[2,512,256]{2,1,0:T(8,128)(2,1)S(1)} collective-permute-done((bf16[2,512,256]{2,1,0:T(8,128)(2,1)S(1)}, bf16[2,512,256]{2,1,0:T(8,128)(2,1)S(1)}, u32[]{:S(2)}, u32[]{:S(2)}) %collective-permute-start.23) | collective-permute-done | bytes 524320 | tf_op jit(solution)/shard_map/ppermute | solution.py:323
  94.6 1.3 %shard_map.178.refs_3_ = bf16[2,4,512,256]{3,2,1,0:T(8,128)(2,1)S(1)} custom-call(f32[7,256]{1,0:T(8,128)S(1)} %concatenate.9.starts.refs_5_.scales, bf16[4,512,256]{2,1,0:T(8,128)(2,1)S(1)} %get-tuple-element.156.grad.refs_2_), custom_call_target="tpu_custom_call" | custom-call | flops 1000 | bytes 1000 | tf_op jit(solution)/shard_map/pallas_call | solution.py:310
  96.0 1.0 shard_map.179
  97.6 5.4 %shard_map.180 = f32[9,512,256]{2,1,0:T(8,128)} custom-call(bf16[4,512,256]{2,1,0:T(8,128)(2,1)S(1)} %get-tuple-element.161.refs_0_, bf16[4,512,256]{2,1,0:T(8,128)(2,1)S(1)} %get-tuple-element.162.refs_1_, bf16[4,512,256]{2,1,0:T(8,128)(2,1)S(1)} %get-tuple-element.156.grad.refs_2_, bf16[2,4,512,256]{3,2,1,0:T(8,128)(2,1)S(1)} %shard_map.178.refs_3_), custom_call_target="tpu_custom_call" | custom-call | flops 1000 | bytes 1000 | tf_op jit(solution)/shard_map/pallas_call | solution.py:310
  (74 shorter events, 14.5 us)
Async XLA Ops:
  0.6 30.2 %collective-permute-start.11 = (bf16[3,3,1024,256]{3,2,1,0:T(8,128)(2,1)}, bf16[3,3,1024,256]{3,2,1,0:T(8,128)(2,1)}, u32[]{:S(2)}, u32[]{:S(2)}) collective-permute-start(bf16[3,3,1024,256]{3,2,1,0:T(8,128)(2,1)} %weight.11), channel_id=1, source_target_pairs={{0,1},{1,0},{2,3},{3,2},{4,5},{5,4},{6,7},{7,6},{8,9},{9,8},{10,11... | collective-permute-start | bytes 14155784 | tf_op jit(solution)/shard_map/ppermute | solution.py:323
  2.7 7.7 %collective-permute-start.1 = (bf16[4,64,128]{2,1,0:T(8,128)(2,1)S(1)}, bf16[4,64,128]{2,1,0:T(8,128)(2,1)S(1)}, u32[]{:S(2)}, u32[]{:S(2)}) collective-permute-start(bf16[4,64,128]{2,1,0:T(8,128)(2,1)S(1)} %get-tuple-element.179), channel_id=1, source_target_pairs={{0,16},{4,20},{8,24},{12,28},{16,0},{20,4},{24,8},{28,12},{1,17},{... | collective-permute-start | bytes 196616 | tf_op jit(solution)/shard_map/ppermute | solution.py:323
  6.4 4.5 %collective-permute-start = (bf16[4,64,128]{2,1,0:T(8,128)(2,1)S(1)}, bf16[4,64,128]{2,1,0:T(8,128)(2,1)S(1)}, u32[]{:S(2)}, u32[]{:S(2)}) collective-permute-start(bf16[4,64,128]{2,1,0:T(8,128)(2,1)S(1)} %get-tuple-element.179), channel_id=1, source_target_pairs={{0,8},{4,12},{8,0},{12,4},{16,24},{20,28},{24,16},{28,20},{1,9},{5... | collective-permute-start | bytes 196616 | tf_op jit(solution)/shard_map/ppermute | solution.py:323
  8.0 6.1 %collective-permute-start.2 = (bf16[4,64,128]{2,1,0:T(8,128)(2,1)S(1)}, bf16[4,64,128]{2,1,0:T(8,128)(2,1)S(1)}, u32[]{:S(2)}, u32[]{:S(2)}) collective-permute-start(bf16[4,64,128]{2,1,0:T(8,128)(2,1)S(1)} %get-tuple-element.179), channel_id=1, source_target_pairs={{0,24},{4,28},{8,16},{12,20},{16,8},{20,12},{24,0},{28,4},{1,25},{... | collective-permute-start | bytes 196616 | tf_op jit(solution)/shard_map/ppermute | solution.py:323
  14.1 10.3 %collective-permute-start.3 = (bf16[4,4,64,128]{3,2,1,0:T(8,128)(2,1)S(1)}, bf16[4,4,64,128]{3,2,1,0:T(8,128)(2,1)S(1)}, u32[]{:S(2)}, u32[]{:S(2)}) collective-permute-start(bf16[4,4,64,128]{3,2,1,0:T(8,128)(2,1)S(1)} %pad_maximum_fusion.refs_0_), channel_id=1, source_target_pairs={{0,6},{1,7},{2,4},{3,5},{4,2},{5,3},{6,0},{7,1},{8,14},{9,15},{10,... | collective-permute-start | bytes 786440 | tf_op jit(solution)/shard_map/ppermute | solution.py:338
  16.6 11.1 %collective-permute-start.6 = (bf16[4,4,64,128]{3,2,1,0:T(8,128)(2,1)S(1)}, bf16[4,4,64,128]{3,2,1,0:T(8,128)(2,1)S(1)}, u32[]{:S(2)}, u32[]{:S(2)}) collective-permute-start(bf16[4,4,64,128]{3,2,1,0:T(8,128)(2,1)S(1)} %pad_maximum_fusion.refs_0_), channel_id=1, source_target_pairs={{0,2},{1,3},{2,0},{3,1},{4,6},{5,7},{6,4},{7,5},{8,10},{9,11},{10,... | collective-permute-start | bytes 786440 | tf_op jit(solution)/shard_map/ppermute | solution.py:323
  17.1 10.7 %collective-permute-start.5 = (bf16[4,4,64,128]{3,2,1,0:T(8,128)(2,1)S(1)}, bf16[4,4,64,128]{3,2,1,0:T(8,128)(2,1)S(1)}, u32[]{:S(2)}, u32[]{:S(2)}) collective-permute-start(bf16[4,4,64,128]{3,2,1,0:T(8,128)(2,1)S(1)} %pad_maximum_fusion.refs_0_), channel_id=1, source_target_pairs={{0,4},{4,0},{8,12},{12,8},{16,20},{20,16},{24,28},{28,24},{1,5},{5... | collective-permute-start | bytes 786440 | tf_op jit(solution)/shard_map/ppermute | solution.py:323
  17.6 5.0 %collective-permute-start.4 = (f32[1,32,256]{2,1,0:T(8,128)}, f32[1,32,256]{2,1,0:T(8,128)S(1)}, u32[]{:S(2)}, u32[]{:S(2)}) collective-permute-start(f32[1,32,256]{2,1,0:T(8,128)} %bitcast.21), channel_id=1, source_target_pairs={{0,16},{4,20},{8,24},{12,28},{16,0},{20,4},{24,8},{28,12},{1,17},{... | collective-permute-start | bytes 98312 | tf_op jit(solution)/shard_map/ppermute | solution.py:323
  22.7 8.1 %collective-permute-start.7 = (bf16[4,4,64,128]{3,2,1,0:T(8,128)(2,1)S(1)}, bf16[4,4,64,128]{3,2,1,0:T(8,128)(2,1)S(1)}, u32[]{:S(2)}, u32[]{:S(2)}) collective-permute-start(bf16[4,4,64,128]{3,2,1,0:T(8,128)(2,1)S(1)} %pad_maximum_fusion.refs_0_), channel_id=1, source_target_pairs={{0,1},{1,0},{2,3},{3,2},{4,5},{5,4},{6,7},{7,6},{8,9},{9,8},{10,11... | collective-permute-start | bytes 786440 | tf_op jit(solution)/shard_map/ppermute | solution.py:323
  27.7 3.2 %collective-permute-start.9 = (bf16[4,4,64,128]{3,2,1,0:T(8,128)(2,1)S(1)}, bf16[4,4,64,128]{3,2,1,0:T(8,128)(2,1)S(1)}, u32[]{:S(2)}, u32[]{:S(2)}) collective-permute-start(bf16[4,4,64,128]{3,2,1,0:T(8,128)(2,1)S(1)} %collective-permute-done.6.refs_2_), channel_id=1, source_target_pairs={{0,1},{1,0},{2,3},{3,2},{4,5},{5,4},{6,7},{7,6},{8,9},{9,8},{10,11... | collective-permute-start | bytes 786440 | tf_op jit(solution)/shard_map/ppermute | solution.py:323
  27.8 3.1 %collective-permute-start.8 = (bf16[4,4,64,128]{3,2,1,0:T(8,128)(2,1)S(1)}, bf16[4,4,64,128]{3,2,1,0:T(8,128)(2,1)S(1)}, u32[]{:S(2)}, u32[]{:S(2)}) collective-permute-start(bf16[4,4,64,128]{3,2,1,0:T(8,128)(2,1)S(1)} %collective-permute-done.5.refs_1_), channel_id=1, source_target_pairs={{0,1},{1,0},{2,3},{3,2},{4,5},{5,4},{6,7},{7,6},{8,9},{9,8},{10,11... | collective-permute-start | bytes 786440 | tf_op jit(solution)/shard_map/ppermute | solution.py:323
  28.2 2.7 %collective-permute-start.10 = (bf16[4,4,64,128]{3,2,1,0:T(8,128)(2,1)S(1)}, bf16[4,4,64,128]{3,2,1,0:T(8,128)(2,1)S(1)}, u32[]{:S(2)}, u32[]{:S(2)}) collective-permute-start(bf16[4,4,64,128]{3,2,1,0:T(8,128)(2,1)S(1)} %collective-permute-done.3.refs_3_), channel_id=1, source_target_pairs={{0,1},{1,0},{2,3},{3,2},{4,5},{5,4},{6,7},{7,6},{8,9},{9,8},{10,11... | collective-permute-start | bytes 786440 | tf_op jit(solution)/shard_map/ppermute | solution.py:323
  30.9 7.3 %slice-start = ((s8[4718592]{0:T(1024)(128)(4,1)}), s8[4194304]{0:T(1024)(128)(4,1)S(1)}, s32[]{:S(2)}) async-start(s8[4718592]{0:T(1024)(128)(4,1)} %bitcast.19), calls=%async_computation | async-start | bytes 8388608
  30.9 7.3 %slice-start.1 = ((s8[4718592]{0:T(1024)(128)(4,1)}), s8[524288]{0:T(1024)(128)(4,1)S(1)}, s32[]{:S(2)}) async-start(s8[4718592]{0:T(1024)(128)(4,1)} %bitcast.19), calls=%async_computation.1 | async-start | bytes 1048576
  35.4 2.6 %collective-permute-start.15 = (bf16[2,512,256]{2,1,0:T(8,128)(2,1)S(1)}, bf16[2,512,256]{2,1,0:T(8,128)(2,1)S(1)}, u32[]{:S(2)}, u32[]{:S(2)}) collective-permute-start(bf16[2,512,256]{2,1,0:T(8,128)(2,1)S(1)} %shard_map.165.low.refs_0_), channel_id=1, source_target_pairs={{0,1},{1,0},{2,3},{3,2},{4,5},{5,4},{6,7},{7,6},{8,9},{9,8},{10,11... | collective-permute-start | bytes 1572872 | tf_op jit(solution)/shard_map/ppermute | solution.py:323
  35.9 9.2 %copy-start.1 = (f32[32,256]{1,0:T(8,128)S(1)}, f32[32,256]{1,0:T(8,128)}, u32[]{:S(2)}) copy-start(f32[32,256]{1,0:T(8,128)} %param.19) | copy-start | bytes 98308
  35.9 2.3 %collective-permute-start.16 = (bf16[2,512,256]{2,1,0:T(8,128)(2,1)S(1)}, bf16[2,512,256]{2,1,0:T(8,128)(2,1)S(1)}, u32[]{:S(2)}, u32[]{:S(2)}) collective-permute-start(bf16[2,512,256]{2,1,0:T(8,128)(2,1)S(1)} %get-tuple-element.115.high.refs_1_), channel_id=1, source_target_pairs={{0,1},{1,0},{2,3},{3,2},{4,5},{5,4},{6,7},{7,6},{8,9},{9,8},{10,11... | collective-permute-start | bytes 1572872 | tf_op jit(solution)/shard_map/ppermute | solution.py:323
  36.0 9.1 %collective-permute-start.13 = (bf16[2,256,256]{2,1,0:T(8,128)(2,1)S(1)}, bf16[2,256,256]{2,1,0:T(8,128)(2,1)S(1)}, u32[]{:S(2)}, u32[]{:S(2)}) collective-permute-start(bf16[2,256,256]{2,1,0:T(8,128)(2,1)S(1)} %get-tuple-element.114), channel_id=1, source_target_pairs={{0,2},{1,3},{2,0},{3,1},{4,6},{5,7},{6,4},{7,5},{8,10},{9,11},{10,... | collective-permute-start | bytes 786440 | tf_op jit(solution)/shard_map/ppermute | solution.py:323
  37.5 18.4 %collective-permute-start.12 = (bf16[2,512,256]{2,1,0:T(8,128)(2,1)S(1)}, bf16[2,512,256]{2,1,0:T(8,128)(2,1)S(1)}, u32[]{:S(2)}, u32[]{:S(2)}) collective-permute-start(bf16[2,512,256]{2,1,0:T(8,128)(2,1)S(1)} %shard_map.165.low.refs_0_), channel_id=1, source_target_pairs={{0,2},{1,3},{2,0},{3,1},{4,6},{5,7},{6,4},{7,5},{8,10},{9,11},{10,... | collective-permute-start | bytes 1572872 | tf_op jit(solution)/shard_map/ppermute | solution.py:323
  45.1 4.8 %collective-permute-start.17 = (bf16[2,256,256]{2,1,0:T(8,128)(2,1)S(1)}, bf16[2,256,256]{2,1,0:T(8,128)(2,1)S(1)}, u32[]{:S(2)}, u32[]{:S(2)}) collective-permute-start(bf16[2,256,256]{2,1,0:T(8,128)(2,1)S(1)} %collective-permute-done.13.picked.refs_5_), channel_id=1, source_target_pairs={{0,1},{1,0},{2,3},{3,2},{4,5},{5,4},{6,7},{7,6},{8,9},{9,8},{10,11... | collective-permute-start | bytes 786440 | tf_op jit(solution)/shard_map/ppermute | solution.py:323
  45.1 4.8 %collective-permute-start.18 = (f32[2,32,256]{2,1,0:T(8,128)S(1)}, f32[2,32,256]{2,1,0:T(8,128)S(1)}, u32[]{:S(2)}, u32[]{:S(2)}) collective-permute-start(f32[2,32,256]{2,1,0:T(8,128)S(1)} %pad_maximum_fusion.2), channel_id=1, source_target_pairs={{0,4},{4,0},{8,12},{12,8},{16,20},{20,16},{24,28},{28,24},{1,5},{5... | collective-permute-start | bytes 196616 | tf_op jit(solution)/shard_map/ppermute | solution.py:323
  46.7 9.2 %collective-permute-start.14 = (bf16[2,256,256]{2,1,0:T(8,128)(2,1)S(1)}, bf16[2,256,256]{2,1,0:T(8,128)(2,1)S(1)}, u32[]{:S(2)}, u32[]{:S(2)}) collective-permute-start(bf16[2,256,256]{2,1,0:T(8,128)(2,1)S(1)} %collective-permute-done.13.picked.refs_5_), channel_id=1, source_target_pairs={{0,4},{4,0},{8,12},{12,8},{16,20},{20,16},{24,28},{28,24},{1,5},{5... | collective-permute-start | bytes 786440 | tf_op jit(solution)/shard_map/ppermute | solution.py:323
  49.9 5.9 %collective-permute-start.19 = (f32[4,32,256]{2,1,0:T(8,128)S(1)}, f32[4,32,256]{2,1,0:T(8,128)S(1)}, u32[]{:S(2)}, u32[]{:S(2)}) collective-permute-start(f32[4,32,256]{2,1,0:T(8,128)S(1)} %pad_maximum_fusion.1), channel_id=1, source_target_pairs={{0,8},{4,12},{8,0},{12,4},{16,24},{20,28},{24,16},{28,20},{1,9},{5... | collective-permute-start | bytes 393224 | tf_op jit(solution)/shard_map/ppermute | solution.py:323
  55.9 2.7 %collective-permute-start.20 = (bf16[2,512,256]{2,1,0:T(8,128)(2,1)S(1)}, bf16[2,512,256]{2,1,0:T(8,128)(2,1)S(1)}, u32[]{:S(2)}, u32[]{:S(2)}) collective-permute-start(bf16[2,512,256]{2,1,0:T(8,128)(2,1)S(1)} %collective-permute-done.12.far.refs_4_), channel_id=1, source_target_pairs={{0,1},{1,0},{2,3},{3,2},{4,5},{5,4},{6,7},{7,6},{8,9},{9,8},{10,11... | collective-permute-start | bytes 1572872 | tf_op jit(solution)/shard_map/ppermute | solution.py:323
  55.9 2.7 %collective-permute-start.21 = (bf16[2,256,256]{2,1,0:T(8,128)(2,1)S(1)}, bf16[2,256,256]{2,1,0:T(8,128)(2,1)S(1)}, u32[]{:S(2)}, u32[]{:S(2)}) collective-permute-start(bf16[2,256,256]{2,1,0:T(8,128)(2,1)S(1)} %collective-permute-done.14.rest.refs_6_), channel_id=1, source_target_pairs={{0,1},{1,0},{2,3},{3,2},{4,5},{5,4},{6,7},{7,6},{8,9},{9,8},{10,11... | collective-permute-start | bytes 786440 | tf_op jit(solution)/shard_map/ppermute | solution.py:323
  65.8 2.7 %collective-permute-start.22 = (bf16[4,512,256]{2,1,0:T(8,128)(2,1)S(1)}, bf16[4,512,256]{2,1,0:T(8,128)(2,1)S(1)}, u32[]{:S(2)}, u32[]{:S(2)}) collective-permute-start(bf16[4,512,256]{2,1,0:T(8,128)(2,1)S(1)} %get-tuple-element.141.grad.one.refs_10_), channel_id=1, source_target_pairs={{0,1},{1,0},{2,3},{3,2},{4,5},{5,4},{6,7},{7,6},{8,9},{9,8},{10,11... | collective-permute-start | bytes 3145736 | tf_op jit(solution)/shard_map/ppermute | solution.py:323
  69.5 9.6 %collective-permute-start.24 = (bf16[2,256,256]{2,1,0:T(8,128)(2,1)S(1)}, bf16[2,256,256]{2,1,0:T(8,128)(2,1)S(1)}, u32[]{:S(2)}, u32[]{:S(2)}) collective-permute-start(bf16[2,256,256]{2,1,0:T(8,128)(2,1)S(1)} %shard_map.174), channel_id=1, source_target_pairs={{0,2},{1,3},{2,0},{3,1},{4,6},{5,7},{6,4},{7,5},{8,10},{9,11},{10,... | collective-permute-start | bytes 786440 | tf_op jit(solution)/shard_map/ppermute | solution.py:323
  79.1 14.4 %collective-permute-start.26 = (bf16[3,3,512,256]{3,2,1,0:T(8,128)(2,1)S(1)}, bf16[3,3,512,256]{3,2,1,0:T(8,128)(2,1)S(1)}, u32[]{:S(2)}, u32[]{:S(2)}) collective-permute-start(bf16[3,3,512,256]{3,2,1,0:T(8,128)(2,1)S(1)} %shard_map.161.refs_4_.weight), channel_id=1, source_target_pairs={{0,1},{1,0},{2,3},{3,2},{4,5},{5,4},{6,7},{7,6},{8,9},{9,8},{10,11... | collective-permute-start | bytes 7077896 | tf_op jit(solution)/shard_map/ppermute | solution.py:323
  79.2 14.3 %collective-permute-start.23 = (bf16[2,512,256]{2,1,0:T(8,128)(2,1)S(1)}, bf16[2,512,256]{2,1,0:T(8,128)(2,1)S(1)}, u32[]{:S(2)}, u32[]{:S(2)}) collective-permute-start(bf16[2,512,256]{2,1,0:T(8,128)(2,1)S(1)} %shard_map.173), channel_id=1, source_target_pairs={{0,2},{1,3},{2,0},{3,1},{4,6},{5,7},{6,4},{7,5},{8,10},{9,11},{10,... | collective-permute-start | bytes 1572872 | tf_op jit(solution)/shard_map/ppermute | solution.py:323
  79.7 12.1 %collective-permute-start.25 = (bf16[2,256,256]{2,1,0:T(8,128)(2,1)S(1)}, bf16[2,256,256]{2,1,0:T(8,128)(2,1)S(1)}, u32[]{:S(2)}, u32[]{:S(2)}) collective-permute-start(bf16[2,256,256]{2,1,0:T(8,128)(2,1)S(1)} %collective-permute-done.24.picked), channel_id=1, source_target_pairs={{0,4},{4,0},{8,12},{12,8},{16,20},{20,16},{24,28},{28,24},{1,5},{5... | collective-permute-start | bytes 786440 | tf_op jit(solution)/shard_map/ppermute | solution.py:323
  94.5 1.5 %collective-permute-start.27 = (bf16[4,96,256]{2,1,0:T(8,128)(2,1)S(1)}, bf16[4,96,256]{2,1,0:T(8,128)(2,1)S(1)}, u32[]{:S(2)}, u32[]{:S(2)}) collective-permute-start(bf16[4,96,256]{2,1,0:T(8,128)(2,1)S(1)} %get-tuple-element.155.one), channel_id=1, source_target_pairs={{0,1},{1,0},{2,3},{3,2},{4,5},{5,4},{6,7},{7,6},{8,9},{9,8},{10,11... | collective-permute-start | bytes 589832 | tf_op jit(solution)/shard_map/ppermute | solution.py:323
  97.0 6.0 %collective-permute-start.28 = (f32[4,64,128]{2,1,0:T(8,128)S(1)}, f32[4,64,128]{2,1,0:T(8,128)S(1)}, u32[]{:S(2)}, u32[]{:S(2)}) collective-permute-start(f32[4,64,128]{2,1,0:T(8,128)S(1)} %get-tuple-element.160), channel_id=1, source_target_pairs={{0,2},{1,3},{2,0},{3,1},{4,6},{5,7},{6,4},{7,5},{8,10},{9,11},{10,... | collective-permute-start | bytes 393224 | tf_op jit(solution)/shard_map/ppermute | solution.py:323
  (6 other events, 5.2 us)
